TPU v7x, 32 devices: a whole 2x2x4 slice. The times are simulated.
32 devices in a mesh: rep: 4 (over x, core), shard: 8 (over z, y).
Axes of the slice: x: 2, y: 2, z: 4, core: 2. Of those that a mesh axis runs over, the one named last changes fastest.
Arguments:
- inputs: bfloat16 [6144, 2048], P(('rep', 'shard')), may hold values from -6 to 6
- attn_gain: bfloat16 [2048], P('shard'), may hold values from 0.25 to 1.75
- in_proj: bfloat16 [2048, 6144], P('shard'), may hold values from -0.125 to 0.125
- query_gain: bfloat16 [2048], P('shard'), may hold values from 0.25 to 1.75
- key_gain: bfloat16 [2048], P('shard'), may hold values from 0.25 to 1.75
- out_proj: bfloat16 [2048, 2048], P('shard'), may hold values from -0.5 to 0.5
- ffn_gain: bfloat16 [2048], P('shard'), may hold values from 0.25 to 1.75
- router_weight: bfloat16 [2048, 32], P('shard'), may hold values from -0.0625 to 0.0625
- gate_weight: bfloat16 [32, 2048, 1024], P('shard'), may hold values from -0.125 to 0.125
- up_weight: bfloat16 [32, 2048, 1024], P('shard'), may hold values from -0.125 to 0.125
- down_weight: bfloat16 [32, 1024, 2048], P('shard'), may hold values from -3 to 3
- routes: int32 [6144, 8], P(('rep', 'shard')), may hold values from 0 to 31, all different within a row; in each aligned block of 192 rows (0 to 191, 192 to 383, ...) at most 96 rows name the same one
- priority: int32 [32, 1536], P(('rep', 'shard')), may hold values from 0 to 1535, each once within a row
- segments: int32 [32, 192], P(('rep', 'shard')), may hold values from 0 to 2, never falling along the last dimension, each value on 1 to 120 neighbouring positions
- grad_out: bfloat16 [6144, 2048], P(('rep', 'shard')), may hold values from -6 to 6
Outputs:
- outputs: bfloat16 [6144, 2048], P(('rep', 'shard'))
- grad_inputs: bfloat16 [6144, 2048], P(('rep', 'shard'))
- grad_attn_gain: float32 [2048], P('shard')
- grad_in_proj: float32 [2048, 6144], P('shard')
- grad_query_gain: float32 [2048], P('shard')
- grad_key_gain: float32 [2048], P('shard')
- grad_out_proj: float32 [2048, 2048], P('shard')
- grad_ffn_gain: float32 [2048], P('shard')
- grad_router: float32 [2048, 32], P('shard')
- grad_gate: float32 [32, 2048, 1024], P('shard')
- grad_up: float32 [32, 2048, 1024], P('shard')
- grad_down: float32 [32, 1024, 2048], P('shard')
Inputs may be any that keep to these rules, and one draw needn't show every extreme that they name: `routes`: each row names 8 different experts. Among the rows of one sequence no expert is named more than 96 times, and in some sequence some expert exactly 96 times. `priority`: each row is a permutation. `segments`: each row never falls and holds all 3 documents, each 1 to 120 positions long, one exactly 120.
All inputs are finite; a program needn't handle non-finite values.
Results may differ from a plain program's by a relative error of at most 0.02.
Values may be sent and summed in bfloat16 or wider, within the bound.
No kernel may reach another device: no remote copies, remote signals or barrier semaphores. Data moves between devices by JAX's collectives and lax.ppermute only.
A program may use at most 448 MiB of HBM per device.

v0:
```python
import jax
import jax.numpy as jnp
from jax import lax
from jax.sharding import PartitionSpec as P

HEADS = 16
HEAD_DIM = 128


norm_eps = 1e-05
rope_base = 10000.0
masked_score = -1e30


def rms_scale(values, gains):
    normed = values * lax.rsqrt(jnp.mean(values * values, axis=-1, keepdims=True) + norm_eps)
    return normed * gains


def rotary_tables(segment_row):
    length = segment_row.shape[0]
    places = jnp.arange(length, dtype=jnp.int32)
    starting = jnp.concatenate(
        [jnp.ones((1,), jnp.int32), (segment_row[1:] != segment_row[:-1]).astype(jnp.int32)]
    )
    first_place = lax.cummax(jnp.where(starting > 0, places, 0), axis=0)
    offsets = (places - first_place).astype(jnp.float32)
    halves = HEAD_DIM // 2
    inverse = rope_base ** (-2.0 * jnp.arange(halves, dtype=jnp.float32) / HEAD_DIM)
    angles = offsets[:, None] * inverse[None, :]
    angles = jnp.concatenate([angles, angles], axis=1)
    return (jnp.cos(angles), jnp.sin(angles))


def rotate(values, cos_table, sin_table):
    halves = values.shape[-1] // 2
    turned = jnp.concatenate([-values[..., halves:], values[..., :halves]], axis=-1)
    return values * cos_table[:, None, :] + turned * sin_table[:, None, :]


def query_key(raw_query, raw_key, query_scale, key_scale, cos_table, sin_table):
    row_count = raw_query.shape[0]
    normed_query = rms_scale(raw_query, query_scale).reshape(row_count, HEADS, HEAD_DIM)
    normed_key = rms_scale(raw_key, key_scale).reshape(row_count, HEADS, HEAD_DIM)
    return (rotate(normed_query, cos_table, sin_table), rotate(normed_key, cos_table, sin_table))


def softmax_rows(logits):
    highest = jnp.max(logits, axis=-1, keepdims=True)
    raised = jnp.exp(logits - highest)
    return raised / jnp.sum(raised, axis=-1, keepdims=True)


def swiglu(gate_pre, up_pre):
    return jax.nn.silu(gate_pre) * up_pre


def contract_rows(left_side, right_side):
    return lax.dot_general(
        left_side, right_side, (((0,), (0,)), ((), ())), preferred_element_type=jnp.float32
    )


def contract_cols(left_side, right_side):
    return lax.dot_general(
        left_side, right_side, (((1,), (1,)), ((), ())), preferred_element_type=jnp.float32
    )


def pick_rows(source_rows, row_picks):
    return jax.vmap(lambda expert_rows, picked: expert_rows[picked])(source_rows, row_picks)


def local(
    inputs,
    attn_gain,
    in_proj,
    query_gain,
    key_gain,
    out_proj,
    ffn_gain,
    router_weight,
    gate_weight,
    up_weight,
    down_weight,
    routes,
    priority,
    segments,
    grad_out,
):
    tokens = inputs.shape[0]
    model_width = inputs.shape[1]
    local_experts = gate_weight.shape[0]
    group_count = lax.axis_size("shard")
    my_index = lax.axis_index("shard")
    expert_count = local_experts * group_count
    route_count = routes.shape[1]
    pair_count = tokens * route_count
    capacity = 5 * pair_count * group_count // (4 * expert_count)
    send_most = 2 * pair_count // expert_count
    segment_row = segments[0]
    cos_table, sin_table = rotary_tables(segment_row)
    hidden_in = inputs.astype(jnp.float32)
    unit_rows = hidden_in * lax.rsqrt(
        jnp.mean(hidden_in * hidden_in, axis=-1, keepdims=True) + norm_eps
    )
    weight_piece = lax.all_gather(in_proj, "shard", axis=0, tiled=True)
    attn_piece = lax.all_gather(attn_gain, "shard", axis=0, tiled=True)
    query_piece = lax.all_gather(query_gain, "shard", axis=0, tiled=True)
    key_piece = lax.all_gather(key_gain, "shard", axis=0, tiled=True)
    scaled = (unit_rows * attn_piece.astype(jnp.float32)).astype(jnp.bfloat16)
    result = (
        jnp.dot(scaled, weight_piece, preferred_element_type=jnp.float32),
        attn_piece.astype(jnp.float32),
        query_piece.astype(jnp.float32),
        key_piece.astype(jnp.float32),
    )
    folded_in = result
    projected = folded_in[0]
    normed_attn, attn_norm_back = jax.vjp(rms_scale, hidden_in, folded_in[1])
    normed_low = normed_attn.astype(jnp.bfloat16)
    raw_query = projected[:, :model_width]
    raw_key = projected[:, model_width : 2 * model_width]
    raw_value = projected[:, 2 * model_width :]

    def rotated_pair(query_raw, key_raw, query_scale, key_scale):
        return query_key(query_raw, key_raw, query_scale, key_scale, cos_table, sin_table)

    (turned_query, turned_key), query_key_back = jax.vjp(
        rotated_pair, raw_query, raw_key, folded_in[2], folded_in[3]
    )
    query_low = turned_query.astype(jnp.bfloat16)
    key_low = turned_key.astype(jnp.bfloat16)
    value_low = raw_value.astype(jnp.bfloat16).reshape(tokens, HEADS, HEAD_DIM)
    places = jnp.arange(tokens, dtype=jnp.int32)
    allowed = (segment_row[:, None] == segment_row[None, :]) & (places[None, :] <= places[:, None])
    score_scale = HEAD_DIM ** (-0.5)

    def masked_scores(queries, key_vecs):
        products = jnp.einsum("qhd,khd->hqk", queries, key_vecs, preferred_element_type=jnp.float32)
        return jnp.where(allowed[None], products * score_scale, masked_score)

    scores = masked_scores(query_low, key_low)
    highest = jnp.max(scores, axis=-1, keepdims=True)
    raised = jnp.exp(scores - highest)
    totals = jnp.sum(raised, axis=-1, keepdims=True)
    attn_probs = raised / totals
    log_total = highest + jnp.log(totals)
    mixed = jnp.einsum(
        "hqk,khd->qhd",
        attn_probs.astype(jnp.bfloat16),
        value_low,
        preferred_element_type=jnp.float32,
    )
    attended = mixed.reshape(tokens, model_width).astype(jnp.bfloat16)
    weight_piece = lax.all_gather(out_proj, "shard", axis=0, tiled=True)
    ffn_piece = lax.all_gather(ffn_gain, "shard", axis=0, tiled=True)
    router_piece = lax.all_gather(router_weight, "shard", axis=0, tiled=True)
    result = (
        jnp.dot(attended, weight_piece, preferred_element_type=jnp.float32),
        ffn_piece.astype(jnp.float32),
        router_piece,
    )
    residual = hidden_in + result[0]
    router_full = result[2]
    normed_ffn, ffn_norm_back = jax.vjp(rms_scale, residual, result[1])
    ffn_low = normed_ffn.astype(jnp.bfloat16)
    logits = jnp.dot(ffn_low, router_full, preferred_element_type=jnp.float32)
    router_probs, router_back = jax.vjp(softmax_rows, logits)
    flat_routes = routes.reshape(pair_count)
    order_row = priority[0]
    ranked_expert = flat_routes[order_row]
    labels = jnp.arange(expert_count, dtype=jnp.int32)
    matches = (ranked_expert[:, None] == labels[None, :]).astype(jnp.int32)
    rank_in = (
        jnp.sum(jnp.cumsum(matches, axis=0, dtype=jnp.int32) * matches, axis=1, dtype=jnp.int32) - 1
    )
    counts = jnp.sum(matches, axis=0, dtype=jnp.int32)
    all_counts = lax.all_gather(counts[None, :], "shard", axis=0, tiled=True)
    base_slots = jnp.cumsum(all_counts, axis=0, dtype=jnp.int32) - all_counts
    my_bases = lax.dynamic_index_in_dim(base_slots, my_index, 0, keepdims=False)
    slot_index = jnp.sum(matches * my_bases[None, :], axis=1, dtype=jnp.int32) + rank_in
    cell_index = ranked_expert * send_most + rank_in
    inverse_order = (
        jnp.zeros((pair_count,), jnp.int32)
        .at[order_row]
        .set(jnp.arange(pair_count, dtype=jnp.int32))
    )
    pair_cell = cell_index[inverse_order].reshape(tokens, route_count)
    pair_keep = (
        (slot_index[inverse_order] < capacity).astype(jnp.float32).reshape(tokens, route_count)
    )
    cell_pair = jnp.zeros((expert_count * send_most,), jnp.int32).at[cell_index].set(order_row)
    cell_live = (jnp.arange(send_most, dtype=jnp.int32)[None, :] < counts[:, None]).reshape(
        expert_count * send_most
    )
    cell_token = cell_pair // route_count
    outgoing = jnp.where(cell_live[:, None], ffn_low[cell_token], 0).reshape(
        expert_count, send_most, model_width
    )
    arrived = lax.all_to_all(outgoing, "shard", split_axis=0, concat_axis=1, tiled=True)
    own_counts = lax.dynamic_slice_in_dim(all_counts, my_index * local_experts, local_experts, 1).T
    own_bases = lax.dynamic_slice_in_dim(base_slots, my_index * local_experts, local_experts, 1).T
    slot_ids = jnp.arange(capacity, dtype=jnp.int32)
    slot_ends = own_bases + own_counts
    source_ids = jnp.sum(
        (slot_ends[:, None, :] <= slot_ids[None, :, None]).astype(jnp.int32),
        axis=2,
        dtype=jnp.int32,
    )
    slot_filled = source_ids < group_count
    source_safe = jnp.minimum(source_ids, group_count - 1)
    slot_rows = (
        source_safe * send_most
        + slot_ids[None, :]
        - jnp.take_along_axis(own_bases, source_safe, axis=1)
    )
    slot_rows = jnp.where(slot_filled, slot_rows, 0)
    expert_in = jnp.where(slot_filled[..., None], pick_rows(arrived, slot_rows), 0)
    gate_pre = jnp.einsum(
        "ecd,edf->ecf", expert_in, gate_weight, preferred_element_type=jnp.float32
    )
    up_pre = jnp.einsum("ecd,edf->ecf", expert_in, up_weight, preferred_element_type=jnp.float32)
    activated, swiglu_back = jax.vjp(swiglu, gate_pre, up_pre)
    act_low = activated.astype(jnp.bfloat16)
    expert_out = jnp.einsum(
        "ecf,efd->ecd", act_low, down_weight, preferred_element_type=jnp.float32
    ).astype(jnp.bfloat16)
    cell_positions = jnp.arange(send_most, dtype=jnp.int32)
    cell_slot = own_bases[:, :, None] + cell_positions[None, None, :]
    cell_used = (cell_positions[None, None, :] < own_counts[:, :, None]) & (cell_slot < capacity)
    cell_slot = jnp.where(cell_used, cell_slot, 0).reshape(local_experts, group_count * send_most)
    cell_used = cell_used.reshape(local_experts, group_count * send_most)
    returning = jnp.where(cell_used[..., None], pick_rows(expert_out, cell_slot), 0)
    returned = lax.all_to_all(returning, "shard", split_axis=1, concat_axis=0, tiled=True).reshape(
        expert_count * send_most, model_width
    )
    pair_rows = returned[pair_cell].astype(jnp.float32)
    pair_weight = jnp.take_along_axis(router_probs, routes, axis=1) * pair_keep
    outputs = (residual + jnp.sum(pair_weight[..., None] * pair_rows, axis=1)).astype(jnp.bfloat16)
    cotangent = grad_out.astype(jnp.float32)
    grad_rows = (
        (pair_weight[..., None] * cotangent[:, None, :])
        .astype(jnp.bfloat16)
        .reshape(pair_count, model_width)
    )
    grad_pair_weight = jnp.sum(pair_rows * cotangent[:, None, :], axis=2) * pair_keep
    route_hits = (routes[..., None] == labels[None, None, :]).astype(jnp.float32)
    grad_router_probs = jnp.sum(grad_pair_weight[..., None] * route_hits, axis=1)
    (grad_logits,) = router_back(grad_router_probs)
    grad_logits_low = grad_logits.astype(jnp.bfloat16)
    outgoing_grad = jnp.where(cell_live[:, None], grad_rows[cell_pair], 0).reshape(
        expert_count, send_most, model_width
    )
    arrived_grad = lax.all_to_all(outgoing_grad, "shard", split_axis=0, concat_axis=1, tiled=True)
    grad_expert_out = jnp.where(slot_filled[..., None], pick_rows(arrived_grad, slot_rows), 0)
    grad_act = jnp.einsum(
        "ecd,efd->ecf", grad_expert_out, down_weight, preferred_element_type=jnp.float32
    )
    grad_down = jnp.einsum(
        "ecf,ecd->efd", act_low, grad_expert_out, preferred_element_type=jnp.float32
    )
    grad_gate_pre, grad_up_pre = swiglu_back(grad_act)
    gate_grad_low = grad_gate_pre.astype(jnp.bfloat16)
    up_grad_low = grad_up_pre.astype(jnp.bfloat16)
    grad_gate = jnp.einsum(
        "ecd,ecf->edf", expert_in, gate_grad_low, preferred_element_type=jnp.float32
    )
    grad_up = jnp.einsum("ecd,ecf->edf", expert_in, up_grad_low, preferred_element_type=jnp.float32)
    grad_expert_in = (
        jnp.einsum("ecf,edf->ecd", gate_grad_low, gate_weight, preferred_element_type=jnp.float32)
        + jnp.einsum("ecf,edf->ecd", up_grad_low, up_weight, preferred_element_type=jnp.float32)
    ).astype(jnp.bfloat16)
    returning_grad = jnp.where(cell_used[..., None], pick_rows(grad_expert_in, cell_slot), 0)
    returned_grad = lax.all_to_all(
        returning_grad, "shard", split_axis=1, concat_axis=0, tiled=True
    ).reshape(expert_count * send_most, model_width)
    grad_ffn_in = jnp.sum(returned_grad[pair_cell].astype(jnp.float32), axis=1) + contract_cols(
        grad_logits_low, router_full
    )
    grad_router_local = contract_rows(ffn_low, grad_logits_low)
    grad_residual_norm, grad_ffn_local = ffn_norm_back(grad_ffn_in)
    grad_residual = cotangent + grad_residual_norm
    residual_low = grad_residual.astype(jnp.bfloat16)
    grad_out_local = lax.psum_scatter(
        contract_rows(attended, residual_low).astype(jnp.bfloat16),
        "shard",
        scatter_dimension=0,
        tiled=True,
    )
    grad_attended = contract_cols(
        residual_low, lax.all_gather(out_proj, "shard", axis=0, tiled=True)
    )
    grad_mixed = grad_attended.astype(jnp.bfloat16).reshape(tokens, HEADS, HEAD_DIM)
    scores_again = masked_scores(query_low, key_low)
    probs_again = jnp.exp(scores_again - log_total)
    grad_probs = jnp.einsum(
        "qhd,khd->hqk", grad_mixed, value_low, preferred_element_type=jnp.float32
    )
    spread = jnp.sum(probs_again * grad_probs, axis=-1, keepdims=True)
    grad_scores = (probs_again * (grad_probs - spread)).astype(jnp.bfloat16)
    grad_query = (
        jnp.einsum("hqk,khd->qhd", grad_scores, key_low, preferred_element_type=jnp.float32)
        * score_scale
    )
    grad_key = (
        jnp.einsum("hqk,qhd->khd", grad_scores, query_low, preferred_element_type=jnp.float32)
        * score_scale
    )
    grad_value = jnp.einsum(
        "hqk,qhd->khd",
        probs_again.astype(jnp.bfloat16),
        grad_mixed,
        preferred_element_type=jnp.float32,
    )
    grad_raw_query, grad_raw_key, grad_query_local, grad_key_local = query_key_back(
        (grad_query, grad_key)
    )
    grad_qkv = jnp.concatenate(
        [grad_raw_query, grad_raw_key, grad_value.reshape(tokens, model_width)], axis=1
    ).astype(jnp.bfloat16)
    grad_in_local = lax.psum_scatter(
        contract_rows(normed_low, grad_qkv).astype(jnp.bfloat16),
        "shard",
        scatter_dimension=0,
        tiled=True,
    )
    grad_normed = contract_cols(grad_qkv, lax.all_gather(in_proj, "shard", axis=0, tiled=True))
    grad_hidden_norm, grad_attn_local = attn_norm_back(grad_normed)
    grad_inputs = (grad_residual + grad_hidden_norm).astype(jnp.bfloat16)
    small_parts = (
        lax.psum_scatter(
            grad_attn_local.astype(jnp.bfloat16), "shard", scatter_dimension=0, tiled=True
        ).astype(jnp.float32),
        lax.psum_scatter(
            grad_query_local.astype(jnp.bfloat16), "shard", scatter_dimension=0, tiled=True
        ).astype(jnp.float32),
        lax.psum_scatter(
            grad_key_local.astype(jnp.bfloat16), "shard", scatter_dimension=0, tiled=True
        ).astype(jnp.float32),
        lax.psum_scatter(
            grad_ffn_local.astype(jnp.bfloat16), "shard", scatter_dimension=0, tiled=True
        ).astype(jnp.float32),
        lax.psum_scatter(
            grad_router_local.astype(jnp.bfloat16), "shard", scatter_dimension=0, tiled=True
        ).astype(jnp.float32),
    )
    summed = (
        lax.psum(grad_in_local, "rep").astype(jnp.float32),
        lax.psum(grad_out_local, "rep").astype(jnp.float32),
        lax.psum(small_parts[0].astype(jnp.bfloat16), "rep").astype(jnp.float32),
        lax.psum(small_parts[1].astype(jnp.bfloat16), "rep").astype(jnp.float32),
        lax.psum(small_parts[2].astype(jnp.bfloat16), "rep").astype(jnp.float32),
        lax.psum(small_parts[3].astype(jnp.bfloat16), "rep").astype(jnp.float32),
        lax.psum(small_parts[4].astype(jnp.bfloat16), "rep").astype(jnp.float32),
        lax.psum(grad_gate.astype(jnp.bfloat16), "rep").astype(jnp.float32),
        lax.psum(grad_up.astype(jnp.bfloat16), "rep").astype(jnp.float32),
        lax.psum(grad_down.astype(jnp.bfloat16), "rep").astype(jnp.float32),
    )
    return (
        outputs,
        grad_inputs,
        summed[2],
        summed[0],
        summed[3],
        summed[4],
        summed[1],
        summed[5],
        summed[6],
        summed[7],
        summed[8],
        summed[9],
    )


def solution(mesh):
    in_specs = (
        P(("rep", "shard"), None),
        P("shard"),
        P("shard", None),
        P("shard"),
        P("shard"),
        P("shard", None),
        P("shard"),
        P("shard", None),
        P("shard", None, None),
        P("shard", None, None),
        P("shard", None, None),
        P(("rep", "shard"), None),
        P(("rep", "shard"), None),
        P(("rep", "shard"), None),
        P(("rep", "shard"), None),
    )
    out_specs = (
        P(("rep", "shard"), None),
        P(("rep", "shard"), None),
        P("shard"),
        P("shard", None),
        P("shard"),
        P("shard"),
        P("shard", None),
        P("shard"),
        P("shard", None),
        P("shard", None, None),
        P("shard", None, None),
        P("shard", None, None),
    )
    return jax.shard_map(local, mesh=mesh, in_specs=in_specs, out_specs=out_specs, check_vma=False)
```

profile of v0, /device:TPU:0, one launch (start us, length us, event | category | flops | bytes accessed | tf_op | source)
XLA Modules:
  0.0 3903.5 jit_solution(6018240902476169997)
XLA Ops:
  8.8 49.9 %all-gather.1 = bf16[8,1,256]{2,1,0:T(2,128)(2,1)S(1)} all-gather(bf16[1,1,256]{2,1,0:T(2,128)(2,1)S(1)} %reshape.794), channel_id=1, replica_groups=mesh['rep'=4,'shard'=8] {'shard'}, dimensions={0}, use_global_device_ids=true | all-gather | bytes 4608 | tf_op jit(solution)/shard_map/all_gather | solution.py:108
  58.8 21.9 all-gather.3
  80.7 22.8 all-gather.2
  104.1 27.4 all-gather.4
  142.1 9.6 all-reduce.5
  183.1 40.8 %all_gather.33 = bf16[2048,32]{0,1:T(8,128)(2,1)S(1)} all-gather(bf16[256,32]{0,1:T(8,128)(2,1)S(1)} %copy-done.62), channel_id=1, replica_groups=mesh['rep'=4,'shard'=8] {'shard'}, dimensions={0}, use_global_device_ids=true | all-gather | bytes 147456 | tf_op jit(solution)/shard_map/all_gather | solution.py:158
  225.8 270.0 %all-gather.8.cloned.1.call-done = bf16[2048,6144]{1,0:T(8,128)(2,1)} async-done(((bf16[256,6144]{1,0:T(8,128)(2,1)}), bf16[2048,6144]{1,0:T(8,128)(2,1)}) %all-gather.8.cloned.1.call-update) | async-done | bytes 25165840 | tf_op jit(solution)/shard_map/all_gather | solution.py:107
  495.9 11.1 fusion.75
  516.1 106.8 %all-gather.10.cloned.1.call-done = bf16[2048,2048]{1,0:T(8,128)(2,1)} async-done(((bf16[256,2048]{1,0:T(8,128)(2,1)}), bf16[2048,2048]{1,0:T(8,128)(2,1)}) %all-gather.10.cloned.1.call-update) | async-done | bytes 8388624 | tf_op jit(solution)/shard_map/all_gather | solution.py:156
  630.7 12.7 gather_fusion.7
  643.9 15.7 gather_fusion.2
  663.2 27.6 gather_fusion.5
  690.8 13.5 broadcast_select_fusion
  704.2 276.4 %all_to_all.66 = bf16[32,96,2048]{2,1,0:T(8,128)(2,1)} all-to-all(bf16[32,96,2048]{2,1,0:T(8,128)(2,1)S(1)} %get-tuple-element.84), channel_id=1, replica_groups=mesh['rep'=4,'shard'=8] {'shard'}, dimensions={0} | all-to-all | bytes 25165824 | tf_op jit(solution)/shard_map/all_to_all | solution.py:201
  996.6 10.8 copy.249
  1007.4 61.9 %gather_fusion.9 = bf16[1920,2048]{1,0:T(8,128)(2,1)} fusion(bf16[4,768,2048]{2,1,0:T(8,128)(2,1)} %bitcast.228, s32[1920]{0:T(1024)S(1)} %reshape.736), kind=kCustom, calls=%fused_computation.9 | custom fusion | bytes 15744000 | tf_op jit(solution)/shard_map/vmap()/gather | solution.py:71
  1069.3 16.2 fusion.9
  1085.5 16.2 fusion.8
  1101.7 156.6 %all-to-all-done.2 = bf16[32,96,2048]{2,1,0:T(8,128)(2,1)} async-done(((bf16[32,96,2048]{2,1,0:T(8,128)(2,1)}), bf16[32,96,2048]{2,1,0:T(8,128)(2,1)}, u32[]{:S(2)}, u32[]{:S(2)}) %all-to-all-start.2) | async-done | bytes 12582944 | tf_op jit(solution)/shard_map/all_to_all | solution.py:255
  1258.3 10.7 copy.257
  1269.0 62.2 %gather_fusion.11 = bf16[1920,2048]{1,0:T(8,128)(2,1)} fusion(bf16[4,768,2048]{2,1,0:T(8,128)(2,1)} %bitcast.227, s32[1920]{0:T(1024)S(1)} %reshape.736), kind=kCustom, calls=%fused_computation.11 | custom fusion | bytes 15744000 | tf_op jit(solution)/shard_map/vmap()/gather | solution.py:71
  1331.2 23.5 multiply_convert_fusion
  1354.6 16.4 fusion.123
  1371.0 17.1 convolution_convert_fusion.5
  1388.1 18.9 add_convert_fusion
  1407.0 127.5 %gather_fusion.12 = bf16[3072,2048]{1,0:T(8,128)(2,1)} fusion(bf16[4,480,2048]{2,1,0:T(8,128)(2,1)} %add_convert_fusion, s32[3072]{0:T(1024)S(1)} %copy-done.4), kind=kCustom, calls=%fused_computation.12 | custom fusion | bytes 25190400 | tf_op jit(solution)/shard_map/vmap()/gather | solution.py:71
  1534.5 127.4 %gather_fusion.10 = bf16[3072,2048]{1,0:T(8,128)(2,1)} fusion(bf16[4,480,2048]{2,1,0:T(8,128)(2,1)} %convolution_convert_fusion.5, s32[3072]{0:T(1024)S(1)} %copy-done.4), kind=kCustom, calls=%fused_computation.10 | custom fusion | bytes 25190400 | tf_op jit(solution)/shard_map/vmap()/gather | solution.py:71
  1661.9 32.5 copy_select_fusion
  1694.4 294.6 %all_to_all.67 = bf16[4,768,2048]{2,0,1:T(4,128)(2,1)} all-to-all(bf16[4,768,2048]{2,0,1:T(4,128)(2,1)S(1)} %get-tuple-element.76), channel_id=1, replica_groups=mesh['rep'=4,'shard'=8] {'shard'}, dimensions={1} | all-to-all | bytes 25165824 | tf_op jit(solution)/shard_map/all_to_all | solution.py:275
  2003.7 14.5 copy.259
  2018.2 18.9 gather_fusion.6
  2046.0 219.7 %all-to-all-done.1 = bf16[4,768,2048]{2,0,1:T(4,128)(2,1)} async-done(((bf16[4,768,2048]{2,0,1:T(4,128)(2,1)}), bf16[4,768,2048]{2,0,1:T(4,128)(2,1)}, u32[]{:S(2)}, u32[]{:S(2)}) %all-to-all-start.1) | async-done | bytes 12582944 | tf_op jit(solution)/shard_map/all_to_all | solution.py:235
  2265.7 14.9 copy.251
  2280.6 19.0 gather_fusion.4
  2337.5 14.3 convolution_convert_fusion
  2352.5 16.3 convolution_convert_fusion.3
  2368.7 16.1 convolution_convert_fusion.2
  2385.8 16.7 convolution_convert_fusion.1
  2402.6 63.4 %reduce-scatter.6.cloned.1.call-done = bf16[256,2048]{1,0:T(8,128)(2,1)} async-done(((bf16[2048,2048]{1,0:T(8,128)(2,1)}), bf16[256,2048]{1,0:T(8,128)(2,1)}) %reduce-scatter.6.cloned.1.call-update) | async-done | bytes 1048592 | tf_op jit(solution)/shard_map/reduce_scatter | solution.py:285
  2465.9 407.6 %reduce-scatter.4.cloned.1.call-done = bf16[256,6144]{1,0:T(8,128)(2,1)} async-done(((bf16[2048,6144]{1,0:T(8,128)(2,1)}), bf16[256,6144]{1,0:T(8,128)(2,1)}) %reduce-scatter.4.cloned.1.call-update) | async-done | bytes 3145744 | tf_op jit(solution)/shard_map/reduce_scatter | solution.py:322
  2874.7 14.6 fusion.21
  2889.3 35.1 all-reduce.10
  2927.5 10.0 reduce-scatter.8.cloned.1.call-done
  2937.5 10.3 all-reduce.11
  2950.7 890.3 %all-reduce.15.cloned.1.call-done = (bf16[256,6144]{1,0:T(8,128)(2,1)}, bf16[256,2048]{1,0:T(8,128)(2,1)}, bf16[4,2048,1024]{2,1,0:T(8,128)(2,1)}, bf16[4,2048,1024]{2,1,0:T(8,128)(2,1)}, bf16[4,1024,2048]{2,1,0:T(8,128)(2,1)}) async-done(((bf16[256,6144]{1,0:T(8,128)(2,1)}, bf16[256,2048]{1,0:T(8,128)(2,1)}, bf16[4,2048,1024]{2,1,0:T(8,128)(2,1)}, bf16[4,2048,1024]{2,1,0:T(8,128)(2,1)}, ...) | async-done | bytes 54525968 | tf_op jit(solution)/shard_map/psum | solution.py:349
  3848.1 23.5 convert_element_type.246
  3871.6 13.1 convert_element_type.248
  3884.7 11.6 convert_element_type.250
  (371 shorter events, 157.3 us)
Async XLA Ops:
  7.2 51.6 %copy-start.85 = (bf16[256]{0:T(256)(128)(2,1)S(1)}, bf16[256]{0:T(256)(128)(2,1)}, u32[]{:S(2)}) copy-start(bf16[256]{0:T(256)(128)(2,1)} %param.19) | copy-start | bytes 1540
  7.2 73.4 %copy-start.86 = (bf16[256]{0:T(256)(128)(2,1)S(1)}, bf16[256]{0:T(256)(128)(2,1)}, u32[]{:S(2)}) copy-start(bf16[256]{0:T(256)(128)(2,1)} %param.18) | copy-start | bytes 1540
  7.2 96.2 %copy-start.63 = (s32[1,192]{1,0:T(1,128)S(1)}, s32[1,192]{1,0:T(1,128)}, u32[]{:S(2)}) copy-start(s32[1,192]{1,0:T(1,128)} %param.28) | copy-start | bytes 2308
  7.2 96.9 %copy-start.87 = (bf16[256]{0:T(256)(128)(2,1)S(1)}, bf16[256]{0:T(256)(128)(2,1)}, u32[]{:S(2)}) copy-start(bf16[256]{0:T(256)(128)(2,1)} %param.21) | copy-start | bytes 1540
  7.2 124.3 %copy-start.20 = (bf16[192,2048]{1,0:T(8,128)(2,1)S(1)}, bf16[192,2048]{1,0:T(8,128)(2,1)}, u32[]{:S(2)}) copy-start(bf16[192,2048]{1,0:T(8,128)(2,1)} %param.29) | copy-start | bytes 2359300
  7.2 124.5 %copy-start.44 = (s32[192,8]{0,1:T(8,128)S(1)}, s32[192,8]{0,1:T(8,128)}, u32[]{:S(2)}) copy-start(s32[192,8]{0,1:T(8,128)} %param.26) | copy-start | bytes 18436
  7.3 124.7 %copy-start.57 = (s32[1,1536]{1,0:T(1,128)S(1)}, s32[1,1536]{1,0:T(1,128)}, u32[]{:S(2)}) copy-start(s32[1,1536]{1,0:T(1,128)} %param.27) | copy-start | bytes 18436
  7.3 488.6 %all-gather.8.cloned.1.call-start = ((), (), s32[]{:S(2)}) async-start(), calls=%async_computation.7 | async-start | bytes 28311552 | tf_op jit(solution)/shard_map/all_gather | solution.py:107
  8.0 614.9 %all-gather.10.cloned.1.call-start = ((), (), s32[]{:S(2)}) async-start(), calls=%async_computation.8 | async-start | bytes 9437184 | tf_op jit(solution)/shard_map/all_gather | solution.py:156
  58.8 437.1 %copy-start.34 = (f32[8,1,256]{2,1,0:T(1,128)}, f32[8,1,256]{2,1,0:T(1,128)S(1)}, u32[]{:S(2)}) copy-start(f32[8,1,256]{2,1,0:T(1,128)S(1)} %convert_element_type.253) | copy-start | bytes 24580
  80.7 428.5 %copy-start.38 = (f32[8,1,256]{2,1,0:T(1,128)}, f32[8,1,256]{2,1,0:T(1,128)S(1)}, u32[]{:S(2)}) copy-start(f32[8,1,256]{2,1,0:T(1,128)S(1)} %convert_element_type.255) | copy-start | bytes 24580
  103.5 405.7 %copy-start.40 = (f32[8,1,256]{2,1,0:T(1,128)}, f32[8,1,256]{2,1,0:T(1,128)S(1)}, u32[]{:S(2)}) copy-start(f32[8,1,256]{2,1,0:T(1,128)S(1)} %convert_element_type.254) | copy-start | bytes 24580
  131.5 496.9 %copy-start.42 = (f32[8,1,256]{2,1,0:T(1,128)}, f32[8,1,256]{2,1,0:T(1,128)S(1)}, u32[]{:S(2)}) copy-start(f32[8,1,256]{2,1,0:T(1,128)S(1)} %convert_element_type.256) | copy-start | bytes 24580
  131.7 527.9 %copy-start.8 = (f32[192,2048]{1,0:T(8,128)}, f32[192,2048]{1,0:T(8,128)S(1)}, u32[]{:S(2)}) copy-start(f32[192,2048]{1,0:T(8,128)S(1)} %convert_element_type.218) | copy-start | bytes 4718596
  151.8 15.8 copy-start.51
  151.9 16.1 copy-start.64
  168.0 15.1 copy-start.62
  168.0 57.4 %copy-start.12 = (bf16[192,2048]{1,0:T(8,128)(2,1)S(1)}, bf16[192,2048]{1,0:T(8,128)(2,1)}, u32[]{:S(2)}) copy-start(bf16[192,2048]{1,0:T(8,128)(2,1)} %param.15) | copy-start | bytes 2359300
  176.6 467.0 %copy-start.58 = (pred[192,8]{0,1:T(8,128)(4,1)}, pred[192,8]{0,1:T(8,128)(4,1)S(1)}, u32[]{:S(2)}) copy-start(pred[192,8]{0,1:T(8,128)(4,1)S(1)} %copy.242) | copy-start | bytes 4612
  224.0 404.7 %copy-start.24 = (bf16[2048,32]{0,1:T(8,128)(2,1)}, bf16[2048,32]{0,1:T(8,128)(2,1)S(1)}, u32[]{:S(2)}) copy-start(bf16[2048,32]{0,1:T(8,128)(2,1)S(1)} %all_gather.33) | copy-start | bytes 393220
  225.6 281.4 %copy-start.72 = (f32[192]{0:T(256)}, f32[192]{0:T(256)S(1)}, u32[]{:S(2)}) copy-start(f32[192]{0:T(256)S(1)} %fusion.29) | copy-start | bytes 2308
  225.6 281.4 %copy-start.53 = (f32[192]{0:T(256)}, f32[192]{0:T(256)S(1)}, u32[]{:S(2)}) copy-start(f32[192]{0:T(256)S(1)} %fusion.103) | copy-start | bytes 2308
  516.1 112.3 %copy-start.22 = (bf16[16,24,8,128]{3,2,1,0:T(8,128)(2,1)}, bf16[16,24,8,128]{3,2,1,0:T(8,128)(2,1)S(1)}, u32[]{:S(2)}) copy-start(bf16[16,24,8,128]{3,2,1,0:T(8,128)(2,1)S(1)} %fusion.49) | copy-start | bytes 2359300
  628.6 15.2 copy-start
  629.0 14.4 copy-start.55
  629.6 13.9 copy-start.60
  643.8 15.9 copy-start.27
  980.7 277.6 %all-to-all-start.2 = ((bf16[32,96,2048]{2,1,0:T(8,128)(2,1)}), bf16[32,96,2048]{2,1,0:T(8,128)(2,1)}, u32[]{:S(2)}, u32[]{:S(2)}) async-start(bf16[32,96,2048]{2,1,0:T(8,128)(2,1)} %get-tuple-element.83), calls=%async_computation.2 | async-start | bytes 25165824 | tf_op jit(solution)/shard_map/all_to_all | solution.py:255
  996.6 334.5 %copy-start.81 = (pred[4,480]{1,0:T(4,128)(4,1)}, pred[4,480]{1,0:T(4,128)(4,1)S(1)}, u32[]{:S(2)}) copy-start(pred[4,480]{1,0:T(4,128)(4,1)S(1)} %broadcast_compare_fusion.1) | copy-start | bytes 5764
  1371.0 17.1 copy-start.88
  1388.1 18.9 copy-start.4
  1534.5 127.4 %copy-start.33 = (pred[4,768]{0,1:T(8,128)(4,1)S(1)}, pred[4,768]{0,1:T(8,128)(4,1)}, u32[]{:S(2)}) copy-start(pred[4,768]{0,1:T(8,128)(4,1)} %fusion.72) | copy-start | bytes 9220
  1989.0 276.7 %all-to-all-start.1 = ((bf16[4,768,2048]{2,0,1:T(4,128)(2,1)}), bf16[4,768,2048]{2,0,1:T(4,128)(2,1)}, u32[]{:S(2)}, u32[]{:S(2)}) async-start(bf16[4,768,2048]{2,0,1:T(4,128)(2,1)} %get-tuple-element.77), calls=%async_computation.1 | async-start | bytes 25165824 | tf_op jit(solution)/shard_map/all_to_all | solution.py:235
  1994.6 471.4 %reduce-scatter.6.cloned.1.call-start = ((), (), s32[]{:S(2)}) async-start(), calls=%async_computation.10 | async-start | bytes 9437184 | tf_op jit(solution)/shard_map/reduce_scatter | solution.py:285
  2280.6 19.0 copy-start.9
  2280.6 19.0 copy-start.28
  2318.7 554.9 %reduce-scatter.4.cloned.1.call-start = ((), (), s32[]{:S(2)}) async-start(), calls=%async_computation.9 | async-start | bytes 28311552 | tf_op jit(solution)/shard_map/reduce_scatter | solution.py:322
  2351.8 585.7 %reduce-scatter.8.cloned.1.call-start = ((), (), s32[]{:S(2)}) async-start(), calls=%async_computation.11 | async-start | bytes 147456 | tf_op jit(solution)/shard_map/reduce_scatter | solution.py:344
  2368.7 16.1 copy-start.1
  2385.8 1455.3 %all-reduce.15.cloned.1.call-start = ((), (), s32[]{:S(2)}) async-start(), calls=%async_computation.12 | async-start | bytes 109051904 | tf_op jit(solution)/shard_map/psum | solution.py:349
  2874.7 50.1 %copy-start.73 = (f32[192]{0:T(256)S(1)}, f32[192]{0:T(256)}, u32[]{:S(2)}) copy-start(f32[192]{0:T(256)} %copy-done.72) | copy-start | bytes 2308
  3846.5 25.1 slice-start.6
  3848.0 23.5 slice-start.7
  3848.0 23.5 slice-start.8
  3848.0 23.5 slice-start.9
  3848.1 36.6 slice-start.2
  3848.1 36.6 slice-start.3
  3871.6 13.1 slice-start.4
  (59 other events, 237.9 us)
Sparse Core Ops, SparseCore 0:
  9.6 486.2 all-gather.7
  498.0 124.8 all-gather.9
  2318.8 147.1 reduce-scatter.5
  2470.7 402.7 reduce-scatter.3
  2877.1 60.4 reduce-scatter.7
  2941.3 899.7 all-reduce.14
where the time goes:
time: 3910 us; the launch traced here: 3900 us
  waiting for transfers between devices  2130 us (54%)
  blocking collectives  789 us (20%)
  local copies, waits for them, and re-layouts  583 us (15%)
  matrix products  223 us (6%)
  other arithmetic  154 us (4%)
    psum x1, waiting for transfers between devices, local(): lax.psum(grad_in_local, 'rep').astype(jnp.float32)  890 us
    reduce_scatter x1, waiting for transfers between devices, local(): lax.psum_scatter(contract_rows(normed_low, grad_qkv).astype(jnp.bfloat16)...  408 us
    gather x6, local copies, waits for them, and re-layouts, pick_rows(): expert_rows[picked]  380 us
    all_to_all x1, blocking collectives, local(): lax.all_to_all(returning_grad, 'shard', split_axis=1, concat_axis=0, tile...  295 us
    all_to_all x1, blocking collectives, local(): lax.all_to_all(outgoing, 'shard', split_axis=0, concat_axis=1, tiled=True)  276 us
    all_gather x1, waiting for transfers between devices, local(): weight_piece = lax.all_gather(in_proj, 'shard', axis=0, tiled=True)  270 us
    all_to_all x1, waiting for transfers between devices, local(): lax.all_to_all(returning, 'shard', split_axis=1, concat_axis=0, tiled=True)  220 us
    all_to_all x1, waiting for transfers between devices, local(): lax.all_to_all(outgoing_grad, 'shard', split_axis=0, concat_axis=1, tiled...  157 us
  transfers between devices with their start and end apart: 8, of which 8 were waited for; matrix products, arithmetic and copies ran while one was open for 8% of the time, Pallas kernels for 0%

commit v1 on v0

--- a/solution.py
+++ b/solution.py
@@ -373,7 +373,458 @@
     )
 
 
+AXES = ("rep", "shard")
+LINE = 4
+SHARDS = 8
+STAGES = ((3, 2, 1, 0), (0, 3, 2, 1), (3, 0, 1, 2), (0, 1, 2, 3))
+
+
+def pairs_of(target):
+    moves = []
+    for rep in range(4):
+        for shard in range(SHARDS):
+            there = target(rep, shard)
+            if there is not None:
+                moves.append((rep * SHARDS + shard, there[0] * SHARDS + there[1]))
+    return moves
+
+
+CORE_SWAP = pairs_of(lambda rep, shard: (rep ^ 1, shard))
+X_SWAP = pairs_of(lambda rep, shard: (rep ^ 2, shard))
+Y_SWAP = pairs_of(lambda rep, shard: (rep, shard ^ 1))
+
+
+def move(values, moves):
+    return lax.ppermute(values, AXES, moves)
+
+
+def in_order(own, other, position):
+    return jnp.where(position == 0, jnp.stack([own, other]), jnp.stack([other, own]))
+
+
+def z_ring(step):
+    return pairs_of(lambda rep, shard: (rep, (shard + 2 * step) % SHARDS))
+
+
+def gather_small(values, z, y):
+    both = in_order(values, move(values, Y_SWAP), y)
+    whole = jnp.zeros((LINE,) + both.shape, both.dtype)
+    for step in range(LINE):
+        piece = both if step == 0 else move(both, z_ring(step))
+        whole = lax.dynamic_update_index_in_dim(whole, piece, lax.rem(z - step + LINE, LINE), 0)
+    return whole.reshape((SHARDS,) + values.shape)
+
+
+def scatter_small(values, z, y):
+    pieces = values.reshape((LINE, 2) + values.shape[1:])
+    mine = lax.dynamic_index_in_dim(pieces, y, 1, keepdims=False)
+    theirs = lax.dynamic_index_in_dim(pieces, 1 - y, 1, keepdims=False)
+    mine = mine + move(theirs, Y_SWAP)
+    total = lax.dynamic_index_in_dim(mine, z, 0, keepdims=False)
+    for step in range(1, LINE):
+        piece = lax.dynamic_index_in_dim(mine, lax.rem(z + step, LINE), 0, keepdims=False)
+        total = total + move(piece, z_ring(step))
+    return total
+
+
+def gather_rows(values, z, y):
+    z_up = pairs_of(lambda rep, shard: (rep, shard + 2) if shard + 2 < SHARDS else None)
+    z_down = pairs_of(lambda rep, shard: (rep, shard - 2) if shard >= 2 else None)
+    up, down = [values], [values]
+    other = [move(values, Y_SWAP)]
+    for step in range(1, LINE):
+        up.append(move(up[-1], z_up))
+        down.append(move(down[-1], z_down))
+    up_other, down_other = [None], [None]
+    for step in range(1, LINE):
+        from_low = lambda rep, shard: (rep, shard ^ 1) if shard // 2 >= step else None
+        from_high = lambda rep, shard: (rep, shard ^ 1) if shard // 2 + step < LINE else None
+        up_other.append(move(up[step], pairs_of(from_low)))
+        down_other.append(move(down[step], pairs_of(from_high)))
+    whole = jnp.zeros((LINE, 2) + values.shape, values.dtype)
+    for step in range(LINE):
+        if step == 0:
+            own, beside = values, other[0]
+        else:
+            own = jnp.where(z >= step, up[step], down[LINE - step])
+            beside = jnp.where(z >= step, up_other[step], down_other[LINE - step])
+        place = lax.rem(z - step + LINE, LINE)
+        both = in_order(own, beside, y)
+        whole = lax.dynamic_update_index_in_dim(whole, both, place, 0)
+    return whole.reshape((SHARDS,) + values.shape)
+
+
+def added(first, *others):
+    total = first.astype(jnp.float32)
+    for other in others:
+        total = total + other.astype(jnp.float32)
+    return total.astype(first.dtype)
+
+
+def scatter_rows(values, z, y):
+    tail = values.shape[1:]
+    pieces = values.reshape((LINE, 2) + tail)
+
+    def piece(place, column):
+        return lax.dynamic_slice(pieces, (place, column) + (0,) * len(tail), (1, 1) + tail).reshape(
+            tail
+        )
+
+    order = jnp.asarray(STAGES, jnp.int32)[z]
+    reduced = []
+    for stage in range(LINE):
+        place = order[stage]
+        reduced.append(added(piece(place, y), move(piece(place, 1 - y), Y_SWAP)))
+
+    def reduced_at(offset):
+        found = None
+        for own in range(LINE):
+            if 0 <= own + offset < LINE:
+                part = reduced[STAGES[own].index(own + offset)]
+                found = part if found is None else jnp.where(z == own, part, found)
+        return found
+
+    from_low = from_high = None
+    for step in range(1, LINE):
+        far = LINE - step
+        upward, downward = reduced_at(far), reduced_at(-far)
+        if from_low is not None:
+            upward, downward = added(upward, from_low), added(downward, from_high)
+        z_up = lambda rep, shard: (rep, shard + 2) if shard // 2 + far < LINE else None
+        z_down = lambda rep, shard: (rep, shard - 2) if shard // 2 >= far else None
+        from_low = move(upward, pairs_of(z_up))
+        from_high = move(downward, pairs_of(z_down))
+    return added(reduced_at(0), from_low, from_high)
+
+
+def turn(values, cos_table, sin_table):
+    halves = values.shape[-1] // 2
+    turned = jnp.concatenate([-values[..., halves:], values[..., :halves]], axis=-1)
+    return values * cos_table + turned * sin_table
+
+
+def turn_back(grads, cos_table, sin_table):
+    halves = grads.shape[-1] // 2
+    swung = grads * sin_table
+    return grads * cos_table + jnp.concatenate([swung[..., halves:], -swung[..., :halves]], axis=-1)
+
+
+def fast_local(
+    inputs,
+    attn_gain,
+    in_proj,
+    query_gain,
+    key_gain,
+    out_proj,
+    ffn_gain,
+    router_weight,
+    gate_weight,
+    up_weight,
+    down_weight,
+    routes,
+    priority,
+    segments,
+    grad_out,
+):
+    f32, bf16 = jnp.float32, jnp.bfloat16
+    tokens, width = inputs.shape
+    rows_each = in_proj.shape[0]
+    local_experts, _, hidden_units = gate_weight.shape
+    expert_count = local_experts * SHARDS
+    route_count = routes.shape[1]
+    pair_count = tokens * route_count
+    capacity = 5 * pair_count * SHARDS // (4 * expert_count)
+    core_experts = local_experts // 2
+    half_heads = HEADS // 2
+    half_width = half_heads * HEAD_DIM
+    rep, shard = lax.axis_index("rep"), lax.axis_index("shard")
+    a, c = rep // 2, lax.rem(rep, 2)
+    z, y = shard // 2, lax.rem(shard, 2)
+
+    gains = jnp.stack([attn_gain, query_gain, key_gain, ffn_gain])
+    gains = gather_small(gains, z, y)
+    gains = gains.transpose(1, 0, 2).reshape(4, width).astype(f32)
+    router_full = gather_small(router_weight, z, y).reshape(width, expert_count)
+    half_gains = lax.dynamic_index_in_dim(
+        gains[1:3].reshape(2, half_heads, 2, HEAD_DIM), a, 2, keepdims=False
+    )
+
+    order_row = priority[0]
+    pair_ids = jnp.arange(pair_count, dtype=jnp.int32)
+    place_of = jnp.sum(
+        jnp.where(order_row[None, :] == pair_ids[:, None], pair_ids[None, :], 0), axis=1
+    ).reshape(tokens, route_count)
+    labels = jnp.arange(expert_count, dtype=jnp.int32)
+    hits = routes.T[None, :, :] == labels[:, None, None]
+    place_at = jnp.sum(jnp.where(hits, place_of.T[None], 0), axis=1)
+    named = jnp.any(hits, axis=1)
+    place_at = jnp.where(named, place_at, pair_count)
+    earlier = jnp.sum((place_at[:, None, :] < place_at[:, :, None]).astype(jnp.int32), axis=2)
+    ranks = jnp.where(named, earlier, -1).astype(bf16)
+    ranks = in_order(ranks, move(ranks, CORE_SWAP), c)
+    ranks = in_order(ranks, move(ranks, X_SWAP), a)
+    ranks = gather_small(ranks, z, y)
+    ranks = ranks.transpose(1, 2, 0, 3, 4).astype(jnp.int32)
+    counts = jnp.sum((ranks >= 0).astype(jnp.int32), axis=4)
+    bases = jnp.cumsum(counts, axis=2) - counts
+    slots = bases[..., None] + ranks
+    slots = jnp.where((ranks >= 0) & (slots < capacity), slots, -1)
+    first_expert = shard * local_experts + c * core_experts
+    slots = lax.dynamic_slice_in_dim(slots, first_expert, core_experts, 3)
+    slots = slots.transpose(0, 1, 3, 2, 4).reshape(2, 2, core_experts, SHARDS * tokens)
+
+    hidden_pair = in_order(inputs, move(inputs, X_SWAP), a).astype(f32)
+    segment_pair = in_order(segments[0], move(segments[0], X_SWAP), a)
+    cos_table, sin_table = jax.vmap(rotary_tables)(segment_pair)
+    cos_table, sin_table = cos_table[:, :, None, :], sin_table[:, :, None, :]
+    in_half = lax.dynamic_slice_in_dim(in_proj, c * (rows_each // 2), rows_each // 2, 0)
+    in_half = lax.dynamic_index_in_dim(
+        in_half.reshape(rows_each // 2, 3 * half_heads, 2, HEAD_DIM), a, 2, keepdims=False
+    ).reshape(rows_each // 2, 3 * half_width)
+    in_half = gather_rows(in_half, z, y)
+    in_half = in_order(in_half, move(in_half, CORE_SWAP), c)
+    in_half = in_half.transpose(1, 0, 2, 3).reshape(width, 3 * half_width)
+    out_rows = rows_each // 4
+    out_half = lax.dynamic_slice_in_dim(out_proj, a * 2 * out_rows + c * out_rows, out_rows, 0)
+    out_half = gather_rows(out_half, z, y)
+    out_half = in_order(out_half, move(out_half, CORE_SWAP), c)
+    out_half = out_half.transpose(1, 0, 2, 3).reshape(half_width, width)
+
+    attn_rate = lax.rsqrt(jnp.mean(hidden_pair * hidden_pair, axis=-1, keepdims=True) + norm_eps)
+    normed_low = (hidden_pair * attn_rate * gains[0]).astype(bf16).reshape(2 * tokens, width)
+    projected = jnp.dot(normed_low, in_half, preferred_element_type=f32)
+    projected = projected.reshape(2, tokens, 3, half_heads, HEAD_DIM)
+    raw_pair = projected[:, :, :2]
+    squares = jnp.sum(raw_pair * raw_pair, axis=(3, 4))
+    squares = squares + move(squares, X_SWAP)
+    pair_rate = lax.rsqrt(squares / width + norm_eps)[..., None, None]
+    pair_unit = raw_pair * pair_rate
+    turned = turn(pair_unit * half_gains, cos_table[:, :, None], sin_table[:, :, None]).astype(bf16)
+    query_low, key_low = turned[:, :, 0], turned[:, :, 1]
+    value_low = projected[:, :, 2].astype(bf16)
+    places = jnp.arange(tokens, dtype=jnp.int32)
+    allowed = (segment_pair[:, :, None] == segment_pair[:, None, :]) & (
+        places[None, :] <= places[:, None]
+    )
+    score_scale = HEAD_DIM ** (-0.5)
+    scores = (
+        jnp.einsum("bqhd,bkhd->bhqk", query_low, key_low, preferred_element_type=f32) * score_scale
+    )
+    scores = jnp.where(allowed[:, None], scores, masked_score)
+    raised = jnp.exp(scores - jnp.max(scores, axis=-1, keepdims=True))
+    probs = raised / jnp.sum(raised, axis=-1, keepdims=True)
+    probs_low = probs.astype(bf16)
+    attended = jnp.einsum("bhqk,bkhd->bqhd", probs_low, value_low, preferred_element_type=f32)
+    attended = attended.astype(bf16).reshape(2 * tokens, half_width)
+    mixed = jnp.dot(attended, out_half, preferred_element_type=f32).reshape(2, tokens, width)
+    mixed_own = lax.dynamic_index_in_dim(mixed, a, 0, keepdims=False)
+    mixed_other = lax.dynamic_index_in_dim(mixed, 1 - a, 0, keepdims=False).astype(bf16)
+    hidden = inputs.astype(f32)
+    residual = hidden + mixed_own + move(mixed_other, X_SWAP).astype(f32)
+
+    ffn_rate = lax.rsqrt(jnp.mean(residual * residual, axis=-1, keepdims=True) + norm_eps)
+    ffn_unit = residual * ffn_rate
+    ffn_low = (ffn_unit * gains[3]).astype(bf16)
+    router_probs = softmax_rows(jnp.dot(ffn_low, router_full, preferred_element_type=f32))
+
+    ffn_own = gather_rows(ffn_low, z, y)
+    cot_own = gather_rows(grad_out, z, y)
+    ffn_near = in_order(ffn_own, move(ffn_own, CORE_SWAP), c)
+    cot_near = in_order(cot_own, move(cot_own, CORE_SWAP), c)
+    ffn_far = move(ffn_own, X_SWAP)
+    cot_far = move(cot_own, X_SWAP)
+    ffn_far = in_order(ffn_far, move(ffn_far, CORE_SWAP), c)
+    cot_far = in_order(cot_far, move(cot_far, CORE_SWAP), c)
+    group_rows = SHARDS * tokens
+
+    gate_own = lax.dynamic_slice_in_dim(gate_weight, c * core_experts, core_experts, 0)
+    up_own = lax.dynamic_slice_in_dim(up_weight, c * core_experts, core_experts, 0)
+    down_own = lax.dynamic_slice_in_dim(down_weight, c * core_experts, core_experts, 0)
+
+    def expert_part(ffn_rows, cot_rows, own_slots):
+        ffn_rows = ffn_rows.reshape(2, group_rows, width)
+        cot_rows = cot_rows.reshape(2, group_rows, width)
+        part_probs = softmax_rows(jnp.dot(ffn_rows, router_full, preferred_element_type=f32))
+        part_probs = lax.dynamic_slice_in_dim(part_probs, first_expert, core_experts, 2)
+        part_probs = part_probs.transpose(0, 2, 1).astype(bf16)
+        match = own_slots[:, :, None, :] == jnp.arange(capacity, dtype=jnp.int32)[:, None]
+        choice = match.astype(bf16).reshape(2, core_experts * capacity, group_rows)
+        weighted = jnp.where(match, part_probs[:, :, None, :], 0).reshape(choice.shape)
+        shape = (2, core_experts, capacity)
+        expert_in = jnp.einsum("gct,gtd->gcd", choice, ffn_rows).reshape(shape + (width,))
+        grad_expert_out = jnp.einsum("gct,gtd->gcd", weighted, cot_rows).reshape(shape + (width,))
+        gate_pre = jnp.einsum("gecd,edf->gecf", expert_in, gate_own, preferred_element_type=f32)
+        up_pre = jnp.einsum("gecd,edf->gecf", expert_in, up_own, preferred_element_type=f32)
+        act, swiglu_back = jax.vjp(swiglu, gate_pre, up_pre)
+        grad_act = jnp.einsum(
+            "gecd,efd->gecf", grad_expert_out, down_own, preferred_element_type=f32
+        )
+        grad_gate_pre, grad_up_pre = swiglu_back(grad_act)
+        act_low = act.astype(bf16)
+        return (
+            choice,
+            weighted,
+            expert_in,
+            grad_expert_out,
+            act_low,
+            grad_gate_pre.astype(bf16),
+            grad_up_pre.astype(bf16),
+            jnp.sum(act * grad_act, axis=3),
+        )
+
+    near = expert_part(
+        ffn_near, cot_near, lax.dynamic_index_in_dim(slots, a, 0, keepdims=False)
+    )
+    choice, weighted, _, _, act_low, gate_low, up_low, slot_score = near
+    expert_out = jnp.einsum("gecf,efd->gecd", act_low, down_own, preferred_element_type=f32)
+    expert_out = expert_out.astype(bf16).reshape(2, core_experts * capacity, width)
+    routed = jnp.einsum("gct,gcd->gtd", weighted, expert_out)
+    grad_expert_in = (
+        jnp.einsum("gecf,edf->gecd", gate_low, gate_own, preferred_element_type=f32)
+        + jnp.einsum("gecf,edf->gecd", up_low, up_own, preferred_element_type=f32)
+    ).astype(bf16)
+    grad_expert_in = grad_expert_in.reshape(2, core_experts * capacity, width)
+    grad_rows = jnp.einsum("gct,gcd->gtd", choice, grad_expert_in)
+    slot_score = slot_score.reshape(2, core_experts, capacity)
+    token_score = jnp.einsum(
+        "gec,gect->get",
+        slot_score,
+        choice.astype(f32).reshape(2, core_experts, capacity, group_rows),
+        precision=lax.Precision.HIGHEST,
+    )
+
+    def core_sum(values):
+        own = lax.dynamic_index_in_dim(values, c, 0, keepdims=False)
+        other = lax.dynamic_index_in_dim(values, 1 - c, 0, keepdims=False)
+        return added(own, move(other, CORE_SWAP))
+
+    grad_rows = core_sum(grad_rows).reshape(SHARDS, tokens, width)
+    grad_ffn_home = scatter_rows(grad_rows, z, y).astype(f32)
+    routed = core_sum(routed).reshape(SHARDS, tokens, width)
+    outputs = (residual + scatter_rows(routed, z, y).astype(f32)).astype(bf16)
+    scores_all = jnp.zeros((2, expert_count, group_rows), f32)
+    scores_all = lax.dynamic_update_slice_in_dim(scores_all, token_score, first_expert, 1)
+    scores_all = core_sum(scores_all).reshape(expert_count, SHARDS, tokens).transpose(1, 0, 2)
+    home_score = scatter_small(scores_all, z, y).T
+
+    grad_logits = home_score - router_probs * jnp.sum(home_score, axis=1, keepdims=True)
+    grad_logits_low = grad_logits.astype(bf16)
+    grad_ffn_in = grad_ffn_home + contract_cols(grad_logits_low, router_full)
+    grad_router_local = contract_rows(ffn_low, grad_logits_low)
+    grad_ffn_local = jnp.sum(grad_ffn_in * ffn_unit, axis=0)
+    scaled = gains[3] * grad_ffn_in
+    cotangent = grad_out.astype(f32)
+    grad_residual = cotangent + ffn_rate * (
+        scaled - ffn_unit * jnp.mean(scaled * ffn_unit, axis=-1, keepdims=True)
+    )
+    residual_low = grad_residual.astype(bf16)
+    residual_pair = in_order(residual_low, move(residual_low, X_SWAP), a)
+    residual_pair = residual_pair.reshape(2 * tokens, width)
+
+    grad_attended = contract_cols(residual_pair, out_half).astype(bf16)
+    grad_attended = grad_attended.reshape(2, tokens, half_heads, HEAD_DIM)
+    grad_out_half = contract_rows(attended, residual_pair).astype(bf16)
+    grad_probs = jnp.einsum("bqhd,bkhd->bhqk", grad_attended, value_low, preferred_element_type=f32)
+    spread = jnp.sum(probs * grad_probs, axis=-1, keepdims=True)
+    grad_scores = (probs * (grad_probs - spread)).astype(bf16)
+    grad_query = (
+        jnp.einsum("bhqk,bkhd->bqhd", grad_scores, key_low, preferred_element_type=f32)
+        * score_scale
+    )
+    grad_key = (
+        jnp.einsum("bhqk,bqhd->bkhd", grad_scores, query_low, preferred_element_type=f32)
+        * score_scale
+    )
+    grad_value = jnp.einsum(
+        "bhqk,bqhd->bkhd", probs_low, grad_attended, preferred_element_type=f32
+    )
+    grad_turned = jnp.stack([grad_query, grad_key], axis=2)
+    grad_pair = turn_back(grad_turned, cos_table[:, :, None], sin_table[:, :, None])
+    grad_pair_gain = jnp.sum(grad_pair * pair_unit, axis=(0, 1))
+    grad_pair = grad_pair * half_gains
+    dots = jnp.sum(grad_pair * pair_unit, axis=(3, 4))
+    dots = (dots + move(dots, X_SWAP)) / width
+    grad_raw = pair_rate * (grad_pair - pair_unit * dots[..., None, None])
+    grad_projected = jnp.concatenate([grad_raw, grad_value[:, :, None]], axis=2).astype(bf16)
+    grad_projected = grad_projected.reshape(2 * tokens, 3 * half_width)
+    grad_in_half = contract_rows(normed_low, grad_projected).astype(bf16)
+    grad_normed = contract_cols(grad_projected, in_half).reshape(2, tokens, width)
+    normed_own = lax.dynamic_index_in_dim(grad_normed, a, 0, keepdims=False)
+    normed_other = lax.dynamic_index_in_dim(grad_normed, 1 - a, 0, keepdims=False).astype(bf16)
+    grad_normed = normed_own + move(normed_other, X_SWAP).astype(f32)
+    home_rate = lax.rsqrt(jnp.mean(hidden * hidden, axis=-1, keepdims=True) + norm_eps)
+    home_unit = hidden * home_rate
+    grad_attn_local = jnp.sum(grad_normed * home_unit, axis=0)
+    scaled = gains[0] * grad_normed
+    grad_inputs = (
+        grad_residual
+        + home_rate * (scaled - home_unit * jnp.mean(scaled * home_unit, axis=-1, keepdims=True))
+    ).astype(bf16)
+
+    in_parts = grad_in_half.reshape(SHARDS, 2, rows_each // 2, 3 * half_width)
+    in_sum = scatter_rows(core_sum(in_parts.transpose(1, 0, 2, 3)), z, y)
+    out_parts = grad_out_half.reshape(SHARDS, 2, out_rows, width)
+    out_sum = scatter_rows(core_sum(out_parts.transpose(1, 0, 2, 3)), z, y)
+    in_sum = in_order(in_sum, move(in_sum, CORE_SWAP), c).reshape(rows_each, 3 * half_width)
+    in_sum = in_order(in_sum, move(in_sum, X_SWAP), a)
+    grad_in = in_sum.reshape(2, rows_each, 3 * half_heads, HEAD_DIM).transpose(1, 2, 0, 3)
+    grad_in = grad_in.reshape(rows_each, 3 * width).astype(f32)
+    out_sum = in_order(out_sum, move(out_sum, CORE_SWAP), c).reshape(2 * out_rows, width)
+    out_sum = in_order(out_sum, move(out_sum, X_SWAP), a)
+    grad_out_proj = out_sum.reshape(rows_each, width).astype(f32)
+
+    pair_gains = jnp.zeros((2, half_heads, 2, HEAD_DIM), f32)
+    pair_gains = lax.dynamic_update_index_in_dim(pair_gains, grad_pair_gain, a, 2)
+    pair_gains = pair_gains.reshape(2, SHARDS, rows_each)
+    small = jnp.concatenate(
+        [
+            grad_attn_local.reshape(SHARDS, 1, rows_each),
+            grad_ffn_local.reshape(SHARDS, 1, rows_each),
+            pair_gains.transpose(1, 0, 2),
+            grad_router_local.T.reshape(expert_count, SHARDS, rows_each).transpose(1, 0, 2),
+        ],
+        axis=1,
+    )
+    small = small + move(small, CORE_SWAP)
+    small = small + move(small, X_SWAP)
+    small = scatter_small(small, z, y)
+
+    far = expert_part(ffn_far, cot_far, lax.dynamic_index_in_dim(slots, 1 - a, 0, keepdims=False))
+
+    def expert_rows(index):
+        return jnp.concatenate([near[index], far[index]], axis=0)
+
+    all_in, all_out, all_act, all_gate, all_up = [expert_rows(index) for index in range(2, 7)]
+    grads = (
+        jnp.einsum("gecd,gecf->edf", all_in, all_gate, preferred_element_type=f32).astype(bf16),
+        jnp.einsum("gecd,gecf->edf", all_in, all_up, preferred_element_type=f32).astype(bf16),
+        jnp.einsum("gecf,gecd->efd", all_act, all_out, preferred_element_type=f32).astype(bf16),
+    )
+    grads = [
+        in_order(grad, move(grad, CORE_SWAP), c)
+        .reshape((local_experts,) + grad.shape[1:])
+        .astype(f32)
+        for grad in grads
+    ]
+    return (
+        outputs,
+        grad_inputs,
+        small[0],
+        grad_in,
+        small[2],
+        small[3],
+        grad_out_proj,
+        small[1],
+        small[4:].T,
+        grads[0],
+        grads[1],
+        grads[2],
+    )
+
+
 def solution(mesh):
+    fits = dict(mesh.shape) == {"rep": 4, "shard": SHARDS}
+    body = fast_local if fits else local
     in_specs = (
         P(("rep", "shard"), None),
         P("shard"),
@@ -405,4 +856,4 @@
         P("shard", None, None),
         P("shard", None, None),
     )
-    return jax.shard_map(local, mesh=mesh, in_specs=in_specs, out_specs=out_specs, check_vma=False)
+    return jax.shard_map(body, mesh=mesh, in_specs=in_specs, out_specs=out_specs, check_vma=False)

time: 3910 us -> 1610 us (0.41)
  waiting for transfers between devices: 2130 us -> 535 us
  blocking collectives: 789 us -> 0 us
  local copies, waits for them, and re-layouts: 583 us -> 150 us
  starting transfers between devices: 11.7 us -> 256 us
  matrix products: 223 us -> 399 us
  other arithmetic: 154 us -> 246 us
    psum x1 -> x0, waiting for transfers between devices: 890 us -> none  [local(): lax.psum(grad_in_local, 'rep').astype(jnp.float32)]
    all_to_all x2 -> x0, blocking collectives: 571 us -> none  [the longest x1 295 us: local(): lax.all_to_all(returning_grad, 'shard', split_axis=1, concat_axis=0, tile...]
    ppermute x0 -> x143, waiting for transfers between devices: none -> 535 us  [move(): return lax.ppermute(values, AXES, moves)]
    gather x21 -> x0, local copies, waits for them, and re-layouts: 507 us -> none  [the longest x6 380 us: pick_rows(): expert_rows[picked]]
    reduce_scatter x3 -> x0, waiting for transfers between devices: 481 us -> none  [the longest x1 408 us: local(): lax.psum_scatter(contract_rows(normed_low, grad_qkv).astype(jnp.bfloat16)...]
    all_gather x2 -> x0, waiting for transfers between devices: 377 us -> none  [the longest x1 270 us: local(): weight_piece = lax.all_gather(in_proj, 'shard', axis=0, tiled=True)]
    all_to_all x2 -> x0, waiting for transfers between devices: 376 us -> none  [the longest x1 220 us: local(): lax.all_to_all(returning, 'shard', split_axis=1, concat_axis=0, tiled=True)]
    ppermute x0 -> x143, starting transfers between devices: none -> 256 us  [move(): return lax.ppermute(values, AXES, moves)]
  transfers between devices with their start and end apart: 8 -> 143, of which waited for: 8 -> 41; matrix products, arithmetic and copies ran while one was open for 8% -> 47% of each run, Pallas kernels for 0% -> 0%
where the time goes in v1:
time: 1610 us; the launch traced here: 1600 us
  waiting for transfers between devices  535 us (33%)
  matrix products  399 us (25%)
  starting transfers between devices  256 us (16%)
  other arithmetic  246 us (15%)
  local copies, waits for them, and re-layouts  150 us (9%)
    ppermute x143, waiting for transfers between devices, move(): return lax.ppermute(values, AXES, moves)  535 us
    ppermute x143, starting transfers between devices, move(): return lax.ppermute(values, AXES, moves)  256 us
    convert_element_type x18, other arithmetic, added(): return total.astype(first.dtype)  60.1 us
    select_n x22, other arithmetic, in_order(): jnp.where(position == 0, jnp.stack([own, other]), jnp.stack([other, own]))  58.6 us
    dot_general x2, matrix products, expert_part(): jnp.einsum('gct,gtd->gcd', weighted, cot_rows).reshape(shape + (width,))  42.2 us
    convert_element_type x3, other arithmetic, fast_local(): grads = [in_order(grad, move(grad, CORE_SWAP), c).reshape((local_experts,...  36.5 us
    dot_general x2, matrix products, expert_part(): jnp.einsum('gct,gtd->gcd', choice, ffn_rows).reshape(shape + (width,))  35.6 us
    dot_general x2, matrix products, expert_part(): jnp.einsum('gecd,edf->gecf', expert_in, gate_own, preferred_element_type=...  35.4 us
  transfers between devices with their start and end apart: 143, of which 41 were waited for; matrix products, arithmetic and copies ran while one was open for 47% of the time, Pallas kernels for 0%

profile of v1, /device:TPU:0, one launch (start us, length us, event | category | flops | bytes accessed | tf_op | source)
XLA Modules:
  0.0 1597.6 jit_solution(9156179899126430231)
XLA Ops:
  37.9 14.3 collective-permute-done.2
  65.2 9.3 collective-permute-done.8
  82.9 14.2 collective-permute-done.14
  103.1 10.7 collective-permute-done.9
  247.1 16.6 %copy.291 = bf16[3072,2048]{1,0:T(8,128)(2,1)} copy(bf16[3072,2048]{0,1:T(8,128)(2,1)} %bitcast.657) | data formatting | bytes 25165824 | tf_op jit(solution)/shard_map/dot_general | solution.py:595
  298.7 9.3 collective-permute-done.35
  308.0 11.2 collective-permute-start.82
  331.8 9.8 collective-permute-done.44
  379.8 9.6 collective-permute-done.52
  401.0 9.7 collective-permute-done.48
  433.4 249.1 %collective-permute-done.37 = bf16[2,32,192]{2,1,0:T(8,128)(2,1)S(1)} collective-permute-done((bf16[2,32,192]{2,1,0:T(8,128)(2,1)S(1)}, bf16[2,32,192]{2,1,0:T(8,128)(2,1)S(1)}, u32[]{:S(2)}, u32[]{:S(2)}) %collective-permute-start.37) | collective-permute-done | bytes 24608 | tf_op jit(solution)/shard_map/ppermute | solution.py:398
  727.6 11.8 fusion.238
  739.5 17.9 %fusion.116 = bf16[2,960,2048]{2,1,0:T(8,128)(2,1)} fusion(pred[2,960,1536]{2,1,0:T(32,128)(4,1)S(1)} %get-tuple-element.145, bf16[1,1536,2048]{2,1,0:T(8,128)(2,1)} %bitcast.83, bf16[1,1536,2048]{2,1,0:T(8,128)(2,1)} %bitcast.81, pred[]{:T(512)S(6)} %eq.73), kind=kOutput, calls=%fused_computation.173 | convolution fusion | flops 12098469888 | bytes 23396352 | tf_op jit(solution)/shard_map/gct,gtd->gcd/dot_general | solution.py:654
  757.4 14.9 fusion.30
  772.2 12.3 fusion.237
  792.1 21.2 %fusion.8 = bf16[2,960,2048]{2,1,0:T(8,128)(2,1)} fusion(bf16[2,960,1536]{2,1,0:T(8,128)(2,1)} %get-tuple-element.143, bf16[1,1536,2048]{2,1,0:T(8,128)(2,1)} %bitcast.131, bf16[1,1536,2048]{2,1,0:T(8,128)(2,1)} %bitcast.129, pred[]{:T(512)S(6)} %eq.73), kind=kOutput, calls=%fused_computation.23 | convolution fusion | flops 12098469888 | bytes 26345472 | tf_op jit(solution)/shard_map/gct,gtd->gcd/dot_general | solution.py:655
  813.3 15.0 fusion.34
  828.2 20.2 %fusion.46 = (bf16[2,2,480,1024]{3,2,0,1:T(8,128)(2,1)}, f32[2,2,480]{2,0,1:T(2,128)S(1)}, bf16[2,2,480,1024]{3,2,0,1:T(8,128)(2,1)}, bf16[2,2,480,1024]{3,2,0,1:T(8,128)(2,1)S(1)}) fusion(f32[2,1024,2,480]{1,3,2,0:T(8,128)} %fusion.30, f32[2,1024,2,480]{1,3,2,0:T(8,128)} %fusion.34, bf16[2,2,480,2048]{3,2,1,0:T(8,128)(2,1)} %bitcast.782, ...), kind=kOutput, calls=%fused_computation.74 | convolution fusion | flops 8088451072 | bytes 43785732 | tf_op jit(solution)/shard_map/gecd,edf->gecf/dot_general | solution.py:656
  853.5 13.6 convert_bitcast_fusion
  875.0 20.4 %fusion.240 = bf16[2,1536,2048]{2,1,0:T(8,128)(2,1)} fusion(bf16[2,960,1536]{2,1,0:T(8,128)(2,1)} %get-tuple-element.143, bf16[2,960,2048]{2,1,0:T(8,128)(2,1)} %bitcast.695), kind=kOutput, calls=%fused_computation.508 | convolution fusion | flops 12079595520 | bytes 26345472 | tf_op jit(solution)/shard_map/gct,gcd->gtd/dot_general | solution.py:681
  902.2 17.7 %fusion.115 = bf16[2,960,2048]{2,1,0:T(8,128)(2,1)} fusion(pred[2,960,1536]{2,1,0:T(32,128)(4,1)S(1)} %copy-done.32, bf16[1,1536,2048]{2,1,0:T(8,128)(2,1)} %bitcast.230, bf16[1,1536,2048]{2,1,0:T(8,128)(2,1)} %bitcast.229, pred[]{:T(512)S(6)} %eq.73), kind=kOutput, calls=%fused_computation.172 | convolution fusion | flops 12098469888 | bytes 23396352 | tf_op jit(solution)/shard_map/gct,gtd->gcd/dot_general | solution.py:654
  919.9 15.1 fusion.38
  935.0 21.0 %fusion.14 = bf16[2,960,2048]{2,1,0:T(8,128)(2,1)} fusion(bf16[2,960,1536]{2,1,0:T(8,128)(2,1)} %get-tuple-element.142, bf16[1,1536,2048]{2,1,0:T(8,128)(2,1)} %bitcast.235, bf16[1,1536,2048]{2,1,0:T(8,128)(2,1)} %bitcast.234, pred[]{:T(512)S(6)} %eq.73), kind=kOutput, calls=%fused_computation.31 | convolution fusion | flops 12098469888 | bytes 26345472 | tf_op jit(solution)/shard_map/gct,gtd->gcd/dot_general | solution.py:655
  956.1 15.2 fusion.32
  971.2 14.7 fusion.28
  986.0 16.2 %fusion.50 = bf16[2,2,480,2048]{3,2,0,1:T(8,128)(2,1)} fusion(f32[2,2048,2,480]{1,3,2,0:T(8,128)} %fusion.28, bf16[2,2,480,1024]{3,2,0,1:T(8,128)(2,1)} %get-tuple-element.78, bf16[4,2048,1024]{2,1,0:T(8,128)(2,1)} %param.27, s32[]{:T(128)S(6)} %select_n.1085), kind=kOutput, calls=%fused_computation.78 | convolution fusion | flops 8060928000 | bytes 35913732 | tf_op jit(solution)/shard_map/gecf,edf->gecd/dot_general | solution.py:683
  1010.2 18.9 %fusion.241 = bf16[2,1536,2048]{2,1,0:T(8,128)(2,1)} fusion(pred[2,960,1536]{2,1,0:T(32,128)(4,1)S(1)} %copy-done.31, bf16[2,960,2048]{2,1,0:T(8,128)(2,1)} %bitcast.696), kind=kOutput, calls=%fused_computation.509 | convolution fusion | flops 12079595520 | bytes 23396352 | tf_op jit(solution)/shard_map/gct,gcd->gtd/dot_general | solution.py:687
  1036.2 19.9 %fusion.63 = (bf16[2,2,480,1024]{3,2,0,1:T(8,128)(2,1)}, bf16[2,2,480,1024]{3,2,0,1:T(8,128)(2,1)}, bf16[2,2,480,1024]{3,2,0,1:T(8,128)(2,1)}) fusion(f32[2,1024,2,480]{1,3,2,0:T(8,128)} %fusion.38, f32[2,1024,2,480]{1,3,2,0:T(8,128)} %fusion.32, bf16[2,2,480,2048]{3,2,1,0:T(8,128)(2,1)} %bitcast.786, bf16[4,2048,1024]{2,1,0:T(8,128)(2,1)} %param.28, ...), kind=kOutput, calls=%fused_computation.96 | convolution fusion | flops 8084520960 | bytes 43778052 | tf_op jit(solution)/shard_map/gecd,edf->gecf/dot_general | solution.py:657
  1056.1 23.2 %bitcast_convert_fusion.3 = bf16[2,1024,2048]{2,1,0:T(8,128)(2,1)} fusion(bf16[2,2,480,1024]{3,2,0,1:T(8,128)(2,1)} %get-tuple-element.80, bf16[2,2,480,1024]{3,2,0,1:T(8,128)(2,1)} %copy-done.87, bf16[2,2,480,2048]{3,2,1,0:T(8,128)(2,1)} %bitcast.792, bf16[2,2,480,2048]{3,2,1,0:T(8,128)(2,1)} %bitcast.790), kind=kOutput, calls=%fused_computation.7 | convolution fusion | flops 16122118144 | bytes 31981568 | tf_op jit(solution)/shard_map/gecf,gecd->efd/dot_general | solution.py:801
  1081.2 23.1 %bitcast_convert_fusion.5 = bf16[2,2048,1024]{2,1,0:T(8,128)(2,1)} fusion(bf16[2,2,480,1024]{3,2,0,1:T(8,128)(2,1)} %get-tuple-element.81, bf16[2,2,480,1024]{3,2,0,1:T(8,128)(2,1)} %get-tuple-element.78, bf16[2,2,480,2048]{3,2,1,0:T(8,128)(2,1)} %bitcast.787, bf16[2,2,480,2048]{3,2,1,0:T(8,128)(2,1)} %bitcast.783), kind=kOutput, calls=%fused_computation.9 | convolution fusion | flops 16122118144 | bytes 31981568 | tf_op jit(solution)/shard_map/gecd,gecf->edf/dot_general | solution.py:799
  1105.0 10.9 fusion.22
  1120.7 11.0 fusion.21
  1134.8 23.3 %bitcast_convert_fusion.4 = bf16[2,2048,1024]{2,1,0:T(8,128)(2,1)} fusion(bf16[2,2,480,1024]{3,2,0,1:T(8,128)(2,1)} %get-tuple-element.82, bf16[2,2,480,1024]{3,2,0,1:T(8,128)(2,1)} %get-tuple-element.83, bf16[2,2,480,2048]{3,2,1,0:T(8,128)(2,1)} %bitcast.788, bf16[2,2,480,2048]{3,2,1,0:T(8,128)(2,1)} %bitcast.784), kind=kOutput, calls=%fused_computation.8 | convolution fusion | flops 16122118144 | bytes 31981568 | tf_op jit(solution)/shard_map/gecd,gecf->edf/dot_general | solution.py:800
  1170.3 11.0 collective-permute-done.89
  1189.2 9.1 collective-permute-done.64
  1210.4 15.7 maximum_select_fusion.2
  1226.1 12.1 bitcast_convert_fusion
  1246.9 15.8 maximum_select_fusion
  1281.2 12.4 bitcast_convert_fusion.2
  1317.0 8.8 convolution_convert_fusion
  1332.4 15.6 maximum_select_fusion.1
  1348.0 11.9 bitcast_convert_fusion.1
  1376.5 9.0 fusion.242
  1387.2 10.3 fusion.20
  1407.1 14.4 collective-permute-done.112
  1431.9 12.2 collective-permute-done.114
  1476.1 8.7 collective-permute-done.61
  1532.3 43.1 %collective-permute-done.135 = bf16[128,2048]{1,0:T(8,128)(2,1)S(1)} collective-permute-done((bf16[128,2048]{1,0:T(8,128)(2,1)S(1)}, bf16[128,2048]{1,0:T(8,128)(2,1)S(1)}, u32[]{:S(2)}, u32[]{:S(2)}) %collective-permute-start.135) | collective-permute-done | bytes 524320 | tf_op jit(solution)/shard_map/ppermute | solution.py:398
  (717 shorter events, 634.1 us)
Async XLA Ops:
  5.9 47.9 %collective-permute-start.7 = (bf16[128,3072]{0,1:T(8,128)(2,1)S(1)}, bf16[128,3072]{0,1:T(8,128)(2,1)}, u32[]{:S(2)}, u32[]{:S(2)}) collective-permute-start(bf16[128,3072]{0,1:T(8,128)(2,1)S(1)} %bitcast.704), channel_id=1, source_target_pairs={{2,0},{3,1},{4,2},{5,3},{6,4},{7,5},{10,8},{11,9},{12,10},{13,11},... | collective-permute-start | bytes 2359304 | tf_op jit(solution)/shard_map/ppermute | solution.py:398
  13.7 41.5 %collective-permute-start.5 = (bf16[128,3072]{0,1:T(8,128)(2,1)S(1)}, bf16[128,3072]{0,1:T(8,128)(2,1)S(1)}, u32[]{:S(2)}, u32[]{:S(2)}) collective-permute-start(bf16[128,3072]{0,1:T(8,128)(2,1)S(1)} %bitcast.706), channel_id=1, source_target_pairs={{0,1},{1,0},{2,3},{3,2},{4,5},{5,4},{6,7},{7,6},{8,9},{9,8},{10,11... | collective-permute-start | bytes 2359304 | tf_op jit(solution)/shard_map/ppermute | solution.py:398
  21.2 127.7 %collective-permute-start.22 = (bf16[64,2048]{1,0:T(8,128)(2,1)}, bf16[64,2048]{1,0:T(8,128)(2,1)}, u32[]{:S(2)}, u32[]{:S(2)}) collective-permute-start(bf16[64,2048]{1,0:T(8,128)(2,1)} %constant_dynamic-slice_fusion.8), channel_id=1, source_target_pairs={{0,2},{1,3},{2,4},{3,5},{4,6},{5,7},{8,10},{9,11},{10,12},{11,13},... | collective-permute-start | bytes 786440 | tf_op jit(solution)/shard_map/ppermute | solution.py:398
  52.2 101.8 %collective-permute-start.21 = (bf16[64,2048]{1,0:T(8,128)(2,1)}, bf16[64,2048]{1,0:T(8,128)(2,1)}, u32[]{:S(2)}, u32[]{:S(2)}) collective-permute-start(bf16[64,2048]{1,0:T(8,128)(2,1)} %constant_dynamic-slice_fusion.8), channel_id=1, source_target_pairs={{0,1},{1,0},{2,3},{3,2},{4,5},{5,4},{6,7},{7,6},{8,9},{9,8},{10,11... | collective-permute-start | bytes 786440 | tf_op jit(solution)/shard_map/ppermute | solution.py:398
  64.5 33.8 %collective-permute-start.13 = (bf16[128,3072]{0,1:T(8,128)(2,1)}, bf16[128,3072]{0,1:T(8,128)(2,1)S(1)}, u32[]{:S(2)}, u32[]{:S(2)}) collective-permute-start(bf16[128,3072]{0,1:T(8,128)(2,1)} %collective-permute-done.12), channel_id=1, source_target_pairs={{4,5},{5,4},{6,7},{7,6},{12,13},{13,12},{14,15},{15,14},{20,21},{2... | collective-permute-start | bytes 2359304 | tf_op jit(solution)/shard_map/ppermute | solution.py:398
  78.3 38.8 %collective-permute-start.17 = (bf16[128,3072]{0,1:T(8,128)(2,1)}, bf16[128,3072]{0,1:T(8,128)(2,1)}, u32[]{:S(2)}, u32[]{:S(2)}) collective-permute-start(bf16[128,3072]{0,1:T(8,128)(2,1)} %collective-permute-done.7), channel_id=1, source_target_pairs={{0,1},{1,0},{2,3},{3,2},{4,5},{5,4},{8,9},{9,8},{10,11},{11,10},{1... | collective-permute-start | bytes 2359304 | tf_op jit(solution)/shard_map/ppermute | solution.py:398
  114.6 38.0 %collective-permute-start.23 = (bf16[64,2048]{1,0:T(8,128)(2,1)}, bf16[64,2048]{1,0:T(8,128)(2,1)}, u32[]{:S(2)}, u32[]{:S(2)}) collective-permute-start(bf16[64,2048]{1,0:T(8,128)(2,1)} %constant_dynamic-slice_fusion.8), channel_id=1, source_target_pairs={{2,0},{3,1},{4,2},{5,3},{6,4},{7,5},{10,8},{11,9},{12,10},{13,11},... | collective-permute-start | bytes 786440 | tf_op jit(solution)/shard_map/ppermute | solution.py:398
  145.9 87.1 %collective-permute-start.18 = (bf16[8,128,3072]{2,1,0:T(8,128)(2,1)}, bf16[8,128,3072]{2,1,0:T(8,128)(2,1)}, u32[]{:S(2)}, u32[]{:S(2)}) collective-permute-start(bf16[8,128,3072]{2,1,0:T(8,128)(2,1)} %bitcast.677), channel_id=1, source_target_pairs={{0,8},{1,9},{2,10},{3,11},{4,12},{5,13},{6,14},{7,15},{8,0},{9,1},... | collective-permute-start | bytes 18874376 | tf_op jit(solution)/shard_map/ppermute | solution.py:398
  146.7 43.9 %collective-permute-start = (bf16[192,2048]{1,0:T(8,128)(2,1)S(1)}, bf16[192,2048]{1,0:T(8,128)(2,1)}, u32[]{:S(2)}, u32[]{:S(2)}) collective-permute-start(bf16[192,2048]{1,0:T(8,128)(2,1)S(1)} %copy-done.6), channel_id=1, source_target_pairs={{0,16},{1,17},{2,18},{3,19},{4,20},{5,21},{6,22},{7,23},{8,24},{9,... | collective-permute-start | bytes 2359304 | tf_op jit(solution)/shard_map/ppermute | solution.py:398
  154.0 42.5 %collective-permute-start.71 = (bf16[192,2048]{1,0:T(8,128)(2,1)}, bf16[192,2048]{1,0:T(8,128)(2,1)S(1)}, u32[]{:S(2)}, u32[]{:S(2)}) collective-permute-start(bf16[192,2048]{1,0:T(8,128)(2,1)} %param.33), channel_id=1, source_target_pairs={{0,1},{1,0},{2,3},{3,2},{4,5},{5,4},{6,7},{7,6},{8,9},{9,8},{10,11... | collective-permute-start | bytes 2359304 | tf_op jit(solution)/shard_map/ppermute | solution.py:398
  216.1 109.8 %collective-permute-start.83 = (bf16[192,2048]{1,0:T(8,128)(2,1)}, bf16[192,2048]{1,0:T(8,128)(2,1)}, u32[]{:S(2)}, u32[]{:S(2)}) collective-permute-start(bf16[192,2048]{1,0:T(8,128)(2,1)} %collective-permute-done.73), channel_id=1, source_target_pairs={{0,1},{1,0},{2,3},{3,2},{4,5},{5,4},{8,9},{9,8},{10,11},{11,10},{1... | collective-permute-start | bytes 2359304 | tf_op jit(solution)/shard_map/ppermute | solution.py:398
  218.6 124.4 %collective-permute-start.76 = (bf16[192,2048]{1,0:T(8,128)(2,1)}, bf16[192,2048]{1,0:T(8,128)(2,1)}, u32[]{:S(2)}, u32[]{:S(2)}) collective-permute-start(bf16[192,2048]{1,0:T(8,128)(2,1)} %collective-permute-done.72), channel_id=1, source_target_pairs={{2,3},{3,2},{4,5},{5,4},{6,7},{7,6},{10,11},{11,10},{12,13},{13,12... | collective-permute-start | bytes 2359304 | tf_op jit(solution)/shard_map/ppermute | solution.py:398
  227.3 45.3 %collective-permute-start.34 = (bf16[8,64,2048]{2,1,0:T(8,128)(2,1)S(1)}, bf16[8,64,2048]{2,1,0:T(8,128)(2,1)}, u32[]{:S(2)}, u32[]{:S(2)}) collective-permute-start(bf16[8,64,2048]{2,1,0:T(8,128)(2,1)S(1)} %bitcast.693), channel_id=1, source_target_pairs={{0,8},{1,9},{2,10},{3,11},{4,12},{5,13},{6,14},{7,15},{8,0},{9,1},... | collective-permute-start | bytes 6291464 | tf_op jit(solution)/shard_map/ppermute | solution.py:398
  228.5 91.5 %collective-permute-start.80 = (bf16[192,2048]{1,0:T(8,128)(2,1)}, bf16[192,2048]{1,0:T(8,128)(2,1)}, u32[]{:S(2)}, u32[]{:S(2)}) collective-permute-start(bf16[192,2048]{1,0:T(8,128)(2,1)} %collective-permute-done.74), channel_id=1, source_target_pairs={{0,1},{1,0},{2,3},{3,2},{8,9},{9,8},{10,11},{11,10},{16,17},{17,16... | collective-permute-start | bytes 2359304 | tf_op jit(solution)/shard_map/ppermute | solution.py:398
  233.0 57.3 %collective-permute-start.75 = (bf16[192,2048]{1,0:T(8,128)(2,1)}, bf16[192,2048]{1,0:T(8,128)(2,1)}, u32[]{:S(2)}, u32[]{:S(2)}) collective-permute-start(bf16[192,2048]{1,0:T(8,128)(2,1)} %collective-permute-done.74), channel_id=1, source_target_pairs={{2,0},{3,1},{4,2},{5,3},{6,4},{7,5},{10,8},{11,9},{12,10},{13,11},... | collective-permute-start | bytes 2359304 | tf_op jit(solution)/shard_map/ppermute | solution.py:398
  360.9 52.9 %collective-permute-start.54 = (bf16[192,2048]{1,0:T(8,128)(2,1)S(1)}, bf16[192,2048]{1,0:T(8,128)(2,1)S(1)}, u32[]{:S(2)}, u32[]{:S(2)}) collective-permute-start(bf16[192,2048]{1,0:T(8,128)(2,1)S(1)} %collective-permute-done.44), channel_id=1, source_target_pairs={{0,1},{1,0},{2,3},{3,2},{4,5},{5,4},{8,9},{9,8},{10,11},{11,10},{1... | collective-permute-start | bytes 2359304 | tf_op jit(solution)/shard_map/ppermute | solution.py:398
  363.4 37.6 %collective-permute-start.47 = (bf16[192,2048]{1,0:T(8,128)(2,1)S(1)}, bf16[192,2048]{1,0:T(8,128)(2,1)S(1)}, u32[]{:S(2)}, u32[]{:S(2)}) collective-permute-start(bf16[192,2048]{1,0:T(8,128)(2,1)S(1)} %collective-permute-done.43), channel_id=1, source_target_pairs={{2,3},{3,2},{4,5},{5,4},{6,7},{7,6},{10,11},{11,10},{12,13},{13,12... | collective-permute-start | bytes 2359304 | tf_op jit(solution)/shard_map/ppermute | solution.py:398
  415.5 303.9 %collective-permute-start.136 = (bf16[8,192,2048]{2,1,0:T(8,128)(2,1)}, bf16[8,192,2048]{2,1,0:T(8,128)(2,1)}, u32[]{:S(2)}, u32[]{:S(2)}) collective-permute-start(bf16[8,192,2048]{2,1,0:T(8,128)(2,1)} %bitcast.82), channel_id=1, source_target_pairs={{0,16},{1,17},{2,18},{3,19},{4,20},{5,21},{6,22},{7,23},{8,24},{9,... | collective-permute-start | bytes 18874376 | tf_op jit(solution)/shard_map/ppermute | solution.py:398
  417.1 307.5 %collective-permute-start.138 = (bf16[8,192,2048]{2,1,0:T(8,128)(2,1)}, bf16[8,192,2048]{2,1,0:T(8,128)(2,1)}, u32[]{:S(2)}, u32[]{:S(2)}) collective-permute-start(bf16[8,192,2048]{2,1,0:T(8,128)(2,1)} %bitcast.130), channel_id=1, source_target_pairs={{0,16},{1,17},{2,18},{3,19},{4,20},{5,21},{6,22},{7,23},{8,24},{9,... | collective-permute-start | bytes 18874376 | tf_op jit(solution)/shard_map/ppermute | solution.py:398
  419.1 308.5 %collective-permute-start.55 = (bf16[8,192,2048]{2,1,0:T(8,128)(2,1)}, bf16[8,192,2048]{2,1,0:T(8,128)(2,1)}, u32[]{:S(2)}, u32[]{:S(2)}) collective-permute-start(bf16[8,192,2048]{2,1,0:T(8,128)(2,1)} %bitcast.82), channel_id=1, source_target_pairs={{0,8},{1,9},{2,10},{3,11},{4,12},{5,13},{6,14},{7,15},{8,0},{9,1},... | collective-permute-start | bytes 18874376 | tf_op jit(solution)/shard_map/ppermute | solution.py:398
  433.1 249.4 %collective-permute-start.37 = (bf16[2,32,192]{2,1,0:T(8,128)(2,1)S(1)}, bf16[2,32,192]{2,1,0:T(8,128)(2,1)S(1)}, u32[]{:S(2)}, u32[]{:S(2)}) collective-permute-start(bf16[2,32,192]{2,1,0:T(8,128)(2,1)S(1)} %maximum_select_fusion.42), channel_id=1, source_target_pairs={{0,16},{1,17},{2,18},{3,19},{4,20},{5,21},{6,22},{7,23},{8,24},{9,... | collective-permute-start | bytes 73736 | tf_op jit(solution)/shard_map/ppermute | solution.py:398
  433.2 261.6 %collective-permute-start.59 = (bf16[2,256,32]{1,2,0:T(8,128)(2,1)S(1)}, bf16[2,256,32]{1,2,0:T(8,128)(2,1)S(1)}, u32[]{:S(2)}, u32[]{:S(2)}) collective-permute-start(bf16[2,256,32]{1,2,0:T(8,128)(2,1)S(1)} %maximum_select_fusion.44), channel_id=1, source_target_pairs={{0,6},{1,7},{2,0},{3,1},{4,2},{5,3},{6,4},{7,5},{8,14},{9,15},{10,... | collective-permute-start | bytes 98312 | tf_op jit(solution)/shard_map/ppermute | solution.py:398
  719.5 52.8 %collective-permute-start.137 = (bf16[8,192,2048]{2,1,0:T(8,128)(2,1)}, bf16[8,192,2048]{2,1,0:T(8,128)(2,1)}, u32[]{:S(2)}, u32[]{:S(2)}) collective-permute-start(bf16[8,192,2048]{2,1,0:T(8,128)(2,1)} %collective-permute-done.136), channel_id=1, source_target_pairs={{0,8},{1,9},{2,10},{3,11},{4,12},{5,13},{6,14},{7,15},{8,0},{9,1},... | collective-permute-start | bytes 18874376 | tf_op jit(solution)/shard_map/ppermute | solution.py:398
  724.1 67.9 %collective-permute-start.84 = (bf16[8,192,2048]{2,1,0:T(8,128)(2,1)}, bf16[8,192,2048]{2,1,0:T(8,128)(2,1)}, u32[]{:S(2)}, u32[]{:S(2)}) collective-permute-start(bf16[8,192,2048]{2,1,0:T(8,128)(2,1)} %bitcast.130), channel_id=1, source_target_pairs={{0,8},{1,9},{2,10},{3,11},{4,12},{5,13},{6,14},{7,15},{8,0},{9,1},... | collective-permute-start | bytes 18874376 | tf_op jit(solution)/shard_map/ppermute | solution.py:398
  724.6 210.5 %collective-permute-start.139 = (bf16[8,192,2048]{2,1,0:T(8,128)(2,1)}, bf16[8,192,2048]{2,1,0:T(8,128)(2,1)}, u32[]{:S(2)}, u32[]{:S(2)}) collective-permute-start(bf16[8,192,2048]{2,1,0:T(8,128)(2,1)} %collective-permute-done.138), channel_id=1, source_target_pairs={{0,8},{1,9},{2,10},{3,11},{4,12},{5,13},{6,14},{7,15},{8,0},{9,1},... | collective-permute-start | bytes 18874376 | tf_op jit(solution)/shard_map/ppermute | solution.py:398
  853.0 226.3 %collective-permute-start.96 = (f32[32,1536]{1,0:T(8,128)}, f32[32,1536]{1,0:T(8,128)}, u32[]{:S(2)}, u32[]{:S(2)}) collective-permute-start(f32[32,1536]{1,0:T(8,128)} %dynamic-slice_bitcast_fusion.20), channel_id=1, source_target_pairs={{0,8},{1,9},{2,10},{3,11},{4,12},{5,13},{6,14},{7,15},{8,0},{9,1},... | collective-permute-start | bytes 589832 | tf_op jit(solution)/shard_map/ppermute | solution.py:398
  902.1 202.8 %collective-permute-start.60 = (bf16[1536,2048]{1,0:T(8,128)(2,1)}, bf16[1536,2048]{1,0:T(8,128)(2,1)}, u32[]{:S(2)}, u32[]{:S(2)}) collective-permute-start(bf16[1536,2048]{1,0:T(8,128)(2,1)} %dynamic-slice_bitcast_fusion.2), channel_id=1, source_target_pairs={{0,8},{1,9},{2,10},{3,11},{4,12},{5,13},{6,14},{7,15},{8,0},{9,1},... | collective-permute-start | bytes 18874376 | tf_op jit(solution)/shard_map/ppermute | solution.py:398
  1035.7 84.9 %collective-permute-start.85 = (bf16[1536,2048]{1,0:T(8,128)(2,1)}, bf16[1536,2048]{1,0:T(8,128)(2,1)}, u32[]{:S(2)}, u32[]{:S(2)}) collective-permute-start(bf16[1536,2048]{1,0:T(8,128)(2,1)} %dynamic-slice_bitcast_fusion.1), channel_id=1, source_target_pairs={{0,8},{1,9},{2,10},{3,11},{4,12},{5,13},{6,14},{7,15},{8,0},{9,1},... | collective-permute-start | bytes 18874376 | tf_op jit(solution)/shard_map/ppermute | solution.py:398
  1104.4 141.2 %collective-permute-start.140 = (bf16[2,2048,1024]{2,1,0:T(8,128)(2,1)}, bf16[2,2048,1024]{2,1,0:T(8,128)(2,1)}, u32[]{:S(2)}, u32[]{:S(2)}) collective-permute-start(bf16[2,2048,1024]{2,1,0:T(8,128)(2,1)} %bitcast_convert_fusion.5), channel_id=1, source_target_pairs={{0,8},{1,9},{2,10},{3,11},{4,12},{5,13},{6,14},{7,15},{8,0},{9,1},... | collective-permute-start | bytes 25165832 | tf_op jit(solution)/shard_map/ppermute | solution.py:398
  1104.4 105.3 %collective-permute-start.142 = (bf16[2,1024,2048]{2,1,0:T(8,128)(2,1)}, bf16[2,1024,2048]{2,1,0:T(8,128)(2,1)}, u32[]{:S(2)}, u32[]{:S(2)}) collective-permute-start(bf16[2,1024,2048]{2,1,0:T(8,128)(2,1)} %bitcast_convert_fusion.3), channel_id=1, source_target_pairs={{0,8},{1,9},{2,10},{3,11},{4,12},{5,13},{6,14},{7,15},{8,0},{9,1},... | collective-permute-start | bytes 25165832 | tf_op jit(solution)/shard_map/ppermute | solution.py:398
  1104.9 53.2 %collective-permute-start.98 = (f32[32,192]{1,0:T(8,128)S(1)}, f32[32,192]{1,0:T(8,128)S(1)}, u32[]{:S(2)}, u32[]{:S(2)}) collective-permute-start(f32[32,192]{1,0:T(8,128)S(1)} %get-tuple-element.131), channel_id=1, source_target_pairs={{0,2},{1,3},{2,4},{3,5},{4,6},{5,7},{6,0},{7,1},{8,10},{9,11},{10,... | collective-permute-start | bytes 73736 | tf_op jit(solution)/shard_map/ppermute | solution.py:398
  1119.3 48.2 %collective-permute-start.62 = (bf16[192,2048]{1,0:T(8,128)(2,1)S(1)}, bf16[192,2048]{1,0:T(8,128)(2,1)S(1)}, u32[]{:S(2)}, u32[]{:S(2)}) collective-permute-start(bf16[192,2048]{1,0:T(8,128)(2,1)S(1)} %get-tuple-element.108), channel_id=1, source_target_pairs={{0,1},{1,0},{2,3},{3,2},{4,5},{5,4},{6,7},{7,6},{8,9},{9,8},{10,11... | collective-permute-start | bytes 2359304 | tf_op jit(solution)/shard_map/ppermute | solution.py:398
  1198.3 134.0 %collective-permute-start.141 = (bf16[2,2048,1024]{2,1,0:T(8,128)(2,1)}, bf16[2,2048,1024]{2,1,0:T(8,128)(2,1)}, u32[]{:S(2)}, u32[]{:S(2)}) collective-permute-start(bf16[2,2048,1024]{2,1,0:T(8,128)(2,1)} %bitcast_convert_fusion.4), channel_id=1, source_target_pairs={{0,8},{1,9},{2,10},{3,11},{4,12},{5,13},{6,14},{7,15},{8,0},{9,1},... | collective-permute-start | bytes 25165832 | tf_op jit(solution)/shard_map/ppermute | solution.py:398
  1198.4 39.9 %collective-permute-start.88 = (bf16[192,2048]{1,0:T(8,128)(2,1)S(1)}, bf16[192,2048]{1,0:T(8,128)(2,1)S(1)}, u32[]{:S(2)}, u32[]{:S(2)}) collective-permute-start(bf16[192,2048]{1,0:T(8,128)(2,1)S(1)} %get-tuple-element.103), channel_id=1, source_target_pairs={{0,1},{1,0},{2,3},{3,2},{4,5},{5,4},{6,7},{7,6},{8,9},{9,8},{10,11... | collective-permute-start | bytes 2359304 | tf_op jit(solution)/shard_map/ppermute | solution.py:398
  1202.4 37.3 %collective-permute-start.91 = (bf16[192,2048]{1,0:T(8,128)(2,1)S(1)}, bf16[192,2048]{1,0:T(8,128)(2,1)S(1)}, u32[]{:S(2)}, u32[]{:S(2)}) collective-permute-start(bf16[192,2048]{1,0:T(8,128)(2,1)S(1)} %get-tuple-element.93), channel_id=1, source_target_pairs={{0,2},{1,3},{2,4},{3,5},{8,10},{9,11},{10,12},{11,13},{16,18},{17,... | collective-permute-start | bytes 2359304 | tf_op jit(solution)/shard_map/ppermute | solution.py:398
  1238.3 121.7 %collective-permute-start.63 = (bf16[192,2048]{1,0:T(8,128)(2,1)}, bf16[192,2048]{1,0:T(8,128)(2,1)}, u32[]{:S(2)}, u32[]{:S(2)}) collective-permute-start(bf16[192,2048]{1,0:T(8,128)(2,1)} %get-tuple-element.107), channel_id=1, source_target_pairs={{0,1},{1,0},{2,3},{3,2},{4,5},{5,4},{6,7},{7,6},{8,9},{9,8},{10,11... | collective-permute-start | bytes 2359304 | tf_op jit(solution)/shard_map/ppermute | solution.py:398
  1239.7 31.1 %collective-permute-start.86 = (bf16[192,2048]{1,0:T(8,128)(2,1)S(1)}, bf16[192,2048]{1,0:T(8,128)(2,1)S(1)}, u32[]{:S(2)}, u32[]{:S(2)}) collective-permute-start(bf16[192,2048]{1,0:T(8,128)(2,1)S(1)} %get-tuple-element.101), channel_id=1, source_target_pairs={{0,1},{1,0},{2,3},{3,2},{4,5},{5,4},{6,7},{7,6},{8,9},{9,8},{10,11... | collective-permute-start | bytes 2359304 | tf_op jit(solution)/shard_map/ppermute | solution.py:398
  1241.0 34.8 %collective-permute-start.92 = (bf16[192,2048]{1,0:T(8,128)(2,1)S(1)}, bf16[192,2048]{1,0:T(8,128)(2,1)S(1)}, u32[]{:S(2)}, u32[]{:S(2)}) collective-permute-start(bf16[192,2048]{1,0:T(8,128)(2,1)S(1)} %get-tuple-element.87), channel_id=1, source_target_pairs={{0,2},{1,3},{2,4},{3,5},{4,6},{5,7},{8,10},{9,11},{10,12},{11,13},... | collective-permute-start | bytes 2359304 | tf_op jit(solution)/shard_map/ppermute | solution.py:398
  1245.5 31.8 %collective-permute-start.95 = (bf16[192,2048]{1,0:T(8,128)(2,1)S(1)}, bf16[192,2048]{1,0:T(8,128)(2,1)S(1)}, u32[]{:S(2)}, u32[]{:S(2)}) collective-permute-start(bf16[192,2048]{1,0:T(8,128)(2,1)S(1)} %get-tuple-element.88), channel_id=1, source_target_pairs={{2,0},{3,1},{4,2},{5,3},{6,4},{7,5},{10,8},{11,9},{12,10},{13,11},... | collective-permute-start | bytes 2359304 | tf_op jit(solution)/shard_map/ppermute | solution.py:398
  1270.8 89.2 %collective-permute-start.66 = (bf16[192,2048]{1,0:T(8,128)(2,1)}, bf16[192,2048]{1,0:T(8,128)(2,1)}, u32[]{:S(2)}, u32[]{:S(2)}) collective-permute-start(bf16[192,2048]{1,0:T(8,128)(2,1)} %get-tuple-element.95), channel_id=1, source_target_pairs={{0,2},{1,3},{2,4},{3,5},{8,10},{9,11},{10,12},{11,13},{16,18},{17,... | collective-permute-start | bytes 2359304 | tf_op jit(solution)/shard_map/ppermute | solution.py:398
  1275.8 84.1 %collective-permute-start.69 = (bf16[192,2048]{1,0:T(8,128)(2,1)}, bf16[192,2048]{1,0:T(8,128)(2,1)}, u32[]{:S(2)}, u32[]{:S(2)}) collective-permute-start(bf16[192,2048]{1,0:T(8,128)(2,1)} %get-tuple-element.96), channel_id=1, source_target_pairs={{4,2},{5,3},{6,4},{7,5},{12,10},{13,11},{14,12},{15,13},{20,18},{2... | collective-permute-start | bytes 2359304 | tf_op jit(solution)/shard_map/ppermute | solution.py:398
  1332.4 54.9 %collective-permute-start.110 = (bf16[8,128,3072]{2,1,0:T(8,128)(2,1)}, bf16[8,128,3072]{2,1,0:T(8,128)(2,1)}, u32[]{:S(2)}, u32[]{:S(2)}) collective-permute-start(bf16[8,128,3072]{2,1,0:T(8,128)(2,1)} %dynamic-slice_bitcast_fusion), channel_id=1, source_target_pairs={{0,8},{1,9},{2,10},{3,11},{4,12},{5,13},{6,14},{7,15},{8,0},{9,1},... | collective-permute-start | bytes 18874376 | tf_op jit(solution)/shard_map/ppermute | solution.py:398
  1386.6 42.6 %collective-permute-start.103 = (bf16[192,2048]{1,0:T(8,128)(2,1)}, bf16[192,2048]{1,0:T(8,128)(2,1)S(1)}, u32[]{:S(2)}, u32[]{:S(2)}) collective-permute-start(bf16[192,2048]{1,0:T(8,128)(2,1)} %fusion.161), channel_id=1, source_target_pairs={{0,16},{1,17},{2,18},{3,19},{4,20},{5,21},{6,22},{7,23},{8,24},{9,... | collective-permute-start | bytes 2359304 | tf_op jit(solution)/shard_map/ppermute | solution.py:398
  1406.5 37.6 %collective-permute-start.114 = (bf16[128,3072]{1,0:T(8,128)(2,1)}, bf16[128,3072]{1,0:T(8,128)(2,1)}, u32[]{:S(2)}, u32[]{:S(2)}) collective-permute-start(bf16[128,3072]{1,0:T(8,128)(2,1)} %get-tuple-element.98), channel_id=1, source_target_pairs={{0,1},{1,0},{2,3},{3,2},{4,5},{5,4},{6,7},{7,6},{8,9},{9,8},{10,11... | collective-permute-start | bytes 2359304 | tf_op jit(solution)/shard_map/ppermute | solution.py:398
  1453.2 31.6 %collective-permute-start.61 = (bf16[192,2048]{1,0:T(8,128)(2,1)S(1)}, bf16[192,2048]{1,0:T(8,128)(2,1)S(1)}, u32[]{:S(2)}, u32[]{:S(2)}) collective-permute-start(bf16[192,2048]{1,0:T(8,128)(2,1)S(1)} %copy-done.47), channel_id=1, source_target_pairs={{0,1},{1,0},{2,3},{3,2},{4,5},{5,4},{6,7},{7,6},{8,9},{9,8},{10,11... | collective-permute-start | bytes 2359304 | tf_op jit(solution)/shard_map/ppermute | solution.py:398
  1454.7 32.8 %collective-permute-start.67 = (bf16[192,2048]{1,0:T(8,128)(2,1)S(1)}, bf16[192,2048]{1,0:T(8,128)(2,1)S(1)}, u32[]{:S(2)}, u32[]{:S(2)}) collective-permute-start(bf16[192,2048]{1,0:T(8,128)(2,1)S(1)} %copy-done.49), channel_id=1, source_target_pairs={{0,2},{1,3},{2,4},{3,5},{4,6},{5,7},{8,10},{9,11},{10,12},{11,13},... | collective-permute-start | bytes 2359304 | tf_op jit(solution)/shard_map/ppermute | solution.py:398
  1527.2 50.4 %collective-permute-start.122 = (bf16[256,3072]{0,1:T(8,128)(2,1)}, bf16[256,3072]{0,1:T(8,128)(2,1)S(1)}, u32[]{:S(2)}, u32[]{:S(2)}) collective-permute-start(bf16[256,3072]{0,1:T(8,128)(2,1)} %copy.292), channel_id=1, source_target_pairs={{0,16},{1,17},{2,18},{3,19},{4,20},{5,21},{6,22},{7,23},{8,24},{9,... | collective-permute-start | bytes 4718600 | tf_op jit(solution)/shard_map/ppermute | solution.py:398
  1530.2 45.2 %collective-permute-start.135 = (bf16[128,2048]{1,0:T(8,128)(2,1)S(1)}, bf16[128,2048]{1,0:T(8,128)(2,1)S(1)}, u32[]{:S(2)}, u32[]{:S(2)}) collective-permute-start(bf16[128,2048]{1,0:T(8,128)(2,1)S(1)} %bitcast.712), channel_id=1, source_target_pairs={{0,16},{1,17},{2,18},{3,19},{4,20},{5,21},{6,22},{7,23},{8,24},{9,... | collective-permute-start | bytes 1572872 | tf_op jit(solution)/shard_map/ppermute | solution.py:398
  (189 other events, 4244.1 us)

commit v2 on v0

--- a/solution.py
+++ b/solution.py
@@ -1,6 +1,8 @@
 import jax
 import jax.numpy as jnp
 from jax import lax
+from jax.experimental import pallas as pl
+from jax.experimental.pallas import tpu as pltpu
 from jax.sharding import PartitionSpec as P
 
 HEADS = 16
@@ -373,7 +375,1037 @@
     )
 
 
+AXES = ("rep", "shard")
+LINE = 4
+SHARDS = 8
+REPS = 4
+
+
+def pairs_of(target):
+    moves = []
+    for rep in range(REPS):
+        for shard in range(SHARDS):
+            there = target(rep, shard)
+            moves.append((rep * SHARDS + shard, there[0] * SHARDS + there[1]))
+    return moves
+
+
+CORE_SWAP = pairs_of(lambda rep, shard: (rep ^ 1, shard))
+X_SWAP = pairs_of(lambda rep, shard: (rep ^ 2, shard))
+Y_SWAP = pairs_of(lambda rep, shard: (rep, shard ^ 1))
+Z_FROM = [pairs_of(lambda rep, shard: (rep, (shard - 2 * k) % SHARDS)) for k in range(LINE)]
+Z_TO = [pairs_of(lambda rep, shard: (rep, (shard + 2 * k) % SHARDS)) for k in range(LINE)]
+
+
+def move(values, moves):
+    return lax.ppermute(values, AXES, moves)
+
+
+def after(values, *others):
+    return lax.optimization_barrier((values,) + others)[0]
+
+
+def gather_small(values):
+    line = jnp.stack([values] + [move(values, Z_FROM[k]) for k in range(1, LINE)])
+    both = jnp.stack([line, move(line, Y_SWAP)], axis=1)
+    return both.reshape((SHARDS,) + values.shape)
+
+
+def gather_rows(values, early=None, late=None, fill=None):
+    moved = {k: move(values, Z_FROM[k]) for k in (1, 3)}
+    moved[2] = move(after(values, moved[1]), Z_FROM[2])
+    mine, beside = {0: values}, {0: move(values, Y_SWAP)}
+    for k in (1, 3, 2):
+        mine[k] = moved[k] if early is None else after(moved[k], early)
+        if k == 2 and fill is not None:
+            mine[k] = after(mine[k], *fill(mine[3]))
+        beside[k] = move(mine[k], Y_SWAP)
+    if late is not None:
+        beside = {k: after(beside[k], late) for k in beside}
+    return [(mine[k], beside[k]) for k in range(LINE)]
+
+
+def flat(pieces):
+    return jnp.concatenate([piece for pair in pieces for piece in pair], axis=0)
+
+
+def added(first, *others):
+    total = first.astype(jnp.float32)
+    for other in others:
+        total = total + other.astype(jnp.float32)
+    return total.astype(first.dtype)
+
+
+def scatter_rows(parts, fills):
+    moved = {}
+    for k in (2, 1, 3, 0):
+        moved[k] = move(added(*[part(2 * k + 1) for part in parts]), Y_SWAP)
+    arrived, reduced, last = [], None, moved[2]
+    for k, fill in zip((2, 1, 3, 0), fills):
+        here = moved[k]
+        if fill is not None:
+            here = after(here, *fill(() if reduced is None else (reduced,)))
+        reduced = added(here, *[part(2 * k) for part in parts])
+        if k > 0:
+            arrived.append(move(reduced, Z_TO[k]))
+    if fills[4] is not None:
+        reduced = after(reduced, *fills[4]((reduced,)))
+    return added(reduced, *arrived)
+
+
+LIMIT = 56 * 2**20
+HIDDEN_BLOCK = 256
+WIDTH_BLOCK = 512
+QUIET = pl.CostEstimate(flops=0, bytes_accessed=0, transcendentals=0)
+
+
+def ordered(kernel, behind):
+    def body(scalar_ref, *refs):
+        return kernel(scalar_ref, *refs[behind:])
+
+    return body
+
+
+HELD = pl.BlockSpec(memory_space=pl.ANY)
+
+
+def copy_block(order_ref, from_ref, into_ref):
+    into_ref[...] = from_ref[...]
+
+
+def pick_columns(values, order, block):
+    rows = values.shape[0]
+    picks = order.shape[0]
+    return pl.pallas_call(
+        copy_block,
+        grid_spec=pltpu.PrefetchScalarGridSpec(
+            num_scalar_prefetch=1,
+            grid=(picks,),
+            in_specs=[pl.BlockSpec((rows, block), lambda i, order: (0, order[i]))],
+            out_specs=pl.BlockSpec((rows, block), lambda i, order: (0, i)),
+        ),
+        out_shape=jax.ShapeDtypeStruct((rows, picks * block), values.dtype),
+        compiler_params=pltpu.CompilerParams(vmem_limit_bytes=32 * 2**20),
+    )(order, values)
+
+
+def thin_kernel(rep_ref, from_ref, into_ref):
+    heads = into_ref.shape[1] // HEAD_DIM
+
+    def take(parity):
+        for head in range(heads):
+            start = (2 * head + parity) * HEAD_DIM
+            into_ref[:, head * HEAD_DIM : (head + 1) * HEAD_DIM] = from_ref[
+                :, start : start + HEAD_DIM
+            ]
+
+    @pl.when(rep_ref[0] < 2)
+    def _():
+        take(0)
+
+    @pl.when(rep_ref[0] >= 2)
+    def _():
+        take(1)
+
+
+def thin_columns(weights, rep, width):
+    rows = weights.shape[0]
+    return pl.pallas_call(
+        thin_kernel,
+        grid_spec=pltpu.PrefetchScalarGridSpec(
+            num_scalar_prefetch=1,
+            grid=(3,),
+            in_specs=[
+                pl.BlockSpec((rows, width // 2), lambda i, rep: (0, 2 * i + lax.rem(rep[0], 2)))
+            ],
+            out_specs=pl.BlockSpec((rows, width // 4), lambda i, rep: (0, i)),
+        ),
+        out_shape=jax.ShapeDtypeStruct((rows, 3 * width // 4), weights.dtype),
+        compiler_params=pltpu.CompilerParams(vmem_limit_bytes=32 * 2**20),
+    )(rep, weights)
+
+
+def weave_kernel(rep_ref, even_ref, odd_ref, into_ref):
+    for head in range(even_ref.shape[2] // HEAD_DIM):
+        part = slice(head * HEAD_DIM, (head + 1) * HEAD_DIM)
+        start = 2 * head * HEAD_DIM
+        into_ref[:, start : start + HEAD_DIM] = even_ref[0, :, part].astype(jnp.float32)
+        into_ref[:, start + HEAD_DIM : start + 2 * HEAD_DIM] = odd_ref[0, :, part].astype(
+            jnp.float32
+        )
+
+
+def weave_columns(pieces, rep, columns, behind):
+    rows = pieces.shape[1]
+    block = columns // 3
+    return pl.pallas_call(
+        ordered(weave_kernel, len(behind)),
+        grid_spec=pltpu.PrefetchScalarGridSpec(
+            num_scalar_prefetch=1,
+            grid=(3, 2),
+            in_specs=[HELD] * len(behind)
+            + [
+                pl.BlockSpec((1, rows, block), lambda i, j, rep: (j ^ rep[0], 0, i)),
+                pl.BlockSpec((1, rows, block), lambda i, j, rep: ((j + 2) ^ rep[0], 0, i)),
+            ],
+            out_specs=pl.BlockSpec((rows, 2 * block), lambda i, j, rep: (0, 2 * i + j)),
+        ),
+        out_shape=jax.ShapeDtypeStruct((rows, 4 * columns), jnp.float32),
+        compiler_params=pltpu.CompilerParams(vmem_limit_bytes=32 * 2**20),
+    )(rep, *behind, pieces, pieces)
+
+
+def widen_kernel(core_ref, own_ref, other_ref, into_ref):
+    mine = pl.program_id(0) == core_ref[0]
+
+    @pl.when(mine)
+    def _():
+        into_ref[...] = own_ref[...].astype(jnp.float32)
+
+    @pl.when(jnp.logical_not(mine))
+    def _():
+        into_ref[...] = other_ref[...].astype(jnp.float32)
+
+
+def widen(own, other, core, behind=()):
+    experts, rows, columns = own.shape
+    block = rows // 4
+    steps = experts * 4
+
+    def place(hold, core, i, j):
+        return jnp.where(i == hold, j, jnp.where(hold == 0, steps - 1, 0))
+
+    own_map = lambda i, j, core: (place(core[0], core, i, j), 0)
+    other_map = lambda i, j, core: (place(1 - core[0], core, i, j), 0)
+    result = pl.pallas_call(
+        ordered(widen_kernel, len(behind)),
+        grid_spec=pltpu.PrefetchScalarGridSpec(
+            num_scalar_prefetch=1,
+            grid=(2, steps),
+            in_specs=[HELD] * len(behind)
+            + [
+                pl.BlockSpec((block, columns), own_map),
+                pl.BlockSpec((block, columns), other_map),
+            ],
+            out_specs=pl.BlockSpec((block, columns), lambda i, j, core: (i * steps + j, 0)),
+        ),
+        out_shape=jax.ShapeDtypeStruct((2 * experts * rows, columns), jnp.float32),
+        compiler_params=pltpu.CompilerParams(vmem_limit_bytes=32 * 2**20),
+        cost_estimate=QUIET,
+    )(
+        core,
+        *behind,
+        own.reshape(experts * rows, columns),
+        other.reshape(experts * rows, columns),
+    )
+    return result.reshape(2 * experts, rows, columns)
+
+
+def slot_rows(slots, capacity):
+    places = lax.broadcasted_iota(jnp.int32, (capacity, slots.shape[1]), 0)
+    return jnp.where(places == slots, 1.0, 0.0).astype(jnp.bfloat16)
+
+
+def slot_columns(slots, columns):
+    places = lax.broadcasted_iota(jnp.int32, (slots.shape[0], columns), 1)
+    found = places == slots[:, 0:1]
+    for expert in range(1, slots.shape[1]):
+        found = found | (places == slots[:, expert : expert + 1])
+    return jnp.where(found, 1.0, 0.0).astype(jnp.bfloat16)
+
+
+def dot_wide(left, right):
+    return jnp.dot(left, right, preferred_element_type=jnp.float32)
+
+
+def pick_rows_into(slots_ref, rows_ref, into_ref):
+    choice = slot_rows(slots_ref[0], into_ref.shape[1])
+    for start in range(0, rows_ref.shape[1], WIDTH_BLOCK):
+        part = slice(start, start + WIDTH_BLOCK)
+        into_ref[0, :, part] = dot_wide(choice, rows_ref[:, part]).astype(jnp.bfloat16)
+
+
+def cotangent_kernel(core_ref, slots_ref, rows_ref, down_ref, picked_ref, slot_ref):
+    @pl.when(pl.program_id(1) == 0)
+    def _():
+        pick_rows_into(slots_ref, rows_ref, picked_ref)
+
+    slot_ref[0] = contract_cols(picked_ref[0], down_ref[0])
+
+
+def cotangent_part(core, slots, rows, down_weight, capacity, behind=()):
+    experts, tokens = slots.shape
+    width, hidden = rows.shape[1], down_weight.shape[1]
+    return pl.pallas_call(
+        ordered(cotangent_kernel, len(behind)),
+        grid_spec=pltpu.PrefetchScalarGridSpec(
+            num_scalar_prefetch=1,
+            grid=(experts, hidden // HIDDEN_BLOCK),
+            in_specs=[HELD] * len(behind)
+            + [
+                pl.BlockSpec((1, 1, tokens), lambda e, n, core: (e, 0, 0)),
+                pl.BlockSpec((tokens, width), lambda e, n, core: (0, 0)),
+                pl.BlockSpec(
+                    (1, HIDDEN_BLOCK, width), lambda e, n, core: (core[0] * experts + e, n, 0)
+                ),
+            ],
+            out_specs=[
+                pl.BlockSpec((1, capacity, width), lambda e, n, core: (e, 0, 0)),
+                pl.BlockSpec((1, capacity, HIDDEN_BLOCK), lambda e, n, core: (e, 0, n)),
+            ],
+        ),
+        out_shape=[
+            jax.ShapeDtypeStruct((experts, capacity, width), jnp.bfloat16),
+            jax.ShapeDtypeStruct((experts, capacity, hidden), jnp.float32),
+        ],
+        compiler_params=pltpu.CompilerParams(vmem_limit_bytes=LIMIT),
+        cost_estimate=QUIET,
+    )(core, *behind, slots[:, None, :], rows, down_weight)
+
+
+def forward_kernel(
+    first_ref,
+    slots_ref,
+    rows_ref,
+    router_ref,
+    gate_ref,
+    up_ref,
+    slot_ref,
+    picked_ref,
+    act_ref,
+    grad_gate_ref,
+    grad_up_ref,
+    score_ref,
+    weight_ref,
+    total_ref,
+):
+    step = pl.program_id(1)
+    mine = first_ref[1] + pl.program_id(0)
+
+    @pl.when(step == 0)
+    def _():
+        pick_rows_into(slots_ref, rows_ref, picked_ref)
+        logits = contract_cols(picked_ref[0], router_ref[...])
+        raised = jnp.exp(logits - jnp.max(logits, axis=1, keepdims=True))
+        label = lax.broadcasted_iota(jnp.int32, raised.shape, 1)
+        own = jnp.sum(jnp.where(label == mine, raised, 0.0), axis=1, keepdims=True)
+        weight_ref[...] = own / jnp.sum(raised, axis=1, keepdims=True)
+        total_ref[...] = jnp.zeros_like(total_ref)
+
+    gate_pre = dot_wide(picked_ref[0], gate_ref[0])
+    up_pre = dot_wide(picked_ref[0], up_ref[0])
+    sigmoid = 1.0 / (1.0 + jnp.exp(-gate_pre))
+    smooth = gate_pre * sigmoid
+    grad_act = weight_ref[...] * slot_ref[0]
+    act = smooth * up_pre
+    act_ref[0] = (weight_ref[...] * act).astype(jnp.bfloat16)
+    grad_gate_ref[0] = (grad_act * up_pre * (sigmoid + smooth * (1.0 - sigmoid))).astype(
+        jnp.bfloat16
+    )
+    grad_up_ref[0] = (grad_act * smooth).astype(jnp.bfloat16)
+    total_ref[...] += jnp.sum(act * grad_act, axis=1, keepdims=True)
+
+    @pl.when(step == pl.num_programs(1) - 1)
+    def _():
+        label = lax.broadcasted_iota(jnp.int32, score_ref.shape[1:], 1)
+        score_ref[0] = jnp.where(label == mine, total_ref[...], 0.0).astype(jnp.bfloat16)
+
+
+def forward_part(first, slots, rows, router_rows, gate_weight, up_weight, slot_cot, behind=()):
+    experts, tokens = slots.shape
+    capacity, hidden = slot_cot.shape[1:]
+    width = rows.shape[1]
+    labels = router_rows.shape[0]
+    weight_spec = pl.BlockSpec(
+        (1, width, HIDDEN_BLOCK), lambda e, n, first: (first[0] * experts + e, 0, n)
+    )
+    hidden_spec = pl.BlockSpec((1, capacity, HIDDEN_BLOCK), lambda e, n, first: (e, 0, n))
+    hidden_shape = jax.ShapeDtypeStruct((experts, capacity, hidden), jnp.bfloat16)
+    return pl.pallas_call(
+        ordered(forward_kernel, len(behind)),
+        grid_spec=pltpu.PrefetchScalarGridSpec(
+            num_scalar_prefetch=1,
+            grid=(experts, hidden // HIDDEN_BLOCK),
+            in_specs=[HELD] * len(behind)
+            + [
+                pl.BlockSpec((1, 1, tokens), lambda e, n, first: (e, 0, 0)),
+                pl.BlockSpec((tokens, width), lambda e, n, first: (0, 0)),
+                pl.BlockSpec((labels, width), lambda e, n, first: (0, 0)),
+                weight_spec,
+                weight_spec,
+                hidden_spec,
+            ],
+            out_specs=[
+                pl.BlockSpec((1, capacity, width), lambda e, n, first: (e, 0, 0)),
+                hidden_spec,
+                hidden_spec,
+                hidden_spec,
+                pl.BlockSpec((1, capacity, HEAD_DIM), lambda e, n, first: (e, 0, 0)),
+            ],
+            scratch_shapes=[
+                pltpu.VMEM((capacity, 1), jnp.float32),
+                pltpu.VMEM((capacity, 1), jnp.float32),
+            ],
+        ),
+        out_shape=[
+            jax.ShapeDtypeStruct((experts, capacity, width), jnp.bfloat16),
+            hidden_shape,
+            hidden_shape,
+            hidden_shape,
+            jax.ShapeDtypeStruct((experts, capacity, HEAD_DIM), jnp.bfloat16),
+        ],
+        compiler_params=pltpu.CompilerParams(vmem_limit_bytes=LIMIT),
+        cost_estimate=QUIET,
+    )(first, *behind, slots[:, None, :], rows, router_rows, gate_weight, up_weight, slot_cot)
+
+
+def backward_kernel(
+    core_ref, slots_ref, grad_gate_ref, grad_up_ref, score_ref, *rest
+):
+    experts, capacity, _ = grad_gate_ref.shape
+    gates, ups = rest[:experts], rest[experts : 2 * experts]
+    into_ref, spread_ref, slot_ref = rest[2 * experts :]
+    step = pl.program_id(0)
+    width = pl.num_programs(0) * WIDTH_BLOCK
+
+    @pl.when(step == 0)
+    def _():
+        spread_ref[...] = slot_columns(slots_ref[...], experts * capacity)
+        scores = score_ref[...].reshape(experts * capacity, HEAD_DIM)
+        into_ref[:, width:] = dot_wide(spread_ref[...], scores).astype(jnp.bfloat16)
+
+    for expert in range(experts):
+        rows = contract_cols(grad_gate_ref[expert], gates[expert][0]) + contract_cols(
+            grad_up_ref[expert], ups[expert][0]
+        )
+        slot_ref[expert * capacity : (expert + 1) * capacity, :] = rows.astype(jnp.bfloat16)
+    start = pl.multiple_of(step * WIDTH_BLOCK, WIDTH_BLOCK)
+    into_ref[:, pl.ds(start, WIDTH_BLOCK)] = dot_wide(spread_ref[...], slot_ref[...]).astype(
+        jnp.bfloat16
+    )
+
+
+def backward_part(core, columns, grad_gate, grad_up, scores, gate_weight, up_weight, behind=()):
+    experts, capacity, hidden = grad_gate.shape
+    tokens, width = columns.shape[0], gate_weight.shape[1]
+
+    def weight_spec(expert):
+        return pl.BlockSpec(
+            (1, WIDTH_BLOCK, hidden), lambda n, core: (core[0] * experts + expert, n, 0)
+        )
+
+    whole = pl.BlockSpec((experts, capacity, hidden), lambda n, core: (0, 0, 0))
+    return pl.pallas_call(
+        ordered(backward_kernel, len(behind)),
+        grid_spec=pltpu.PrefetchScalarGridSpec(
+            num_scalar_prefetch=1,
+            grid=(width // WIDTH_BLOCK,),
+            in_specs=[HELD] * len(behind)
+            + [
+                pl.BlockSpec(columns.shape, lambda n, core: (0, 0)),
+                whole,
+                whole,
+                pl.BlockSpec((experts, capacity, HEAD_DIM), lambda n, core: (0, 0, 0)),
+            ]
+            + [weight_spec(expert) for expert in range(experts)] * 2,
+            out_specs=pl.BlockSpec((tokens, width + HEAD_DIM), lambda n, core: (0, 0)),
+            scratch_shapes=[
+                pltpu.VMEM((tokens, experts * capacity), jnp.bfloat16),
+                pltpu.VMEM((experts * capacity, WIDTH_BLOCK), jnp.bfloat16),
+            ],
+        ),
+        out_shape=jax.ShapeDtypeStruct((tokens, width + HEAD_DIM), jnp.bfloat16),
+        compiler_params=pltpu.CompilerParams(vmem_limit_bytes=LIMIT),
+        cost_estimate=QUIET,
+    )(
+        core,
+        *behind,
+        columns,
+        grad_gate,
+        grad_up,
+        scores,
+        *[gate_weight] * experts,
+        *[up_weight] * experts,
+    )
+
+
+def routed_kernel(core_ref, slots_ref, act_ref, *rest):
+    experts, capacity, _ = act_ref.shape
+    downs = rest[:experts]
+    into_ref, spread_ref, slot_ref = rest[experts:]
+
+    @pl.when(pl.program_id(0) == 0)
+    def _():
+        spread_ref[...] = slot_columns(slots_ref[...], experts * capacity)
+
+    for expert in range(experts):
+        rows = dot_wide(act_ref[expert], downs[expert][0])
+        slot_ref[expert * capacity : (expert + 1) * capacity, :] = rows.astype(jnp.bfloat16)
+    into_ref[...] = dot_wide(spread_ref[...], slot_ref[...]).astype(jnp.bfloat16)
+
+
+def routed_part(core, columns, act, down_weight, behind=()):
+    experts, capacity, hidden = act.shape
+    tokens, width = columns.shape[0], down_weight.shape[2]
+
+    def weight_spec(expert):
+        return pl.BlockSpec(
+            (1, hidden, WIDTH_BLOCK), lambda n, core: (core[0] * experts + expert, 0, n)
+        )
+
+    return pl.pallas_call(
+        ordered(routed_kernel, len(behind)),
+        grid_spec=pltpu.PrefetchScalarGridSpec(
+            num_scalar_prefetch=1,
+            grid=(width // WIDTH_BLOCK,),
+            in_specs=[HELD] * len(behind)
+            + [
+                pl.BlockSpec(columns.shape, lambda n, core: (0, 0)),
+                pl.BlockSpec((experts, capacity, hidden), lambda n, core: (0, 0, 0)),
+            ]
+            + [weight_spec(expert) for expert in range(experts)],
+            out_specs=pl.BlockSpec((tokens, WIDTH_BLOCK), lambda n, core: (0, n)),
+            scratch_shapes=[
+                pltpu.VMEM((tokens, experts * capacity), jnp.bfloat16),
+                pltpu.VMEM((experts * capacity, WIDTH_BLOCK), jnp.bfloat16),
+            ],
+        ),
+        out_shape=jax.ShapeDtypeStruct((tokens, width), jnp.bfloat16),
+        compiler_params=pltpu.CompilerParams(vmem_limit_bytes=LIMIT),
+        cost_estimate=QUIET,
+    )(core, *behind, columns, act, *[down_weight] * experts)
+
+
+def roll_half(values):
+    return pltpu.roll(values, HEAD_DIM // 2, 1)
+
+
+def head_parts(raw_ref, rate_ref, gain_ref, cos_ref, sin_ref, head):
+    part_width = gain_ref.shape[1]
+    units, turned = [], []
+    for which in range(2):
+        start = which * part_width + head * HEAD_DIM
+        unit = raw_ref[:, start : start + HEAD_DIM] * rate_ref[:, which : which + 1]
+        gain = gain_ref[which : which + 1, head * HEAD_DIM : (head + 1) * HEAD_DIM]
+        scaled = unit * gain
+        units.append((unit, gain))
+        turned.append(
+            (scaled * cos_ref[...] + roll_half(scaled) * sin_ref[...]).astype(jnp.bfloat16)
+        )
+    start = 2 * part_width + head * HEAD_DIM
+    value = raw_ref[:, start : start + HEAD_DIM].astype(jnp.bfloat16)
+    return units, turned, value
+
+
+def head_probs(turned, column_ref, row_ref):
+    scores = contract_cols(turned[0], turned[1]) * HEAD_DIM ** (-0.5)
+    length = scores.shape[0]
+    reader = lax.broadcasted_iota(jnp.int32, (length, length), 0)
+    source = lax.broadcasted_iota(jnp.int32, (length, length), 1)
+    allowed = (column_ref[...] == row_ref[0]) & (source <= reader)
+    scores = jnp.where(allowed, scores, masked_score)
+    raised = jnp.exp(scores - jnp.max(scores, axis=1, keepdims=True))
+    return raised / jnp.sum(raised, axis=1, keepdims=True)
+
+
+def attend_kernel(raw_ref, rate_ref, gain_ref, cos_ref, sin_ref, column_ref, row_ref, into_ref):
+    for head in range(gain_ref.shape[1] // HEAD_DIM):
+        _, turned, value = head_parts(raw_ref, rate_ref, gain_ref, cos_ref, sin_ref, head)
+        probs = head_probs(turned, column_ref, row_ref).astype(jnp.bfloat16)
+        into_ref[:, head * HEAD_DIM : (head + 1) * HEAD_DIM] = dot_wide(probs, value).astype(
+            jnp.bfloat16
+        )
+
+
+def attend_back_kernel(
+    raw_ref,
+    rate_ref,
+    gain_ref,
+    cos_ref,
+    sin_ref,
+    column_ref,
+    row_ref,
+    grad_ref,
+    pair_ref,
+    value_ref,
+    dots_ref,
+    gains_ref,
+):
+    score_scale = HEAD_DIM ** (-0.5)
+    part_width = gain_ref.shape[1]
+    dots = [0.0, 0.0]
+    for head in range(part_width // HEAD_DIM):
+        units, turned, value = head_parts(raw_ref, rate_ref, gain_ref, cos_ref, sin_ref, head)
+        probs = head_probs(turned, column_ref, row_ref)
+        here = slice(head * HEAD_DIM, (head + 1) * HEAD_DIM)
+        grad = grad_ref[:, here]
+        grad_probs = contract_cols(grad, value)
+        mean_grad = jnp.sum(probs * grad_probs, axis=1, keepdims=True)
+        grad_scores = (probs * (grad_probs - mean_grad)).astype(jnp.bfloat16)
+        value_ref[:, here] = contract_rows(probs.astype(jnp.bfloat16), grad).astype(jnp.bfloat16)
+        grads = (
+            dot_wide(grad_scores, turned[1]) * score_scale,
+            contract_rows(grad_scores, turned[0]) * score_scale,
+        )
+        for which in range(2):
+            unit, gain = units[which]
+            back = grads[which] * cos_ref[...] + roll_half(grads[which] * sin_ref[...])
+            gains_ref[0, which : which + 1, here] = jnp.sum(back * unit, axis=0, keepdims=True)
+            back = back * gain
+            start = which * part_width + head * HEAD_DIM
+            pair_ref[:, start : start + HEAD_DIM] = back
+            dots[which] += jnp.sum(back * unit, axis=1, keepdims=True)
+    dots_ref[:, 0:1] = dots[0]
+    dots_ref[:, 1:2] = dots[1]
+
+
+def join_kernel(raw_ref, rate_ref, pair_ref, value_ref, dots_ref, into_ref):
+    part_width = value_ref.shape[1]
+    for which in range(2):
+        here = slice(which * part_width, (which + 1) * part_width)
+        rate = rate_ref[:, which : which + 1]
+        shift = dots_ref[:, which : which + 1] * rate
+        into_ref[:, here] = (rate * (pair_ref[:, here] - raw_ref[:, here] * shift)).astype(
+            jnp.bfloat16
+        )
+    into_ref[:, 2 * part_width :] = value_ref[...]
+
+
+def row_blocks(count, *arrays):
+    return [pl.BlockSpec((array.shape[0] // count, array.shape[1]), lambda i: (i, 0)) for array in arrays]
+
+
+def attention_specs(raw, rate, gains, cos_table, sin_table, columns, rows):
+    count = rows.shape[0]
+    return (
+        row_blocks(count, raw, rate)
+        + [pl.BlockSpec(gains.shape, lambda i: (0, 0))]
+        + row_blocks(count, cos_table, sin_table, columns)
+        + [pl.BlockSpec((1, 1, rows.shape[2]), lambda i: (i, 0, 0))]
+    )
+
+
+def attend(raw, rate, gains, cos_table, sin_table, columns, rows):
+    count = rows.shape[0]
+    operands = (raw, rate, gains, cos_table, sin_table, columns, rows)
+    result = jax.ShapeDtypeStruct((raw.shape[0], gains.shape[1]), jnp.bfloat16)
+    return pl.pallas_call(
+        attend_kernel,
+        grid=(count,),
+        in_specs=attention_specs(*operands),
+        out_specs=row_blocks(count, result)[0],
+        out_shape=result,
+        compiler_params=pltpu.CompilerParams(vmem_limit_bytes=LIMIT),
+        cost_estimate=QUIET,
+    )(*operands)
+
+
+def attend_back(raw, rate, gains, cos_table, sin_table, columns, rows, grads, behind=()):
+    count = rows.shape[0]
+    operands = (raw, rate, gains, cos_table, sin_table, columns, rows)
+    results = [
+        jax.ShapeDtypeStruct((raw.shape[0], 2 * gains.shape[1]), jnp.float32),
+        jax.ShapeDtypeStruct((raw.shape[0], gains.shape[1]), jnp.bfloat16),
+        jax.ShapeDtypeStruct((raw.shape[0], 2), jnp.float32),
+    ]
+    gain_result = jax.ShapeDtypeStruct((count,) + gains.shape, jnp.float32)
+    return pl.pallas_call(
+        lambda *refs: attend_back_kernel(*refs[len(behind) :]),
+        grid=(count,),
+        in_specs=[HELD] * len(behind) + attention_specs(*operands) + row_blocks(count, grads),
+        out_specs=row_blocks(count, *results)
+        + [pl.BlockSpec((1,) + gains.shape, lambda i: (i, 0, 0))],
+        out_shape=results + [gain_result],
+        compiler_params=pltpu.CompilerParams(vmem_limit_bytes=LIMIT),
+        cost_estimate=QUIET,
+    )(*behind, *operands, grads)
+
+
+def join_grads(raw, rate, pair, value, dots, count):
+    operands = (raw, rate, pair, value, dots)
+    result = jax.ShapeDtypeStruct(raw.shape, jnp.bfloat16)
+    return pl.pallas_call(
+        join_kernel,
+        grid=(count,),
+        in_specs=row_blocks(count, *operands),
+        out_specs=row_blocks(count, result)[0],
+        out_shape=result,
+        compiler_params=pltpu.CompilerParams(vmem_limit_bytes=LIMIT),
+        cost_estimate=QUIET,
+    )(*operands)
+
+
+def rep_sum(values):
+    values = values + move(values, CORE_SWAP).reshape((2, 2) + values.shape[1:])[:, ::-1].reshape(
+        values.shape
+    )
+    swapped = move(values, X_SWAP)
+    return values + jnp.concatenate([swapped[2:], swapped[:2]], axis=0)
+
+
+def fast_local(
+    inputs,
+    attn_gain,
+    in_proj,
+    query_gain,
+    key_gain,
+    out_proj,
+    ffn_gain,
+    router_weight,
+    gate_weight,
+    up_weight,
+    down_weight,
+    routes,
+    priority,
+    segments,
+    grad_out,
+):
+    f32, bf16 = jnp.float32, jnp.bfloat16
+    tokens, width = inputs.shape
+    rows_each = in_proj.shape[0]
+    local_experts, _, hidden_units = gate_weight.shape
+    expert_count = local_experts * SHARDS
+    route_count = routes.shape[1]
+    pair_count = tokens * route_count
+    capacity = 5 * pair_count * SHARDS // (4 * expert_count)
+    core_experts = local_experts // 2
+    heads = HEADS // REPS
+    part_width = heads * HEAD_DIM
+    group_rows = SHARDS * tokens
+    rep, shard = lax.axis_index("rep"), lax.axis_index("shard")
+    a, c = rep // 2, lax.rem(rep, 2)
+    z, y = shard // 2, lax.rem(shard, 2)
+    rep_ref = rep.astype(jnp.int32).reshape(1)
+    core_ref = c.astype(jnp.int32).reshape(1)
+    near_shards = lax.rem(z + jnp.arange(LINE, dtype=jnp.int32), LINE)[:, None] * 2 + (
+        y ^ jnp.arange(2, dtype=jnp.int32)[None, :]
+    )
+    near_shards = near_shards.reshape(SHARDS)
+    shard_ids = jnp.arange(SHARDS, dtype=jnp.int32)
+    place_of_shard = jnp.sum(
+        jnp.where(near_shards[None, :] == shard_ids[:, None], shard_ids[None, :], 0), axis=1
+    )
+
+    in_pieces = gather_rows(thin_columns(in_proj, rep_ref, width))
+    in_part = flat(in_pieces)
+
+    order_row = priority[0]
+    pair_ids = jnp.arange(pair_count, dtype=jnp.int32)
+    place_of = jnp.sum(
+        jnp.where(order_row[None, :] == pair_ids[:, None], pair_ids[None, :], 0), axis=1
+    ).reshape(tokens, route_count)
+    labels = jnp.arange(expert_count, dtype=jnp.int32)
+    hits = routes.T[None, :, :] == labels[:, None, None]
+    place_at = jnp.sum(jnp.where(hits, place_of.T[None], 0), axis=1)
+    named = jnp.any(hits, axis=1)
+    place_at = jnp.where(named, place_at, pair_count)
+    earlier = jnp.sum((place_at[:, None, :] < place_at[:, :, None]).astype(jnp.int32), axis=2)
+    ranks = jnp.where(named, earlier, -1).astype(bf16)
+    ranks = jnp.concatenate([ranks, segments.astype(bf16)], axis=0)
+    ranks = jnp.stack([ranks, move(ranks, CORE_SWAP)])
+    ranks = jnp.concatenate([ranks, move(ranks, X_SWAP)])
+    segment_rows = ranks[:, expert_count, :].astype(jnp.int32)
+    ranks = gather_small(ranks)[:, :, :expert_count].astype(jnp.int32)
+    counts = jnp.sum((ranks >= 0).astype(jnp.int32), axis=3)
+    before = (near_shards[None, :] < near_shards[:, None])[:, :, None, None]
+    bases = jnp.sum(jnp.where(before, counts[None], 0), axis=1)
+    slots = bases[..., None] + ranks
+    slots = jnp.where((ranks >= 0) & (slots < capacity), slots, -1)
+    first_expert = shard * local_experts + c * core_experts
+    slots = lax.dynamic_slice_in_dim(slots, first_expert, core_experts, 2)
+    slots = slots.transpose(1, 2, 0, 3)
+    shard_slots = jnp.take(slots, place_of_shard, axis=2)
+    slots = slots.reshape(REPS, core_experts, group_rows)
+    shard_slots = shard_slots.reshape(REPS, core_experts, group_rows)
+    shifts = jnp.arange(core_experts, dtype=jnp.int32)[:, None] * capacity
+
+    def columns_of(table):
+        return jnp.where(table >= 0, table + shifts, -1).transpose(0, 2, 1)
+
+    columns, shard_columns = columns_of(slots[:2]), columns_of(shard_slots[:2])
+
+    small_in = jnp.stack([attn_gain, query_gain, key_gain, ffn_gain])
+    small_in = jnp.concatenate([small_in, router_weight.T], axis=0)
+    small_in = jnp.take(gather_small(small_in), place_of_shard, axis=0)
+    small_in = small_in.transpose(1, 0, 2).reshape(4 + expert_count, width)
+    gains = small_in[:4].astype(f32)
+    router_rows = small_in[4:]
+    part_gains = lax.dynamic_slice(
+        gains[1:3].reshape(2, HEADS // 2, 2, HEAD_DIM),
+        (0, c * heads, a, 0),
+        (2, heads, 1, HEAD_DIM),
+    ).reshape(2, part_width)
+
+    hidden = inputs.astype(f32)
+    home_rate = lax.rsqrt(jnp.mean(hidden * hidden, axis=-1, keepdims=True) + norm_eps)
+    inputs_all = jnp.stack([inputs, move(inputs, X_SWAP)])
+    inputs_all = jnp.stack([inputs_all, move(inputs_all, CORE_SWAP)], axis=1)
+    inputs_all = inputs_all.reshape(REPS * tokens, width)
+    inputs_all = pick_columns(inputs_all, near_shards, rows_each).astype(f32)
+    unit_all = inputs_all * lax.rsqrt(
+        jnp.mean(inputs_all * inputs_all, axis=-1, keepdims=True) + norm_eps
+    )
+    near_gain = jnp.take(gains[0].reshape(SHARDS, rows_each), near_shards, axis=0).reshape(width)
+    normed_low = (unit_all * near_gain).astype(bf16)
+    cot_across = move(grad_out, X_SWAP)
+    normed_low = after(normed_low, slots, shard_slots, columns, shard_columns, cot_across)
+    cot_own = after(grad_out, in_part)
+    cot_own = lax.all_gather(cot_own, "shard", tiled=True)
+    cos_table, sin_table = jax.vmap(rotary_tables)(segment_rows)
+    sin_table = jnp.where(jnp.arange(HEAD_DIM) < HEAD_DIM // 2, -sin_table, sin_table)
+    cos_table = cos_table.reshape(REPS * tokens, HEAD_DIM)
+    sin_table = sin_table.reshape(REPS * tokens, HEAD_DIM)
+
+    out_rows = rows_each // 4
+    out_own = lax.dynamic_slice_in_dim(out_proj, rep * out_rows, out_rows, 0)
+    out_own = after(out_own, in_pieces[2][0])
+
+    projected = jnp.dot(normed_low, in_part, preferred_element_type=f32)
+    squares = jnp.stack(
+        [
+            jnp.sum(projected[:, k * part_width : (k + 1) * part_width] ** 2, axis=1)
+            for k in range(2)
+        ],
+        axis=1,
+    )
+    squares = rep_sum(squares.reshape(REPS, tokens, 2)).reshape(REPS * tokens, 2)
+    pair_rate = lax.rsqrt(squares / width + norm_eps)
+    attention_operands = (
+        projected,
+        pair_rate,
+        part_gains,
+        cos_table,
+        sin_table,
+        segment_rows.reshape(REPS * tokens, 1),
+        segment_rows[:, None, :],
+    )
+    attended = attend(*attention_operands).reshape(2, 2, tokens, part_width)
+    out_pieces = gather_rows(out_own, early=projected, late=attended)
+    out_own = flat(out_pieces).reshape(SHARDS, out_rows, width)
+    out_other = move(out_own, CORE_SWAP)
+    out_part = jnp.where(
+        c == 0,
+        jnp.concatenate([out_own, out_other], axis=1),
+        jnp.concatenate([out_other, out_own], axis=1),
+    ).reshape(SHARDS * 2 * out_rows, width)
+    attended = jnp.concatenate([attended[:, 0], move(attended[:, 1], CORE_SWAP)], axis=2)
+    attended = attended.reshape(2 * tokens, 2 * part_width)
+    head_of_place = ((near_shards // heads) ^ c) * heads + lax.rem(near_shards, heads)
+    place_of_head = jnp.sum(
+        jnp.where(head_of_place[None, :] == shard_ids[:, None], shard_ids[None, :], 0), axis=1
+    )
+    attended = pick_columns(attended, head_of_place, HEAD_DIM)
+    mixed = jnp.dot(attended, out_part, preferred_element_type=f32).reshape(2, tokens, width)
+    residual = hidden + mixed[0] + move(mixed[1].astype(bf16), X_SWAP).astype(f32)
+
+    ffn_rate = lax.rsqrt(jnp.mean(residual * residual, axis=-1, keepdims=True) + norm_eps)
+    ffn_unit = residual * ffn_rate
+    ffn_low = (ffn_unit * gains[3]).astype(bf16)
+    router_probs = softmax_rows(contract_cols(ffn_low, router_rows))
+
+    def cot_part(group, rows, behind=()):
+        return cotangent_part(core_ref, shard_slots[group], rows, down_weight, capacity, behind)
+
+    first_ref = jnp.stack([c, first_expert]).astype(jnp.int32)
+
+    def ffn_part(group, rows, slot_cot, behind=()):
+        return forward_part(
+            first_ref, slots[group], rows, router_rows, gate_weight, up_weight, slot_cot, behind
+        )
+
+    made = {}
+
+    def fill_cot(follow):
+        beside = move(cot_own, CORE_SWAP)
+        own_part = cot_part(0, cot_own, (follow,))
+        made["cot"] = [own_part, cot_part(1, beside, (own_part[1],))]
+        return [made["cot"][1][1]]
+
+    ffn_pieces = gather_rows(ffn_low, fill=fill_cot)
+    near_cot = made["cot"]
+    ffn_own = flat(ffn_pieces)
+    ffn_beside = move(ffn_own, CORE_SWAP)
+    ffn_far = move(ffn_own, X_SWAP)
+    cot_across = lax.all_gather(after(cot_across, ffn_own), "shard", tiled=True)
+
+    near = [ffn_part(0, ffn_own, near_cot[0][1]), ffn_part(1, ffn_beside, near_cot[1][1])]
+
+    def rows_back(group, behind=()):
+        _, _, grad_gate, grad_up, scores = near[group]
+        return backward_part(
+            core_ref, columns[group], grad_gate, grad_up, scores, gate_weight, up_weight, behind
+        ).reshape(SHARDS, tokens, -1)
+
+    grad_other = rows_back(1)
+    grad_own = rows_back(0, (grad_other,))
+    grad_other = move(grad_other, CORE_SWAP)
+
+    def routed_rows(group, behind):
+        return routed_part(core_ref, shard_columns[group], near[group][1], down_weight, behind)
+
+    def fill_routed_other(follow):
+        made["routed_other"] = routed_rows(1, (grad_own,))
+        return [made["routed_other"]]
+
+    def fill_routed_own(follow):
+        made["routed_own"] = routed_rows(0, follow + (made["routed_other"], ffn_far))
+        return [made["routed_own"]]
+
+    def fill_far_cot(follow):
+        made["far_cot"] = cot_part(2, cot_across, follow + (made["routed_own"],))
+        return [made["far_cot"][1]]
+
+    def fill_other_cot(follow):
+        rows = move(after(cot_across, made["routed_other"]), CORE_SWAP)
+        made["other_cot"] = cot_part(3, rows, follow + (made["far_cot"][1],))
+        return [made["other_cot"][1]]
+
+    grad_home = scatter_rows(
+        [lambda place: grad_own[place], lambda place: grad_other[place]],
+        [fill_routed_other, fill_routed_own, fill_far_cot, fill_other_cot, None],
+    )
+    routed = added(made["routed_own"], move(made["routed_other"], CORE_SWAP))
+    routed = lax.psum_scatter(
+        after(routed, grad_home), "shard", scatter_dimension=0, tiled=True
+    )
+    ffn_far = [ffn_far, move(ffn_far, CORE_SWAP)]
+
+    grad_ffn_home = grad_home[:, :width]
+    home_score = grad_home[:, width : width + expert_count].astype(f32)
+    grad_logits = home_score - router_probs * jnp.sum(home_score, axis=1, keepdims=True)
+    grad_logits_low = grad_logits.astype(bf16)
+
+    grad_ffn_in = grad_ffn_home.astype(f32) + jnp.dot(
+        grad_logits_low, router_rows, preferred_element_type=f32
+    )
+    grad_router_local = contract_rows(grad_logits_low, ffn_low)
+    grad_ffn_local = jnp.sum(grad_ffn_in * ffn_unit, axis=0)
+    scaled = gains[3] * grad_ffn_in
+    grad_residual = grad_out.astype(f32) + ffn_rate * (
+        scaled - ffn_unit * jnp.mean(scaled * ffn_unit, axis=-1, keepdims=True)
+    )
+    residual_low = grad_residual.astype(bf16)
+    residual_other = move(residual_low, X_SWAP)
+    residual_pair = jnp.concatenate([residual_low, residual_other], axis=0)
+
+    grad_attended = contract_cols(residual_pair, out_part).astype(bf16)
+    grad_attended = pick_columns(grad_attended, place_of_head, HEAD_DIM)
+    grad_attended = grad_attended.reshape(2, tokens, 2 * part_width)
+    mine, theirs = grad_attended[:, :, :part_width], grad_attended[:, :, part_width:]
+    grad_attended = jnp.stack([mine, move(theirs, CORE_SWAP)], axis=1)
+    grad_attended = grad_attended.reshape(REPS * tokens, part_width)
+    grad_pair, grad_value, dots, grad_pair_gain = attend_back(*attention_operands, grad_attended)
+    grad_pair_gain = jnp.sum(grad_pair_gain, axis=0).reshape(2, heads, HEAD_DIM)
+    dots = rep_sum(dots.reshape(REPS, tokens, 2)).reshape(REPS * tokens, 2) / width
+    grad_projected = join_grads(projected, pair_rate, grad_pair, grad_value, dots, REPS)
+
+    grad_in_part = contract_rows(normed_low, grad_projected).astype(bf16)
+    grad_in_part = grad_in_part.reshape(SHARDS, rows_each, 3 * part_width)
+    grad_normed = contract_cols(grad_projected, in_part)
+    grad_attn_part = jnp.sum(grad_normed * unit_all, axis=0)
+
+    pair_gains = jnp.zeros((2, HEADS // 2, 2, HEAD_DIM), f32)
+    pair_gains = lax.dynamic_update_slice(
+        pair_gains, grad_pair_gain[:, :, None], (0, c * heads, a, 0)
+    )
+    small = jnp.concatenate(
+        [grad_ffn_local[None], pair_gains.reshape(2, width), grad_router_local], axis=0
+    )
+    small = jnp.take(small.reshape(-1, SHARDS, rows_each), near_shards, axis=1)
+    small = jnp.concatenate([grad_attn_part.reshape(1, SHARDS, rows_each), small], axis=0)
+    small = jnp.pad(small, ((0, HEAD_DIM - small.shape[0]), (0, 0), (0, 0)))
+    small = small.astype(bf16).transpose(1, 2, 0)
+
+    far_cot = [made["far_cot"], made["other_cot"]]
+
+    def fill_far(follow):
+        made["far"] = ffn_part(2, ffn_far[0], far_cot[0][1], (grad_projected,))
+        return [made["far"][3]]
+
+    normed_other = grad_normed.astype(bf16).reshape(2, 2, tokens, width)
+    normed_mine = added(normed_other[:, 0], move(normed_other[:, 1], CORE_SWAP))
+    normed_across = move(normed_mine[1], X_SWAP)
+
+    def fill_other(follow):
+        made["other"] = ffn_part(
+            3, ffn_far[1], far_cot[1][1], follow + (made["far"][3], normed_mine)
+        )
+        return [made["other"][3]]
+
+    def weight_grad(left, right, follow):
+        left = jnp.concatenate([after(left[0], *follow)] + left[1:], axis=1)
+        right = jnp.concatenate(right, axis=1)
+        return jnp.einsum("ecd,ecf->edf", left, right, preferred_element_type=f32).astype(bf16)
+
+    def groups(index):
+        return [part[index] for part in (near[0], near[1], made["far"], made["other"])]
+
+    def fill_down(follow):
+        cots = [part[0] for part in near_cot + far_cot]
+        made["down"] = weight_grad(groups(1), cots, follow + (normed_across,))
+        return [made["down"]]
+
+    def fill_gate(follow):
+        made["gate"] = weight_grad(groups(0), groups(2), follow)
+        return [made["gate"]]
+
+    in_sum = scatter_rows(
+        [lambda place: jnp.concatenate([grad_in_part[place], small[place]], axis=1)],
+        [fill_far, fill_other, None, fill_down, fill_gate],
+    )
+    in_other = move(in_sum, X_SWAP)
+    grad_up = weight_grad(groups(0), groups(3), (in_sum,))
+    in_all = jnp.stack([in_sum, after(in_other, grad_up)])
+    in_beside = move(in_all, CORE_SWAP)
+    down_all = widen(made["down"], move(made["down"], CORE_SWAP), core_ref, (grad_up,))
+    in_all = jnp.stack([in_all, in_beside], axis=1).reshape((REPS,) + in_sum.shape)
+    grad_in = weave_columns(in_all, rep_ref, 3 * part_width, (down_all,))
+    small = jnp.sum(in_all[:, :, 3 * part_width :].astype(f32), axis=0).T
+    gate_all = widen(made["gate"], move(made["gate"], CORE_SWAP), core_ref, (down_all,))
+    up_all = widen(grad_up, move(grad_up, CORE_SWAP), core_ref, (gate_all,))
+
+    outputs = (residual + after(routed, in_sum).astype(f32)).astype(bf16)
+    grad_normed = added(normed_mine[0], normed_across)
+    grad_normed = pick_columns(grad_normed, place_of_shard, rows_each).astype(f32)
+    home_unit = hidden * home_rate
+    scaled = gains[0] * grad_normed
+    grad_inputs = (
+        grad_residual
+        + home_rate * (scaled - home_unit * jnp.mean(scaled * home_unit, axis=-1, keepdims=True))
+    ).astype(bf16)
+
+    grad_out_part = contract_rows(after(attended, made["far"][3]), residual_pair).astype(bf16)
+    out_parts = grad_out_part.reshape(SHARDS, 2, out_rows, width)
+    out_own = lax.dynamic_index_in_dim(out_parts, c, 1, keepdims=False)
+    out_other = lax.dynamic_index_in_dim(out_parts, 1 - c, 1, keepdims=False)
+    out_sum = added(out_own, move(out_other, CORE_SWAP))
+    out_sum = jnp.take(out_sum, place_of_shard, axis=0).reshape(SHARDS * out_rows, width)
+    out_sum = after(out_sum, in_sum, routed)
+    out_sum = lax.psum_scatter(out_sum, "shard", scatter_dimension=0, tiled=True)
+    out_sum = jnp.stack([out_sum, move(out_sum, X_SWAP)])
+    out_sum = jnp.stack([out_sum, move(out_sum, CORE_SWAP)], axis=1)
+    out_sum = out_sum.reshape(REPS, out_rows, width)
+    out_sum = jnp.take(out_sum, rep ^ jnp.arange(REPS, dtype=jnp.int32), axis=0)
+    grad_out_proj = out_sum.reshape(rows_each, width).astype(f32)
+    return (
+        outputs,
+        grad_inputs,
+        small[0],
+        grad_in,
+        small[2],
+        small[3],
+        grad_out_proj,
+        small[1],
+        small[4 : 4 + expert_count].T,
+        gate_all,
+        up_all,
+        down_all,
+    )
+
+
 def solution(mesh):
+    fits = dict(mesh.shape) == {"rep": REPS, "shard": SHARDS}
+    body = fast_local if fits else local
     in_specs = (
         P(("rep", "shard"), None),
         P("shard"),
@@ -405,4 +1437,4 @@
         P("shard", None, None),
         P("shard", None, None),
     )
-    return jax.shard_map(local, mesh=mesh, in_specs=in_specs, out_specs=out_specs, check_vma=False)
+    return jax.shard_map(body, mesh=mesh, in_specs=in_specs, out_specs=out_specs, check_vma=False)

time: 3910 us -> 1150 us (0.29)
  waiting for transfers between devices: 2130 us -> 366 us
  blocking collectives: 789 us -> 0 us
  local copies, waits for them, and re-layouts: 583 us -> 93 us
  Pallas kernels: 0 us -> 367 us
  matrix products: 223 us -> 104 us
  starting transfers between devices: 11.7 us -> 99.2 us
  other arithmetic: 154 us -> 101 us
    psum x1 -> x0, waiting for transfers between devices: 890 us -> none  [local(): lax.psum(grad_in_local, 'rep').astype(jnp.float32)]
    all_to_all x2 -> x0, blocking collectives: 571 us -> none  [the longest x1 295 us: local(): lax.all_to_all(returning_grad, 'shard', split_axis=1, concat_axis=0, tile...]
    gather x21 -> x7, local copies, waits for them, and re-layouts: 507 us -> 5.44 us  [the longest x1 2.12 us: fast_local(): jnp.take(out_sum, place_of_shard, axis=0).reshape(SHARDS * out_rows, width)]
    reduce_scatter x3 -> x2, waiting for transfers between devices: 481 us -> 38.1 us  [the longest x1 38.1 us: fast_local(): lax.psum_scatter(out_sum, 'shard', scatter_dimension=0, tiled=True)]
    all_gather x2, waiting for transfers between devices: 377 us -> 0.01 us  [the longest x1 0.01 us: fast_local(): cot_across = lax.all_gather(after(cot_across, ffn_own), 'shard', tiled=True)]
    all_to_all x2 -> x0, waiting for transfers between devices: 376 us -> none  [the longest x1 220 us: local(): lax.all_to_all(returning, 'shard', split_axis=1, concat_axis=0, tiled=True)]
    pallas_call x0 -> x24, Pallas kernels: none -> 367 us  [the longest x4 112 us: forward_part(): pl.pallas_call(ordered(forward_kernel, len(behind)), grid_spec=pltpu.Pref...]
    ppermute x0 -> x74, waiting for transfers between devices: none -> 328 us  [move(): return lax.ppermute(values, AXES, moves)]
  transfers between devices with their start and end apart: 8 -> 78, of which waited for: 8 -> 27; matrix products, arithmetic and copies ran while one was open for 8% -> 23% of each run, Pallas kernels for 0% -> 32%
where the time goes in v2:
time: 1150 us
  Pallas kernels  367 us (32%)
  waiting for transfers between devices  366 us (32%)
  matrix products  104 us (9%)
  other arithmetic  101 us (9%)
  starting transfers between devices  99.2 us (9%)
  local copies, waits for them, and re-layouts  93 us (8%)
  between operations  15.6 us (1%)
    ppermute x74, waiting for transfers between devices, move(): return lax.ppermute(values, AXES, moves)  328 us
    pallas_call x4, Pallas kernels, forward_part(): pl.pallas_call(ordered(forward_kernel, len(behind)), grid_spec=pltpu.Pref...  112 us
    ppermute x74, starting transfers between devices, move(): return lax.ppermute(values, AXES, moves)  99 us
    pallas_call x4, Pallas kernels, cotangent_part(): pl.pallas_call(ordered(cotangent_kernel, len(behind)), grid_spec=pltpu.Pr...  76.3 us
    dot_general x3, matrix products, weight_grad(): jnp.einsum('ecd,ecf->edf', left, right, preferred_element_type=f32)  69.4 us
    pallas_call x3, Pallas kernels, widen(): pl.pallas_call(ordered(widen_kernel, len(behind)), grid_spec=pltpu.Prefet...  51.2 us
    unnamed x149, local copies, waits for them, and re-layouts  49.8 us
    pallas_call x2, Pallas kernels, backward_part(): pl.pallas_call(ordered(backward_kernel, len(behind)), grid_spec=pltpu.Pre...  48.9 us
  transfers between devices with their start and end apart: 78, of which 27 were waited for; matrix products, arithmetic and copies ran while one was open for 23% of the time, Pallas kernels for 32%

profile of v2, /device:TPU:0, one launch (start us, length us, event | category | flops | bytes accessed | tf_op | source)
XLA Modules:
  0.0 1146.3 jit_solution(1956285708425469359)
XLA Ops:
  26.4 11.4 collective-permute-done.14
  44.4 26.3 %collective-permute-done.2 = bf16[36,256]{1,0:T(8,128)(2,1)S(1)} collective-permute-done((bf16[36,256]{1,0:T(8,128)(2,1)S(1)}, bf16[36,256]{1,0:T(8,128)(2,1)S(1)}, u32[]{:S(2)}, u32[]{:S(2)}) %collective-permute-start.2) | collective-permute-done | bytes 18464 | tf_op jit(solution)/shard_map/ppermute | solution.py:401
  72.8 17.5 %collective-permute-done.16 = bf16[256,1536]{1,0:T(8,128)(2,1)S(1)} collective-permute-done((bf16[256,1536]{1,0:T(8,128)(2,1)S(1)}, bf16[256,1536]{1,0:T(8,128)(2,1)S(1)}, u32[]{:S(2)}, u32[]{:S(2)}) %collective-permute-start.16) | collective-permute-done | bytes 786464 | tf_op jit(solution)/shard_map/ppermute | solution.py:401
  101.0 9.8 collective-permute-done.17
  113.8 12.0 %collective-permute-done.19 = bf16[256,1536]{1,0:T(8,128)(2,1)S(1)} collective-permute-done((bf16[256,1536]{1,0:T(8,128)(2,1)}, bf16[256,1536]{1,0:T(8,128)(2,1)S(1)}, u32[]{:S(2)}, u32[]{:S(2)}) %collective-permute-start.19) | collective-permute-done | bytes 786464 | tf_op jit(solution)/shard_map/ppermute | solution.py:401
  146.5 7.9 collective-permute-done.11
  176.1 11.0 collective-permute-done.24
  194.1 8.1 fusion.120.raw_ref.refs_0_
  205.6 13.7 %collective-permute-done.26 = bf16[64,2048]{1,0:T(8,128)(2,1)} collective-permute-done((bf16[64,2048]{1,0:T(8,128)(2,1)S(1)}, bf16[64,2048]{1,0:T(8,128)(2,1)}, u32[]{:S(2)}, u32[]{:S(2)}) %collective-permute-start.26) | collective-permute-done | bytes 262176 | tf_op jit(solution)/shard_map/ppermute | solution.py:401
  227.0 10.2 shard_map.240
  262.8 17.8 %collective-permute-done.31 = bf16[192,2048]{1,0:T(8,128)(2,1)S(1)} collective-permute-done((bf16[192,2048]{1,0:T(8,128)(2,1)S(1)}, bf16[192,2048]{1,0:T(8,128)(2,1)S(1)}, u32[]{:S(2)}, u32[]{:S(2)}) %collective-permute-start.31) | collective-permute-done | bytes 786464 | tf_op jit(solution)/shard_map/ppermute | solution.py:401
  283.0 7.6 collective-permute-start.33
  290.8 17.8 %collective-permute-done.33 = bf16[192,2048]{1,0:T(8,128)(2,1)S(1)} collective-permute-done((bf16[192,2048]{1,0:T(8,128)(2,1)S(1)}, bf16[192,2048]{1,0:T(8,128)(2,1)S(1)}, u32[]{:S(2)}, u32[]{:S(2)}) %collective-permute-start.33) | collective-permute-done | bytes 786464 | tf_op jit(solution)/shard_map/ppermute | solution.py:401
  313.1 13.0 %collective-permute-done.36.refs_0_ = bf16[192,2048]{1,0:T(8,128)(2,1)} collective-permute-done((bf16[192,2048]{1,0:T(8,128)(2,1)S(1)}, bf16[192,2048]{1,0:T(8,128)(2,1)}, u32[]{:S(2)}, u32[]{:S(2)}) %collective-permute-start.36) | collective-permute-done | bytes 786464 | tf_op jit(solution)/shard_map/ppermute | solution.py:401
  327.1 19.0 %shard_map.242 = (bf16[2,480,2048]{2,1,0:T(8,128)(2,1)}, f32[2,480,1024]{2,1,0:T(8,128)}) custom-call(s32[1]{0:T(128)} %bitcast.47.scalar_ref, bf16[192,2048]{1,0:T(8,128)(2,1)} %collective-permute-done.36.refs_0_, s32[2,1,1536]{2,1,0:T(1,128)} %broadcast_in_dim_squeeze.25.refs_1_, bf16[1536,2048]{1,0:T(8,128)(2,1)} %all-gather.3.cloned.1.call-done.refs_2_, ...), custom_call_target="tpu_custom_call" | custom-call | tf_op jit(solution)/shard_map/pallas_call | solution.py:639
  346.1 19.0 %shard_map.243 = (bf16[2,480,2048]{2,1,0:T(8,128)(2,1)}, f32[2,480,1024]{2,1,0:T(8,128)}) custom-call(s32[1]{0:T(128)} %bitcast.47.scalar_ref, f32[2,480,1024]{2,1,0:T(8,128)} %get-tuple-element.87.refs_0_.refs_5_, s32[2,1,1536]{2,1,0:T(1,128)} %broadcast_in_dim_squeeze.26.refs_1_, bf16[1536,2048]{1,0:T(8,128)(2,1)} %collective-permute-done.37.refs_2_, ...), custom_call_target="tpu_custom_call" | custom-call | tf_op jit(solution)/shard_map/pallas_call | solution.py:639
  373.3 8.3 collective-permute-done.38
  390.5 5.7 collective-permute-done.40.refs_1_
  396.2 27.8 %shard_map.244 = (bf16[2,480,2048]{2,1,0:T(8,128)(2,1)}, bf16[2,480,1024]{2,1,0:T(8,128)(2,1)}, bf16[2,480,1024]{2,1,0:T(8,128)(2,1)}, bf16[2,480,1024]{2,1,0:T(8,128)(2,1)}, bf16[2,480,128]{2,1,0:T(8,128)(2,1)}) custom-call(s32[2]{0:T(128)} %pad_add_fusion.scalar_ref, s32[2,1,1536]{2,1,0:T(1,128)} %broadcast_in_dim_squeeze.24.refs_0_, ...), custom_call_target="tpu_custom_call" | custom-call | tf_op jit(solution)/shard_map/pallas_call | solution.py:724
  424.0 24.5 %shard_map.245 = bf16[1536,2176]{1,0:T(8,128)(2,1)} custom-call(s32[1]{0:T(128)} %bitcast.47.scalar_ref, s32[1536,2]{1,0:T(8,128)} %get-tuple-element.213.refs_0_, bf16[2,480,1024]{2,1,0:T(8,128)(2,1)} %get-tuple-element.90.refs_1_, bf16[2,480,1024]{2,1,0:T(8,128)(2,1)} %get-tuple-element.91.refs_2_, bf16[2,480,128]{2,1,0:T(8,128)(2,1)} %get-tuple-element.92.refs_3_, ...), custom_call_target="tpu_custom_call" | custom-call | tf_op jit(solution)/shard_map/pallas_call | solution.py:798
  453.4 28.4 %shard_map.246 = (bf16[2,480,2048]{2,1,0:T(8,128)(2,1)}, bf16[2,480,1024]{2,1,0:T(8,128)(2,1)}, bf16[2,480,1024]{2,1,0:T(8,128)(2,1)}, bf16[2,480,1024]{2,1,0:T(8,128)(2,1)}, bf16[2,480,128]{2,1,0:T(8,128)(2,1)}) custom-call(s32[2]{0:T(128)} %pad_add_fusion.scalar_ref, s32[2,1,1536]{2,1,0:T(1,128)} %broadcast_in_dim_squeeze.27.refs_0_, ...), custom_call_target="tpu_custom_call" | custom-call | tf_op jit(solution)/shard_map/pallas_call | solution.py:724
  481.7 24.4 %shard_map.247 = bf16[1536,2176]{1,0:T(8,128)(2,1)} custom-call(s32[1]{0:T(128)} %bitcast.47.scalar_ref, bf16[8,192,2176]{2,1,0:T(8,128)(2,1)} %bitcast.306, s32[1536,2]{1,0:T(8,128)} %get-tuple-element.212.refs_1_, bf16[2,480,1024]{2,1,0:T(8,128)(2,1)} %get-tuple-element.93.refs_2_, bf16[2,480,1024]{2,1,0:T(8,128)(2,1)} %get-tuple-element.94.refs_3_, ...), custom_call_target="tpu_custom_call" | custom-call | tf_op jit(solution)/shard_map/pallas_call | solution.py:798
  506.2 16.6 %shard_map.248.refs_1_ = bf16[1536,2048]{1,0:T(8,128)(2,1)} custom-call(s32[1]{0:T(128)} %bitcast.47.scalar_ref, bf16[8,192,2176]{2,1,0:T(8,128)(2,1)} %bitcast.303, s32[1536,2]{1,0:T(8,128)} %get-tuple-element.211.refs_1_, bf16[2,480,1024]{2,1,0:T(8,128)(2,1)} %get-tuple-element.96.refs_2_, bf16[4,1024,2048]{2,1,0:T(8,128)(2,1)} %refs_4_.12, ...), custom_call_target="tpu_custom_call" | custom-call | tf_op jit(solution)/shard_map/pallas_call | solution.py:856
  525.5 20.0 %collective-permute-done.42 = bf16[192,2176]{1,0:T(8,128)(2,1)S(1)} collective-permute-done((bf16[192,2176]{1,0:T(8,128)(2,1)S(1)}, bf16[192,2176]{1,0:T(8,128)(2,1)S(1)}, u32[]{:S(2)}, u32[]{:S(2)}) %collective-permute-start.42) | collective-permute-done | bytes 835616 | tf_op jit(solution)/shard_map/ppermute | solution.py:401
  549.8 36.8 %collective-permute-done.43.refs_2_ = bf16[1536,2048]{1,0:T(8,128)(2,1)} collective-permute-done((bf16[1536,2048]{1,0:T(8,128)(2,1)}, bf16[1536,2048]{1,0:T(8,128)(2,1)}, u32[]{:S(2)}, u32[]{:S(2)}) %collective-permute-start.43) | collective-permute-done | bytes 6291488 | tf_op jit(solution)/shard_map/ppermute | solution.py:401
  586.7 16.3 %shard_map.249.refs_1_ = bf16[1536,2048]{1,0:T(8,128)(2,1)} custom-call(s32[1]{0:T(128)} %bitcast.47.scalar_ref, bf16[192,2176]{1,0:T(8,128)(2,1)} %get-tuple-element.197.refs_0_, bf16[1536,2048]{1,0:T(8,128)(2,1)} %shard_map.248.refs_1_, bf16[1536,2048]{1,0:T(8,128)(2,1)} %collective-permute-done.43.refs_2_, s32[1536,2]{1,0:T(8,128)} %get-tuple-element.210.refs_3_, ...), custom_call_target="tpu_custom_call" | custom-call | tf_op jit(solution)/shard_map/pallas_call | solution.py:856
  608.4 19.0 %shard_map.250 = (bf16[2,480,2048]{2,1,0:T(8,128)(2,1)}, f32[2,480,1024]{2,1,0:T(8,128)}) custom-call(s32[1]{0:T(128)} %bitcast.47.scalar_ref, bf16[192,2176]{1,0:T(8,128)(2,1)} %get-tuple-element.194.refs_0_, bf16[1536,2048]{1,0:T(8,128)(2,1)} %shard_map.249.refs_1_, s32[2,1,1536]{2,1,0:T(1,128)} %broadcast_in_dim_squeeze.28.refs_2_, ...), custom_call_target="tpu_custom_call" | custom-call | tf_op jit(solution)/shard_map/pallas_call | solution.py:639
  638.0 19.3 %shard_map.251 = (bf16[2,480,2048]{2,1,0:T(8,128)(2,1)}, f32[2,480,1024]{2,1,0:T(8,128)}) custom-call(s32[1]{0:T(128)} %bitcast.47.scalar_ref, bf16[192,2176]{1,0:T(8,128)(2,1)} %get-tuple-element.193.refs_0_, f32[2,480,1024]{2,1,0:T(8,128)} %get-tuple-element.101.refs_1_.refs_6_, s32[2,1,1536]{2,1,0:T(1,128)} %broadcast_in_dim_squeeze.29.refs_2_, ...), custom_call_target="tpu_custom_call" | custom-call | tf_op jit(solution)/shard_map/pallas_call | solution.py:639
  657.3 32.7 %collective-permute-done.49 = bf16[192,2176]{1,0:T(8,128)(2,1)} collective-permute-done((bf16[192,2176]{1,0:T(8,128)(2,1)}, bf16[192,2176]{1,0:T(8,128)(2,1)}, u32[]{:S(2)}, u32[]{:S(2)}) %collective-permute-start.49) | collective-permute-done | bytes 835616 | tf_op jit(solution)/shard_map/ppermute | solution.py:401
  697.9 15.6 %collective-permute-done.52 = bf16[192,2048]{1,0:T(8,128)(2,1)S(1)} collective-permute-done((bf16[192,2048]{1,0:T(8,128)(2,1)S(1)}, bf16[192,2048]{1,0:T(8,128)(2,1)S(1)}, u32[]{:S(2)}, u32[]{:S(2)}) %collective-permute-start.52) | collective-permute-done | bytes 786464 | tf_op jit(solution)/shard_map/ppermute | solution.py:401
  721.6 20.1 %shard_map.253 = (f32[768,1024]{1,0:T(8,128)}, bf16[768,512]{1,0:T(8,128)(2,1)}, f32[768,2]{1,0:T(8,128)}, f32[4,2,512]{2,1,0:T(2,128)}) custom-call(f32[768,1536]{1,0:T(8,128)} %copy-done.11, f32[768,2]{1,0:T(8,128)} %fusion.82.rate_ref.refs_1_, f32[2,512]{1,0:T(2,128)} %bitcast.363, f32[768,128]{1,0:T(8,128)} %get-tuple-element.232.cos_ref.refs_3_, ...), custom_call_target="tpu_custom_call" | custom-call | tf_op jit(solution)/shard_map/pallas_call | solution.py:1012
  750.0 6.4 shard_map.254.refs_0_
  756.3 9.8 fusion.113
  766.1 7.1 convolution_convert_fusion
  784.5 11.0 add_convert_fusion
  801.9 27.9 %shard_map.255 = (bf16[2,480,2048]{2,1,0:T(8,128)(2,1)}, bf16[2,480,1024]{2,1,0:T(8,128)(2,1)}, bf16[2,480,1024]{2,1,0:T(8,128)(2,1)}, bf16[2,480,1024]{2,1,0:T(8,128)(2,1)}, bf16[2,480,128]{2,1,0:T(8,128)(2,1)}) custom-call(s32[2]{0:T(128)} %pad_add_fusion.scalar_ref, bf16[768,1536]{1,0:T(8,128)(2,1)} %shard_map.254.refs_0_, ...), custom_call_target="tpu_custom_call" | custom-call | tf_op jit(solution)/shard_map/pallas_call | solution.py:724
  839.8 19.7 %collective-permute-start.62 = (bf16[256,1664]{1,0:T(8,128)(2,1)S(1)}, bf16[256,1664]{1,0:T(8,128)(2,1)}, u32[]{:S(2)}, u32[]{:S(2)}) collective-permute-start(bf16[256,1664]{1,0:T(8,128)(2,1)S(1)} %add_convert_fusion.4.refs_0_), channel_id=1, source_target_pairs={{0,4},{1,5},{2,6},{3,7},{4,0},{5,1},{6,2},{7,3},{8,12},{9,13},{10,... | collective-permute-start | bytes 2555912 | tf_op jit(solution)/shard_map/ppermute | solution.py:401
  859.5 28.0 %shard_map.256 = (bf16[2,480,2048]{2,1,0:T(8,128)(2,1)}, bf16[2,480,1024]{2,1,0:T(8,128)(2,1)}, bf16[2,480,1024]{2,1,0:T(8,128)(2,1)}, bf16[2,480,1024]{2,1,0:T(8,128)(2,1)}, bf16[2,480,128]{2,1,0:T(8,128)(2,1)}) custom-call(s32[2]{0:T(128)} %pad_add_fusion.scalar_ref, bf16[256,1664]{1,0:T(8,128)(2,1)} %copy-done.27, ...), custom_call_target="tpu_custom_call" | custom-call | tf_op jit(solution)/shard_map/pallas_call | solution.py:724
  895.7 23.2 %fusion.38 = bf16[2,1024,2048]{2,1,0:T(8,128)(2,1)} fusion(bf16[2,480,2048]{2,1,0:T(8,128)(2,1)} %get-tuple-element.119, bf16[2,480,2048]{2,1,0:T(8,128)(2,1)} %get-tuple-element.118, bf16[2,480,2048]{2,1,0:T(8,128)(2,1)} %get-tuple-element.117, bf16[2,480,2048]{2,1,0:T(8,128)(2,1)} %get-tuple-element.116, bf16[2,480,1024]{2,1,0:T(8,128)(2,1)} %get-tuple-element.115, ...), kind=kOutput, calls=%fused_computation.57 | convolution fusion | flops 16204693504 | bytes 31981568 | tf_op jit(solution)/shard_map/ecd,ecf->edf/dot_general | solution.py:1338
  920.3 23.0 %fusion.46 = bf16[2,2048,1024]{2,1,0:T(8,128)(2,1)} fusion(bf16[2,480,1024]{2,1,0:T(8,128)(2,1)} %get-tuple-element.127, bf16[2,480,1024]{2,1,0:T(8,128)(2,1)} %get-tuple-element.126, bf16[2,480,1024]{2,1,0:T(8,128)(2,1)} %get-tuple-element.90.refs_1_, bf16[2,480,1024]{2,1,0:T(8,128)(2,1)} %get-tuple-element.93.refs_2_, ...), kind=kOutput, calls=%fused_computation.59 | convolution fusion | flops 16204693504 | bytes 31981568 | tf_op jit(solution)/shard_map/ecd,ecf->edf/dot_general | solution.py:1338
  943.8 7.8 collective-permute-done.62
  954.8 23.1 %fusion.43.refs_0_ = bf16[2,2048,1024]{2,1,0:T(8,128)(2,1)} fusion(bf16[2,480,1024]{2,1,0:T(8,128)(2,1)} %get-tuple-element.129, bf16[2,480,1024]{2,1,0:T(8,128)(2,1)} %get-tuple-element.113.refs_1_, bf16[2,480,1024]{2,1,0:T(8,128)(2,1)} %get-tuple-element.91.refs_2_, bf16[2,480,1024]{2,1,0:T(8,128)(2,1)S(1)} %copy-done.34, ...), kind=kOutput, calls=%fused_computation.58 | convolution fusion | flops 16204693504 | bytes 31981568 | tf_op jit(solution)/shard_map/ecd,ecf->edf/dot_general | solution.py:1338
  984.6 9.6 collective-permute-done.69
  1004.3 19.4 %collective-permute-done.66 = bf16[256,1664]{1,0:T(8,128)(2,1)S(1)} collective-permute-done((bf16[256,1664]{1,0:T(8,128)(2,1)S(1)}, bf16[256,1664]{1,0:T(8,128)(2,1)S(1)}, u32[]{:S(2)}, u32[]{:S(2)}) %collective-permute-start.66) | collective-permute-done | bytes 852000 | tf_op jit(solution)/shard_map/ppermute | solution.py:401
  1030.0 38.1 %reduce-scatter.5.cloned.1.call-done = bf16[64,2048]{1,0:T(8,128)(2,1)} async-done(((bf16[512,2048]{1,0:T(8,128)(2,1)}), bf16[64,2048]{1,0:T(8,128)(2,1)}) %reduce-scatter.5.cloned.1.call-update) | async-done | bytes 262160 | tf_op jit(solution)/shard_map/reduce_scatter | solution.py:1384
  1078.0 17.0 %shard_map.258 = f32[4096,2048]{1,0:T(8,128)} custom-call(s32[1]{0:T(128)} %bitcast.47.scalar_ref, bf16[2,2048,1024]{2,1,0:T(8,128)(2,1)S(1)} %copy-done.2, bf16[2048,2048]{1,0:T(8,128)(2,1)S(1)} %bitcast.296, bf16[2048,2048]{1,0:T(8,128)(2,1)} %bitcast.99.refs_2_), custom_call_target="tpu_custom_call" | custom-call | tf_op jit(solution)/shard_map/pallas_call | solution.py:580
  1100.7 17.1 %shard_map.260 = f32[8192,1024]{1,0:T(8,128)} custom-call(s32[1]{0:T(128)} %bitcast.47.scalar_ref, f32[4,1024,2048]{2,1,0:T(8,128)} %bitcast.299, bf16[4096,1024]{1,0:T(8,128)(2,1)S(1)} %bitcast.295, bf16[4096,1024]{1,0:T(8,128)(2,1)} %bitcast.115.refs_2_), custom_call_target="tpu_custom_call" | custom-call | tf_op jit(solution)/shard_map/pallas_call | solution.py:580
  1117.9 17.1 %shard_map.261 = f32[8192,1024]{1,0:T(8,128)} custom-call(s32[1]{0:T(128)} %bitcast.47.scalar_ref, f32[4,2048,1024]{2,1,0:T(8,128)} %bitcast.301, bf16[4096,1024]{1,0:T(8,128)(2,1)S(1)} %bitcast.288, bf16[4096,1024]{1,0:T(8,128)(2,1)} %bitcast.118.refs_2_), custom_call_target="tpu_custom_call" | custom-call | tf_op jit(solution)/shard_map/pallas_call | solution.py:580
  (504 shorter events, 287.6 us)
Async XLA Ops:
  7.2 239.9 %all-gather.3.cloned.1.call-start = ((), (), s32[]{:S(2)}) async-start(), calls=%async_computation.2 | async-start | bytes 7077888 | tf_op jit(solution)/shard_map/all_gather | solution.py:1153
  10.8 31.6 %collective-permute-start.4 = (bf16[36,256]{1,0:T(8,128)(2,1)S(1)}, bf16[36,256]{1,0:T(8,128)(2,1)S(1)}, u32[]{:S(2)}, u32[]{:S(2)}) collective-permute-start(bf16[36,256]{1,0:T(8,128)(2,1)S(1)} %concatenate.114), channel_id=1, source_target_pairs={{0,2},{1,3},{2,4},{3,5},{4,6},{5,7},{6,0},{7,1},{8,10},{9,11},{10,... | collective-permute-start | bytes 55304 | tf_op jit(solution)/shard_map/ppermute | solution.py:401
  13.9 30.0 %collective-permute-start.3 = (bf16[36,256]{1,0:T(8,128)(2,1)S(1)}, bf16[36,256]{1,0:T(8,128)(2,1)S(1)}, u32[]{:S(2)}, u32[]{:S(2)}) collective-permute-start(bf16[36,256]{1,0:T(8,128)(2,1)S(1)} %concatenate.114), channel_id=1, source_target_pairs={{0,4},{1,5},{2,6},{3,7},{4,0},{5,1},{6,2},{7,3},{8,12},{9,13},{10,... | collective-permute-start | bytes 55304 | tf_op jit(solution)/shard_map/ppermute | solution.py:401
  20.2 52.0 %collective-permute-start.13 = (bf16[256,1536]{1,0:T(8,128)(2,1)S(1)}, bf16[256,1536]{1,0:T(8,128)(2,1)}, u32[]{:S(2)}, u32[]{:S(2)}) collective-permute-start(bf16[256,1536]{1,0:T(8,128)(2,1)S(1)} %shard_map.239), channel_id=1, source_target_pairs={{0,1},{1,0},{2,3},{3,2},{4,5},{5,4},{6,7},{7,6},{8,9},{9,8},{10,11... | collective-permute-start | bytes 2359304 | tf_op jit(solution)/shard_map/ppermute | solution.py:401
  37.7 52.6 %collective-permute-start.16 = (bf16[256,1536]{1,0:T(8,128)(2,1)S(1)}, bf16[256,1536]{1,0:T(8,128)(2,1)S(1)}, u32[]{:S(2)}, u32[]{:S(2)}) collective-permute-start(bf16[256,1536]{1,0:T(8,128)(2,1)S(1)} %shard_map.239), channel_id=1, source_target_pairs={{0,4},{1,5},{2,6},{3,7},{4,0},{5,1},{6,2},{7,3},{8,12},{9,13},{10,... | collective-permute-start | bytes 2359304 | tf_op jit(solution)/shard_map/ppermute | solution.py:401
  39.0 57.0 %collective-permute-start.18 = (bf16[256,1536]{1,0:T(8,128)(2,1)S(1)}, bf16[256,1536]{1,0:T(8,128)(2,1)}, u32[]{:S(2)}, u32[]{:S(2)}) collective-permute-start(bf16[256,1536]{1,0:T(8,128)(2,1)S(1)} %shard_map.239), channel_id=1, source_target_pairs={{0,2},{1,3},{2,4},{3,5},{4,6},{5,7},{6,0},{7,1},{8,10},{9,11},{10,... | collective-permute-start | bytes 2359304 | tf_op jit(solution)/shard_map/ppermute | solution.py:401
  42.4 55.0 %collective-permute-start.15 = (bf16[256,1536]{1,0:T(8,128)(2,1)}, bf16[256,1536]{1,0:T(8,128)(2,1)}, u32[]{:S(2)}, u32[]{:S(2)}) collective-permute-start(bf16[256,1536]{1,0:T(8,128)(2,1)} %collective-permute-done.14), channel_id=1, source_target_pairs={{0,1},{1,0},{2,3},{3,2},{4,5},{5,4},{6,7},{7,6},{8,9},{9,8},{10,11... | collective-permute-start | bytes 2359304 | tf_op jit(solution)/shard_map/ppermute | solution.py:401
  44.0 26.7 %collective-permute-start.2 = (bf16[36,256]{1,0:T(8,128)(2,1)S(1)}, bf16[36,256]{1,0:T(8,128)(2,1)S(1)}, u32[]{:S(2)}, u32[]{:S(2)}) collective-permute-start(bf16[36,256]{1,0:T(8,128)(2,1)S(1)} %concatenate.114), channel_id=1, source_target_pairs={{0,6},{1,7},{2,0},{3,1},{4,2},{5,3},{6,4},{7,5},{8,14},{9,15},{10,... | collective-permute-start | bytes 55304 | tf_op jit(solution)/shard_map/ppermute | solution.py:401
  70.7 123.4 %collective-permute-start.12 = (bf16[192,2048]{1,0:T(8,128)(2,1)}, bf16[192,2048]{1,0:T(8,128)(2,1)}, u32[]{:S(2)}, u32[]{:S(2)}) collective-permute-start(bf16[192,2048]{1,0:T(8,128)(2,1)} %param.29), channel_id=1, source_target_pairs={{0,16},{1,17},{2,18},{3,19},{4,20},{5,21},{6,22},{7,23},{8,24},{9,... | collective-permute-start | bytes 2359304 | tf_op jit(solution)/shard_map/ppermute | solution.py:401
  72.2 87.7 %collective-permute-start = (bf16[192,2048]{1,0:T(8,128)(2,1)S(1)}, bf16[192,2048]{1,0:T(8,128)(2,1)}, u32[]{:S(2)}, u32[]{:S(2)}) collective-permute-start(bf16[192,2048]{1,0:T(8,128)(2,1)S(1)} %copy-done.16), channel_id=1, source_target_pairs={{0,16},{1,17},{2,18},{3,19},{4,20},{5,21},{6,22},{7,23},{8,24},{9,... | collective-permute-start | bytes 2359304 | tf_op jit(solution)/shard_map/ppermute | solution.py:401
  96.0 30.9 %collective-permute-start.7 = (bf16[2,33,192]{2,1,0:T(8,128)(2,1)S(1)}, bf16[2,33,192]{2,1,0:T(8,128)(2,1)S(1)}, u32[]{:S(2)}, u32[]{:S(2)}) collective-permute-start(bf16[2,33,192]{2,1,0:T(8,128)(2,1)S(1)} %pad_maximum_fusion.34), channel_id=1, source_target_pairs={{0,16},{1,17},{2,18},{3,19},{4,20},{5,21},{6,22},{7,23},{8,24},{9,... | collective-permute-start | bytes 76040 | tf_op jit(solution)/shard_map/ppermute | solution.py:401
  97.5 28.4 %collective-permute-start.19 = (bf16[256,1536]{1,0:T(8,128)(2,1)}, bf16[256,1536]{1,0:T(8,128)(2,1)S(1)}, u32[]{:S(2)}, u32[]{:S(2)}) collective-permute-start(bf16[256,1536]{1,0:T(8,128)(2,1)} %collective-permute-done.18), channel_id=1, source_target_pairs={{0,1},{1,0},{2,3},{3,2},{4,5},{5,4},{6,7},{7,6},{8,9},{9,8},{10,11... | collective-permute-start | bytes 2359304 | tf_op jit(solution)/shard_map/ppermute | solution.py:401
  126.8 395.9 %all-gather.5.cloned.1.call-start = ((), (), s32[]{:S(2)}) async-start(), calls=%async_computation.3 | async-start | bytes 7077888 | tf_op jit(solution)/shard_map/all_gather | solution.py:1229
  175.2 30.4 %collective-permute-start.28 = (bf16[64,2048]{1,0:T(8,128)(2,1)S(1)}, bf16[64,2048]{1,0:T(8,128)(2,1)S(1)}, u32[]{:S(2)}, u32[]{:S(2)}) collective-permute-start(bf16[64,2048]{1,0:T(8,128)(2,1)S(1)} %constant_dynamic-slice_fusion), channel_id=1, source_target_pairs={{0,2},{1,3},{2,4},{3,5},{4,6},{5,7},{6,0},{7,1},{8,10},{9,11},{10,... | collective-permute-start | bytes 786440 | tf_op jit(solution)/shard_map/ppermute | solution.py:401
  175.6 61.6 %collective-permute-start.23 = (bf16[64,2048]{1,0:T(8,128)(2,1)S(1)}, bf16[64,2048]{1,0:T(8,128)(2,1)}, u32[]{:S(2)}, u32[]{:S(2)}) collective-permute-start(bf16[64,2048]{1,0:T(8,128)(2,1)S(1)} %constant_dynamic-slice_fusion), channel_id=1, source_target_pairs={{0,1},{1,0},{2,3},{3,2},{4,5},{5,4},{6,7},{7,6},{8,9},{9,8},{10,11... | collective-permute-start | bytes 786440 | tf_op jit(solution)/shard_map/ppermute | solution.py:401
  187.2 32.2 %collective-permute-start.26 = (bf16[64,2048]{1,0:T(8,128)(2,1)S(1)}, bf16[64,2048]{1,0:T(8,128)(2,1)}, u32[]{:S(2)}, u32[]{:S(2)}) collective-permute-start(bf16[64,2048]{1,0:T(8,128)(2,1)S(1)} %constant_dynamic-slice_fusion), channel_id=1, source_target_pairs={{0,4},{1,5},{2,6},{3,7},{4,0},{5,1},{6,2},{7,3},{8,12},{9,13},{10,... | collective-permute-start | bytes 786440 | tf_op jit(solution)/shard_map/ppermute | solution.py:401
  247.1 99.0 %collective-permute-start.37 = (bf16[1536,2048]{1,0:T(8,128)(2,1)}, bf16[1536,2048]{1,0:T(8,128)(2,1)}, u32[]{:S(2)}, u32[]{:S(2)}) collective-permute-start(bf16[1536,2048]{1,0:T(8,128)(2,1)} %all-gather.3.cloned.1.call-done.refs_2_), channel_id=1, source_target_pairs={{0,8},{1,9},{2,10},{3,11},{4,12},{5,13},{6,14},{7,15},{8,0},{9,1},... | collective-permute-start | bytes 18874376 | tf_op jit(solution)/shard_map/ppermute | solution.py:401
  283.0 25.6 %collective-permute-start.33 = (bf16[192,2048]{1,0:T(8,128)(2,1)S(1)}, bf16[192,2048]{1,0:T(8,128)(2,1)S(1)}, u32[]{:S(2)}, u32[]{:S(2)}) collective-permute-start(bf16[192,2048]{1,0:T(8,128)(2,1)S(1)} %get-tuple-element.85), channel_id=1, source_target_pairs={{0,6},{1,7},{2,0},{3,1},{4,2},{5,3},{6,4},{7,5},{8,14},{9,15},{10,... | collective-permute-start | bytes 2359304 | tf_op jit(solution)/shard_map/ppermute | solution.py:401
  290.6 35.5 %collective-permute-start.36 = (bf16[192,2048]{1,0:T(8,128)(2,1)S(1)}, bf16[192,2048]{1,0:T(8,128)(2,1)}, u32[]{:S(2)}, u32[]{:S(2)}) collective-permute-start(bf16[192,2048]{1,0:T(8,128)(2,1)S(1)} %get-tuple-element.85), channel_id=1, source_target_pairs={{0,2},{1,3},{2,4},{3,5},{4,6},{5,7},{6,0},{7,1},{8,10},{9,11},{10,... | collective-permute-start | bytes 2359304 | tf_op jit(solution)/shard_map/ppermute | solution.py:401
  308.6 56.5 %collective-permute-start.35 = (bf16[192,2048]{1,0:T(8,128)(2,1)S(1)}, bf16[192,2048]{1,0:T(8,128)(2,1)}, u32[]{:S(2)}, u32[]{:S(2)}) collective-permute-start(bf16[192,2048]{1,0:T(8,128)(2,1)S(1)} %get-tuple-element.85), channel_id=1, source_target_pairs={{0,4},{1,5},{2,6},{3,7},{4,0},{5,1},{6,2},{7,3},{8,12},{9,13},{10,... | collective-permute-start | bytes 2359304 | tf_op jit(solution)/shard_map/ppermute | solution.py:401
  309.6 56.5 %collective-permute-start.32 = (bf16[192,2048]{1,0:T(8,128)(2,1)S(1)}, bf16[192,2048]{1,0:T(8,128)(2,1)}, u32[]{:S(2)}, u32[]{:S(2)}) collective-permute-start(bf16[192,2048]{1,0:T(8,128)(2,1)S(1)} %get-tuple-element.85), channel_id=1, source_target_pairs={{0,1},{1,0},{2,3},{3,2},{4,5},{5,4},{6,7},{7,6},{8,9},{9,8},{10,11... | collective-permute-start | bytes 2359304 | tf_op jit(solution)/shard_map/ppermute | solution.py:401
  310.6 58.5 %collective-permute-start.34 = (bf16[192,2048]{1,0:T(8,128)(2,1)S(1)}, bf16[192,2048]{1,0:T(8,128)(2,1)}, u32[]{:S(2)}, u32[]{:S(2)}) collective-permute-start(bf16[192,2048]{1,0:T(8,128)(2,1)S(1)} %collective-permute-done.33), channel_id=1, source_target_pairs={{0,1},{1,0},{2,3},{3,2},{4,5},{5,4},{6,7},{7,6},{8,9},{9,8},{10,11... | collective-permute-start | bytes 2359304 | tf_op jit(solution)/shard_map/ppermute | solution.py:401
  326.1 58.6 %collective-permute-start.39 = (bf16[192,2048]{1,0:T(8,128)(2,1)}, bf16[192,2048]{1,0:T(8,128)(2,1)S(1)}, u32[]{:S(2)}, u32[]{:S(2)}) collective-permute-start(bf16[192,2048]{1,0:T(8,128)(2,1)} %collective-permute-done.36.refs_0_), channel_id=1, source_target_pairs={{0,1},{1,0},{2,3},{3,2},{4,5},{5,4},{6,7},{7,6},{8,9},{9,8},{10,11... | collective-permute-start | bytes 2359304 | tf_op jit(solution)/shard_map/ppermute | solution.py:401
  385.7 616.9 %reduce-scatter.3.cloned.1.call-start = ((), (), s32[]{:S(2)}) async-start(), calls=%async_computation.4 | async-start | bytes 7077888 | tf_op jit(solution)/shard_map/reduce_scatter | solution.py:1268
  448.4 74.4 %collective-permute-start.41 = (bf16[8,192,2176]{2,1,0:T(8,128)(2,1)}, bf16[8,192,2176]{2,1,0:T(8,128)(2,1)}, u32[]{:S(2)}, u32[]{:S(2)}) collective-permute-start(bf16[8,192,2176]{2,1,0:T(8,128)(2,1)} %bitcast.305), channel_id=1, source_target_pairs={{0,8},{1,9},{2,10},{3,11},{4,12},{5,13},{6,14},{7,15},{8,0},{9,1},... | collective-permute-start | bytes 20054024 | tf_op jit(solution)/shard_map/ppermute | solution.py:401
  448.6 138.1 %collective-permute-start.43 = (bf16[1536,2048]{1,0:T(8,128)(2,1)}, bf16[1536,2048]{1,0:T(8,128)(2,1)}, u32[]{:S(2)}, u32[]{:S(2)}) collective-permute-start(bf16[1536,2048]{1,0:T(8,128)(2,1)} %constant_dynamic-update-slice_fusion.18.refs_1_), channel_id=1, source_target_pairs={{0,16},{1,17},{2,18},{3,19},{4,20},{5,21},{6,22},{7,23},{8,24},{9,... | collective-permute-start | bytes 18874376 | tf_op jit(solution)/shard_map/ppermute | solution.py:401
  522.7 115.3 %collective-permute-start.48 = (bf16[1536,2048]{1,0:T(8,128)(2,1)}, bf16[1536,2048]{1,0:T(8,128)(2,1)}, u32[]{:S(2)}, u32[]{:S(2)}) collective-permute-start(bf16[1536,2048]{1,0:T(8,128)(2,1)} %all-gather.5.cloned.1.call-done.refs_3_), channel_id=1, source_target_pairs={{0,8},{1,9},{2,10},{3,11},{4,12},{5,13},{6,14},{7,15},{8,0},{9,1},... | collective-permute-start | bytes 18874376 | tf_op jit(solution)/shard_map/ppermute | solution.py:401
  548.8 54.1 %collective-permute-start.47 = (bf16[192,2176]{1,0:T(8,128)(2,1)S(1)}, bf16[192,2176]{1,0:T(8,128)(2,1)S(1)}, u32[]{:S(2)}, u32[]{:S(2)}) collective-permute-start(bf16[192,2176]{1,0:T(8,128)(2,1)S(1)} %get-tuple-element.196), channel_id=1, source_target_pairs={{0,1},{1,0},{2,3},{3,2},{4,5},{5,4},{6,7},{7,6},{8,9},{9,8},{10,11... | collective-permute-start | bytes 2506760 | tf_op jit(solution)/shard_map/ppermute | solution.py:401
  631.3 26.0 %collective-permute-start.45 = (bf16[192,2176]{1,0:T(8,128)(2,1)}, bf16[192,2176]{1,0:T(8,128)(2,1)}, u32[]{:S(2)}, u32[]{:S(2)}) collective-permute-start(bf16[192,2176]{1,0:T(8,128)(2,1)} %get-tuple-element.192), channel_id=1, source_target_pairs={{0,1},{1,0},{2,3},{3,2},{4,5},{5,4},{6,7},{7,6},{8,9},{9,8},{10,11... | collective-permute-start | bytes 2506760 | tf_op jit(solution)/shard_map/ppermute | solution.py:401
  632.3 57.7 %collective-permute-start.49 = (bf16[192,2176]{1,0:T(8,128)(2,1)}, bf16[192,2176]{1,0:T(8,128)(2,1)}, u32[]{:S(2)}, u32[]{:S(2)}) collective-permute-start(bf16[192,2176]{1,0:T(8,128)(2,1)} %get-tuple-element.197.refs_0_), channel_id=1, source_target_pairs={{0,4},{1,5},{2,6},{3,7},{4,0},{5,1},{6,2},{7,3},{8,12},{9,13},{10,... | collective-permute-start | bytes 2506760 | tf_op jit(solution)/shard_map/ppermute | solution.py:401
  632.8 57.1 %collective-permute-start.50 = (bf16[192,2176]{1,0:T(8,128)(2,1)}, bf16[192,2176]{1,0:T(8,128)(2,1)}, u32[]{:S(2)}, u32[]{:S(2)}) collective-permute-start(bf16[192,2176]{1,0:T(8,128)(2,1)} %get-tuple-element.194.refs_0_), channel_id=1, source_target_pairs={{0,2},{1,3},{2,4},{3,5},{4,6},{5,7},{6,0},{7,1},{8,10},{9,11},{10,... | collective-permute-start | bytes 2506760 | tf_op jit(solution)/shard_map/ppermute | solution.py:401
  635.7 54.3 %collective-permute-start.51 = (bf16[192,2176]{1,0:T(8,128)(2,1)}, bf16[192,2176]{1,0:T(8,128)(2,1)}, u32[]{:S(2)}, u32[]{:S(2)}) collective-permute-start(bf16[192,2176]{1,0:T(8,128)(2,1)} %get-tuple-element.193.refs_0_), channel_id=1, source_target_pairs={{0,6},{1,7},{2,0},{3,1},{4,2},{5,3},{6,4},{7,5},{8,14},{9,15},{10,... | collective-permute-start | bytes 2506760 | tf_op jit(solution)/shard_map/ppermute | solution.py:401
  697.8 86.7 %collective-permute-start.44 = (bf16[1536,2048]{1,0:T(8,128)(2,1)}, bf16[1536,2048]{1,0:T(8,128)(2,1)}, u32[]{:S(2)}, u32[]{:S(2)}) collective-permute-start(bf16[1536,2048]{1,0:T(8,128)(2,1)} %shard_map.248.refs_1_), channel_id=1, source_target_pairs={{0,8},{1,9},{2,10},{3,11},{4,12},{5,13},{6,14},{7,15},{8,0},{9,1},... | collective-permute-start | bytes 18874376 | tf_op jit(solution)/shard_map/ppermute | solution.py:401
  719.0 120.8 %collective-permute-start.61 = (bf16[1536,2048]{1,0:T(8,128)(2,1)}, bf16[1536,2048]{1,0:T(8,128)(2,1)}, u32[]{:S(2)}, u32[]{:S(2)}) collective-permute-start(bf16[1536,2048]{1,0:T(8,128)(2,1)} %collective-permute-done.43.refs_2_), channel_id=1, source_target_pairs={{0,8},{1,9},{2,10},{3,11},{4,12},{5,13},{6,14},{7,15},{8,0},{9,1},... | collective-permute-start | bytes 18874376 | tf_op jit(solution)/shard_map/ppermute | solution.py:401
  781.9 48.9 %collective-permute-start.57 = (bf16[256,1664]{1,0:T(8,128)(2,1)}, bf16[256,1664]{1,0:T(8,128)(2,1)}, u32[]{:S(2)}, u32[]{:S(2)}) collective-permute-start(bf16[256,1664]{1,0:T(8,128)(2,1)} %pad_maximum_fusion.21), channel_id=1, source_target_pairs={{0,1},{1,0},{2,3},{3,2},{4,5},{5,4},{6,7},{7,6},{8,9},{9,8},{10,11... | collective-permute-start | bytes 2555912 | tf_op jit(solution)/shard_map/ppermute | solution.py:401
  784.5 49.9 %collective-permute-start.58 = (bf16[2,192,2048]{2,1,0:T(8,128)(2,1)}, bf16[2,192,2048]{2,1,0:T(8,128)(2,1)}, u32[]{:S(2)}, u32[]{:S(2)}) collective-permute-start(bf16[2,192,2048]{2,1,0:T(8,128)(2,1)} %slice_bitcast_fusion), channel_id=1, source_target_pairs={{0,8},{1,9},{2,10},{3,11},{4,12},{5,13},{6,14},{7,15},{8,0},{9,1},... | collective-permute-start | bytes 4718600 | tf_op jit(solution)/shard_map/ppermute | solution.py:401
  795.6 272.5 %reduce-scatter.5.cloned.1.call-start = ((), (), s32[]{:S(2)}) async-start(), calls=%async_computation.5 | async-start | bytes 2359296 | tf_op jit(solution)/shard_map/reduce_scatter | solution.py:1384
  797.8 36.1 %collective-permute-start.60 = (bf16[256,1664]{1,0:T(8,128)(2,1)}, bf16[256,1664]{1,0:T(8,128)(2,1)}, u32[]{:S(2)}, u32[]{:S(2)}) collective-permute-start(bf16[256,1664]{1,0:T(8,128)(2,1)} %pad_maximum_fusion.22), channel_id=1, source_target_pairs={{0,1},{1,0},{2,3},{3,2},{4,5},{5,4},{6,7},{7,6},{8,9},{9,8},{10,11... | collective-permute-start | bytes 2555912 | tf_op jit(solution)/shard_map/ppermute | solution.py:401
  800.6 118.3 %collective-permute-start.56 = (bf16[256,1664]{1,0:T(8,128)(2,1)}, bf16[256,1664]{1,0:T(8,128)(2,1)}, u32[]{:S(2)}, u32[]{:S(2)}) collective-permute-start(bf16[256,1664]{1,0:T(8,128)(2,1)} %pad_maximum_fusion.20), channel_id=1, source_target_pairs={{0,1},{1,0},{2,3},{3,2},{4,5},{5,4},{6,7},{7,6},{8,9},{9,8},{10,11... | collective-permute-start | bytes 2555912 | tf_op jit(solution)/shard_map/ppermute | solution.py:401
  830.8 56.7 %collective-permute-start.63 = (bf16[256,1664]{1,0:T(8,128)(2,1)}, bf16[256,1664]{1,0:T(8,128)(2,1)}, u32[]{:S(2)}, u32[]{:S(2)}) collective-permute-start(bf16[256,1664]{1,0:T(8,128)(2,1)} %pad_maximum_fusion.23), channel_id=1, source_target_pairs={{0,1},{1,0},{2,3},{3,2},{4,5},{5,4},{6,7},{7,6},{8,9},{9,8},{10,11... | collective-permute-start | bytes 2555912 | tf_op jit(solution)/shard_map/ppermute | solution.py:401
  833.9 110.0 %collective-permute-start.65 = (bf16[256,1664]{1,0:T(8,128)(2,1)}, bf16[256,1664]{1,0:T(8,128)(2,1)}, u32[]{:S(2)}, u32[]{:S(2)}) collective-permute-start(bf16[256,1664]{1,0:T(8,128)(2,1)} %add_convert_fusion.5), channel_id=1, source_target_pairs={{0,6},{1,7},{2,0},{3,1},{4,2},{5,3},{6,4},{7,5},{8,14},{9,15},{10,... | collective-permute-start | bytes 2555912 | tf_op jit(solution)/shard_map/ppermute | solution.py:401
  836.6 58.2 %collective-permute-start.59 = (bf16[192,2048]{1,0:T(8,128)(2,1)S(1)}, bf16[192,2048]{1,0:T(8,128)(2,1)S(1)}, u32[]{:S(2)}, u32[]{:S(2)}) collective-permute-start(bf16[192,2048]{1,0:T(8,128)(2,1)S(1)} %slice_bitcast_fusion.11), channel_id=1, source_target_pairs={{0,16},{1,17},{2,18},{3,19},{4,20},{5,21},{6,22},{7,23},{8,24},{9,... | collective-permute-start | bytes 2359304 | tf_op jit(solution)/shard_map/ppermute | solution.py:401
  839.8 111.9 %collective-permute-start.62 = (bf16[256,1664]{1,0:T(8,128)(2,1)S(1)}, bf16[256,1664]{1,0:T(8,128)(2,1)}, u32[]{:S(2)}, u32[]{:S(2)}) collective-permute-start(bf16[256,1664]{1,0:T(8,128)(2,1)S(1)} %add_convert_fusion.4.refs_0_), channel_id=1, source_target_pairs={{0,4},{1,5},{2,6},{3,7},{4,0},{5,1},{6,2},{7,3},{8,12},{9,13},{10,... | collective-permute-start | bytes 2555912 | tf_op jit(solution)/shard_map/ppermute | solution.py:401
  889.9 61.8 %collective-permute-start.64 = (bf16[256,1664]{1,0:T(8,128)(2,1)}, bf16[256,1664]{1,0:T(8,128)(2,1)}, u32[]{:S(2)}, u32[]{:S(2)}) collective-permute-start(bf16[256,1664]{1,0:T(8,128)(2,1)} %add_convert_fusion.2), channel_id=1, source_target_pairs={{0,2},{1,3},{2,4},{3,5},{4,6},{5,7},{6,0},{7,1},{8,10},{9,11},{10,... | collective-permute-start | bytes 2555912 | tf_op jit(solution)/shard_map/ppermute | solution.py:401
  943.3 155.7 %collective-permute-start.72 = (bf16[2,2048,1024]{2,1,0:T(8,128)(2,1)}, bf16[2,2048,1024]{2,1,0:T(8,128)(2,1)}, u32[]{:S(2)}, u32[]{:S(2)}) collective-permute-start(bf16[2,2048,1024]{2,1,0:T(8,128)(2,1)} %fusion.46), channel_id=1, source_target_pairs={{0,8},{1,9},{2,10},{3,11},{4,12},{5,13},{6,14},{7,15},{8,0},{9,1},... | collective-permute-start | bytes 25165832 | tf_op jit(solution)/shard_map/ppermute | solution.py:401
  943.3 127.9 %collective-permute-start.68 = (bf16[2,1024,2048]{2,1,0:T(8,128)(2,1)}, bf16[2,1024,2048]{2,1,0:T(8,128)(2,1)}, u32[]{:S(2)}, u32[]{:S(2)}) collective-permute-start(bf16[2,1024,2048]{2,1,0:T(8,128)(2,1)} %fusion.38), channel_id=1, source_target_pairs={{0,8},{1,9},{2,10},{3,11},{4,12},{5,13},{6,14},{7,15},{8,0},{9,1},... | collective-permute-start | bytes 25165832 | tf_op jit(solution)/shard_map/ppermute | solution.py:401
  977.9 139.9 %collective-permute-start.73 = (bf16[2,2048,1024]{2,1,0:T(8,128)(2,1)}, bf16[2,2048,1024]{2,1,0:T(8,128)(2,1)}, u32[]{:S(2)}, u32[]{:S(2)}) collective-permute-start(bf16[2,2048,1024]{2,1,0:T(8,128)(2,1)} %fusion.43.refs_0_), channel_id=1, source_target_pairs={{0,8},{1,9},{2,10},{3,11},{4,12},{5,13},{6,14},{7,15},{8,0},{9,1},... | collective-permute-start | bytes 25165832 | tf_op jit(solution)/shard_map/ppermute | solution.py:401
  1068.1 66.8 %collective-permute-start.70 = (bf16[64,2048]{1,0:T(8,128)(2,1)}, bf16[64,2048]{1,0:T(8,128)(2,1)S(1)}, u32[]{:S(2)}, u32[]{:S(2)}) collective-permute-start(bf16[64,2048]{1,0:T(8,128)(2,1)} %reduce-scatter.5.cloned.1.call-done), channel_id=1, source_target_pairs={{0,16},{1,17},{2,18},{3,19},{4,20},{5,21},{6,22},{7,23},{8,24},{9,... | collective-permute-start | bytes 786440 | tf_op jit(solution)/shard_map/ppermute | solution.py:401
  (91 other events, 1950.0 us)
Sparse Core Ops, SparseCore 0:
  126.9 118.4 all-gather.2
  385.8 99.1 all-gather.4
  795.7 195.0 reduce-scatter.2
  1002.8 65.2 reduce-scatter.4

commit v3 on v2

--- a/solution.py
+++ b/solution.py
@@ -1,3 +1,5 @@
+import functools
+
 import jax
 import jax.numpy as jnp
 from jax import lax
@@ -393,6 +395,11 @@
 CORE_SWAP = pairs_of(lambda rep, shard: (rep ^ 1, shard))
 X_SWAP = pairs_of(lambda rep, shard: (rep ^ 2, shard))
 Y_SWAP = pairs_of(lambda rep, shard: (rep, shard ^ 1))
+SHARD_SWAP = [
+    pairs_of(lambda rep, shard: (rep, shard ^ 1)),
+    pairs_of(lambda rep, shard: (rep, shard ^ 2)),
+    pairs_of(lambda rep, shard: (rep, shard ^ 4)),
+]
 Z_FROM = [pairs_of(lambda rep, shard: (rep, (shard - 2 * k) % SHARDS)) for k in range(LINE)]
 Z_TO = [pairs_of(lambda rep, shard: (rep, (shard + 2 * k) % SHARDS)) for k in range(LINE)]
 
@@ -405,23 +412,24 @@
     return lax.optimization_barrier((values,) + others)[0]
 
 
-def gather_small(values):
-    line = jnp.stack([values] + [move(values, Z_FROM[k]) for k in range(1, LINE)])
-    both = jnp.stack([line, move(line, Y_SWAP)], axis=1)
+def gather_small(values, hold):
+    low = jnp.stack([values, move(values, SHARD_SWAP[1])])
+    high = jnp.stack([low, move(low, SHARD_SWAP[2])])
+    both = jnp.stack([high, move(after(high, *hold), SHARD_SWAP[0])], axis=2)
     return both.reshape((SHARDS,) + values.shape)
 
 
-def gather_rows(values, early=None, late=None, fill=None):
+def gather_rows(values, early=None, late=(), fill=None, first=()):
     moved = {k: move(values, Z_FROM[k]) for k in (1, 3)}
-    moved[2] = move(after(values, moved[1]), Z_FROM[2])
+    moved[2] = move(after(values, moved[1], *first), Z_FROM[2])
     mine, beside = {0: values}, {0: move(values, Y_SWAP)}
     for k in (1, 3, 2):
         mine[k] = moved[k] if early is None else after(moved[k], early)
         if k == 2 and fill is not None:
             mine[k] = after(mine[k], *fill(mine[3]))
         beside[k] = move(mine[k], Y_SWAP)
-    if late is not None:
-        beside = {k: after(beside[k], late) for k in beside}
+    if late:
+        beside = {k: after(beside[k], *late) for k in beside}
     return [(mine[k], beside[k]) for k in range(LINE)]
 
 
@@ -437,19 +445,18 @@
 
 
 def scatter_rows(parts, fills):
-    moved = {}
-    for k in (2, 1, 3, 0):
-        moved[k] = move(added(*[part(2 * k + 1) for part in parts]), Y_SWAP)
-    arrived, reduced, last = [], None, moved[2]
+    away = {k: added(*[part(2 * k + 1) for part in parts]) for k in (2, 1, 3, 0)}
+    moved = {k: move(away[k], Y_SWAP) for k in (2, 1, 3, 0)}
+    arrived, reduced = [], away[2]
     for k, fill in zip((2, 1, 3, 0), fills):
         here = moved[k]
         if fill is not None:
-            here = after(here, *fill(() if reduced is None else (reduced,)))
+            here = after(here, *fill((reduced,)))
         reduced = added(here, *[part(2 * k) for part in parts])
         if k > 0:
             arrived.append(move(reduced, Z_TO[k]))
     if fills[4] is not None:
-        reduced = after(reduced, *fills[4]((reduced,)))
+        reduced, *arrived = fills[4]((reduced, *arrived))
     return added(reduced, *arrived)
 
 
@@ -457,6 +464,7 @@
 HIDDEN_BLOCK = 256
 WIDTH_BLOCK = 512
 QUIET = pl.CostEstimate(flops=0, bytes_accessed=0, transcendentals=0)
+LOUD = pl.CostEstimate(flops=10**11, bytes_accessed=0, transcendentals=0)
 
 
 def ordered(kernel, behind):
@@ -659,7 +667,7 @@
             jax.ShapeDtypeStruct((experts, capacity, hidden), jnp.float32),
         ],
         compiler_params=pltpu.CompilerParams(vmem_limit_bytes=LIMIT),
-        cost_estimate=QUIET,
+        cost_estimate=LOUD,
     )(core, *behind, slots[:, None, :], rows, down_weight)
 
 
@@ -711,7 +719,7 @@
         score_ref[0] = jnp.where(label == mine, total_ref[...], 0.0).astype(jnp.bfloat16)
 
 
-def forward_part(first, slots, rows, router_rows, gate_weight, up_weight, slot_cot, behind=()):
+def forward_part(first, slots, rows, router_rows, gate_weight, up_weight, slot_cot, behind=(), cost=QUIET):
     experts, tokens = slots.shape
     capacity, hidden = slot_cot.shape[1:]
     width = rows.shape[1]
@@ -755,7 +763,7 @@
             jax.ShapeDtypeStruct((experts, capacity, HEAD_DIM), jnp.bfloat16),
         ],
         compiler_params=pltpu.CompilerParams(vmem_limit_bytes=LIMIT),
-        cost_estimate=QUIET,
+        cost_estimate=cost,
     )(first, *behind, slots[:, None, :], rows, router_rows, gate_weight, up_weight, slot_cot)
 
 
@@ -829,10 +837,10 @@
     )
 
 
-def routed_kernel(core_ref, slots_ref, act_ref, *rest):
+def routed_kernel(more, core_ref, slots_ref, act_ref, *rest):
     experts, capacity, _ = act_ref.shape
     downs = rest[:experts]
-    into_ref, spread_ref, slot_ref = rest[experts:]
+    into_ref, spread_ref, slot_ref = rest[experts + more :]
 
     @pl.when(pl.program_id(0) == 0)
     def _():
@@ -841,10 +849,13 @@
     for expert in range(experts):
         rows = dot_wide(act_ref[expert], downs[expert][0])
         slot_ref[expert * capacity : (expert + 1) * capacity, :] = rows.astype(jnp.bfloat16)
-    into_ref[...] = dot_wide(spread_ref[...], slot_ref[...]).astype(jnp.bfloat16)
-
-
-def routed_part(core, columns, act, down_weight, behind=()):
+    total = dot_wide(spread_ref[...], slot_ref[...])
+    for extra in rest[experts : experts + more]:
+        total += extra[...].astype(jnp.float32)
+    into_ref[...] = total.astype(jnp.bfloat16)
+
+
+def routed_part(core, columns, act, down_weight, extra=(), behind=()):
     experts, capacity, hidden = act.shape
     tokens, width = columns.shape[0], down_weight.shape[2]
 
@@ -853,8 +864,9 @@
             (1, hidden, WIDTH_BLOCK), lambda n, core: (core[0] * experts + expert, 0, n)
         )
 
+    rows_spec = pl.BlockSpec((tokens, WIDTH_BLOCK), lambda n, core: (0, n))
     return pl.pallas_call(
-        ordered(routed_kernel, len(behind)),
+        ordered(functools.partial(routed_kernel, len(extra)), len(behind)),
         grid_spec=pltpu.PrefetchScalarGridSpec(
             num_scalar_prefetch=1,
             grid=(width // WIDTH_BLOCK,),
@@ -863,8 +875,9 @@
                 pl.BlockSpec(columns.shape, lambda n, core: (0, 0)),
                 pl.BlockSpec((experts, capacity, hidden), lambda n, core: (0, 0, 0)),
             ]
-            + [weight_spec(expert) for expert in range(experts)],
-            out_specs=pl.BlockSpec((tokens, WIDTH_BLOCK), lambda n, core: (0, n)),
+            + [weight_spec(expert) for expert in range(experts)]
+            + [rows_spec] * len(extra),
+            out_specs=rows_spec,
             scratch_shapes=[
                 pltpu.VMEM((tokens, experts * capacity), jnp.bfloat16),
                 pltpu.VMEM((experts * capacity, WIDTH_BLOCK), jnp.bfloat16),
@@ -872,8 +885,8 @@
         ),
         out_shape=jax.ShapeDtypeStruct((tokens, width), jnp.bfloat16),
         compiler_params=pltpu.CompilerParams(vmem_limit_bytes=LIMIT),
-        cost_estimate=QUIET,
-    )(core, *behind, columns, act, *[down_weight] * experts)
+        cost_estimate=LOUD,
+    )(core, *behind, columns, act, *[down_weight] * experts, *extra)
 
 
 def roll_half(values):
@@ -1086,9 +1099,6 @@
         jnp.where(near_shards[None, :] == shard_ids[:, None], shard_ids[None, :], 0), axis=1
     )
 
-    in_pieces = gather_rows(thin_columns(in_proj, rep_ref, width))
-    in_part = flat(in_pieces)
-
     order_row = priority[0]
     pair_ids = jnp.arange(pair_count, dtype=jnp.int32)
     place_of = jnp.sum(
@@ -1102,10 +1112,24 @@
     earlier = jnp.sum((place_at[:, None, :] < place_at[:, :, None]).astype(jnp.int32), axis=2)
     ranks = jnp.where(named, earlier, -1).astype(bf16)
     ranks = jnp.concatenate([ranks, segments.astype(bf16)], axis=0)
+    ranks = jnp.pad(ranks, ((0, 0), (0, rows_each - tokens)))
     ranks = jnp.stack([ranks, move(ranks, CORE_SWAP)])
     ranks = jnp.concatenate([ranks, move(ranks, X_SWAP)])
-    segment_rows = ranks[:, expert_count, :].astype(jnp.int32)
-    ranks = gather_small(ranks)[:, :, :expert_count].astype(jnp.int32)
+    segment_rows = ranks[:, expert_count, :tokens].astype(jnp.int32)
+
+    inputs_across = move(inputs, X_SWAP)
+    small_in = jnp.stack([attn_gain, query_gain, key_gain, ffn_gain])
+    small_in = jnp.concatenate(
+        [small_in, router_weight.T, ranks.reshape(REPS * (expert_count + 1), rows_each)], axis=0
+    )
+    in_pieces = gather_rows(
+        thin_columns(in_proj, rep_ref, width), first=(inputs_across, segment_rows)
+    )
+    small_in = gather_small(small_in, (in_pieces[2][0], in_pieces[1][1], in_pieces[3][1]))
+    ranks = small_in[:, 4 + expert_count :, :tokens]
+    ranks = jnp.take(ranks, near_shards ^ shard, axis=0)
+    ranks = ranks.reshape(SHARDS, REPS, expert_count + 1, tokens)[:, :, :expert_count]
+    ranks = ranks.astype(jnp.int32)
     counts = jnp.sum((ranks >= 0).astype(jnp.int32), axis=3)
     before = (near_shards[None, :] < near_shards[:, None])[:, :, None, None]
     bases = jnp.sum(jnp.where(before, counts[None], 0), axis=1)
@@ -1124,9 +1148,14 @@
 
     columns, shard_columns = columns_of(slots[:2]), columns_of(shard_slots[:2])
 
-    small_in = jnp.stack([attn_gain, query_gain, key_gain, ffn_gain])
-    small_in = jnp.concatenate([small_in, router_weight.T], axis=0)
-    small_in = jnp.take(gather_small(small_in), place_of_shard, axis=0)
+    in_part = flat(
+        [
+            (mine, after(beside, slots, shard_slots, columns, shard_columns))
+            for mine, beside in in_pieces
+        ]
+    )
+
+    small_in = jnp.take(small_in[:, : 4 + expert_count], shard_ids ^ shard, axis=0)
     small_in = small_in.transpose(1, 0, 2).reshape(4 + expert_count, width)
     gains = small_in[:4].astype(f32)
     router_rows = small_in[4:]
@@ -1138,7 +1167,7 @@
 
     hidden = inputs.astype(f32)
     home_rate = lax.rsqrt(jnp.mean(hidden * hidden, axis=-1, keepdims=True) + norm_eps)
-    inputs_all = jnp.stack([inputs, move(inputs, X_SWAP)])
+    inputs_all = jnp.stack([inputs, inputs_across])
     inputs_all = jnp.stack([inputs_all, move(inputs_all, CORE_SWAP)], axis=1)
     inputs_all = inputs_all.reshape(REPS * tokens, width)
     inputs_all = pick_columns(inputs_all, near_shards, rows_each).astype(f32)
@@ -1148,7 +1177,7 @@
     near_gain = jnp.take(gains[0].reshape(SHARDS, rows_each), near_shards, axis=0).reshape(width)
     normed_low = (unit_all * near_gain).astype(bf16)
     cot_across = move(grad_out, X_SWAP)
-    normed_low = after(normed_low, slots, shard_slots, columns, shard_columns, cot_across)
+    normed_low = after(normed_low, cot_across)
     cot_own = after(grad_out, in_part)
     cot_own = lax.all_gather(cot_own, "shard", tiled=True)
     cos_table, sin_table = jax.vmap(rotary_tables)(segment_rows)
@@ -1180,7 +1209,7 @@
         segment_rows[:, None, :],
     )
     attended = attend(*attention_operands).reshape(2, 2, tokens, part_width)
-    out_pieces = gather_rows(out_own, early=projected, late=attended)
+    out_pieces = gather_rows(out_own, early=projected, late=(attended,))
     out_own = flat(out_pieces).reshape(SHARDS, out_rows, width)
     out_other = move(out_own, CORE_SWAP)
     out_part = jnp.where(
@@ -1208,9 +1237,17 @@
 
     first_ref = jnp.stack([c, first_expert]).astype(jnp.int32)
 
-    def ffn_part(group, rows, slot_cot, behind=()):
+    def ffn_part(group, rows, slot_cot, behind=(), cost=QUIET):
         return forward_part(
-            first_ref, slots[group], rows, router_rows, gate_weight, up_weight, slot_cot, behind
+            first_ref,
+            slots[group],
+            rows,
+            router_rows,
+            gate_weight,
+            up_weight,
+            slot_cot,
+            behind,
+            cost,
         )
 
     made = {}
@@ -1219,16 +1256,17 @@
         beside = move(cot_own, CORE_SWAP)
         own_part = cot_part(0, cot_own, (follow,))
         made["cot"] = [own_part, cot_part(1, beside, (own_part[1],))]
-        return [made["cot"][1][1]]
+        return [own_part[1]]
 
     ffn_pieces = gather_rows(ffn_low, fill=fill_cot)
     near_cot = made["cot"]
-    ffn_own = flat(ffn_pieces)
+    ffn_own = after(flat(ffn_pieces), near_cot[1][1])
     ffn_beside = move(ffn_own, CORE_SWAP)
-    ffn_far = move(ffn_own, X_SWAP)
-    cot_across = lax.all_gather(after(cot_across, ffn_own), "shard", tiled=True)
-
-    near = [ffn_part(0, ffn_own, near_cot[0][1]), ffn_part(1, ffn_beside, near_cot[1][1])]
+    ffn_far = [move(jnp.concatenate(pair, axis=0), X_SWAP) for pair in ffn_pieces]
+    cot_across = lax.all_gather(after(cot_across, ffn_pieces[2][0]), "shard", tiled=True)
+
+    near = [ffn_part(0, ffn_own, near_cot[0][1])]
+    near.append(ffn_part(1, ffn_beside, near_cot[1][1], (near[0][1],)))
 
     def rows_back(group, behind=()):
         _, _, grad_gate, grad_up, scores = near[group]
@@ -1236,38 +1274,41 @@
             core_ref, columns[group], grad_gate, grad_up, scores, gate_weight, up_weight, behind
         ).reshape(SHARDS, tokens, -1)
 
-    grad_other = rows_back(1)
+    grad_other = rows_back(1, (ffn_far[0], ffn_far[1]))
     grad_own = rows_back(0, (grad_other,))
     grad_other = move(grad_other, CORE_SWAP)
 
-    def routed_rows(group, behind):
-        return routed_part(core_ref, shard_columns[group], near[group][1], down_weight, behind)
+    def routed_rows(group, extra, behind):
+        return routed_part(
+            core_ref, shard_columns[group], near[group][1], down_weight, extra, behind
+        )
 
     def fill_routed_other(follow):
-        made["routed_other"] = routed_rows(1, (grad_own,))
+        made["routed_other"] = routed_rows(1, (), follow + (ffn_far[2], cot_across))
         return [made["routed_other"]]
 
+    def fill_far_cot(follow):
+        made["far_cot"] = cot_part(2, cot_across, follow)
+        return [made["far_cot"][1]]
+
     def fill_routed_own(follow):
-        made["routed_own"] = routed_rows(0, follow + (made["routed_other"], ffn_far))
-        return [made["routed_own"]]
-
-    def fill_far_cot(follow):
-        made["far_cot"] = cot_part(2, cot_across, follow + (made["routed_own"],))
-        return [made["far_cot"][1]]
+        extra = (move(made["routed_other"], CORE_SWAP),)
+        made["routed"] = routed_rows(0, extra, follow)
+        return [made["routed"]]
 
     def fill_other_cot(follow):
-        rows = move(after(cot_across, made["routed_other"]), CORE_SWAP)
-        made["other_cot"] = cot_part(3, rows, follow + (made["far_cot"][1],))
+        rows = move(after(cot_across, made["routed"]), CORE_SWAP)
+        made["other_cot"] = cot_part(3, rows, follow)
         return [made["other_cot"][1]]
 
     grad_home = scatter_rows(
         [lambda place: grad_own[place], lambda place: grad_other[place]],
         [fill_routed_other, fill_routed_own, fill_far_cot, fill_other_cot, None],
     )
-    routed = added(made["routed_own"], move(made["routed_other"], CORE_SWAP))
     routed = lax.psum_scatter(
-        after(routed, grad_home), "shard", scatter_dimension=0, tiled=True
-    )
+        after(made["routed"], grad_home), "shard", scatter_dimension=0, tiled=True
+    )
+    ffn_far = jnp.concatenate([after(part, made["other_cot"][1]) for part in ffn_far], axis=0)
     ffn_far = [ffn_far, move(ffn_far, CORE_SWAP)]
 
     grad_ffn_home = grad_home[:, :width]
@@ -1316,10 +1357,17 @@
     small = jnp.pad(small, ((0, HEAD_DIM - small.shape[0]), (0, 0), (0, 0)))
     small = small.astype(bf16).transpose(1, 2, 0)
 
+    grad_out_part = contract_rows(after(attended, grad_projected), residual_pair).astype(bf16)
+    out_parts = grad_out_part.reshape(SHARDS, 2, out_rows, width)
+    out_own = lax.dynamic_index_in_dim(out_parts, c, 1, keepdims=False)
+    out_other = lax.dynamic_index_in_dim(out_parts, 1 - c, 1, keepdims=False)
+    out_sum = added(out_own, move(out_other, CORE_SWAP))
+    out_sum = jnp.take(out_sum, place_of_shard, axis=0).reshape(SHARDS * out_rows, width)
+
     far_cot = [made["far_cot"], made["other_cot"]]
 
     def fill_far(follow):
-        made["far"] = ffn_part(2, ffn_far[0], far_cot[0][1], (grad_projected,))
+        made["far"] = ffn_part(2, ffn_far[0], far_cot[0][1], follow, LOUD)
         return [made["far"][3]]
 
     normed_other = grad_normed.astype(bf16).reshape(2, 2, tokens, width)
@@ -1328,40 +1376,51 @@
 
     def fill_other(follow):
         made["other"] = ffn_part(
-            3, ffn_far[1], far_cot[1][1], follow + (made["far"][3], normed_mine)
+            3, ffn_far[1], far_cot[1][1], follow + (made["far"][3], normed_mine, routed), LOUD
         )
         return [made["other"][3]]
 
     def weight_grad(left, right, follow):
-        left = jnp.concatenate([after(left[0], *follow)] + left[1:], axis=1)
+        first, *follow = lax.optimization_barrier((left[0],) + follow)
+        left = jnp.concatenate([first] + left[1:], axis=1)
         right = jnp.concatenate(right, axis=1)
-        return jnp.einsum("ecd,ecf->edf", left, right, preferred_element_type=f32).astype(bf16)
+        grad = jnp.einsum("ecd,ecf->edf", left, right, preferred_element_type=f32).astype(bf16)
+        return grad, follow
 
     def groups(index):
         return [part[index] for part in (near[0], near[1], made["far"], made["other"])]
 
     def fill_down(follow):
         cots = [part[0] for part in near_cot + far_cot]
-        made["down"] = weight_grad(groups(1), cots, follow + (normed_across,))
-        return [made["down"]]
-
-    def fill_gate(follow):
-        made["gate"] = weight_grad(groups(0), groups(2), follow)
-        return [made["gate"]]
+        reduced, low, high, third = follow
+        made["down"], (reduced, low, high, _) = weight_grad(
+            groups(1), cots, (reduced, low, high, normed_across)
+        )
+        return after(reduced, made["down"]), low, high, third
 
     in_sum = scatter_rows(
         [lambda place: jnp.concatenate([grad_in_part[place], small[place]], axis=1)],
-        [fill_far, fill_other, None, fill_down, fill_gate],
+        [fill_far, None, None, fill_other, fill_down],
     )
     in_other = move(in_sum, X_SWAP)
-    grad_up = weight_grad(groups(0), groups(3), (in_sum,))
-    in_all = jnp.stack([in_sum, after(in_other, grad_up)])
+    out_sum = lax.psum_scatter(
+        after(out_sum, routed), "shard", scatter_dimension=0, tiled=True
+    )
+    made["gate"], (in_sum, out_sum) = weight_grad(groups(0), groups(2), (in_sum, out_sum))
+    out_across = move(out_sum, X_SWAP)
+    down_all = widen(
+        made["down"],
+        move(made["down"], CORE_SWAP),
+        core_ref,
+        (made["gate"], in_other, out_across),
+    )
+    in_all = jnp.stack([in_sum, after(in_other, made["gate"])])
     in_beside = move(in_all, CORE_SWAP)
-    down_all = widen(made["down"], move(made["down"], CORE_SWAP), core_ref, (grad_up,))
+    grad_up, (_, in_beside) = weight_grad(groups(0), groups(3), (down_all, in_beside))
     in_all = jnp.stack([in_all, in_beside], axis=1).reshape((REPS,) + in_sum.shape)
-    grad_in = weave_columns(in_all, rep_ref, 3 * part_width, (down_all,))
+    grad_in = weave_columns(in_all, rep_ref, 3 * part_width, (grad_up,))
     small = jnp.sum(in_all[:, :, 3 * part_width :].astype(f32), axis=0).T
-    gate_all = widen(made["gate"], move(made["gate"], CORE_SWAP), core_ref, (down_all,))
+    gate_all = widen(made["gate"], move(made["gate"], CORE_SWAP), core_ref, (grad_up,))
     up_all = widen(grad_up, move(grad_up, CORE_SWAP), core_ref, (gate_all,))
 
     outputs = (residual + after(routed, in_sum).astype(f32)).astype(bf16)
@@ -1374,15 +1433,7 @@
         + home_rate * (scaled - home_unit * jnp.mean(scaled * home_unit, axis=-1, keepdims=True))
     ).astype(bf16)
 
-    grad_out_part = contract_rows(after(attended, made["far"][3]), residual_pair).astype(bf16)
-    out_parts = grad_out_part.reshape(SHARDS, 2, out_rows, width)
-    out_own = lax.dynamic_index_in_dim(out_parts, c, 1, keepdims=False)
-    out_other = lax.dynamic_index_in_dim(out_parts, 1 - c, 1, keepdims=False)
-    out_sum = added(out_own, move(out_other, CORE_SWAP))
-    out_sum = jnp.take(out_sum, place_of_shard, axis=0).reshape(SHARDS * out_rows, width)
-    out_sum = after(out_sum, in_sum, routed)
-    out_sum = lax.psum_scatter(out_sum, "shard", scatter_dimension=0, tiled=True)
-    out_sum = jnp.stack([out_sum, move(out_sum, X_SWAP)])
+    out_sum = jnp.stack([out_sum, out_across])
     out_sum = jnp.stack([out_sum, move(out_sum, CORE_SWAP)], axis=1)
     out_sum = out_sum.reshape(REPS, out_rows, width)
     out_sum = jnp.take(out_sum, rep ^ jnp.arange(REPS, dtype=jnp.int32), axis=0)

time: 1150 us -> 1060 us (0.922)
  waiting for transfers between devices: 366 us -> 278 us
  starting transfers between devices: 99.2 us -> 68.4 us
  local copies, waits for them, and re-layouts: 93 us -> 120 us
    ppermute x74 -> x72, waiting for transfers between devices: 328 us -> 278 us  [move(): return lax.ppermute(values, AXES, moves)]
    reduce_scatter x2, waiting for transfers between devices: 38.1 us -> 0.01 us  [the longest x1 0.01 us: fast_local(): lax.psum_scatter(after(made['routed'], grad_home), 'shard', scatter_dimen...]
    ppermute x74 -> x72, starting transfers between devices: 99 us -> 67.6 us  [move(): return lax.ppermute(values, AXES, moves)]
    unnamed x149 -> x236, local copies, waits for them, and re-layouts: 49.8 us -> 66.2 us
    convert_element_type x14 -> x13, other arithmetic: 42.4 us -> 29.2 us  [added(): return total.astype(first.dtype)]
  transfers between devices with their start and end apart: 78 -> 76, of which waited for: 27 -> 25; matrix products, arithmetic and copies ran while one was open for 23% -> 28% of each run, Pallas kernels for 32% -> 30%
where the time goes in v3:
time: 1060 us; the launch traced here: 1050 us
  Pallas kernels  369 us (35%)
  waiting for transfers between devices  278 us (26%)
  local copies, waits for them, and re-layouts  120 us (11%)
  matrix products  101 us (10%)
  other arithmetic  98 us (9%)
  starting transfers between devices  68.4 us (6%)
  between operations  15.7 us (1%)
    ppermute x72, waiting for transfers between devices, move(): return lax.ppermute(values, AXES, moves)  278 us
    pallas_call x4, Pallas kernels, forward_part(): pl.pallas_call(ordered(forward_kernel, len(behind)), grid_spec=pltpu.Pref...  113 us
    pallas_call x4, Pallas kernels, cotangent_part(): pl.pallas_call(ordered(cotangent_kernel, len(behind)), grid_spec=pltpu.Pr...  76.5 us
    dot_general x3, matrix products, weight_grad(): jnp.einsum('ecd,ecf->edf', left, right, preferred_element_type=f32)  69.2 us
    ppermute x72, starting transfers between devices, move(): return lax.ppermute(values, AXES, moves)  67.6 us
    unnamed x236, local copies, waits for them, and re-layouts  66.2 us
    pallas_call x3, Pallas kernels, widen(): pl.pallas_call(ordered(widen_kernel, len(behind)), grid_spec=pltpu.Prefet...  50.8 us
    pallas_call x2, Pallas kernels, backward_part(): pl.pallas_call(ordered(backward_kernel, len(behind)), grid_spec=pltpu.Pre...  49 us
  transfers between devices with their start and end apart: 76, of which 25 were waited for; matrix products, arithmetic and copies ran while one was open for 28% of the time, Pallas kernels for 30%

profile of v3, /device:TPU:0, one launch (start us, length us, event | category | flops | bytes accessed | tf_op | source)
XLA Modules:
  0.0 1050.7 jit_solution(9352749067834969157)
XLA Ops:
  29.9 12.7 %collective-permute-done.3 = bf16[2,33,256]{2,1,0:T(8,128)(2,1)S(1)} collective-permute-done((bf16[2,33,256]{2,1,0:T(8,128)(2,1)S(1)}, bf16[2,33,256]{2,1,0:T(8,128)(2,1)S(1)}, u32[]{:S(2)}, u32[]{:S(2)}) %collective-permute-start.3) | collective-permute-done | bytes 33824 | tf_op jit(solution)/shard_map/ppermute | solution.py:408
  45.2 5.5 collective-permute-done.6
  59.4 34.6 %collective-permute-done.5 = bf16[2,168,256]{2,1,0:T(8,128)(2,1)S(1)} collective-permute-done((bf16[2,168,256]{2,1,0:T(8,128)(2,1)S(1)}, bf16[2,168,256]{2,1,0:T(8,128)(2,1)S(1)}, u32[]{:S(2)}, u32[]{:S(2)}) %collective-permute-start.5) | collective-permute-done | bytes 172064 | tf_op jit(solution)/shard_map/ppermute | solution.py:408
  110.5 4.5 convert_reduce_fusion.1
  123.6 3.9 fusion.71
  138.0 7.5 collective-permute-done.14
  159.6 8.1 fusion.125.raw_ref.refs_0_
  179.9 10.2 shard_map.240
  198.8 3.7 collective-permute-done.17
  203.8 5.2 maximum_select_fusion
  211.8 19.1 %collective-permute-done.26 = bf16[192,2048]{1,0:T(8,128)(2,1)S(1)} collective-permute-done((bf16[192,2048]{1,0:T(8,128)(2,1)S(1)}, bf16[192,2048]{1,0:T(8,128)(2,1)S(1)}, u32[]{:S(2)}, u32[]{:S(2)}) %collective-permute-start.26) | collective-permute-done | bytes 786464 | tf_op jit(solution)/shard_map/ppermute | solution.py:408
  238.8 26.1 %collective-permute-done.29 = bf16[192,2048]{1,0:T(8,128)(2,1)} collective-permute-done((bf16[192,2048]{1,0:T(8,128)(2,1)S(1)}, bf16[192,2048]{1,0:T(8,128)(2,1)}, u32[]{:S(2)}, u32[]{:S(2)}) %collective-permute-start.29) | collective-permute-done | bytes 786464 | tf_op jit(solution)/shard_map/ppermute | solution.py:408
  268.4 15.8 %collective-permute-done.33.refs_0_ = bf16[192,2048]{1,0:T(8,128)(2,1)S(1)} collective-permute-done((bf16[192,2048]{1,0:T(8,128)(2,1)S(1)}, bf16[192,2048]{1,0:T(8,128)(2,1)S(1)}, u32[]{:S(2)}, u32[]{:S(2)}) %collective-permute-start.33) | collective-permute-done | bytes 786464 | tf_op jit(solution)/shard_map/ppermute | solution.py:408
  285.0 19.0 %shard_map.242 = (bf16[2,480,2048]{2,1,0:T(8,128)(2,1)}, f32[2,480,1024]{2,1,0:T(8,128)}) custom-call(s32[1]{0:T(128)} %bitcast.42.scalar_ref, bf16[192,2048]{1,0:T(8,128)(2,1)} %copy-done.35, s32[2,1,1536]{2,1,0:T(1,128)} %broadcast_in_dim_squeeze.25.refs_1_, bf16[1536,2048]{1,0:T(8,128)(2,1)} %all-gather.3.cloned.1.call-done.refs_2_, ...), custom_call_target="tpu_custom_call" | custom-call | flops 99999997952 | tf_op jit(solution)/shard_map/pallas_call | solution.py:647
  304.0 13.3 %collective-permute-done.32 = bf16[192,2048]{1,0:T(8,128)(2,1)S(1)} collective-permute-done((bf16[192,2048]{1,0:T(8,128)(2,1)S(1)}, bf16[192,2048]{1,0:T(8,128)(2,1)S(1)}, u32[]{:S(2)}, u32[]{:S(2)}) %collective-permute-start.32) | collective-permute-done | bytes 786464 | tf_op jit(solution)/shard_map/ppermute | solution.py:408
  325.1 11.6 %collective-permute-done.34 = bf16[192,2048]{1,0:T(8,128)(2,1)S(1)} collective-permute-done((bf16[192,2048]{1,0:T(8,128)(2,1)S(1)}, bf16[192,2048]{1,0:T(8,128)(2,1)S(1)}, u32[]{:S(2)}, u32[]{:S(2)}) %collective-permute-start.34) | collective-permute-done | bytes 786464 | tf_op jit(solution)/shard_map/ppermute | solution.py:408
  339.8 19.1 %shard_map.243 = (bf16[2,480,2048]{2,1,0:T(8,128)(2,1)}, f32[2,480,1024]{2,1,0:T(8,128)}) custom-call(s32[1]{0:T(128)} %bitcast.42.scalar_ref, f32[2,480,1024]{2,1,0:T(8,128)} %get-tuple-element.107.refs_0_.refs_5_, s32[2,1,1536]{2,1,0:T(1,128)} %broadcast_in_dim_squeeze.26.refs_1_, bf16[1536,2048]{1,0:T(8,128)(2,1)} %collective-permute-done.36.refs_2_, ...), custom_call_target="tpu_custom_call" | custom-call | flops 99999997952 | tf_op jit(solution)/shard_map/pallas_call | solution.py:647
  371.3 27.8 %shard_map.244 = (bf16[2,480,2048]{2,1,0:T(8,128)(2,1)}, bf16[2,480,1024]{2,1,0:T(8,128)(2,1)}, bf16[2,480,1024]{2,1,0:T(8,128)(2,1)}, bf16[2,480,1024]{2,1,0:T(8,128)(2,1)}, bf16[2,480,128]{2,1,0:T(8,128)(2,1)}) custom-call(s32[2]{0:T(128)} %pad_add_fusion.scalar_ref, s32[2,1,1536]{2,1,0:T(1,128)} %broadcast_in_dim_squeeze.24.refs_0_, ...), custom_call_target="tpu_custom_call" | custom-call | tf_op jit(solution)/shard_map/pallas_call | solution.py:732
  399.2 28.3 %shard_map.245 = (bf16[2,480,2048]{2,1,0:T(8,128)(2,1)}, bf16[2,480,1024]{2,1,0:T(8,128)(2,1)}, bf16[2,480,1024]{2,1,0:T(8,128)(2,1)}, bf16[2,480,1024]{2,1,0:T(8,128)(2,1)}, bf16[2,480,128]{2,1,0:T(8,128)(2,1)}) custom-call(s32[2]{0:T(128)} %pad_add_fusion.scalar_ref, bf16[2,480,1024]{2,1,0:T(8,128)(2,1)} %get-tuple-element.142.refs_0_.refs_2_, ...), custom_call_target="tpu_custom_call" | custom-call | tf_op jit(solution)/shard_map/pallas_call | solution.py:732
  427.5 5.2 collective-permute-done.31.refs_1_
  432.7 24.6 %shard_map.246 = bf16[1536,2176]{1,0:T(8,128)(2,1)} custom-call(s32[1]{0:T(128)} %bitcast.42.scalar_ref, bf16[384,2048]{1,0:T(8,128)(2,1)} %collective-permute-done.28.refs_0_, bf16[384,2048]{1,0:T(8,128)(2,1)} %collective-permute-done.31.refs_1_, s32[1536,2]{1,0:T(8,128)} %get-tuple-element.243.refs_2_, bf16[2,480,1024]{2,1,0:T(8,128)(2,1)} %get-tuple-element.112.refs_3_, ...), custom_call_target="tpu_custom_call" | custom-call | tf_op jit(solution)/shard_map/pallas_call | solution.py:806
  462.7 24.4 %shard_map.247 = bf16[1536,2176]{1,0:T(8,128)(2,1)} custom-call(s32[1]{0:T(128)} %bitcast.42.scalar_ref, bf16[8,192,2176]{2,1,0:T(8,128)(2,1)} %bitcast.300, s32[1536,2]{1,0:T(8,128)} %get-tuple-element.242.refs_1_, bf16[2,480,1024]{2,1,0:T(8,128)(2,1)} %get-tuple-element.115.refs_2_, bf16[2,480,1024]{2,1,0:T(8,128)(2,1)} %get-tuple-element.116.refs_3_, ...), custom_call_target="tpu_custom_call" | custom-call | tf_op jit(solution)/shard_map/pallas_call | solution.py:806
  492.2 4.7 collective-permute-done.40.refs_1_
  497.0 16.8 %shard_map.248 = bf16[1536,2048]{1,0:T(8,128)(2,1)} custom-call(s32[1]{0:T(128)} %bitcast.42.scalar_ref, bf16[192,2176]{1,0:T(8,128)(2,1)} %fusion.60.refs_0_, bf16[384,2048]{1,0:T(8,128)(2,1)} %collective-permute-done.40.refs_1_, bf16[1536,2048]{1,0:T(8,128)(2,1)} %all-gather.5.cloned.1.call-done.refs_2_, s32[1536,2]{1,0:T(8,128)} %get-tuple-element.241.refs_3_, ...), custom_call_target="tpu_custom_call" | custom-call | flops 99999997952 | tf_op jit(solution)/shard_map/pallas_call | solution.py:868
  521.9 13.0 %collective-permute-done.39 = bf16[192,2176]{1,0:T(8,128)(2,1)} collective-permute-done((bf16[192,2176]{1,0:T(8,128)(2,1)S(1)}, bf16[192,2176]{1,0:T(8,128)(2,1)}, u32[]{:S(2)}, u32[]{:S(2)}) %collective-permute-start.39) | collective-permute-done | bytes 835616 | tf_op jit(solution)/shard_map/ppermute | solution.py:408
  541.8 17.2 %shard_map.249 = bf16[1536,2048]{1,0:T(8,128)(2,1)} custom-call(s32[1]{0:T(128)} %bitcast.42.scalar_ref, bf16[192,2176]{1,0:T(8,128)(2,1)} %get-tuple-element.227.refs_0_, s32[1536,2]{1,0:T(8,128)} %get-tuple-element.240.refs_1_, bf16[2,480,1024]{2,1,0:T(8,128)(2,1)} %get-tuple-element.142.refs_0_.refs_2_, bf16[4,1024,2048]{2,1,0:T(8,128)(2,1)} %refs_3_.11, ...), custom_call_target="tpu_custom_call" | custom-call | flops 99999997952 | tf_op jit(solution)/shard_map/pallas_call | solution.py:868
  564.0 19.1 %shard_map.250 = (bf16[2,480,2048]{2,1,0:T(8,128)(2,1)}, f32[2,480,1024]{2,1,0:T(8,128)}) custom-call(s32[1]{0:T(128)} %bitcast.42.scalar_ref, bf16[192,2176]{1,0:T(8,128)(2,1)} %get-tuple-element.224.refs_0_, s32[2,1,1536]{2,1,0:T(1,128)} %broadcast_in_dim_squeeze.28.refs_1_, bf16[1536,2048]{1,0:T(8,128)(2,1)} %all-gather.5.cloned.1.call-done.refs_2_, ...), custom_call_target="tpu_custom_call" | custom-call | flops 99999997952 | tf_op jit(solution)/shard_map/pallas_call | solution.py:647
  589.7 19.4 %shard_map.251 = (bf16[2,480,2048]{2,1,0:T(8,128)(2,1)}, f32[2,480,1024]{2,1,0:T(8,128)}) custom-call(s32[1]{0:T(128)} %bitcast.42.scalar_ref, bf16[192,2176]{1,0:T(8,128)(2,1)} %copy-done.55, s32[2,1,1536]{2,1,0:T(1,128)} %broadcast_in_dim_squeeze.29.refs_1_, bf16[1536,2048]{1,0:T(8,128)(2,1)} %collective-permute-done.45.refs_2_, ...), custom_call_target="tpu_custom_call" | custom-call | flops 99999997952 | tf_op jit(solution)/shard_map/pallas_call | solution.py:647
  628.1 9.5 collective-permute-done.49
  646.3 20.2 %shard_map.253 = (f32[768,1024]{1,0:T(8,128)}, bf16[768,512]{1,0:T(8,128)(2,1)}, f32[768,2]{1,0:T(8,128)}, f32[4,2,512]{2,1,0:T(2,128)}) custom-call(f32[768,1536]{1,0:T(8,128)} %copy-done.13, f32[768,2]{1,0:T(8,128)} %fusion.83.rate_ref.refs_1_, f32[2,512]{1,0:T(2,128)} %bitcast.355, f32[768,128]{1,0:T(8,128)} %get-tuple-element.262.cos_ref.refs_3_, ...), custom_call_target="tpu_custom_call" | custom-call | tf_op jit(solution)/shard_map/pallas_call | solution.py:1025
  674.6 6.4 shard_map.254
  681.0 9.3 fusion.118
  690.4 7.1 convolution_convert_fusion
  712.5 28.0 %shard_map.255 = (bf16[2,480,2048]{2,1,0:T(8,128)(2,1)}, bf16[2,480,1024]{2,1,0:T(8,128)(2,1)}, bf16[2,480,1024]{2,1,0:T(8,128)(2,1)}, bf16[2,480,1024]{2,1,0:T(8,128)(2,1)}, bf16[2,480,128]{2,1,0:T(8,128)(2,1)}) custom-call(s32[2]{0:T(128)} %pad_add_fusion.scalar_ref, bf16[256,1664]{1,0:T(8,128)(2,1)} %pad_maximum_fusion.26.refs_0_, ...), custom_call_target="tpu_custom_call" | custom-call | flops 99999997952 | tf_op jit(solution)/shard_map/pallas_call | solution.py:732
  742.7 7.8 collective-permute-done.58
  757.1 15.3 %collective-permute-done.54 = bf16[256,1664]{1,0:T(8,128)(2,1)S(1)} collective-permute-done((bf16[256,1664]{1,0:T(8,128)(2,1)S(1)}, bf16[256,1664]{1,0:T(8,128)(2,1)S(1)}, u32[]{:S(2)}, u32[]{:S(2)}) %collective-permute-start.54) | collective-permute-done | bytes 852000 | tf_op jit(solution)/shard_map/ppermute | solution.py:408
  790.2 28.5 %shard_map.256 = (bf16[2,480,2048]{2,1,0:T(8,128)(2,1)}, bf16[2,480,1024]{2,1,0:T(8,128)(2,1)}, bf16[2,480,1024]{2,1,0:T(8,128)(2,1)}, bf16[2,480,1024]{2,1,0:T(8,128)(2,1)}, bf16[2,480,128]{2,1,0:T(8,128)(2,1)}) custom-call(s32[2]{0:T(128)} %pad_add_fusion.scalar_ref, bf16[256,1664]{1,0:T(8,128)(2,1)} %add_convert_fusion.4.refs_0_, ...), custom_call_target="tpu_custom_call" | custom-call | flops 99999997952 | tf_op jit(solution)/shard_map/pallas_call | solution.py:732
  820.1 26.4 %collective-permute-done.59 = bf16[256,1664]{1,0:T(8,128)(2,1)} collective-permute-done((bf16[256,1664]{1,0:T(8,128)(2,1)}, bf16[256,1664]{1,0:T(8,128)(2,1)}, u32[]{:S(2)}, u32[]{:S(2)}) %collective-permute-start.59) | collective-permute-done | bytes 852000 | tf_op jit(solution)/shard_map/ppermute | solution.py:408
  846.5 23.1 %fusion.38 = bf16[2,1024,2048]{2,1,0:T(8,128)(2,1)} fusion(bf16[2,480,2048]{2,1,0:T(8,128)(2,1)} %get-tuple-element.148, bf16[2,480,2048]{2,1,0:T(8,128)(2,1)} %get-tuple-element.147, bf16[2,480,2048]{2,1,0:T(8,128)(2,1)} %get-tuple-element.146, bf16[2,480,2048]{2,1,0:T(8,128)(2,1)} %get-tuple-element.145, bf16[2,480,1024]{2,1,0:T(8,128)(2,1)} %get-tuple-element.144, ...), kind=kOutput, calls=%fused_computation.57 | convolution fusion | flops 16204693504 | bytes 31981568 | tf_op jit(solution)/shard_map/ecd,ecf->edf/dot_general | solution.py:1387
  871.2 19.8 %collective-permute-done.63 = bf16[256,1664]{1,0:T(8,128)(2,1)S(1)} collective-permute-done((bf16[256,1664]{1,0:T(8,128)(2,1)S(1)}, bf16[256,1664]{1,0:T(8,128)(2,1)S(1)}, u32[]{:S(2)}, u32[]{:S(2)}) %collective-permute-start.63) | collective-permute-done | bytes 852000 | tf_op jit(solution)/shard_map/ppermute | solution.py:408
  894.3 23.2 %fusion.46.refs_0_ = bf16[2,2048,1024]{2,1,0:T(8,128)(2,1)} fusion(bf16[2,480,1024]{2,1,0:T(8,128)(2,1)} %get-tuple-element.161, bf16[2,480,1024]{2,1,0:T(8,128)(2,1)} %get-tuple-element.160, bf16[2,480,1024]{2,1,0:T(8,128)(2,1)} %get-tuple-element.112.refs_3_, bf16[2,480,1024]{2,1,0:T(8,128)(2,1)} %get-tuple-element.115.refs_2_, ...), kind=kOutput, calls=%fused_computation.59 | convolution fusion | flops 16204693504 | bytes 31981568 | tf_op jit(solution)/shard_map/ecd,ecf->edf/dot_general | solution.py:1387
  919.7 7.9 collective-permute-done.66.refs_2_
  934.4 16.9 %shard_map.258 = f32[4096,2048]{1,0:T(8,128)} custom-call(s32[1]{0:T(128)} %bitcast.42.scalar_ref, bf16[2,2048,1024]{2,1,0:T(8,128)(2,1)S(1)} %copy-done.3, bf16[256,1664]{1,0:T(8,128)(2,1)S(1)} %collective-permute-done.65.refs_1_, bf16[64,2048]{1,0:T(8,128)(2,1)S(1)} %collective-permute-done.66.refs_2_, bf16[2048,2048]{1,0:T(8,128)(2,1)S(1)} %bitcast.291, ...), custom_call_target="tpu_custom_call" | custom-call | tf_op jit(solution)/shard_map/pallas_call | solution.py:588
  952.6 23.0 %fusion.43.refs_0_ = bf16[2,2048,1024]{2,1,0:T(8,128)(2,1)} fusion(bf16[2,480,1024]{2,1,0:T(8,128)(2,1)} %get-tuple-element.138, bf16[2,480,1024]{2,1,0:T(8,128)(2,1)} %get-tuple-element.137.refs_1_, bf16[2,480,1024]{2,1,0:T(8,128)(2,1)} %get-tuple-element.113.refs_4_, bf16[2,480,1024]{2,1,0:T(8,128)(2,1)} %get-tuple-element.116.refs_3_, ...), kind=kOutput, calls=%fused_computation.58 | convolution fusion | flops 16204693504 | bytes 31981568 | tf_op jit(solution)/shard_map/ecd,ecf->edf/dot_general | solution.py:1387
  982.3 7.2 collective-permute-done.69
  997.6 3.9 shard_map.259
  1010.1 16.9 %shard_map.260 = f32[8192,1024]{1,0:T(8,128)} custom-call(s32[1]{0:T(128)} %bitcast.42.scalar_ref, bf16[2,2048,1024]{2,1,0:T(8,128)(2,1)S(1)} %copy-done.2, bf16[4096,1024]{1,0:T(8,128)(2,1)S(1)} %bitcast.286, bf16[4096,1024]{1,0:T(8,128)(2,1)} %bitcast.108.refs_2_), custom_call_target="tpu_custom_call" | custom-call | tf_op jit(solution)/shard_map/pallas_call | solution.py:588
  1027.0 17.0 %shard_map.261 = f32[8192,1024]{1,0:T(8,128)} custom-call(s32[1]{0:T(128)} %bitcast.42.scalar_ref, f32[4,2048,1024]{2,1,0:T(8,128)} %bitcast.295, bf16[4096,1024]{1,0:T(8,128)(2,1)S(1)} %bitcast.285, bf16[4096,1024]{1,0:T(8,128)(2,1)} %bitcast.111.refs_2_), custom_call_target="tpu_custom_call" | custom-call | tf_op jit(solution)/shard_map/pallas_call | solution.py:588
  (600 shorter events, 297.3 us)
Async XLA Ops:
  7.2 277.4 %all-gather.3.cloned.1.call-start = ((), (), s32[]{:S(2)}) async-start(), calls=%async_computation.2 | async-start | bytes 7077888 | tf_op jit(solution)/shard_map/all_gather | solution.py:1182
  9.7 117.8 %collective-permute-start.13 = (bf16[256,1536]{1,0:T(8,128)(2,1)S(1)}, bf16[256,1536]{1,0:T(8,128)(2,1)}, u32[]{:S(2)}, u32[]{:S(2)}) collective-permute-start(bf16[256,1536]{1,0:T(8,128)(2,1)S(1)} %shard_map.239), channel_id=1, source_target_pairs={{0,1},{1,0},{2,3},{3,2},{4,5},{5,4},{6,7},{7,6},{8,9},{9,8},{10,11... | collective-permute-start | bytes 2359304 | tf_op jit(solution)/shard_map/ppermute | solution.py:408
  12.7 39.9 %collective-permute-start.9 = (bf16[256,1536]{1,0:T(8,128)(2,1)S(1)}, bf16[256,1536]{1,0:T(8,128)(2,1)}, u32[]{:S(2)}, u32[]{:S(2)}) collective-permute-start(bf16[256,1536]{1,0:T(8,128)(2,1)S(1)} %shard_map.239), channel_id=1, source_target_pairs={{0,2},{1,3},{2,4},{3,5},{4,6},{5,7},{6,0},{7,1},{8,10},{9,11},{10,... | collective-permute-start | bytes 2359304 | tf_op jit(solution)/shard_map/ppermute | solution.py:408
  14.3 36.4 %collective-permute-start.6 = (bf16[256,1536]{1,0:T(8,128)(2,1)S(1)}, bf16[256,1536]{1,0:T(8,128)(2,1)}, u32[]{:S(2)}, u32[]{:S(2)}) collective-permute-start(bf16[256,1536]{1,0:T(8,128)(2,1)S(1)} %shard_map.239), channel_id=1, source_target_pairs={{0,6},{1,7},{2,0},{3,1},{4,2},{5,3},{6,4},{7,5},{8,14},{9,15},{10,... | collective-permute-start | bytes 2359304 | tf_op jit(solution)/shard_map/ppermute | solution.py:408
  21.8 28.9 %collective-permute-start = (bf16[192,2048]{1,0:T(8,128)(2,1)S(1)}, bf16[192,2048]{1,0:T(8,128)(2,1)}, u32[]{:S(2)}, u32[]{:S(2)}) collective-permute-start(bf16[192,2048]{1,0:T(8,128)(2,1)S(1)} %copy-done.17), channel_id=1, source_target_pairs={{0,16},{1,17},{2,18},{3,19},{4,20},{5,21},{6,22},{7,23},{8,24},{9,... | collective-permute-start | bytes 2359304 | tf_op jit(solution)/shard_map/ppermute | solution.py:408
  50.7 44.8 %collective-permute-start.7 = (bf16[256,1536]{1,0:T(8,128)(2,1)S(1)}, bf16[256,1536]{1,0:T(8,128)(2,1)}, u32[]{:S(2)}, u32[]{:S(2)}) collective-permute-start(bf16[256,1536]{1,0:T(8,128)(2,1)S(1)} %shard_map.239), channel_id=1, source_target_pairs={{0,4},{1,5},{2,6},{3,7},{4,0},{5,1},{6,2},{7,3},{8,12},{9,13},{10,... | collective-permute-start | bytes 2359304 | tf_op jit(solution)/shard_map/ppermute | solution.py:408
  52.1 43.4 %collective-permute-start.8 = (bf16[256,1536]{1,0:T(8,128)(2,1)}, bf16[256,1536]{1,0:T(8,128)(2,1)}, u32[]{:S(2)}, u32[]{:S(2)}) collective-permute-start(bf16[256,1536]{1,0:T(8,128)(2,1)} %collective-permute-done.6), channel_id=1, source_target_pairs={{0,1},{1,0},{2,3},{3,2},{4,5},{5,4},{6,7},{7,6},{8,9},{9,8},{10,11... | collective-permute-start | bytes 2359304 | tf_op jit(solution)/shard_map/ppermute | solution.py:408
  52.6 42.9 %collective-permute-start.10 = (bf16[256,1536]{1,0:T(8,128)(2,1)}, bf16[256,1536]{1,0:T(8,128)(2,1)}, u32[]{:S(2)}, u32[]{:S(2)}) collective-permute-start(bf16[256,1536]{1,0:T(8,128)(2,1)} %collective-permute-done.9), channel_id=1, source_target_pairs={{0,1},{1,0},{2,3},{3,2},{4,5},{5,4},{6,7},{7,6},{8,9},{9,8},{10,11... | collective-permute-start | bytes 2359304 | tf_op jit(solution)/shard_map/ppermute | solution.py:408
  55.4 38.6 %collective-permute-start.5 = (bf16[2,168,256]{2,1,0:T(8,128)(2,1)S(1)}, bf16[2,168,256]{2,1,0:T(8,128)(2,1)S(1)}, u32[]{:S(2)}, u32[]{:S(2)}) collective-permute-start(bf16[2,168,256]{2,1,0:T(8,128)(2,1)S(1)} %get-tuple-element.266), channel_id=1, source_target_pairs={{0,4},{1,5},{2,6},{3,7},{4,0},{5,1},{6,2},{7,3},{8,12},{9,13},{10,... | collective-permute-start | bytes 516104 | tf_op jit(solution)/shard_map/ppermute | solution.py:408
  93.9 65.7 %collective-permute-start.12 = (bf16[192,2048]{1,0:T(8,128)(2,1)S(1)}, bf16[192,2048]{1,0:T(8,128)(2,1)}, u32[]{:S(2)}, u32[]{:S(2)}) collective-permute-start(bf16[192,2048]{1,0:T(8,128)(2,1)S(1)} %copy-done.31), channel_id=1, source_target_pairs={{0,16},{1,17},{2,18},{3,19},{4,20},{5,21},{6,22},{7,23},{8,24},{9,... | collective-permute-start | bytes 2359304 | tf_op jit(solution)/shard_map/ppermute | solution.py:408
  100.6 51.6 %collective-permute-start.1 = (bf16[2,192,2048]{2,1,0:T(8,128)(2,1)}, bf16[2,192,2048]{2,1,0:T(8,128)(2,1)}, u32[]{:S(2)}, u32[]{:S(2)}) collective-permute-start(bf16[2,192,2048]{2,1,0:T(8,128)(2,1)} %get-tuple-element.245), channel_id=1, source_target_pairs={{0,8},{1,9},{2,10},{3,11},{4,12},{5,13},{6,14},{7,15},{8,0},{9,1},... | collective-permute-start | bytes 4718600 | tf_op jit(solution)/shard_map/ppermute | solution.py:408
  102.5 68.5 %collective-permute-start.23 = (bf16[64,2048]{1,0:T(8,128)(2,1)S(1)}, bf16[64,2048]{1,0:T(8,128)(2,1)}, u32[]{:S(2)}, u32[]{:S(2)}) collective-permute-start(bf16[64,2048]{1,0:T(8,128)(2,1)S(1)} %copy-done.50), channel_id=1, source_target_pairs={{0,2},{1,3},{2,4},{3,5},{4,6},{5,7},{6,0},{7,1},{8,10},{9,11},{10,... | collective-permute-start | bytes 786440 | tf_op jit(solution)/shard_map/ppermute | solution.py:408
  106.4 83.7 %collective-permute-start.18 = (bf16[64,2048]{1,0:T(8,128)(2,1)S(1)}, bf16[64,2048]{1,0:T(8,128)(2,1)}, u32[]{:S(2)}, u32[]{:S(2)}) collective-permute-start(bf16[64,2048]{1,0:T(8,128)(2,1)S(1)} %copy-done.50), channel_id=1, source_target_pairs={{0,1},{1,0},{2,3},{3,2},{4,5},{5,4},{6,7},{7,6},{8,9},{9,8},{10,11... | collective-permute-start | bytes 786440 | tf_op jit(solution)/shard_map/ppermute | solution.py:408
  145.5 25.5 %collective-permute-start.21 = (bf16[64,2048]{1,0:T(8,128)(2,1)S(1)}, bf16[64,2048]{1,0:T(8,128)(2,1)}, u32[]{:S(2)}, u32[]{:S(2)}) collective-permute-start(bf16[64,2048]{1,0:T(8,128)(2,1)S(1)} %copy-done.50), channel_id=1, source_target_pairs={{0,4},{1,5},{2,6},{3,7},{4,0},{5,1},{6,2},{7,3},{8,12},{9,13},{10,... | collective-permute-start | bytes 786440 | tf_op jit(solution)/shard_map/ppermute | solution.py:408
  151.9 345.0 %all-gather.5.cloned.1.call-start = ((), (), s32[]{:S(2)}) async-start(), calls=%async_computation.3 | async-start | bytes 7077888 | tf_op jit(solution)/shard_map/all_gather | solution.py:1266
  234.2 30.7 %collective-permute-start.29 = (bf16[192,2048]{1,0:T(8,128)(2,1)S(1)}, bf16[192,2048]{1,0:T(8,128)(2,1)}, u32[]{:S(2)}, u32[]{:S(2)}) collective-permute-start(bf16[192,2048]{1,0:T(8,128)(2,1)S(1)} %get-tuple-element.105), channel_id=1, source_target_pairs={{0,6},{1,7},{2,0},{3,1},{4,2},{5,3},{6,4},{7,5},{8,14},{9,15},{10,... | collective-permute-start | bytes 2359304 | tf_op jit(solution)/shard_map/ppermute | solution.py:408
  234.3 49.8 %collective-permute-start.33 = (bf16[192,2048]{1,0:T(8,128)(2,1)S(1)}, bf16[192,2048]{1,0:T(8,128)(2,1)S(1)}, u32[]{:S(2)}, u32[]{:S(2)}) collective-permute-start(bf16[192,2048]{1,0:T(8,128)(2,1)S(1)} %get-tuple-element.105), channel_id=1, source_target_pairs={{0,2},{1,3},{2,4},{3,5},{4,6},{5,7},{6,0},{7,1},{8,10},{9,11},{10,... | collective-permute-start | bytes 2359304 | tf_op jit(solution)/shard_map/ppermute | solution.py:408
  238.5 79.3 %collective-permute-start.27 = (bf16[192,2048]{1,0:T(8,128)(2,1)S(1)}, bf16[192,2048]{1,0:T(8,128)(2,1)}, u32[]{:S(2)}, u32[]{:S(2)}) collective-permute-start(bf16[192,2048]{1,0:T(8,128)(2,1)S(1)} %get-tuple-element.105), channel_id=1, source_target_pairs={{0,1},{1,0},{2,3},{3,2},{4,5},{5,4},{6,7},{7,6},{8,9},{9,8},{10,11... | collective-permute-start | bytes 2359304 | tf_op jit(solution)/shard_map/ppermute | solution.py:408
  264.9 52.3 %collective-permute-start.32 = (bf16[192,2048]{1,0:T(8,128)(2,1)S(1)}, bf16[192,2048]{1,0:T(8,128)(2,1)S(1)}, u32[]{:S(2)}, u32[]{:S(2)}) collective-permute-start(bf16[192,2048]{1,0:T(8,128)(2,1)S(1)} %get-tuple-element.105), channel_id=1, source_target_pairs={{0,4},{1,5},{2,6},{3,7},{4,0},{5,1},{6,2},{7,3},{8,12},{9,13},{10,... | collective-permute-start | bytes 2359304 | tf_op jit(solution)/shard_map/ppermute | solution.py:408
  267.9 54.2 %collective-permute-start.30 = (bf16[192,2048]{1,0:T(8,128)(2,1)}, bf16[192,2048]{1,0:T(8,128)(2,1)}, u32[]{:S(2)}, u32[]{:S(2)}) collective-permute-start(bf16[192,2048]{1,0:T(8,128)(2,1)} %collective-permute-done.29), channel_id=1, source_target_pairs={{0,1},{1,0},{2,3},{3,2},{4,5},{5,4},{6,7},{7,6},{8,9},{9,8},{10,11... | collective-permute-start | bytes 2359304 | tf_op jit(solution)/shard_map/ppermute | solution.py:408
  284.1 54.6 %collective-permute-start.35 = (bf16[192,2048]{1,0:T(8,128)(2,1)S(1)}, bf16[192,2048]{1,0:T(8,128)(2,1)S(1)}, u32[]{:S(2)}, u32[]{:S(2)}) collective-permute-start(bf16[192,2048]{1,0:T(8,128)(2,1)S(1)} %collective-permute-done.33.refs_0_), channel_id=1, source_target_pairs={{0,1},{1,0},{2,3},{3,2},{4,5},{5,4},{6,7},{7,6},{8,9},{9,8},{10,11... | collective-permute-start | bytes 2359304 | tf_op jit(solution)/shard_map/ppermute | solution.py:408
  284.7 55.1 %collective-permute-start.36 = (bf16[1536,2048]{1,0:T(8,128)(2,1)}, bf16[1536,2048]{1,0:T(8,128)(2,1)}, u32[]{:S(2)}, u32[]{:S(2)}) collective-permute-start(bf16[1536,2048]{1,0:T(8,128)(2,1)} %all-gather.3.cloned.1.call-done.refs_2_), channel_id=1, source_target_pairs={{0,8},{1,9},{2,10},{3,11},{4,12},{5,13},{6,14},{7,15},{8,0},{9,1},... | collective-permute-start | bytes 18874376 | tf_op jit(solution)/shard_map/ppermute | solution.py:408
  358.8 40.4 %collective-permute-start.37 = (bf16[1536,2048]{1,0:T(8,128)(2,1)}, bf16[1536,2048]{1,0:T(8,128)(2,1)}, u32[]{:S(2)}, u32[]{:S(2)}) collective-permute-start(bf16[1536,2048]{1,0:T(8,128)(2,1)} %constant_dynamic-update-slice_fusion.18.refs_1_), channel_id=1, source_target_pairs={{0,8},{1,9},{2,10},{3,11},{4,12},{5,13},{6,14},{7,15},{8,0},{9,1},... | collective-permute-start | bytes 18874376 | tf_op jit(solution)/shard_map/ppermute | solution.py:408
  358.9 431.2 %reduce-scatter.3.cloned.1.call-start = ((), (), s32[]{:S(2)}) async-start(), calls=%async_computation.4 | async-start | bytes 7077888 | tf_op jit(solution)/shard_map/reduce_scatter | solution.py:1308
  361.9 65.6 %collective-permute-start.28 = (bf16[384,2048]{1,0:T(8,128)(2,1)}, bf16[384,2048]{1,0:T(8,128)(2,1)}, u32[]{:S(2)}, u32[]{:S(2)}) collective-permute-start(bf16[384,2048]{1,0:T(8,128)(2,1)} %pad_maximum_fusion.16), channel_id=1, source_target_pairs={{0,16},{1,17},{2,18},{3,19},{4,20},{5,21},{6,22},{7,23},{8,24},{9,... | collective-permute-start | bytes 4718600 | tf_op jit(solution)/shard_map/ppermute | solution.py:408
  366.1 66.6 %collective-permute-start.31 = (bf16[384,2048]{1,0:T(8,128)(2,1)}, bf16[384,2048]{1,0:T(8,128)(2,1)}, u32[]{:S(2)}, u32[]{:S(2)}) collective-permute-start(bf16[384,2048]{1,0:T(8,128)(2,1)} %pad_maximum_fusion.17), channel_id=1, source_target_pairs={{0,16},{1,17},{2,18},{3,19},{4,20},{5,21},{6,22},{7,23},{8,24},{9,... | collective-permute-start | bytes 4718600 | tf_op jit(solution)/shard_map/ppermute | solution.py:408
  457.3 29.8 %collective-permute-start.38 = (bf16[8,192,2176]{2,1,0:T(8,128)(2,1)}, bf16[8,192,2176]{2,1,0:T(8,128)(2,1)S(1)}, u32[]{:S(2)}, u32[]{:S(2)}) collective-permute-start(bf16[8,192,2176]{2,1,0:T(8,128)(2,1)} %bitcast.299), channel_id=1, source_target_pairs={{0,8},{1,9},{2,10},{3,11},{4,12},{5,13},{6,14},{7,15},{8,0},{9,1},... | collective-permute-start | bytes 20054024 | tf_op jit(solution)/shard_map/ppermute | solution.py:408
  459.9 37.0 %collective-permute-start.40 = (bf16[384,2048]{1,0:T(8,128)(2,1)}, bf16[384,2048]{1,0:T(8,128)(2,1)}, u32[]{:S(2)}, u32[]{:S(2)}) collective-permute-start(bf16[384,2048]{1,0:T(8,128)(2,1)} %pad_maximum_fusion.18), channel_id=1, source_target_pairs={{0,16},{1,17},{2,18},{3,19},{4,20},{5,21},{6,22},{7,23},{8,24},{9,... | collective-permute-start | bytes 4718600 | tf_op jit(solution)/shard_map/ppermute | solution.py:408
  513.8 28.0 %collective-permute-start.41 = (bf16[1536,2048]{1,0:T(8,128)(2,1)}, bf16[1536,2048]{1,0:T(8,128)(2,1)}, u32[]{:S(2)}, u32[]{:S(2)}) collective-permute-start(bf16[1536,2048]{1,0:T(8,128)(2,1)} %shard_map.248), channel_id=1, source_target_pairs={{0,8},{1,9},{2,10},{3,11},{4,12},{5,13},{6,14},{7,15},{8,0},{9,1},... | collective-permute-start | bytes 18874376 | tf_op jit(solution)/shard_map/ppermute | solution.py:408
  520.4 93.7 %collective-permute-start.55 = (bf16[384,2048]{1,0:T(8,128)(2,1)}, bf16[384,2048]{1,0:T(8,128)(2,1)}, u32[]{:S(2)}, u32[]{:S(2)}) collective-permute-start(bf16[384,2048]{1,0:T(8,128)(2,1)} %pad_maximum_fusion.20), channel_id=1, source_target_pairs={{0,16},{1,17},{2,18},{3,19},{4,20},{5,21},{6,22},{7,23},{8,24},{9,... | collective-permute-start | bytes 4718600 | tf_op jit(solution)/shard_map/ppermute | solution.py:408
  539.0 70.1 %collective-permute-start.46 = (bf16[192,2176]{1,0:T(8,128)(2,1)}, bf16[192,2176]{1,0:T(8,128)(2,1)}, u32[]{:S(2)}, u32[]{:S(2)}) collective-permute-start(bf16[192,2176]{1,0:T(8,128)(2,1)} %get-tuple-element.227.refs_0_), channel_id=1, source_target_pairs={{0,4},{1,5},{2,6},{3,7},{4,0},{5,1},{6,2},{7,3},{8,12},{9,13},{10,... | collective-permute-start | bytes 2506760 | tf_op jit(solution)/shard_map/ppermute | solution.py:408
  564.0 45.1 %collective-permute-start.47 = (bf16[192,2176]{1,0:T(8,128)(2,1)}, bf16[192,2176]{1,0:T(8,128)(2,1)}, u32[]{:S(2)}, u32[]{:S(2)}) collective-permute-start(bf16[192,2176]{1,0:T(8,128)(2,1)} %get-tuple-element.224.refs_0_), channel_id=1, source_target_pairs={{0,2},{1,3},{2,4},{3,5},{4,6},{5,7},{6,0},{7,1},{8,10},{9,11},{10,... | collective-permute-start | bytes 2506760 | tf_op jit(solution)/shard_map/ppermute | solution.py:408
  586.1 25.3 %collective-permute-start.48 = (bf16[192,2176]{1,0:T(8,128)(2,1)S(1)}, bf16[192,2176]{1,0:T(8,128)(2,1)S(1)}, u32[]{:S(2)}, u32[]{:S(2)}) collective-permute-start(bf16[192,2176]{1,0:T(8,128)(2,1)S(1)} %get-tuple-element.223.refs_0_), channel_id=1, source_target_pairs={{0,6},{1,7},{2,0},{3,1},{4,2},{5,3},{6,4},{7,5},{8,14},{9,15},{10,... | collective-permute-start | bytes 2506760 | tf_op jit(solution)/shard_map/ppermute | solution.py:408
  614.2 280.1 %reduce-scatter.5.cloned.1.call-start = ((), (), s32[]{:S(2)}) async-start(), calls=%async_computation.5 | async-start | bytes 2359296 | tf_op jit(solution)/shard_map/reduce_scatter | solution.py:1406
  644.8 145.4 %collective-permute-start.57 = (bf16[1536,2048]{1,0:T(8,128)(2,1)}, bf16[1536,2048]{1,0:T(8,128)(2,1)}, u32[]{:S(2)}, u32[]{:S(2)}) collective-permute-start(bf16[1536,2048]{1,0:T(8,128)(2,1)} %constant_dynamic-update-slice_fusion.26.refs_2_), channel_id=1, source_target_pairs={{0,8},{1,9},{2,10},{3,11},{4,12},{5,13},{6,14},{7,15},{8,0},{9,1},... | collective-permute-start | bytes 18874376 | tf_op jit(solution)/shard_map/ppermute | solution.py:408
  702.4 72.7 %collective-permute-start.56 = (bf16[2,192,2048]{2,1,0:T(8,128)(2,1)}, bf16[2,192,2048]{2,1,0:T(8,128)(2,1)}, u32[]{:S(2)}, u32[]{:S(2)}) collective-permute-start(bf16[2,192,2048]{2,1,0:T(8,128)(2,1)} %slice_bitcast_fusion), channel_id=1, source_target_pairs={{0,8},{1,9},{2,10},{3,11},{4,12},{5,13},{6,14},{7,15},{8,0},{9,1},... | collective-permute-start | bytes 4718600 | tf_op jit(solution)/shard_map/ppermute | solution.py:408
  706.4 74.1 %collective-permute-start.64 = (bf16[8,64,2048]{2,1,0:T(8,128)(2,1)}, bf16[8,64,2048]{2,1,0:T(8,128)(2,1)}, u32[]{:S(2)}, u32[]{:S(2)}) collective-permute-start(bf16[8,64,2048]{2,1,0:T(8,128)(2,1)} %dynamic-slice_bitcast_fusion), channel_id=1, source_target_pairs={{0,8},{1,9},{2,10},{3,11},{4,12},{5,13},{6,14},{7,15},{8,0},{9,1},... | collective-permute-start | bytes 6291464 | tf_op jit(solution)/shard_map/ppermute | solution.py:408
  709.5 43.7 %collective-permute-start.60 = (bf16[256,1664]{1,0:T(8,128)(2,1)}, bf16[256,1664]{1,0:T(8,128)(2,1)}, u32[]{:S(2)}, u32[]{:S(2)}) collective-permute-start(bf16[256,1664]{1,0:T(8,128)(2,1)} %pad_maximum_fusion.27), channel_id=1, source_target_pairs={{0,1},{1,0},{2,3},{3,2},{4,5},{5,4},{6,7},{7,6},{8,9},{9,8},{10,11... | collective-permute-start | bytes 2555912 | tf_op jit(solution)/shard_map/ppermute | solution.py:408
  712.1 38.4 %collective-permute-start.58 = (bf16[256,1664]{1,0:T(8,128)(2,1)}, bf16[256,1664]{1,0:T(8,128)(2,1)}, u32[]{:S(2)}, u32[]{:S(2)}) collective-permute-start(bf16[256,1664]{1,0:T(8,128)(2,1)} %pad_maximum_fusion.26.refs_0_), channel_id=1, source_target_pairs={{0,1},{1,0},{2,3},{3,2},{4,5},{5,4},{6,7},{7,6},{8,9},{9,8},{10,11... | collective-permute-start | bytes 2555912 | tf_op jit(solution)/shard_map/ppermute | solution.py:408
  753.2 65.5 %collective-permute-start.53 = (bf16[256,1664]{1,0:T(8,128)(2,1)}, bf16[256,1664]{1,0:T(8,128)(2,1)}, u32[]{:S(2)}, u32[]{:S(2)}) collective-permute-start(bf16[256,1664]{1,0:T(8,128)(2,1)} %pad_maximum_fusion.24), channel_id=1, source_target_pairs={{0,1},{1,0},{2,3},{3,2},{4,5},{5,4},{6,7},{7,6},{8,9},{9,8},{10,11... | collective-permute-start | bytes 2555912 | tf_op jit(solution)/shard_map/ppermute | solution.py:408
  772.4 47.6 %collective-permute-start.61 = (bf16[256,1664]{1,0:T(8,128)(2,1)}, bf16[256,1664]{1,0:T(8,128)(2,1)}, u32[]{:S(2)}, u32[]{:S(2)}) collective-permute-start(bf16[256,1664]{1,0:T(8,128)(2,1)} %add_convert_fusion.1), channel_id=1, source_target_pairs={{0,2},{1,3},{2,4},{3,5},{4,6},{5,7},{6,0},{7,1},{8,10},{9,11},{10,... | collective-permute-start | bytes 2555912 | tf_op jit(solution)/shard_map/ppermute | solution.py:408
  775.1 71.4 %collective-permute-start.59 = (bf16[256,1664]{1,0:T(8,128)(2,1)}, bf16[256,1664]{1,0:T(8,128)(2,1)}, u32[]{:S(2)}, u32[]{:S(2)}) collective-permute-start(bf16[256,1664]{1,0:T(8,128)(2,1)} %add_convert_fusion.2), channel_id=1, source_target_pairs={{0,4},{1,5},{2,6},{3,7},{4,0},{5,1},{6,2},{7,3},{8,12},{9,13},{10,... | collective-permute-start | bytes 2555912 | tf_op jit(solution)/shard_map/ppermute | solution.py:408
  781.0 65.5 %collective-permute-start.62 = (bf16[192,2048]{1,0:T(8,128)(2,1)}, bf16[192,2048]{1,0:T(8,128)(2,1)}, u32[]{:S(2)}, u32[]{:S(2)}) collective-permute-start(bf16[192,2048]{1,0:T(8,128)(2,1)} %slice_bitcast_fusion.11), channel_id=1, source_target_pairs={{0,16},{1,17},{2,18},{3,19},{4,20},{5,21},{6,22},{7,23},{8,24},{9,... | collective-permute-start | bytes 2359304 | tf_op jit(solution)/shard_map/ppermute | solution.py:408
  869.6 58.1 %collective-permute-start.67 = (bf16[2,1024,2048]{2,1,0:T(8,128)(2,1)}, bf16[2,1024,2048]{2,1,0:T(8,128)(2,1)}, u32[]{:S(2)}, u32[]{:S(2)}) collective-permute-start(bf16[2,1024,2048]{2,1,0:T(8,128)(2,1)} %fusion.38), channel_id=1, source_target_pairs={{0,8},{1,9},{2,10},{3,11},{4,12},{5,13},{6,14},{7,15},{8,0},{9,1},... | collective-permute-start | bytes 25165832 | tf_op jit(solution)/shard_map/ppermute | solution.py:408
  892.8 24.7 %collective-permute-start.65 = (bf16[256,1664]{1,0:T(8,128)(2,1)S(1)}, bf16[256,1664]{1,0:T(8,128)(2,1)S(1)}, u32[]{:S(2)}, u32[]{:S(2)}) collective-permute-start(bf16[256,1664]{1,0:T(8,128)(2,1)S(1)} %add_convert_fusion), channel_id=1, source_target_pairs={{0,16},{1,17},{2,18},{3,19},{4,20},{5,21},{6,22},{7,23},{8,24},{9,... | collective-permute-start | bytes 2555912 | tf_op jit(solution)/shard_map/ppermute | solution.py:408
  918.9 32.4 %collective-permute-start.68 = (bf16[2,256,1664]{2,1,0:T(8,128)(2,1)S(1)}, bf16[2,256,1664]{2,1,0:T(8,128)(2,1)S(1)}, u32[]{:S(2)}, u32[]{:S(2)}) collective-permute-start(bf16[2,256,1664]{2,1,0:T(8,128)(2,1)S(1)} %get-tuple-element.239), channel_id=1, source_target_pairs={{0,8},{1,9},{2,10},{3,11},{4,12},{5,13},{6,14},{7,15},{8,0},{9,1},... | collective-permute-start | bytes 5111816 | tf_op jit(solution)/shard_map/ppermute | solution.py:408
  919.5 83.8 %collective-permute-start.70 = (bf16[2,2048,1024]{2,1,0:T(8,128)(2,1)}, bf16[2,2048,1024]{2,1,0:T(8,128)(2,1)}, u32[]{:S(2)}, u32[]{:S(2)}) collective-permute-start(bf16[2,2048,1024]{2,1,0:T(8,128)(2,1)} %fusion.46.refs_0_), channel_id=1, source_target_pairs={{0,8},{1,9},{2,10},{3,11},{4,12},{5,13},{6,14},{7,15},{8,0},{9,1},... | collective-permute-start | bytes 25165832 | tf_op jit(solution)/shard_map/ppermute | solution.py:408
  975.6 51.4 %collective-permute-start.71 = (bf16[2,2048,1024]{2,1,0:T(8,128)(2,1)}, bf16[2,2048,1024]{2,1,0:T(8,128)(2,1)}, u32[]{:S(2)}, u32[]{:S(2)}) collective-permute-start(bf16[2,2048,1024]{2,1,0:T(8,128)(2,1)} %fusion.43.refs_0_), channel_id=1, source_target_pairs={{0,8},{1,9},{2,10},{3,11},{4,12},{5,13},{6,14},{7,15},{8,0},{9,1},... | collective-permute-start | bytes 25165832 | tf_op jit(solution)/shard_map/ppermute | solution.py:408
  (131 other events, 2133.6 us)
Sparse Core Ops, SparseCore 0:
  152.0 106.2 all-gather.2
  359.0 97.9 all-gather.4
  614.3 118.4 reduce-scatter.2
  790.3 81.0 reduce-scatter.4

commit v4 on v3

--- a/solution.py
+++ b/solution.py
@@ -419,12 +419,12 @@
     return both.reshape((SHARDS,) + values.shape)
 
 
-def gather_rows(values, early=None, late=(), fill=None, first=()):
+def gather_rows(values, early=(), late=(), fill=None, first=()):
     moved = {k: move(values, Z_FROM[k]) for k in (1, 3)}
     moved[2] = move(after(values, moved[1], *first), Z_FROM[2])
     mine, beside = {0: values}, {0: move(values, Y_SWAP)}
     for k in (1, 3, 2):
-        mine[k] = moved[k] if early is None else after(moved[k], early)
+        mine[k] = after(moved[k], *early) if early else moved[k]
         if k == 2 and fill is not None:
             mine[k] = after(mine[k], *fill(mine[3]))
         beside[k] = move(mine[k], Y_SWAP)
@@ -444,14 +444,17 @@
     return total.astype(first.dtype)
 
 
-def scatter_rows(parts, fills):
+def scatter_rows(parts, fills, hold=False):
     away = {k: added(*[part(2 * k + 1) for part in parts]) for k in (2, 1, 3, 0)}
-    moved = {k: move(away[k], Y_SWAP) for k in (2, 1, 3, 0)}
+    moved = {2: move(away[2], Y_SWAP)}
     arrived, reduced = [], away[2]
     for k, fill in zip((2, 1, 3, 0), fills):
-        here = moved[k]
-        if fill is not None:
-            here = after(here, *fill((reduced,)))
+        filled = [] if fill is None else fill((reduced,))
+        if k == 2:
+            for other in (1, 3, 0):
+                held = after(away[other], *filled) if hold else away[other]
+                moved[other] = move(held, Y_SWAP)
+        here = after(moved[k], *filled) if filled else moved[k]
         reduced = added(here, *[part(2 * k) for part in parts])
         if k > 0:
             arrived.append(move(reduced, Z_TO[k]))
@@ -1129,7 +1132,87 @@
     ranks = small_in[:, 4 + expert_count :, :tokens]
     ranks = jnp.take(ranks, near_shards ^ shard, axis=0)
     ranks = ranks.reshape(SHARDS, REPS, expert_count + 1, tokens)[:, :, :expert_count]
-    ranks = ranks.astype(jnp.int32)
+    in_part = flat(in_pieces)
+
+    small_in = jnp.take(small_in[:, : 4 + expert_count], shard_ids ^ shard, axis=0)
+    small_in = small_in.transpose(1, 0, 2).reshape(4 + expert_count, width)
+    gains = small_in[:4].astype(f32)
+    router_rows = small_in[4:]
+    part_gains = lax.dynamic_slice(
+        gains[1:3].reshape(2, HEADS // 2, 2, HEAD_DIM),
+        (0, c * heads, a, 0),
+        (2, heads, 1, HEAD_DIM),
+    ).reshape(2, part_width)
+
+    hidden = inputs.astype(f32)
+    home_rate = lax.rsqrt(jnp.mean(hidden * hidden, axis=-1, keepdims=True) + norm_eps)
+    inputs_all = jnp.stack([inputs, inputs_across])
+    inputs_all = jnp.stack([inputs_all, move(inputs_all, CORE_SWAP)], axis=1)
+    inputs_all = inputs_all.reshape(REPS * tokens, width)
+    inputs_all = pick_columns(inputs_all, near_shards, rows_each).astype(f32)
+    unit_all = inputs_all * lax.rsqrt(
+        jnp.mean(inputs_all * inputs_all, axis=-1, keepdims=True) + norm_eps
+    )
+    near_gain = jnp.take(gains[0].reshape(SHARDS, rows_each), near_shards, axis=0).reshape(width)
+    normed_low = (unit_all * near_gain).astype(bf16)
+    cot_across = move(grad_out, X_SWAP)
+    normed_low = after(normed_low, cot_across)
+    cot_own = after(grad_out, in_part)
+    cot_own = lax.all_gather(cot_own, "shard", tiled=True)
+    cos_table, sin_table = jax.vmap(rotary_tables)(segment_rows)
+    sin_table = jnp.where(jnp.arange(HEAD_DIM) < HEAD_DIM // 2, -sin_table, sin_table)
+    cos_table = cos_table.reshape(REPS * tokens, HEAD_DIM)
+    sin_table = sin_table.reshape(REPS * tokens, HEAD_DIM)
+
+    out_rows = rows_each // 4
+    out_own = lax.dynamic_slice_in_dim(out_proj, rep * out_rows, out_rows, 0)
+    out_own = after(out_own, in_pieces[2][0])
+
+    projected = jnp.dot(normed_low, in_part, preferred_element_type=f32)
+    squares = jnp.stack(
+        [
+            jnp.sum(projected[:, k * part_width : (k + 1) * part_width] ** 2, axis=1)
+            for k in range(2)
+        ],
+        axis=1,
+    )
+    squares = rep_sum(squares.reshape(REPS, tokens, 2)).reshape(REPS * tokens, 2)
+    pair_rate = lax.rsqrt(squares / width + norm_eps)
+    attention_operands = (
+        projected,
+        pair_rate,
+        part_gains,
+        cos_table,
+        sin_table,
+        segment_rows.reshape(REPS * tokens, 1),
+        segment_rows[:, None, :],
+    )
+    attended = attend(*attention_operands).reshape(2, 2, tokens, part_width)
+    out_pieces = gather_rows(out_own, early=(projected,), late=(attended,))
+    out_own = flat(out_pieces).reshape(SHARDS, out_rows, width)
+    out_other = move(out_own, CORE_SWAP)
+    out_part = jnp.where(
+        c == 0,
+        jnp.concatenate([out_own, out_other], axis=1),
+        jnp.concatenate([out_other, out_own], axis=1),
+    ).reshape(SHARDS * 2 * out_rows, width)
+    attended = jnp.concatenate([attended[:, 0], move(attended[:, 1], CORE_SWAP)], axis=2)
+    attended = attended.reshape(2 * tokens, 2 * part_width)
+    head_of_place = ((near_shards // heads) ^ c) * heads + lax.rem(near_shards, heads)
+    place_of_head = jnp.sum(
+        jnp.where(head_of_place[None, :] == shard_ids[:, None], shard_ids[None, :], 0), axis=1
+    )
+    attended = pick_columns(attended, head_of_place, HEAD_DIM)
+    mixed = jnp.dot(attended, out_part, preferred_element_type=f32).reshape(2, tokens, width)
+    mixed_across = move(mixed[1].astype(bf16), X_SWAP)
+    residual = hidden + mixed[0] + mixed_across.astype(f32)
+
+    ffn_rate = lax.rsqrt(jnp.mean(residual * residual, axis=-1, keepdims=True) + norm_eps)
+    ffn_unit = residual * ffn_rate
+    ffn_low = (ffn_unit * gains[3]).astype(bf16)
+    router_probs = softmax_rows(contract_cols(ffn_low, router_rows))
+
+    ranks = after(ranks, mixed_across).astype(jnp.int32)
     counts = jnp.sum((ranks >= 0).astype(jnp.int32), axis=3)
     before = (near_shards[None, :] < near_shards[:, None])[:, :, None, None]
     bases = jnp.sum(jnp.where(before, counts[None], 0), axis=1)
@@ -1148,90 +1231,6 @@
 
     columns, shard_columns = columns_of(slots[:2]), columns_of(shard_slots[:2])
 
-    in_part = flat(
-        [
-            (mine, after(beside, slots, shard_slots, columns, shard_columns))
-            for mine, beside in in_pieces
-        ]
-    )
-
-    small_in = jnp.take(small_in[:, : 4 + expert_count], shard_ids ^ shard, axis=0)
-    small_in = small_in.transpose(1, 0, 2).reshape(4 + expert_count, width)
-    gains = small_in[:4].astype(f32)
-    router_rows = small_in[4:]
-    part_gains = lax.dynamic_slice(
-        gains[1:3].reshape(2, HEADS // 2, 2, HEAD_DIM),
-        (0, c * heads, a, 0),
-        (2, heads, 1, HEAD_DIM),
-    ).reshape(2, part_width)
-
-    hidden = inputs.astype(f32)
-    home_rate = lax.rsqrt(jnp.mean(hidden * hidden, axis=-1, keepdims=True) + norm_eps)
-    inputs_all = jnp.stack([inputs, inputs_across])
-    inputs_all = jnp.stack([inputs_all, move(inputs_all, CORE_SWAP)], axis=1)
-    inputs_all = inputs_all.reshape(REPS * tokens, width)
-    inputs_all = pick_columns(inputs_all, near_shards, rows_each).astype(f32)
-    unit_all = inputs_all * lax.rsqrt(
-        jnp.mean(inputs_all * inputs_all, axis=-1, keepdims=True) + norm_eps
-    )
-    near_gain = jnp.take(gains[0].reshape(SHARDS, rows_each), near_shards, axis=0).reshape(width)
-    normed_low = (unit_all * near_gain).astype(bf16)
-    cot_across = move(grad_out, X_SWAP)
-    normed_low = after(normed_low, cot_across)
-    cot_own = after(grad_out, in_part)
-    cot_own = lax.all_gather(cot_own, "shard", tiled=True)
-    cos_table, sin_table = jax.vmap(rotary_tables)(segment_rows)
-    sin_table = jnp.where(jnp.arange(HEAD_DIM) < HEAD_DIM // 2, -sin_table, sin_table)
-    cos_table = cos_table.reshape(REPS * tokens, HEAD_DIM)
-    sin_table = sin_table.reshape(REPS * tokens, HEAD_DIM)
-
-    out_rows = rows_each // 4
-    out_own = lax.dynamic_slice_in_dim(out_proj, rep * out_rows, out_rows, 0)
-    out_own = after(out_own, in_pieces[2][0])
-
-    projected = jnp.dot(normed_low, in_part, preferred_element_type=f32)
-    squares = jnp.stack(
-        [
-            jnp.sum(projected[:, k * part_width : (k + 1) * part_width] ** 2, axis=1)
-            for k in range(2)
-        ],
-        axis=1,
-    )
-    squares = rep_sum(squares.reshape(REPS, tokens, 2)).reshape(REPS * tokens, 2)
-    pair_rate = lax.rsqrt(squares / width + norm_eps)
-    attention_operands = (
-        projected,
-        pair_rate,
-        part_gains,
-        cos_table,
-        sin_table,
-        segment_rows.reshape(REPS * tokens, 1),
-        segment_rows[:, None, :],
-    )
-    attended = attend(*attention_operands).reshape(2, 2, tokens, part_width)
-    out_pieces = gather_rows(out_own, early=projected, late=(attended,))
-    out_own = flat(out_pieces).reshape(SHARDS, out_rows, width)
-    out_other = move(out_own, CORE_SWAP)
-    out_part = jnp.where(
-        c == 0,
-        jnp.concatenate([out_own, out_other], axis=1),
-        jnp.concatenate([out_other, out_own], axis=1),
-    ).reshape(SHARDS * 2 * out_rows, width)
-    attended = jnp.concatenate([attended[:, 0], move(attended[:, 1], CORE_SWAP)], axis=2)
-    attended = attended.reshape(2 * tokens, 2 * part_width)
-    head_of_place = ((near_shards // heads) ^ c) * heads + lax.rem(near_shards, heads)
-    place_of_head = jnp.sum(
-        jnp.where(head_of_place[None, :] == shard_ids[:, None], shard_ids[None, :], 0), axis=1
-    )
-    attended = pick_columns(attended, head_of_place, HEAD_DIM)
-    mixed = jnp.dot(attended, out_part, preferred_element_type=f32).reshape(2, tokens, width)
-    residual = hidden + mixed[0] + move(mixed[1].astype(bf16), X_SWAP).astype(f32)
-
-    ffn_rate = lax.rsqrt(jnp.mean(residual * residual, axis=-1, keepdims=True) + norm_eps)
-    ffn_unit = residual * ffn_rate
-    ffn_low = (ffn_unit * gains[3]).astype(bf16)
-    router_probs = softmax_rows(contract_cols(ffn_low, router_rows))
-
     def cot_part(group, rows, behind=()):
         return cotangent_part(core_ref, shard_slots[group], rows, down_weight, capacity, behind)
 
@@ -1258,7 +1257,9 @@
         made["cot"] = [own_part, cot_part(1, beside, (own_part[1],))]
         return [own_part[1]]
 
-    ffn_pieces = gather_rows(ffn_low, fill=fill_cot)
+    ffn_pieces = gather_rows(
+        ffn_low, early=(slots, shard_slots, columns, shard_columns), fill=fill_cot
+    )
     near_cot = made["cot"]
     ffn_own = after(flat(ffn_pieces), near_cot[1][1])
     ffn_beside = move(ffn_own, CORE_SWAP)
@@ -1367,7 +1368,9 @@
     far_cot = [made["far_cot"], made["other_cot"]]
 
     def fill_far(follow):
-        made["far"] = ffn_part(2, ffn_far[0], far_cot[0][1], follow, LOUD)
+        made["far"] = ffn_part(
+            2, ffn_far[0], far_cot[0][1], follow + (ffn_far[1],), LOUD
+        )
         return [made["far"][3]]
 
     normed_other = grad_normed.astype(bf16).reshape(2, 2, tokens, width)
@@ -1376,7 +1379,7 @@
 
     def fill_other(follow):
         made["other"] = ffn_part(
-            3, ffn_far[1], far_cot[1][1], follow + (made["far"][3], normed_mine, routed), LOUD
+            3, ffn_far[1], far_cot[1][1], follow + (made["far"][3], normed_mine, routed, out_sum), LOUD
         )
         return [made["other"][3]]
 
@@ -1390,41 +1393,49 @@
     def groups(index):
         return [part[index] for part in (near[0], near[1], made["far"], made["other"])]
 
-    def fill_down(follow):
+    def fence(follow):
+        return [made["other"][3]]
+
+    out_home = lax.psum_scatter(
+        after(out_sum, routed), "shard", scatter_dimension=0, tiled=True
+    )
+
+    def fill_weights(follow):
         cots = [part[0] for part in near_cot + far_cot]
-        reduced, low, high, third = follow
-        made["down"], (reduced, low, high, _) = weight_grad(
-            groups(1), cots, (reduced, low, high, normed_across)
+        reduced, first, second, third = follow
+        down, _ = weight_grad(groups(1), cots, ())
+        gate, (down, first, reduced, _) = weight_grad(
+            groups(0), groups(2), (down, first, reduced, normed_across)
         )
-        return after(reduced, made["down"]), low, high, third
+        up, (gate, second, third, home) = weight_grad(
+            groups(0), groups(3), (gate, second, third, out_home)
+        )
+        made["down"], made["gate"], made["up"], made["home"] = down, gate, up, home
+        return reduced, first, second, third
 
     in_sum = scatter_rows(
         [lambda place: jnp.concatenate([grad_in_part[place], small[place]], axis=1)],
-        [fill_far, None, None, fill_other, fill_down],
+        [fill_far, fill_other, fence, fence, fill_weights],
+        hold=True,
     )
     in_other = move(in_sum, X_SWAP)
-    out_sum = lax.psum_scatter(
-        after(out_sum, routed), "shard", scatter_dimension=0, tiled=True
-    )
-    made["gate"], (in_sum, out_sum) = weight_grad(groups(0), groups(2), (in_sum, out_sum))
-    out_across = move(out_sum, X_SWAP)
+    grad_up, out_home = made["up"], made["home"]
     down_all = widen(
-        made["down"],
-        move(made["down"], CORE_SWAP),
-        core_ref,
-        (made["gate"], in_other, out_across),
-    )
-    in_all = jnp.stack([in_sum, after(in_other, made["gate"])])
+        made["down"], move(made["down"], CORE_SWAP), core_ref, (grad_up,)
+    )
+    in_all = jnp.stack([in_sum, after(in_other, down_all)])
     in_beside = move(in_all, CORE_SWAP)
-    grad_up, (_, in_beside) = weight_grad(groups(0), groups(3), (down_all, in_beside))
+    out_across = move(after(out_home, down_all), X_SWAP)
+    gate_all = widen(
+        made["gate"], move(made["gate"], CORE_SWAP), core_ref, (down_all, out_across)
+    )
     in_all = jnp.stack([in_all, in_beside], axis=1).reshape((REPS,) + in_sum.shape)
-    grad_in = weave_columns(in_all, rep_ref, 3 * part_width, (grad_up,))
+    grad_in = weave_columns(in_all, rep_ref, 3 * part_width, (gate_all,))
     small = jnp.sum(in_all[:, :, 3 * part_width :].astype(f32), axis=0).T
-    gate_all = widen(made["gate"], move(made["gate"], CORE_SWAP), core_ref, (grad_up,))
     up_all = widen(grad_up, move(grad_up, CORE_SWAP), core_ref, (gate_all,))
 
-    outputs = (residual + after(routed, in_sum).astype(f32)).astype(bf16)
-    grad_normed = added(normed_mine[0], normed_across)
+    outputs = (residual + after(routed, down_all).astype(f32)).astype(bf16)
+    grad_normed = after(added(normed_mine[0], normed_across), down_all)
     grad_normed = pick_columns(grad_normed, place_of_shard, rows_each).astype(f32)
     home_unit = hidden * home_rate
     scaled = gains[0] * grad_normed
@@ -1433,7 +1444,7 @@
         + home_rate * (scaled - home_unit * jnp.mean(scaled * home_unit, axis=-1, keepdims=True))
     ).astype(bf16)
 
-    out_sum = jnp.stack([out_sum, out_across])
+    out_sum = jnp.stack([out_home, out_across])
     out_sum = jnp.stack([out_sum, move(out_sum, CORE_SWAP)], axis=1)
     out_sum = out_sum.reshape(REPS, out_rows, width)
     out_sum = jnp.take(out_sum, rep ^ jnp.arange(REPS, dtype=jnp.int32), axis=0)

time: 1060 us -> 1020 us (0.962)
  waiting for transfers between devices: 278 us -> 244 us
    ppermute x72, waiting for transfers between devices: 278 us -> 244 us  [move(): return lax.ppermute(values, AXES, moves)]
    unnamed x236 -> x248, local copies, waits for them, and re-layouts: 66.2 us -> 67.5 us
  transfers between devices with their start and end apart: 76 -> 76, of which waited for: 25 -> 26; matrix products, arithmetic and copies ran while one was open for 28% -> 29% of each run, Pallas kernels for 30% -> 31%
where the time goes in v4:
time: 1020 us; the launch traced here: 1010 us
  Pallas kernels  369 us (36%)
  waiting for transfers between devices  244 us (24%)
  local copies, waits for them, and re-layouts  115 us (11%)
  other arithmetic  104 us (10%)
  matrix products  98.5 us (10%)
  starting transfers between devices  66.1 us (6%)
  between operations  16 us (2%)
    ppermute x72, waiting for transfers between devices, move(): return lax.ppermute(values, AXES, moves)  244 us
    pallas_call x4, Pallas kernels, forward_part(): pl.pallas_call(ordered(forward_kernel, len(behind)), grid_spec=pltpu.Pref...  112 us
    pallas_call x4, Pallas kernels, cotangent_part(): pl.pallas_call(ordered(cotangent_kernel, len(behind)), grid_spec=pltpu.Pr...  76.8 us
    dot_general x3, matrix products, weight_grad(): jnp.einsum('ecd,ecf->edf', left, right, preferred_element_type=f32)  69.4 us
    unnamed x248, local copies, waits for them, and re-layouts  67.5 us
    ppermute x72, starting transfers between devices, move(): return lax.ppermute(values, AXES, moves)  65.8 us
    pallas_call x3, Pallas kernels, widen(): pl.pallas_call(ordered(widen_kernel, len(behind)), grid_spec=pltpu.Prefet...  51 us
    pallas_call x2, Pallas kernels, backward_part(): pl.pallas_call(ordered(backward_kernel, len(behind)), grid_spec=pltpu.Pre...  49.2 us
  transfers between devices with their start and end apart: 76, of which 26 were waited for; matrix products, arithmetic and copies ran while one was open for 29% of the time, Pallas kernels for 31%

profile of v4, /device:TPU:0, one launch (start us, length us, event | category | flops | bytes accessed | tf_op | source)
XLA Modules:
  0.0 1012.5 jit_solution(12316933788820105920)
XLA Ops:
  28.0 14.7 %collective-permute-done.3 = bf16[2,33,256]{2,1,0:T(8,128)(2,1)S(1)} collective-permute-done((bf16[2,33,256]{2,1,0:T(8,128)(2,1)S(1)}, bf16[2,33,256]{2,1,0:T(8,128)(2,1)S(1)}, u32[]{:S(2)}, u32[]{:S(2)}) %collective-permute-start.3) | collective-permute-done | bytes 33824 | tf_op jit(solution)/shard_map/ppermute | solution.py:408
  46.4 5.3 collective-permute-done.4
  58.7 20.8 %collective-permute-done.5 = bf16[2,168,256]{2,1,0:T(8,128)(2,1)S(1)} collective-permute-done((bf16[2,168,256]{2,1,0:T(8,128)(2,1)S(1)}, bf16[2,168,256]{2,1,0:T(8,128)(2,1)S(1)}, u32[]{:S(2)}, u32[]{:S(2)}) %collective-permute-start.5) | collective-permute-done | bytes 172064 | tf_op jit(solution)/shard_map/ppermute | solution.py:408
  88.7 7.2 collective-permute-done.7
  95.9 19.1 %collective-permute-done.10 = bf16[256,1536]{1,0:T(8,128)(2,1)S(1)} collective-permute-done((bf16[256,1536]{1,0:T(8,128)(2,1)}, bf16[256,1536]{1,0:T(8,128)(2,1)S(1)}, u32[]{:S(2)}, u32[]{:S(2)}) %collective-permute-start.10) | collective-permute-done | bytes 786464 | tf_op jit(solution)/shard_map/ppermute | solution.py:408
  124.2 4.3 collective-permute-done.11
  137.7 11.2 %collective-permute-done.14 = bf16[256,1536]{1,0:T(8,128)(2,1)} collective-permute-done((bf16[256,1536]{1,0:T(8,128)(2,1)}, bf16[256,1536]{1,0:T(8,128)(2,1)}, u32[]{:S(2)}, u32[]{:S(2)}) %collective-permute-start.14) | collective-permute-done | bytes 786464 | tf_op jit(solution)/shard_map/ppermute | solution.py:408
  154.2 8.1 fusion.124.raw_ref.refs_0_
  173.3 10.2 %shard_map.240 = bf16[768,512]{1,0:T(8,128)(2,1)} custom-call(f32[768,1536]{1,0:T(8,128)} %copy-done.12, f32[768,2]{1,0:T(8,128)} %fusion.82.rate_ref.refs_1_, f32[2,512]{1,0:T(2,128)} %bitcast.352, f32[768,128]{1,0:T(8,128)} %get-tuple-element.274.cos_ref.refs_3_, f32[768,128]{1,0:T(8,128)} %get-tuple-element.273.sin_ref.refs_4_, ...), custom_call_target="tpu_custom_call" | custom-call | tf_op jit(solution)/shard_map/pallas_call | solution.py:1008
  193.8 3.9 collective-permute-done.17
  199.0 5.7 maximum_select_fusion
  209.9 16.8 %collective-permute-done.26 = bf16[192,2048]{1,0:T(8,128)(2,1)} collective-permute-done((bf16[192,2048]{1,0:T(8,128)(2,1)S(1)}, bf16[192,2048]{1,0:T(8,128)(2,1)}, u32[]{:S(2)}, u32[]{:S(2)}) %collective-permute-start.26) | collective-permute-done | bytes 786464 | tf_op jit(solution)/shard_map/ppermute | solution.py:408
  227.9 4.4 convert_reduce_fusion.1
  243.5 24.4 %collective-permute-done.29 = bf16[192,2048]{1,0:T(8,128)(2,1)} collective-permute-done((bf16[192,2048]{1,0:T(8,128)(2,1)S(1)}, bf16[192,2048]{1,0:T(8,128)(2,1)}, u32[]{:S(2)}, u32[]{:S(2)}) %collective-permute-start.29) | collective-permute-done | bytes 786464 | tf_op jit(solution)/shard_map/ppermute | solution.py:408
  278.5 8.5 collective-permute-done.33.refs_0_
  289.1 31.2 %collective-permute-done.32 = bf16[192,2048]{1,0:T(8,128)(2,1)} collective-permute-done((bf16[192,2048]{1,0:T(8,128)(2,1)S(1)}, bf16[192,2048]{1,0:T(8,128)(2,1)}, u32[]{:S(2)}, u32[]{:S(2)}) %collective-permute-start.32) | collective-permute-done | bytes 786464 | tf_op jit(solution)/shard_map/ppermute | solution.py:408
  320.3 19.5 %shard_map.242 = (bf16[2,480,2048]{2,1,0:T(8,128)(2,1)}, f32[2,480,1024]{2,1,0:T(8,128)}) custom-call(s32[1]{0:T(128)} %bitcast.32.scalar_ref, bf16[192,2048]{1,0:T(8,128)(2,1)} %copy-done.41, s32[2,1,1536]{2,1,0:T(1,128)} %broadcast_in_dim_squeeze.25.refs_1_, bf16[1536,2048]{1,0:T(8,128)(2,1)} %all-gather.3.cloned.1.call-done.refs_2_, ...), custom_call_target="tpu_custom_call" | custom-call | flops 99999997952 | tf_op jit(solution)/shard_map/pallas_call | solution.py:650
  348.8 11.1 %collective-permute-done.34 = bf16[192,2048]{1,0:T(8,128)(2,1)S(1)} collective-permute-done((bf16[192,2048]{1,0:T(8,128)(2,1)}, bf16[192,2048]{1,0:T(8,128)(2,1)S(1)}, u32[]{:S(2)}, u32[]{:S(2)}) %collective-permute-start.34) | collective-permute-done | bytes 786464 | tf_op jit(solution)/shard_map/ppermute | solution.py:408
  362.8 19.1 %shard_map.243 = (bf16[2,480,2048]{2,1,0:T(8,128)(2,1)}, f32[2,480,1024]{2,1,0:T(8,128)}) custom-call(s32[1]{0:T(128)} %bitcast.32.scalar_ref, f32[2,480,1024]{2,1,0:T(8,128)} %get-tuple-element.113.refs_0_.refs_5_, s32[2,1,1536]{2,1,0:T(1,128)} %broadcast_in_dim_squeeze.26.refs_1_, bf16[1536,2048]{1,0:T(8,128)(2,1)} %collective-permute-done.36.refs_2_, ...), custom_call_target="tpu_custom_call" | custom-call | flops 99999997952 | tf_op jit(solution)/shard_map/pallas_call | solution.py:650
  394.1 28.0 %shard_map.244 = (bf16[2,480,2048]{2,1,0:T(8,128)(2,1)}, bf16[2,480,1024]{2,1,0:T(8,128)(2,1)}, bf16[2,480,1024]{2,1,0:T(8,128)(2,1)}, bf16[2,480,1024]{2,1,0:T(8,128)(2,1)}, bf16[2,480,128]{2,1,0:T(8,128)(2,1)}) custom-call(s32[2]{0:T(128)} %pad_add_fusion.scalar_ref, s32[2,1,1536]{2,1,0:T(1,128)} %broadcast_in_dim_squeeze.24.refs_0_, ...), custom_call_target="tpu_custom_call" | custom-call | tf_op jit(solution)/shard_map/pallas_call | solution.py:735
  422.1 27.8 %shard_map.245 = (bf16[2,480,2048]{2,1,0:T(8,128)(2,1)}, bf16[2,480,1024]{2,1,0:T(8,128)(2,1)}, bf16[2,480,1024]{2,1,0:T(8,128)(2,1)}, bf16[2,480,1024]{2,1,0:T(8,128)(2,1)}, bf16[2,480,128]{2,1,0:T(8,128)(2,1)}) custom-call(s32[2]{0:T(128)} %pad_add_fusion.scalar_ref, bf16[2,480,1024]{2,1,0:T(8,128)(2,1)} %get-tuple-element.117.refs_0_.refs_2_, ...), custom_call_target="tpu_custom_call" | custom-call | tf_op jit(solution)/shard_map/pallas_call | solution.py:735
  450.0 5.5 collective-permute-done.31.refs_1_
  455.4 24.8 %shard_map.246 = bf16[1536,2176]{1,0:T(8,128)(2,1)} custom-call(s32[1]{0:T(128)} %bitcast.32.scalar_ref, bf16[384,2048]{1,0:T(8,128)(2,1)} %collective-permute-done.28.refs_0_, bf16[384,2048]{1,0:T(8,128)(2,1)} %collective-permute-done.31.refs_1_, s32[1536,2]{1,0:T(8,128)} %get-tuple-element.255.refs_2_, bf16[2,480,1024]{2,1,0:T(8,128)(2,1)} %get-tuple-element.118.refs_3_, ...), custom_call_target="tpu_custom_call" | custom-call | tf_op jit(solution)/shard_map/pallas_call | solution.py:809
  485.5 24.4 %shard_map.247 = bf16[1536,2176]{1,0:T(8,128)(2,1)} custom-call(s32[1]{0:T(128)} %bitcast.32.scalar_ref, bf16[8,192,2176]{2,1,0:T(8,128)(2,1)} %bitcast.301, s32[1536,2]{1,0:T(8,128)} %get-tuple-element.254.refs_1_, bf16[2,480,1024]{2,1,0:T(8,128)(2,1)} %get-tuple-element.121.refs_2_, bf16[2,480,1024]{2,1,0:T(8,128)(2,1)} %get-tuple-element.122.refs_3_, ...), custom_call_target="tpu_custom_call" | custom-call | tf_op jit(solution)/shard_map/pallas_call | solution.py:809
  515.1 4.7 collective-permute-done.40.refs_1_
  519.8 17.0 %shard_map.248 = bf16[1536,2048]{1,0:T(8,128)(2,1)} custom-call(s32[1]{0:T(128)} %bitcast.32.scalar_ref, bf16[192,2176]{1,0:T(8,128)(2,1)} %fusion.60.refs_0_, bf16[384,2048]{1,0:T(8,128)(2,1)} %collective-permute-done.40.refs_1_, bf16[1536,2048]{1,0:T(8,128)(2,1)} %all-gather.5.cloned.1.call-done.refs_2_, s32[1536,2]{1,0:T(8,128)} %get-tuple-element.253.refs_3_, ...), custom_call_target="tpu_custom_call" | custom-call | flops 99999997952 | tf_op jit(solution)/shard_map/pallas_call | solution.py:871
  545.0 13.0 %collective-permute-done.39 = bf16[192,2176]{1,0:T(8,128)(2,1)} collective-permute-done((bf16[192,2176]{1,0:T(8,128)(2,1)S(1)}, bf16[192,2176]{1,0:T(8,128)(2,1)}, u32[]{:S(2)}, u32[]{:S(2)}) %collective-permute-start.39) | collective-permute-done | bytes 835616 | tf_op jit(solution)/shard_map/ppermute | solution.py:408
  558.0 3.6 fusion.56
  562.2 17.2 %shard_map.249 = bf16[1536,2048]{1,0:T(8,128)(2,1)} custom-call(s32[1]{0:T(128)} %bitcast.32.scalar_ref, bf16[192,2176]{1,0:T(8,128)(2,1)} %get-tuple-element.239.refs_0_, s32[1536,2]{1,0:T(8,128)} %get-tuple-element.252.refs_1_, bf16[2,480,1024]{2,1,0:T(8,128)(2,1)} %get-tuple-element.117.refs_0_.refs_2_, bf16[4,1024,2048]{2,1,0:T(8,128)(2,1)} %refs_3_.11, ...), custom_call_target="tpu_custom_call" | custom-call | flops 99999997952 | tf_op jit(solution)/shard_map/pallas_call | solution.py:871
  585.7 19.1 %shard_map.250 = (bf16[2,480,2048]{2,1,0:T(8,128)(2,1)}, f32[2,480,1024]{2,1,0:T(8,128)}) custom-call(s32[1]{0:T(128)} %bitcast.32.scalar_ref, bf16[192,2176]{1,0:T(8,128)(2,1)} %get-tuple-element.236.refs_0_, s32[2,1,1536]{2,1,0:T(1,128)} %broadcast_in_dim_squeeze.28.refs_1_, bf16[1536,2048]{1,0:T(8,128)(2,1)} %all-gather.5.cloned.1.call-done.refs_2_, ...), custom_call_target="tpu_custom_call" | custom-call | flops 99999997952 | tf_op jit(solution)/shard_map/pallas_call | solution.py:650
  608.7 3.8 collective-permute-start.48
  612.5 19.2 %shard_map.251 = (bf16[2,480,2048]{2,1,0:T(8,128)(2,1)}, f32[2,480,1024]{2,1,0:T(8,128)}) custom-call(s32[1]{0:T(128)} %bitcast.32.scalar_ref, bf16[192,2176]{1,0:T(8,128)(2,1)} %copy-done.62, s32[2,1,1536]{2,1,0:T(1,128)} %broadcast_in_dim_squeeze.29.refs_1_, bf16[1536,2048]{1,0:T(8,128)(2,1)} %collective-permute-done.45.refs_2_, ...), custom_call_target="tpu_custom_call" | custom-call | flops 99999997952 | tf_op jit(solution)/shard_map/pallas_call | solution.py:650
  651.1 9.7 collective-permute-done.49
  668.6 20.1 %shard_map.253 = (f32[768,1024]{1,0:T(8,128)}, bf16[768,512]{1,0:T(8,128)(2,1)}, f32[768,2]{1,0:T(8,128)}, f32[4,2,512]{2,1,0:T(2,128)}) custom-call(f32[768,1536]{1,0:T(8,128)} %copy-done.12, f32[768,2]{1,0:T(8,128)} %fusion.82.rate_ref.refs_1_, f32[2,512]{1,0:T(2,128)} %bitcast.353, f32[768,128]{1,0:T(8,128)} %get-tuple-element.274.cos_ref.refs_3_, ...), custom_call_target="tpu_custom_call" | custom-call | tf_op jit(solution)/shard_map/pallas_call | solution.py:1028
  697.0 6.5 shard_map.254
  703.5 8.0 fusion.117
  720.7 5.4 convolution_convert_fusion
  750.0 28.0 %shard_map.255 = (bf16[2,480,2048]{2,1,0:T(8,128)(2,1)}, bf16[2,480,1024]{2,1,0:T(8,128)(2,1)}, bf16[2,480,1024]{2,1,0:T(8,128)(2,1)}, bf16[2,480,1024]{2,1,0:T(8,128)(2,1)}, bf16[2,480,128]{2,1,0:T(8,128)(2,1)}) custom-call(s32[2]{0:T(128)} %pad_add_fusion.scalar_ref, bf16[256,1664]{1,0:T(8,128)(2,1)} %pad_maximum_fusion.24.refs_0_, ...), custom_call_target="tpu_custom_call" | custom-call | flops 99999997952 | tf_op jit(solution)/shard_map/pallas_call | solution.py:735
  783.7 27.8 %shard_map.256 = (bf16[2,480,2048]{2,1,0:T(8,128)(2,1)}, bf16[2,480,1024]{2,1,0:T(8,128)(2,1)}, bf16[2,480,1024]{2,1,0:T(8,128)(2,1)}, bf16[2,480,1024]{2,1,0:T(8,128)(2,1)}, bf16[2,480,128]{2,1,0:T(8,128)(2,1)}) custom-call(s32[2]{0:T(128)} %pad_add_fusion.scalar_ref, bf16[256,1664]{1,0:T(8,128)(2,1)} %add_convert_fusion.4.refs_0_, ...), custom_call_target="tpu_custom_call" | custom-call | flops 99999997952 | tf_op jit(solution)/shard_map/pallas_call | solution.py:735
  811.5 23.3 %fusion.38 = bf16[2,1024,2048]{2,1,0:T(8,128)(2,1)} fusion(bf16[2,480,2048]{2,1,0:T(8,128)(2,1)} %get-tuple-element.151, bf16[2,480,2048]{2,1,0:T(8,128)(2,1)} %get-tuple-element.150, bf16[2,480,2048]{2,1,0:T(8,128)(2,1)} %get-tuple-element.149, bf16[2,480,2048]{2,1,0:T(8,128)(2,1)} %get-tuple-element.148, bf16[2,480,1024]{2,1,0:T(8,128)(2,1)} %get-tuple-element.147, ...), kind=kOutput, calls=%fused_computation.57 | convolution fusion | flops 16204693504 | bytes 31981568 | tf_op jit(solution)/shard_map/ecd,ecf->edf/dot_general | solution.py:1390
  841.8 6.8 collective-permute-done.63
  852.0 23.4 %fusion.46 = bf16[2,2048,1024]{2,1,0:T(8,128)(2,1)} fusion(bf16[2,480,1024]{2,1,0:T(8,128)(2,1)} %get-tuple-element.160, bf16[2,480,1024]{2,1,0:T(8,128)(2,1)} %get-tuple-element.159, bf16[2,480,1024]{2,1,0:T(8,128)(2,1)} %get-tuple-element.118.refs_3_, bf16[2,480,1024]{2,1,0:T(8,128)(2,1)} %get-tuple-element.121.refs_2_, ...), kind=kOutput, calls=%fused_computation.59 | convolution fusion | flops 16204693504 | bytes 31981568 | tf_op jit(solution)/shard_map/ecd,ecf->edf/dot_general | solution.py:1390
  875.4 12.9 %collective-permute-done.64 = bf16[256,1664]{1,0:T(8,128)(2,1)} collective-permute-done((bf16[256,1664]{1,0:T(8,128)(2,1)}, bf16[256,1664]{1,0:T(8,128)(2,1)}, u32[]{:S(2)}, u32[]{:S(2)}) %collective-permute-start.64) | collective-permute-done | bytes 852000 | tf_op jit(solution)/shard_map/ppermute | solution.py:408
  888.3 22.7 %fusion.43.refs_0_ = bf16[2,2048,1024]{2,1,0:T(8,128)(2,1)} fusion(bf16[2,480,1024]{2,1,0:T(8,128)(2,1)} %get-tuple-element.153, bf16[2,480,1024]{2,1,0:T(8,128)(2,1)} %get-tuple-element.144.refs_1_, bf16[2,480,1024]{2,1,0:T(8,128)(2,1)} %get-tuple-element.119.refs_4_, bf16[2,480,1024]{2,1,0:T(8,128)(2,1)S(1)} %copy-done.55, ...), kind=kOutput, calls=%fused_computation.58 | convolution fusion | flops 16204693504 | bytes 31981568 | tf_op jit(solution)/shard_map/ecd,ecf->edf/dot_general | solution.py:1390
  922.6 16.9 %shard_map.257 = f32[4096,2048]{1,0:T(8,128)} custom-call(s32[1]{0:T(128)} %bitcast.32.scalar_ref, bf16[2,2048,1024]{2,1,0:T(8,128)(2,1)S(1)} %copy-done.2, bf16[2048,2048]{1,0:T(8,128)(2,1)S(1)} %bitcast.291, bf16[2048,2048]{1,0:T(8,128)(2,1)} %bitcast.89.refs_2_), custom_call_target="tpu_custom_call" | custom-call | tf_op jit(solution)/shard_map/pallas_call | solution.py:591
  965.9 17.0 %shard_map.259 = f32[8192,1024]{1,0:T(8,128)} custom-call(s32[1]{0:T(128)} %bitcast.32.scalar_ref, f32[4,1024,2048]{2,1,0:T(8,128)} %bitcast.297, bf16[64,2048]{1,0:T(8,128)(2,1)S(1)} %collective-permute-done.68.refs_1_, bf16[4096,1024]{1,0:T(8,128)(2,1)S(1)} %bitcast.290, bf16[4096,1024]{1,0:T(8,128)(2,1)} %bitcast.100.refs_3_), custom_call_target="tpu_custom_call" | custom-call | tf_op jit(solution)/shard_map/pallas_call | solution.py:591
  982.9 4.0 shard_map.260
  988.6 17.0 %shard_map.261 = f32[8192,1024]{1,0:T(8,128)} custom-call(s32[1]{0:T(128)} %bitcast.32.scalar_ref, f32[4,2048,1024]{2,1,0:T(8,128)} %bitcast.295, bf16[4096,1024]{1,0:T(8,128)(2,1)S(1)} %bitcast.285, bf16[4096,1024]{1,0:T(8,128)(2,1)} %bitcast.111.refs_2_), custom_call_target="tpu_custom_call" | custom-call | tf_op jit(solution)/shard_map/pallas_call | solution.py:591
  (612 shorter events, 293.4 us)
Async XLA Ops:
  7.2 313.1 %all-gather.3.cloned.1.call-start = ((), (), s32[]{:S(2)}) async-start(), calls=%async_computation.2 | async-start | bytes 7077888 | tf_op jit(solution)/shard_map/all_gather | solution.py:1161
  9.7 74.9 %collective-permute-start.13 = (bf16[256,1536]{1,0:T(8,128)(2,1)S(1)}, bf16[256,1536]{1,0:T(8,128)(2,1)}, u32[]{:S(2)}, u32[]{:S(2)}) collective-permute-start(bf16[256,1536]{1,0:T(8,128)(2,1)S(1)} %shard_map.239), channel_id=1, source_target_pairs={{0,1},{1,0},{2,3},{3,2},{4,5},{5,4},{6,7},{7,6},{8,9},{9,8},{10,11... | collective-permute-start | bytes 2359304 | tf_op jit(solution)/shard_map/ppermute | solution.py:408
  12.8 67.3 %collective-permute-start.9 = (bf16[256,1536]{1,0:T(8,128)(2,1)S(1)}, bf16[256,1536]{1,0:T(8,128)(2,1)}, u32[]{:S(2)}, u32[]{:S(2)}) collective-permute-start(bf16[256,1536]{1,0:T(8,128)(2,1)S(1)} %shard_map.239), channel_id=1, source_target_pairs={{0,2},{1,3},{2,4},{3,5},{4,6},{5,7},{6,0},{7,1},{8,10},{9,11},{10,... | collective-permute-start | bytes 2359304 | tf_op jit(solution)/shard_map/ppermute | solution.py:408
  14.3 41.0 %collective-permute-start.6 = (bf16[256,1536]{1,0:T(8,128)(2,1)S(1)}, bf16[256,1536]{1,0:T(8,128)(2,1)}, u32[]{:S(2)}, u32[]{:S(2)}) collective-permute-start(bf16[256,1536]{1,0:T(8,128)(2,1)S(1)} %shard_map.239), channel_id=1, source_target_pairs={{0,6},{1,7},{2,0},{3,1},{4,2},{5,3},{6,4},{7,5},{8,14},{9,15},{10,... | collective-permute-start | bytes 2359304 | tf_op jit(solution)/shard_map/ppermute | solution.py:408
  21.9 35.0 %collective-permute-start = (bf16[192,2048]{1,0:T(8,128)(2,1)S(1)}, bf16[192,2048]{1,0:T(8,128)(2,1)}, u32[]{:S(2)}, u32[]{:S(2)}) collective-permute-start(bf16[192,2048]{1,0:T(8,128)(2,1)S(1)} %copy-done.16), channel_id=1, source_target_pairs={{0,16},{1,17},{2,18},{3,19},{4,20},{5,21},{6,22},{7,23},{8,24},{9,... | collective-permute-start | bytes 2359304 | tf_op jit(solution)/shard_map/ppermute | solution.py:408
  51.8 27.7 %collective-permute-start.5 = (bf16[2,168,256]{2,1,0:T(8,128)(2,1)S(1)}, bf16[2,168,256]{2,1,0:T(8,128)(2,1)S(1)}, u32[]{:S(2)}, u32[]{:S(2)}) collective-permute-start(bf16[2,168,256]{2,1,0:T(8,128)(2,1)S(1)} %get-tuple-element.278), channel_id=1, source_target_pairs={{0,4},{1,5},{2,6},{3,7},{4,0},{5,1},{6,2},{7,3},{8,12},{9,13},{10,... | collective-permute-start | bytes 516104 | tf_op jit(solution)/shard_map/ppermute | solution.py:408
  55.4 82.3 %collective-permute-start.12 = (bf16[192,2048]{1,0:T(8,128)(2,1)S(1)}, bf16[192,2048]{1,0:T(8,128)(2,1)}, u32[]{:S(2)}, u32[]{:S(2)}) collective-permute-start(bf16[192,2048]{1,0:T(8,128)(2,1)S(1)} %copy-done.33), channel_id=1, source_target_pairs={{0,16},{1,17},{2,18},{3,19},{4,20},{5,21},{6,22},{7,23},{8,24},{9,... | collective-permute-start | bytes 2359304 | tf_op jit(solution)/shard_map/ppermute | solution.py:408
  56.9 39.0 %collective-permute-start.7 = (bf16[256,1536]{1,0:T(8,128)(2,1)S(1)}, bf16[256,1536]{1,0:T(8,128)(2,1)}, u32[]{:S(2)}, u32[]{:S(2)}) collective-permute-start(bf16[256,1536]{1,0:T(8,128)(2,1)S(1)} %shard_map.239), channel_id=1, source_target_pairs={{0,4},{1,5},{2,6},{3,7},{4,0},{5,1},{6,2},{7,3},{8,12},{9,13},{10,... | collective-permute-start | bytes 2359304 | tf_op jit(solution)/shard_map/ppermute | solution.py:408
  79.5 38.0 %collective-permute-start.8 = (bf16[256,1536]{1,0:T(8,128)(2,1)}, bf16[256,1536]{1,0:T(8,128)(2,1)S(1)}, u32[]{:S(2)}, u32[]{:S(2)}) collective-permute-start(bf16[256,1536]{1,0:T(8,128)(2,1)} %collective-permute-done.6), channel_id=1, source_target_pairs={{0,1},{1,0},{2,3},{3,2},{4,5},{5,4},{6,7},{7,6},{8,9},{9,8},{10,11... | collective-permute-start | bytes 2359304 | tf_op jit(solution)/shard_map/ppermute | solution.py:408
  80.0 35.0 %collective-permute-start.10 = (bf16[256,1536]{1,0:T(8,128)(2,1)}, bf16[256,1536]{1,0:T(8,128)(2,1)S(1)}, u32[]{:S(2)}, u32[]{:S(2)}) collective-permute-start(bf16[256,1536]{1,0:T(8,128)(2,1)} %collective-permute-done.9), channel_id=1, source_target_pairs={{0,1},{1,0},{2,3},{3,2},{4,5},{5,4},{6,7},{7,6},{8,9},{9,8},{10,11... | collective-permute-start | bytes 2359304 | tf_op jit(solution)/shard_map/ppermute | solution.py:408
  84.6 45.5 %collective-permute-start.1 = (bf16[2,192,2048]{2,1,0:T(8,128)(2,1)}, bf16[2,192,2048]{2,1,0:T(8,128)(2,1)}, u32[]{:S(2)}, u32[]{:S(2)}) collective-permute-start(bf16[2,192,2048]{2,1,0:T(8,128)(2,1)} %get-tuple-element.257), channel_id=1, source_target_pairs={{0,8},{1,9},{2,10},{3,11},{4,12},{5,13},{6,14},{7,15},{8,0},{9,1},... | collective-permute-start | bytes 4718600 | tf_op jit(solution)/shard_map/ppermute | solution.py:408
  95.9 69.6 %collective-permute-start.23 = (bf16[64,2048]{1,0:T(8,128)(2,1)}, bf16[64,2048]{1,0:T(8,128)(2,1)}, u32[]{:S(2)}, u32[]{:S(2)}) collective-permute-start(bf16[64,2048]{1,0:T(8,128)(2,1)} %constant_dynamic-slice_fusion.1), channel_id=1, source_target_pairs={{0,2},{1,3},{2,4},{3,5},{4,6},{5,7},{6,0},{7,1},{8,10},{9,11},{10,... | collective-permute-start | bytes 786440 | tf_op jit(solution)/shard_map/ppermute | solution.py:408
  122.7 60.8 %collective-permute-start.18 = (bf16[64,2048]{1,0:T(8,128)(2,1)}, bf16[64,2048]{1,0:T(8,128)(2,1)}, u32[]{:S(2)}, u32[]{:S(2)}) collective-permute-start(bf16[64,2048]{1,0:T(8,128)(2,1)} %constant_dynamic-slice_fusion.1), channel_id=1, source_target_pairs={{0,1},{1,0},{2,3},{3,2},{4,5},{5,4},{6,7},{7,6},{8,9},{9,8},{10,11... | collective-permute-start | bytes 786440 | tf_op jit(solution)/shard_map/ppermute | solution.py:408
  130.1 35.4 %collective-permute-start.21 = (bf16[64,2048]{1,0:T(8,128)(2,1)}, bf16[64,2048]{1,0:T(8,128)(2,1)S(1)}, u32[]{:S(2)}, u32[]{:S(2)}) collective-permute-start(bf16[64,2048]{1,0:T(8,128)(2,1)} %constant_dynamic-slice_fusion.1), channel_id=1, source_target_pairs={{0,4},{1,5},{2,6},{3,7},{4,0},{5,1},{6,2},{7,3},{8,12},{9,13},{10,... | collective-permute-start | bytes 786440 | tf_op jit(solution)/shard_map/ppermute | solution.py:408
  154.0 365.8 %all-gather.5.cloned.1.call-start = ((), (), s32[]{:S(2)}) async-start(), calls=%async_computation.3 | async-start | bytes 7077888 | tf_op jit(solution)/shard_map/all_gather | solution.py:1267
  237.8 30.1 %collective-permute-start.29 = (bf16[192,2048]{1,0:T(8,128)(2,1)S(1)}, bf16[192,2048]{1,0:T(8,128)(2,1)}, u32[]{:S(2)}, u32[]{:S(2)}) collective-permute-start(bf16[192,2048]{1,0:T(8,128)(2,1)S(1)} %get-tuple-element.109), channel_id=1, source_target_pairs={{0,6},{1,7},{2,0},{3,1},{4,2},{5,3},{6,4},{7,5},{8,14},{9,15},{10,... | collective-permute-start | bytes 2359304 | tf_op jit(solution)/shard_map/ppermute | solution.py:408
  242.1 45.0 %collective-permute-start.33 = (bf16[192,2048]{1,0:T(8,128)(2,1)S(1)}, bf16[192,2048]{1,0:T(8,128)(2,1)S(1)}, u32[]{:S(2)}, u32[]{:S(2)}) collective-permute-start(bf16[192,2048]{1,0:T(8,128)(2,1)S(1)} %get-tuple-element.109), channel_id=1, source_target_pairs={{0,2},{1,3},{2,4},{3,5},{4,6},{5,7},{6,0},{7,1},{8,10},{9,11},{10,... | collective-permute-start | bytes 2359304 | tf_op jit(solution)/shard_map/ppermute | solution.py:408
  242.2 98.2 %collective-permute-start.27 = (bf16[192,2048]{1,0:T(8,128)(2,1)S(1)}, bf16[192,2048]{1,0:T(8,128)(2,1)}, u32[]{:S(2)}, u32[]{:S(2)}) collective-permute-start(bf16[192,2048]{1,0:T(8,128)(2,1)S(1)} %get-tuple-element.109), channel_id=1, source_target_pairs={{0,1},{1,0},{2,3},{3,2},{4,5},{5,4},{6,7},{7,6},{8,9},{9,8},{10,11... | collective-permute-start | bytes 2359304 | tf_op jit(solution)/shard_map/ppermute | solution.py:408
  267.8 52.4 %collective-permute-start.32 = (bf16[192,2048]{1,0:T(8,128)(2,1)S(1)}, bf16[192,2048]{1,0:T(8,128)(2,1)}, u32[]{:S(2)}, u32[]{:S(2)}) collective-permute-start(bf16[192,2048]{1,0:T(8,128)(2,1)S(1)} %get-tuple-element.109), channel_id=1, source_target_pairs={{0,4},{1,5},{2,6},{3,7},{4,0},{5,1},{6,2},{7,3},{8,12},{9,13},{10,... | collective-permute-start | bytes 2359304 | tf_op jit(solution)/shard_map/ppermute | solution.py:408
  287.1 74.8 %collective-permute-start.35 = (bf16[192,2048]{1,0:T(8,128)(2,1)S(1)}, bf16[192,2048]{1,0:T(8,128)(2,1)S(1)}, u32[]{:S(2)}, u32[]{:S(2)}) collective-permute-start(bf16[192,2048]{1,0:T(8,128)(2,1)S(1)} %collective-permute-done.33.refs_0_), channel_id=1, source_target_pairs={{0,1},{1,0},{2,3},{3,2},{4,5},{5,4},{6,7},{7,6},{8,9},{9,8},{10,11... | collective-permute-start | bytes 2359304 | tf_op jit(solution)/shard_map/ppermute | solution.py:408
  287.6 56.9 %collective-permute-start.30 = (bf16[192,2048]{1,0:T(8,128)(2,1)}, bf16[192,2048]{1,0:T(8,128)(2,1)}, u32[]{:S(2)}, u32[]{:S(2)}) collective-permute-start(bf16[192,2048]{1,0:T(8,128)(2,1)} %collective-permute-done.29), channel_id=1, source_target_pairs={{0,1},{1,0},{2,3},{3,2},{4,5},{5,4},{6,7},{7,6},{8,9},{9,8},{10,11... | collective-permute-start | bytes 2359304 | tf_op jit(solution)/shard_map/ppermute | solution.py:408
  320.3 42.5 %collective-permute-start.36 = (bf16[1536,2048]{1,0:T(8,128)(2,1)}, bf16[1536,2048]{1,0:T(8,128)(2,1)}, u32[]{:S(2)}, u32[]{:S(2)}) collective-permute-start(bf16[1536,2048]{1,0:T(8,128)(2,1)} %all-gather.3.cloned.1.call-done.refs_2_), channel_id=1, source_target_pairs={{0,8},{1,9},{2,10},{3,11},{4,12},{5,13},{6,14},{7,15},{8,0},{9,1},... | collective-permute-start | bytes 18874376 | tf_op jit(solution)/shard_map/ppermute | solution.py:408
  381.9 40.2 %collective-permute-start.37 = (bf16[1536,2048]{1,0:T(8,128)(2,1)}, bf16[1536,2048]{1,0:T(8,128)(2,1)}, u32[]{:S(2)}, u32[]{:S(2)}) collective-permute-start(bf16[1536,2048]{1,0:T(8,128)(2,1)} %constant_dynamic-update-slice_fusion.18.refs_1_), channel_id=1, source_target_pairs={{0,8},{1,9},{2,10},{3,11},{4,12},{5,13},{6,14},{7,15},{8,0},{9,1},... | collective-permute-start | bytes 18874376 | tf_op jit(solution)/shard_map/ppermute | solution.py:408
  382.0 401.6 %reduce-scatter.3.cloned.1.call-start = ((), (), s32[]{:S(2)}) async-start(), calls=%async_computation.4 | async-start | bytes 7077888 | tf_op jit(solution)/shard_map/reduce_scatter | solution.py:1309
  384.6 65.3 %collective-permute-start.28 = (bf16[384,2048]{1,0:T(8,128)(2,1)}, bf16[384,2048]{1,0:T(8,128)(2,1)}, u32[]{:S(2)}, u32[]{:S(2)}) collective-permute-start(bf16[384,2048]{1,0:T(8,128)(2,1)} %pad_maximum_fusion.16), channel_id=1, source_target_pairs={{0,16},{1,17},{2,18},{3,19},{4,20},{5,21},{6,22},{7,23},{8,24},{9,... | collective-permute-start | bytes 4718600 | tf_op jit(solution)/shard_map/ppermute | solution.py:408
  388.9 66.5 %collective-permute-start.31 = (bf16[384,2048]{1,0:T(8,128)(2,1)}, bf16[384,2048]{1,0:T(8,128)(2,1)}, u32[]{:S(2)}, u32[]{:S(2)}) collective-permute-start(bf16[384,2048]{1,0:T(8,128)(2,1)} %pad_maximum_fusion.17), channel_id=1, source_target_pairs={{0,16},{1,17},{2,18},{3,19},{4,20},{5,21},{6,22},{7,23},{8,24},{9,... | collective-permute-start | bytes 4718600 | tf_op jit(solution)/shard_map/ppermute | solution.py:408
  480.2 29.7 %collective-permute-start.38 = (bf16[8,192,2176]{2,1,0:T(8,128)(2,1)}, bf16[8,192,2176]{2,1,0:T(8,128)(2,1)S(1)}, u32[]{:S(2)}, u32[]{:S(2)}) collective-permute-start(bf16[8,192,2176]{2,1,0:T(8,128)(2,1)} %bitcast.300), channel_id=1, source_target_pairs={{0,8},{1,9},{2,10},{3,11},{4,12},{5,13},{6,14},{7,15},{8,0},{9,1},... | collective-permute-start | bytes 20054024 | tf_op jit(solution)/shard_map/ppermute | solution.py:408
  482.8 37.0 %collective-permute-start.40 = (bf16[384,2048]{1,0:T(8,128)(2,1)}, bf16[384,2048]{1,0:T(8,128)(2,1)}, u32[]{:S(2)}, u32[]{:S(2)}) collective-permute-start(bf16[384,2048]{1,0:T(8,128)(2,1)} %pad_maximum_fusion.18), channel_id=1, source_target_pairs={{0,16},{1,17},{2,18},{3,19},{4,20},{5,21},{6,22},{7,23},{8,24},{9,... | collective-permute-start | bytes 4718600 | tf_op jit(solution)/shard_map/ppermute | solution.py:408
  536.9 25.3 %collective-permute-start.41 = (bf16[1536,2048]{1,0:T(8,128)(2,1)}, bf16[1536,2048]{1,0:T(8,128)(2,1)}, u32[]{:S(2)}, u32[]{:S(2)}) collective-permute-start(bf16[1536,2048]{1,0:T(8,128)(2,1)} %shard_map.248), channel_id=1, source_target_pairs={{0,8},{1,9},{2,10},{3,11},{4,12},{5,13},{6,14},{7,15},{8,0},{9,1},... | collective-permute-start | bytes 18874376 | tf_op jit(solution)/shard_map/ppermute | solution.py:408
  543.6 93.7 %collective-permute-start.53 = (bf16[384,2048]{1,0:T(8,128)(2,1)}, bf16[384,2048]{1,0:T(8,128)(2,1)}, u32[]{:S(2)}, u32[]{:S(2)}) collective-permute-start(bf16[384,2048]{1,0:T(8,128)(2,1)} %pad_maximum_fusion.20), channel_id=1, source_target_pairs={{0,16},{1,17},{2,18},{3,19},{4,20},{5,21},{6,22},{7,23},{8,24},{9,... | collective-permute-start | bytes 4718600 | tf_op jit(solution)/shard_map/ppermute | solution.py:408
  562.2 69.5 %collective-permute-start.46 = (bf16[192,2176]{1,0:T(8,128)(2,1)}, bf16[192,2176]{1,0:T(8,128)(2,1)}, u32[]{:S(2)}, u32[]{:S(2)}) collective-permute-start(bf16[192,2176]{1,0:T(8,128)(2,1)} %get-tuple-element.239.refs_0_), channel_id=1, source_target_pairs={{0,4},{1,5},{2,6},{3,7},{4,0},{5,1},{6,2},{7,3},{8,12},{9,13},{10,... | collective-permute-start | bytes 2506760 | tf_op jit(solution)/shard_map/ppermute | solution.py:408
  585.7 46.0 %collective-permute-start.47 = (bf16[192,2176]{1,0:T(8,128)(2,1)}, bf16[192,2176]{1,0:T(8,128)(2,1)}, u32[]{:S(2)}, u32[]{:S(2)}) collective-permute-start(bf16[192,2176]{1,0:T(8,128)(2,1)} %get-tuple-element.236.refs_0_), channel_id=1, source_target_pairs={{0,2},{1,3},{2,4},{3,5},{4,6},{5,7},{6,0},{7,1},{8,10},{9,11},{10,... | collective-permute-start | bytes 2506760 | tf_op jit(solution)/shard_map/ppermute | solution.py:408
  608.7 25.9 %collective-permute-start.48 = (bf16[192,2176]{1,0:T(8,128)(2,1)S(1)}, bf16[192,2176]{1,0:T(8,128)(2,1)S(1)}, u32[]{:S(2)}, u32[]{:S(2)}) collective-permute-start(bf16[192,2176]{1,0:T(8,128)(2,1)S(1)} %get-tuple-element.235.refs_0_), channel_id=1, source_target_pairs={{0,6},{1,7},{2,0},{3,1},{4,2},{5,3},{6,4},{7,5},{8,14},{9,15},{10,... | collective-permute-start | bytes 2506760 | tf_op jit(solution)/shard_map/ppermute | solution.py:408
  637.4 250.9 %reduce-scatter.5.cloned.1.call-start = ((), (), s32[]{:S(2)}) async-start(), calls=%async_computation.5 | async-start | bytes 2359296 | tf_op jit(solution)/shard_map/reduce_scatter | solution.py:1399
  667.1 82.8 %collective-permute-start.54 = (bf16[1536,2048]{1,0:T(8,128)(2,1)}, bf16[1536,2048]{1,0:T(8,128)(2,1)}, u32[]{:S(2)}, u32[]{:S(2)}) collective-permute-start(bf16[1536,2048]{1,0:T(8,128)(2,1)} %constant_dynamic-update-slice_fusion.26.refs_3_), channel_id=1, source_target_pairs={{0,8},{1,9},{2,10},{3,11},{4,12},{5,13},{6,14},{7,15},{8,0},{9,1},... | collective-permute-start | bytes 18874376 | tf_op jit(solution)/shard_map/ppermute | solution.py:408
  713.0 24.6 %collective-permute-start.56 = (bf16[2,192,2048]{2,1,0:T(8,128)(2,1)}, bf16[2,192,2048]{2,1,0:T(8,128)(2,1)}, u32[]{:S(2)}, u32[]{:S(2)}) collective-permute-start(bf16[2,192,2048]{2,1,0:T(8,128)(2,1)} %slice_bitcast_fusion), channel_id=1, source_target_pairs={{0,8},{1,9},{2,10},{3,11},{4,12},{5,13},{6,14},{7,15},{8,0},{9,1},... | collective-permute-start | bytes 4718600 | tf_op jit(solution)/shard_map/ppermute | solution.py:408
  733.1 44.9 %collective-permute-start.55 = (bf16[256,1664]{1,0:T(8,128)(2,1)}, bf16[256,1664]{1,0:T(8,128)(2,1)}, u32[]{:S(2)}, u32[]{:S(2)}) collective-permute-start(bf16[256,1664]{1,0:T(8,128)(2,1)} %pad_maximum_fusion.24.refs_0_), channel_id=1, source_target_pairs={{0,1},{1,0},{2,3},{3,2},{4,5},{5,4},{6,7},{7,6},{8,9},{9,8},{10,11... | collective-permute-start | bytes 2555912 | tf_op jit(solution)/shard_map/ppermute | solution.py:408
  740.7 96.4 %collective-permute-start.60 = (bf16[192,2048]{1,0:T(8,128)(2,1)}, bf16[192,2048]{1,0:T(8,128)(2,1)}, u32[]{:S(2)}, u32[]{:S(2)}) collective-permute-start(bf16[192,2048]{1,0:T(8,128)(2,1)} %slice_bitcast_fusion.11), channel_id=1, source_target_pairs={{0,16},{1,17},{2,18},{3,19},{4,20},{5,21},{6,22},{7,23},{8,24},{9,... | collective-permute-start | bytes 2359304 | tf_op jit(solution)/shard_map/ppermute | solution.py:408
  780.3 56.8 %collective-permute-start.58 = (bf16[256,1664]{1,0:T(8,128)(2,1)}, bf16[256,1664]{1,0:T(8,128)(2,1)}, u32[]{:S(2)}, u32[]{:S(2)}) collective-permute-start(bf16[256,1664]{1,0:T(8,128)(2,1)} %add_convert_fusion.4.refs_0_), channel_id=1, source_target_pairs={{0,4},{1,5},{2,6},{3,7},{4,0},{5,1},{6,2},{7,3},{8,12},{9,13},{10,... | collective-permute-start | bytes 2555912 | tf_op jit(solution)/shard_map/ppermute | solution.py:408
  781.2 53.7 %collective-permute-start.59 = (bf16[256,1664]{1,0:T(8,128)(2,1)}, bf16[256,1664]{1,0:T(8,128)(2,1)S(1)}, u32[]{:S(2)}, u32[]{:S(2)}) collective-permute-start(bf16[256,1664]{1,0:T(8,128)(2,1)} %pad_maximum_fusion.25), channel_id=1, source_target_pairs={{0,1},{1,0},{2,3},{3,2},{4,5},{5,4},{6,7},{7,6},{8,9},{9,8},{10,11... | collective-permute-start | bytes 2555912 | tf_op jit(solution)/shard_map/ppermute | solution.py:408
  781.6 55.5 %collective-permute-start.61 = (bf16[256,1664]{1,0:T(8,128)(2,1)}, bf16[256,1664]{1,0:T(8,128)(2,1)}, u32[]{:S(2)}, u32[]{:S(2)}) collective-permute-start(bf16[256,1664]{1,0:T(8,128)(2,1)} %pad_maximum_fusion.26), channel_id=1, source_target_pairs={{0,1},{1,0},{2,3},{3,2},{4,5},{5,4},{6,7},{7,6},{8,9},{9,8},{10,11... | collective-permute-start | bytes 2555912 | tf_op jit(solution)/shard_map/ppermute | solution.py:408
  783.2 65.4 %collective-permute-start.63 = (bf16[256,1664]{1,0:T(8,128)(2,1)}, bf16[256,1664]{1,0:T(8,128)(2,1)S(1)}, u32[]{:S(2)}, u32[]{:S(2)}) collective-permute-start(bf16[256,1664]{1,0:T(8,128)(2,1)} %pad_maximum_fusion.27), channel_id=1, source_target_pairs={{0,1},{1,0},{2,3},{3,2},{4,5},{5,4},{6,7},{7,6},{8,9},{9,8},{10,11... | collective-permute-start | bytes 2555912 | tf_op jit(solution)/shard_map/ppermute | solution.py:408
  839.4 35.9 %collective-permute-start.62 = (bf16[256,1664]{1,0:T(8,128)(2,1)}, bf16[256,1664]{1,0:T(8,128)(2,1)}, u32[]{:S(2)}, u32[]{:S(2)}) collective-permute-start(bf16[256,1664]{1,0:T(8,128)(2,1)} %add_convert_fusion.2), channel_id=1, source_target_pairs={{0,2},{1,3},{2,4},{3,5},{4,6},{5,7},{6,0},{7,1},{8,10},{9,11},{10,... | collective-permute-start | bytes 2555912 | tf_op jit(solution)/shard_map/ppermute | solution.py:408
  849.8 38.5 %collective-permute-start.64 = (bf16[256,1664]{1,0:T(8,128)(2,1)}, bf16[256,1664]{1,0:T(8,128)(2,1)}, u32[]{:S(2)}, u32[]{:S(2)}) collective-permute-start(bf16[256,1664]{1,0:T(8,128)(2,1)} %add_convert_fusion.1), channel_id=1, source_target_pairs={{0,6},{1,7},{2,0},{3,1},{4,2},{5,3},{6,4},{7,5},{8,14},{9,15},{10,... | collective-permute-start | bytes 2555912 | tf_op jit(solution)/shard_map/ppermute | solution.py:408
  852.0 63.9 %collective-permute-start.65 = (bf16[2,1024,2048]{2,1,0:T(8,128)(2,1)}, bf16[2,1024,2048]{2,1,0:T(8,128)(2,1)}, u32[]{:S(2)}, u32[]{:S(2)}) collective-permute-start(bf16[2,1024,2048]{2,1,0:T(8,128)(2,1)} %fusion.38), channel_id=1, source_target_pairs={{0,8},{1,9},{2,10},{3,11},{4,12},{5,13},{6,14},{7,15},{8,0},{9,1},... | collective-permute-start | bytes 25165832 | tf_op jit(solution)/shard_map/ppermute | solution.py:408
  888.3 74.2 %collective-permute-start.69 = (bf16[2,2048,1024]{2,1,0:T(8,128)(2,1)}, bf16[2,2048,1024]{2,1,0:T(8,128)(2,1)}, u32[]{:S(2)}, u32[]{:S(2)}) collective-permute-start(bf16[2,2048,1024]{2,1,0:T(8,128)(2,1)} %fusion.46), channel_id=1, source_target_pairs={{0,8},{1,9},{2,10},{3,11},{4,12},{5,13},{6,14},{7,15},{8,0},{9,1},... | collective-permute-start | bytes 25165832 | tf_op jit(solution)/shard_map/ppermute | solution.py:408
  911.0 75.9 %collective-permute-start.71 = (bf16[2,2048,1024]{2,1,0:T(8,128)(2,1)}, bf16[2,2048,1024]{2,1,0:T(8,128)(2,1)}, u32[]{:S(2)}, u32[]{:S(2)}) collective-permute-start(bf16[2,2048,1024]{2,1,0:T(8,128)(2,1)} %fusion.43.refs_0_), channel_id=1, source_target_pairs={{0,8},{1,9},{2,10},{3,11},{4,12},{5,13},{6,14},{7,15},{8,0},{9,1},... | collective-permute-start | bytes 25165832 | tf_op jit(solution)/shard_map/ppermute | solution.py:408
  913.7 25.9 %collective-permute-start.66 = (bf16[256,1664]{1,0:T(8,128)(2,1)S(1)}, bf16[256,1664]{1,0:T(8,128)(2,1)}, u32[]{:S(2)}, u32[]{:S(2)}) collective-permute-start(bf16[256,1664]{1,0:T(8,128)(2,1)S(1)} %add_convert_fusion), channel_id=1, source_target_pairs={{0,16},{1,17},{2,18},{3,19},{4,20},{5,21},{6,22},{7,23},{8,24},{9,... | collective-permute-start | bytes 2555912 | tf_op jit(solution)/shard_map/ppermute | solution.py:408
  (137 other events, 1969.2 us)
Sparse Core Ops, SparseCore 0:
  154.1 103.3 all-gather.2
  382.1 96.3 all-gather.4
  637.5 118.2 reduce-scatter.2
  783.8 91.4 reduce-scatter.4

commit v5 on v4

--- a/solution.py
+++ b/solution.py
@@ -414,8 +414,8 @@
 
 def gather_small(values, hold):
     low = jnp.stack([values, move(values, SHARD_SWAP[1])])
-    high = jnp.stack([low, move(low, SHARD_SWAP[2])])
-    both = jnp.stack([high, move(after(high, *hold), SHARD_SWAP[0])], axis=2)
+    high = jnp.stack([low, move(after(low, *hold), SHARD_SWAP[2])])
+    both = jnp.stack([high, move(high, SHARD_SWAP[0])], axis=2)
     return both.reshape((SHARDS,) + values.shape)
 
 
@@ -1258,7 +1258,7 @@
         return [own_part[1]]
 
     ffn_pieces = gather_rows(
-        ffn_low, early=(slots, shard_slots, columns, shard_columns), fill=fill_cot
+        ffn_low, fill=fill_cot
     )
     near_cot = made["cot"]
     ffn_own = after(flat(ffn_pieces), near_cot[1][1])

time: 1020 us -> 994 us (0.975)
  waiting for transfers between devices: 244 us -> 208 us
    ppermute x72, waiting for transfers between devices: 244 us -> 208 us  [move(): return lax.ppermute(values, AXES, moves)]
    unnamed x248 -> x256, local copies, waits for them, and re-layouts: 67.5 us -> 70.3 us
  transfers between devices with their start and end apart: 76 -> 76, of which waited for: 26 -> 23; matrix products, arithmetic and copies ran while one was open for 29% -> 30% of each run, Pallas kernels for 31% -> 32%
where the time goes in v5:
time: 994 us; the launch traced here: 984 us
  Pallas kernels  369 us (37%)
  waiting for transfers between devices  208 us (21%)
  local copies, waits for them, and re-layouts  120 us (12%)
  other arithmetic  107 us (11%)
  matrix products  98.5 us (10%)
  starting transfers between devices  64.9 us (7%)
  between operations  16 us (2%)
    ppermute x72, waiting for transfers between devices, move(): return lax.ppermute(values, AXES, moves)  208 us
    pallas_call x4, Pallas kernels, forward_part(): pl.pallas_call(ordered(forward_kernel, len(behind)), grid_spec=pltpu.Pref...  112 us
    pallas_call x4, Pallas kernels, cotangent_part(): pl.pallas_call(ordered(cotangent_kernel, len(behind)), grid_spec=pltpu.Pr...  76.3 us
    unnamed x256, local copies, waits for them, and re-layouts  70.3 us
    dot_general x3, matrix products, weight_grad(): jnp.einsum('ecd,ecf->edf', left, right, preferred_element_type=f32)  69.3 us
    ppermute x72, starting transfers between devices, move(): return lax.ppermute(values, AXES, moves)  64.4 us
    pallas_call x3, Pallas kernels, widen(): pl.pallas_call(ordered(widen_kernel, len(behind)), grid_spec=pltpu.Prefet...  51 us
    pallas_call x2, Pallas kernels, backward_part(): pl.pallas_call(ordered(backward_kernel, len(behind)), grid_spec=pltpu.Pre...  49.1 us
  transfers between devices with their start and end apart: 76, of which 23 were waited for; matrix products, arithmetic and copies ran while one was open for 30% of the time, Pallas kernels for 32%

profile of v5, /device:TPU:0, one launch (start us, length us, event | category | flops | bytes accessed | tf_op | source)
XLA Modules:
  0.0 983.9 jit_solution(10238666592336629012)
XLA Ops:
  28.0 14.7 %collective-permute-done.3 = bf16[2,33,256]{2,1,0:T(8,128)(2,1)S(1)} collective-permute-done((bf16[2,33,256]{2,1,0:T(8,128)(2,1)S(1)}, bf16[2,33,256]{2,1,0:T(8,128)(2,1)S(1)}, u32[]{:S(2)}, u32[]{:S(2)}) %collective-permute-start.3) | collective-permute-done | bytes 33824 | tf_op jit(solution)/shard_map/ppermute | solution.py:408
  62.9 25.0 %collective-permute-done.6 = bf16[256,1536]{1,0:T(8,128)(2,1)} collective-permute-done((bf16[256,1536]{1,0:T(8,128)(2,1)S(1)}, bf16[256,1536]{1,0:T(8,128)(2,1)}, u32[]{:S(2)}, u32[]{:S(2)}) %collective-permute-start.6) | collective-permute-done | bytes 786464 | tf_op jit(solution)/shard_map/ppermute | solution.py:408
  88.1 3.7 collective-permute-start.19
  92.7 15.8 %collective-permute-done.10 = bf16[2,168,256]{2,1,0:T(8,128)(2,1)S(1)} collective-permute-done((bf16[2,168,256]{2,1,0:T(8,128)(2,1)S(1)}, bf16[2,168,256]{2,1,0:T(8,128)(2,1)S(1)}, u32[]{:S(2)}, u32[]{:S(2)}) %collective-permute-start.10) | collective-permute-done | bytes 172064 | tf_op jit(solution)/shard_map/ppermute | solution.py:408
  113.4 6.2 collective-permute-done.11
  131.6 8.2 collective-permute-done.14
  146.6 4.6 fusion.35
  151.2 8.1 fusion.124.raw_ref.refs_0_
  170.0 10.2 %shard_map.240 = bf16[768,512]{1,0:T(8,128)(2,1)} custom-call(f32[768,1536]{1,0:T(8,128)} %copy-done.12, f32[768,2]{1,0:T(8,128)} %fusion.82.rate_ref.refs_1_, f32[2,512]{1,0:T(2,128)} %bitcast.348, f32[768,128]{1,0:T(8,128)} %get-tuple-element.268.cos_ref.refs_3_, f32[768,128]{1,0:T(8,128)} %get-tuple-element.267.sin_ref.refs_4_, ...), custom_call_target="tpu_custom_call" | custom-call | tf_op jit(solution)/shard_map/pallas_call | solution.py:1008
  190.0 3.9 collective-permute-done.17
  195.2 5.8 maximum_select_fusion
  206.1 16.8 %collective-permute-done.26 = bf16[192,2048]{1,0:T(8,128)(2,1)} collective-permute-done((bf16[192,2048]{1,0:T(8,128)(2,1)S(1)}, bf16[192,2048]{1,0:T(8,128)(2,1)}, u32[]{:S(2)}, u32[]{:S(2)}) %collective-permute-start.26) | collective-permute-done | bytes 786464 | tf_op jit(solution)/shard_map/ppermute | solution.py:408
  227.4 4.2 collective-permute-start.29
  233.7 4.4 convert_reduce_fusion.1
  241.4 30.2 %collective-permute-done.29 = bf16[192,2048]{1,0:T(8,128)(2,1)} collective-permute-done((bf16[192,2048]{1,0:T(8,128)(2,1)S(1)}, bf16[192,2048]{1,0:T(8,128)(2,1)}, u32[]{:S(2)}, u32[]{:S(2)}) %collective-permute-start.29) | collective-permute-done | bytes 786464 | tf_op jit(solution)/shard_map/ppermute | solution.py:408
  276.0 19.0 %shard_map.242 = (bf16[2,480,2048]{2,1,0:T(8,128)(2,1)}, f32[2,480,1024]{2,1,0:T(8,128)}) custom-call(s32[1]{0:T(128)} %bitcast.32.scalar_ref, bf16[192,2048]{1,0:T(8,128)(2,1)} %copy-done.40, s32[2,1,1536]{2,1,0:T(1,128)} %broadcast_in_dim_squeeze.25.refs_1_, bf16[1536,2048]{1,0:T(8,128)(2,1)} %all-gather.3.cloned.1.call-done.refs_2_, ...), custom_call_target="tpu_custom_call" | custom-call | flops 99999997952 | tf_op jit(solution)/shard_map/pallas_call | solution.py:650
  295.1 13.5 %collective-permute-done.32 = bf16[192,2048]{1,0:T(8,128)(2,1)S(1)} collective-permute-done((bf16[192,2048]{1,0:T(8,128)(2,1)S(1)}, bf16[192,2048]{1,0:T(8,128)(2,1)S(1)}, u32[]{:S(2)}, u32[]{:S(2)}) %collective-permute-start.32) | collective-permute-done | bytes 786464 | tf_op jit(solution)/shard_map/ppermute | solution.py:408
  316.3 11.1 %collective-permute-done.34 = bf16[192,2048]{1,0:T(8,128)(2,1)S(1)} collective-permute-done((bf16[192,2048]{1,0:T(8,128)(2,1)S(1)}, bf16[192,2048]{1,0:T(8,128)(2,1)S(1)}, u32[]{:S(2)}, u32[]{:S(2)}) %collective-permute-start.34) | collective-permute-done | bytes 786464 | tf_op jit(solution)/shard_map/ppermute | solution.py:408
  330.3 19.1 %shard_map.243 = (bf16[2,480,2048]{2,1,0:T(8,128)(2,1)}, f32[2,480,1024]{2,1,0:T(8,128)}) custom-call(s32[1]{0:T(128)} %bitcast.32.scalar_ref, f32[2,480,1024]{2,1,0:T(8,128)} %get-tuple-element.107.refs_0_.refs_5_, s32[2,1,1536]{2,1,0:T(1,128)} %broadcast_in_dim_squeeze.26.refs_1_, bf16[1536,2048]{1,0:T(8,128)(2,1)} %collective-permute-done.36.refs_2_, ...), custom_call_target="tpu_custom_call" | custom-call | flops 99999997952 | tf_op jit(solution)/shard_map/pallas_call | solution.py:650
  366.8 28.4 %shard_map.244 = (bf16[2,480,2048]{2,1,0:T(8,128)(2,1)}, bf16[2,480,1024]{2,1,0:T(8,128)(2,1)}, bf16[2,480,1024]{2,1,0:T(8,128)(2,1)}, bf16[2,480,1024]{2,1,0:T(8,128)(2,1)}, bf16[2,480,128]{2,1,0:T(8,128)(2,1)}) custom-call(s32[2]{0:T(128)} %pad_add_fusion.scalar_ref, s32[2,1,1536]{2,1,0:T(1,128)} %broadcast_in_dim_squeeze.24.refs_0_, ...), custom_call_target="tpu_custom_call" | custom-call | tf_op jit(solution)/shard_map/pallas_call | solution.py:735
  395.2 27.8 %shard_map.245 = (bf16[2,480,2048]{2,1,0:T(8,128)(2,1)}, bf16[2,480,1024]{2,1,0:T(8,128)(2,1)}, bf16[2,480,1024]{2,1,0:T(8,128)(2,1)}, bf16[2,480,1024]{2,1,0:T(8,128)(2,1)}, bf16[2,480,128]{2,1,0:T(8,128)(2,1)}) custom-call(s32[2]{0:T(128)} %pad_add_fusion.scalar_ref, bf16[2,480,1024]{2,1,0:T(8,128)(2,1)} %get-tuple-element.111.refs_0_.refs_2_, ...), custom_call_target="tpu_custom_call" | custom-call | tf_op jit(solution)/shard_map/pallas_call | solution.py:735
  423.0 24.6 %shard_map.246 = bf16[1536,2176]{1,0:T(8,128)(2,1)} custom-call(s32[1]{0:T(128)} %bitcast.32.scalar_ref, bf16[384,2048]{1,0:T(8,128)(2,1)} %collective-permute-done.28.refs_0_, bf16[384,2048]{1,0:T(8,128)(2,1)} %collective-permute-done.31.refs_1_, s32[1536,2]{1,0:T(8,128)} %get-tuple-element.249.refs_2_, bf16[2,480,1024]{2,1,0:T(8,128)(2,1)} %get-tuple-element.112.refs_3_, ...), custom_call_target="tpu_custom_call" | custom-call | tf_op jit(solution)/shard_map/pallas_call | solution.py:809
  452.9 24.4 %shard_map.247 = bf16[1536,2176]{1,0:T(8,128)(2,1)} custom-call(s32[1]{0:T(128)} %bitcast.32.scalar_ref, bf16[8,192,2176]{2,1,0:T(8,128)(2,1)} %bitcast.297, s32[1536,2]{1,0:T(8,128)} %get-tuple-element.248.refs_1_, bf16[2,480,1024]{2,1,0:T(8,128)(2,1)} %get-tuple-element.115.refs_2_, bf16[2,480,1024]{2,1,0:T(8,128)(2,1)} %get-tuple-element.116.refs_3_, ...), custom_call_target="tpu_custom_call" | custom-call | tf_op jit(solution)/shard_map/pallas_call | solution.py:809
  482.4 4.8 collective-permute-done.40.refs_1_
  487.3 17.0 %shard_map.248 = bf16[1536,2048]{1,0:T(8,128)(2,1)} custom-call(s32[1]{0:T(128)} %bitcast.32.scalar_ref, bf16[192,2176]{1,0:T(8,128)(2,1)} %fusion.60.refs_0_, bf16[384,2048]{1,0:T(8,128)(2,1)} %collective-permute-done.40.refs_1_, bf16[1536,2048]{1,0:T(8,128)(2,1)} %all-gather.5.cloned.1.call-done.refs_2_, s32[1536,2]{1,0:T(8,128)} %get-tuple-element.247.refs_3_, ...), custom_call_target="tpu_custom_call" | custom-call | flops 99999997952 | tf_op jit(solution)/shard_map/pallas_call | solution.py:871
  512.6 12.9 %collective-permute-done.39 = bf16[192,2176]{1,0:T(8,128)(2,1)} collective-permute-done((bf16[192,2176]{1,0:T(8,128)(2,1)S(1)}, bf16[192,2176]{1,0:T(8,128)(2,1)}, u32[]{:S(2)}, u32[]{:S(2)}) %collective-permute-start.39) | collective-permute-done | bytes 835616 | tf_op jit(solution)/shard_map/ppermute | solution.py:408
  525.5 3.6 fusion.56
  529.6 17.2 %shard_map.249 = bf16[1536,2048]{1,0:T(8,128)(2,1)} custom-call(s32[1]{0:T(128)} %bitcast.32.scalar_ref, bf16[192,2176]{1,0:T(8,128)(2,1)} %get-tuple-element.233.refs_0_, s32[1536,2]{1,0:T(8,128)} %get-tuple-element.246.refs_1_, bf16[2,480,1024]{2,1,0:T(8,128)(2,1)} %get-tuple-element.111.refs_0_.refs_2_, bf16[4,1024,2048]{2,1,0:T(8,128)(2,1)} %refs_3_.11, ...), custom_call_target="tpu_custom_call" | custom-call | flops 99999997952 | tf_op jit(solution)/shard_map/pallas_call | solution.py:871
  554.1 19.1 %shard_map.250 = (bf16[2,480,2048]{2,1,0:T(8,128)(2,1)}, f32[2,480,1024]{2,1,0:T(8,128)}) custom-call(s32[1]{0:T(128)} %bitcast.32.scalar_ref, bf16[192,2176]{1,0:T(8,128)(2,1)} %get-tuple-element.230.refs_0_, s32[2,1,1536]{2,1,0:T(1,128)} %broadcast_in_dim_squeeze.28.refs_1_, bf16[1536,2048]{1,0:T(8,128)(2,1)} %all-gather.5.cloned.1.call-done.refs_2_, ...), custom_call_target="tpu_custom_call" | custom-call | flops 99999997952 | tf_op jit(solution)/shard_map/pallas_call | solution.py:650
  576.1 3.8 collective-permute-start.48
  580.0 19.2 %shard_map.251 = (bf16[2,480,2048]{2,1,0:T(8,128)(2,1)}, f32[2,480,1024]{2,1,0:T(8,128)}) custom-call(s32[1]{0:T(128)} %bitcast.32.scalar_ref, bf16[192,2176]{1,0:T(8,128)(2,1)} %copy-done.63, s32[2,1,1536]{2,1,0:T(1,128)} %broadcast_in_dim_squeeze.29.refs_1_, bf16[1536,2048]{1,0:T(8,128)(2,1)} %collective-permute-done.45.refs_2_, ...), custom_call_target="tpu_custom_call" | custom-call | flops 99999997952 | tf_op jit(solution)/shard_map/pallas_call | solution.py:650
  599.2 4.4 collective-permute-done.48
  620.3 9.5 collective-permute-done.49
  638.6 20.1 %shard_map.253 = (f32[768,1024]{1,0:T(8,128)}, bf16[768,512]{1,0:T(8,128)(2,1)}, f32[768,2]{1,0:T(8,128)}, f32[4,2,512]{2,1,0:T(2,128)}) custom-call(f32[768,1536]{1,0:T(8,128)} %copy-done.12, f32[768,2]{1,0:T(8,128)} %fusion.82.rate_ref.refs_1_, f32[2,512]{1,0:T(2,128)} %bitcast.349, f32[768,128]{1,0:T(8,128)} %get-tuple-element.268.cos_ref.refs_3_, ...), custom_call_target="tpu_custom_call" | custom-call | tf_op jit(solution)/shard_map/pallas_call | solution.py:1028
  667.1 6.5 shard_map.254
  673.5 8.1 fusion.117
  691.5 5.4 convolution_convert_fusion
  720.9 28.0 %shard_map.255 = (bf16[2,480,2048]{2,1,0:T(8,128)(2,1)}, bf16[2,480,1024]{2,1,0:T(8,128)(2,1)}, bf16[2,480,1024]{2,1,0:T(8,128)(2,1)}, bf16[2,480,1024]{2,1,0:T(8,128)(2,1)}, bf16[2,480,128]{2,1,0:T(8,128)(2,1)}) custom-call(s32[2]{0:T(128)} %pad_add_fusion.scalar_ref, bf16[256,1664]{1,0:T(8,128)(2,1)} %pad_maximum_fusion.24.refs_0_, ...), custom_call_target="tpu_custom_call" | custom-call | flops 99999997952 | tf_op jit(solution)/shard_map/pallas_call | solution.py:735
  754.6 27.8 %shard_map.256 = (bf16[2,480,2048]{2,1,0:T(8,128)(2,1)}, bf16[2,480,1024]{2,1,0:T(8,128)(2,1)}, bf16[2,480,1024]{2,1,0:T(8,128)(2,1)}, bf16[2,480,1024]{2,1,0:T(8,128)(2,1)}, bf16[2,480,128]{2,1,0:T(8,128)(2,1)}) custom-call(s32[2]{0:T(128)} %pad_add_fusion.scalar_ref, bf16[256,1664]{1,0:T(8,128)(2,1)} %add_convert_fusion.4.refs_0_, ...), custom_call_target="tpu_custom_call" | custom-call | flops 99999997952 | tf_op jit(solution)/shard_map/pallas_call | solution.py:735
  782.5 23.3 %fusion.38 = bf16[2,1024,2048]{2,1,0:T(8,128)(2,1)} fusion(bf16[2,480,2048]{2,1,0:T(8,128)(2,1)} %get-tuple-element.145, bf16[2,480,2048]{2,1,0:T(8,128)(2,1)} %get-tuple-element.144, bf16[2,480,2048]{2,1,0:T(8,128)(2,1)} %get-tuple-element.143, bf16[2,480,2048]{2,1,0:T(8,128)(2,1)} %get-tuple-element.142, bf16[2,480,1024]{2,1,0:T(8,128)(2,1)} %get-tuple-element.141, ...), kind=kOutput, calls=%fused_computation.57 | convolution fusion | flops 16204693504 | bytes 31981568 | tf_op jit(solution)/shard_map/ecd,ecf->edf/dot_general | solution.py:1390
  811.8 7.7 collective-permute-done.63
  822.7 23.3 %fusion.46 = bf16[2,2048,1024]{2,1,0:T(8,128)(2,1)} fusion(bf16[2,480,1024]{2,1,0:T(8,128)(2,1)} %get-tuple-element.154, bf16[2,480,1024]{2,1,0:T(8,128)(2,1)} %get-tuple-element.153, bf16[2,480,1024]{2,1,0:T(8,128)(2,1)} %get-tuple-element.112.refs_3_, bf16[2,480,1024]{2,1,0:T(8,128)(2,1)} %get-tuple-element.115.refs_2_, ...), kind=kOutput, calls=%fused_computation.59 | convolution fusion | flops 16204693504 | bytes 31981568 | tf_op jit(solution)/shard_map/ecd,ecf->edf/dot_general | solution.py:1390
  846.1 13.2 %collective-permute-done.64 = bf16[256,1664]{1,0:T(8,128)(2,1)} collective-permute-done((bf16[256,1664]{1,0:T(8,128)(2,1)}, bf16[256,1664]{1,0:T(8,128)(2,1)}, u32[]{:S(2)}, u32[]{:S(2)}) %collective-permute-start.64) | collective-permute-done | bytes 852000 | tf_op jit(solution)/shard_map/ppermute | solution.py:408
  859.3 22.7 %fusion.43.refs_0_ = bf16[2,2048,1024]{2,1,0:T(8,128)(2,1)} fusion(bf16[2,480,1024]{2,1,0:T(8,128)(2,1)} %get-tuple-element.147, bf16[2,480,1024]{2,1,0:T(8,128)(2,1)} %get-tuple-element.138.refs_1_, bf16[2,480,1024]{2,1,0:T(8,128)(2,1)} %get-tuple-element.113.refs_4_, bf16[2,480,1024]{2,1,0:T(8,128)(2,1)S(1)} %copy-done.55, ...), kind=kOutput, calls=%fused_computation.58 | convolution fusion | flops 16204693504 | bytes 31981568 | tf_op jit(solution)/shard_map/ecd,ecf->edf/dot_general | solution.py:1390
  893.9 16.9 %shard_map.257 = f32[4096,2048]{1,0:T(8,128)} custom-call(s32[1]{0:T(128)} %bitcast.32.scalar_ref, bf16[2,2048,1024]{2,1,0:T(8,128)(2,1)S(1)} %copy-done.2, bf16[2048,2048]{1,0:T(8,128)(2,1)S(1)} %bitcast.287, bf16[2048,2048]{1,0:T(8,128)(2,1)} %bitcast.89.refs_2_), custom_call_target="tpu_custom_call" | custom-call | tf_op jit(solution)/shard_map/pallas_call | solution.py:591
  937.2 17.0 %shard_map.259 = f32[8192,1024]{1,0:T(8,128)} custom-call(s32[1]{0:T(128)} %bitcast.32.scalar_ref, f32[4,1024,2048]{2,1,0:T(8,128)} %bitcast.293, bf16[64,2048]{1,0:T(8,128)(2,1)S(1)} %collective-permute-done.68.refs_1_, bf16[4096,1024]{1,0:T(8,128)(2,1)S(1)} %bitcast.286, bf16[4096,1024]{1,0:T(8,128)(2,1)} %bitcast.100.refs_3_), custom_call_target="tpu_custom_call" | custom-call | tf_op jit(solution)/shard_map/pallas_call | solution.py:591
  954.2 4.0 shard_map.260
  959.9 17.0 %shard_map.261 = f32[8192,1024]{1,0:T(8,128)} custom-call(s32[1]{0:T(128)} %bitcast.32.scalar_ref, f32[4,2048,1024]{2,1,0:T(8,128)} %bitcast.291, bf16[4096,1024]{1,0:T(8,128)(2,1)S(1)} %bitcast.281, bf16[4096,1024]{1,0:T(8,128)(2,1)} %bitcast.111.refs_2_), custom_call_target="tpu_custom_call" | custom-call | tf_op jit(solution)/shard_map/pallas_call | solution.py:591
  (622 shorter events, 285.6 us)
Async XLA Ops:
  7.2 268.8 %all-gather.3.cloned.1.call-start = ((), (), s32[]{:S(2)}) async-start(), calls=%async_computation.2 | async-start | bytes 7077888 | tf_op jit(solution)/shard_map/all_gather | solution.py:1161
  9.7 49.0 %collective-permute-start.13 = (bf16[256,1536]{1,0:T(8,128)(2,1)S(1)}, bf16[256,1536]{1,0:T(8,128)(2,1)}, u32[]{:S(2)}, u32[]{:S(2)}) collective-permute-start(bf16[256,1536]{1,0:T(8,128)(2,1)S(1)} %shard_map.239), channel_id=1, source_target_pairs={{0,1},{1,0},{2,3},{3,2},{4,5},{5,4},{6,7},{7,6},{8,9},{9,8},{10,11... | collective-permute-start | bytes 2359304 | tf_op jit(solution)/shard_map/ppermute | solution.py:408
  12.8 41.4 %collective-permute-start.8 = (bf16[256,1536]{1,0:T(8,128)(2,1)S(1)}, bf16[256,1536]{1,0:T(8,128)(2,1)}, u32[]{:S(2)}, u32[]{:S(2)}) collective-permute-start(bf16[256,1536]{1,0:T(8,128)(2,1)S(1)} %shard_map.239), channel_id=1, source_target_pairs={{0,2},{1,3},{2,4},{3,5},{4,6},{5,7},{6,0},{7,1},{8,10},{9,11},{10,... | collective-permute-start | bytes 2359304 | tf_op jit(solution)/shard_map/ppermute | solution.py:408
  14.3 36.4 %collective-permute-start.5 = (bf16[256,1536]{1,0:T(8,128)(2,1)S(1)}, bf16[256,1536]{1,0:T(8,128)(2,1)}, u32[]{:S(2)}, u32[]{:S(2)}) collective-permute-start(bf16[256,1536]{1,0:T(8,128)(2,1)S(1)} %shard_map.239), channel_id=1, source_target_pairs={{0,6},{1,7},{2,0},{3,1},{4,2},{5,3},{6,4},{7,5},{8,14},{9,15},{10,... | collective-permute-start | bytes 2359304 | tf_op jit(solution)/shard_map/ppermute | solution.py:408
  21.9 30.4 %collective-permute-start = (bf16[192,2048]{1,0:T(8,128)(2,1)S(1)}, bf16[192,2048]{1,0:T(8,128)(2,1)}, u32[]{:S(2)}, u32[]{:S(2)}) collective-permute-start(bf16[192,2048]{1,0:T(8,128)(2,1)S(1)} %copy-done.16), channel_id=1, source_target_pairs={{0,16},{1,17},{2,18},{3,19},{4,20},{5,21},{6,22},{7,23},{8,24},{9,... | collective-permute-start | bytes 2359304 | tf_op jit(solution)/shard_map/ppermute | solution.py:408
  50.8 100.4 %collective-permute-start.12 = (bf16[192,2048]{1,0:T(8,128)(2,1)S(1)}, bf16[192,2048]{1,0:T(8,128)(2,1)}, u32[]{:S(2)}, u32[]{:S(2)}) collective-permute-start(bf16[192,2048]{1,0:T(8,128)(2,1)S(1)} %copy-done.32), channel_id=1, source_target_pairs={{0,16},{1,17},{2,18},{3,19},{4,20},{5,21},{6,22},{7,23},{8,24},{9,... | collective-permute-start | bytes 2359304 | tf_op jit(solution)/shard_map/ppermute | solution.py:408
  52.2 35.7 %collective-permute-start.6 = (bf16[256,1536]{1,0:T(8,128)(2,1)S(1)}, bf16[256,1536]{1,0:T(8,128)(2,1)}, u32[]{:S(2)}, u32[]{:S(2)}) collective-permute-start(bf16[256,1536]{1,0:T(8,128)(2,1)S(1)} %shard_map.239), channel_id=1, source_target_pairs={{0,4},{1,5},{2,6},{3,7},{4,0},{5,1},{6,2},{7,3},{8,12},{9,13},{10,... | collective-permute-start | bytes 2359304 | tf_op jit(solution)/shard_map/ppermute | solution.py:408
  53.6 38.1 %collective-permute-start.7 = (bf16[256,1536]{1,0:T(8,128)(2,1)}, bf16[256,1536]{1,0:T(8,128)(2,1)S(1)}, u32[]{:S(2)}, u32[]{:S(2)}) collective-permute-start(bf16[256,1536]{1,0:T(8,128)(2,1)} %collective-permute-done.5), channel_id=1, source_target_pairs={{0,1},{1,0},{2,3},{3,2},{4,5},{5,4},{6,7},{7,6},{8,9},{9,8},{10,11... | collective-permute-start | bytes 2359304 | tf_op jit(solution)/shard_map/ppermute | solution.py:408
  54.1 34.0 %collective-permute-start.9 = (bf16[256,1536]{1,0:T(8,128)(2,1)}, bf16[256,1536]{1,0:T(8,128)(2,1)S(1)}, u32[]{:S(2)}, u32[]{:S(2)}) collective-permute-start(bf16[256,1536]{1,0:T(8,128)(2,1)} %collective-permute-done.8), channel_id=1, source_target_pairs={{0,1},{1,0},{2,3},{3,2},{4,5},{5,4},{6,7},{7,6},{8,9},{9,8},{10,11... | collective-permute-start | bytes 2359304 | tf_op jit(solution)/shard_map/ppermute | solution.py:408
  58.7 66.8 %collective-permute-start.1 = (bf16[2,192,2048]{2,1,0:T(8,128)(2,1)}, bf16[2,192,2048]{2,1,0:T(8,128)(2,1)}, u32[]{:S(2)}, u32[]{:S(2)}) collective-permute-start(bf16[2,192,2048]{2,1,0:T(8,128)(2,1)} %get-tuple-element.251), channel_id=1, source_target_pairs={{0,8},{1,9},{2,10},{3,11},{4,12},{5,13},{6,14},{7,15},{8,0},{9,1},... | collective-permute-start | bytes 4718600 | tf_op jit(solution)/shard_map/ppermute | solution.py:408
  87.9 74.6 %collective-permute-start.23 = (bf16[64,2048]{1,0:T(8,128)(2,1)S(1)}, bf16[64,2048]{1,0:T(8,128)(2,1)}, u32[]{:S(2)}, u32[]{:S(2)}) collective-permute-start(bf16[64,2048]{1,0:T(8,128)(2,1)S(1)} %copy-done.59), channel_id=1, source_target_pairs={{0,2},{1,3},{2,4},{3,5},{4,6},{5,7},{6,0},{7,1},{8,10},{9,11},{10,... | collective-permute-start | bytes 786440 | tf_op jit(solution)/shard_map/ppermute | solution.py:408
  88.1 23.8 %collective-permute-start.19 = (bf16[64,2048]{1,0:T(8,128)(2,1)S(1)}, bf16[64,2048]{1,0:T(8,128)(2,1)S(1)}, u32[]{:S(2)}, u32[]{:S(2)}) collective-permute-start(bf16[64,2048]{1,0:T(8,128)(2,1)S(1)} %copy-done.59), channel_id=1, source_target_pairs={{0,6},{1,7},{2,0},{3,1},{4,2},{5,3},{6,4},{7,5},{8,14},{9,15},{10,... | collective-permute-start | bytes 786440 | tf_op jit(solution)/shard_map/ppermute | solution.py:408
  111.9 68.3 %collective-permute-start.18 = (bf16[64,2048]{1,0:T(8,128)(2,1)S(1)}, bf16[64,2048]{1,0:T(8,128)(2,1)}, u32[]{:S(2)}, u32[]{:S(2)}) collective-permute-start(bf16[64,2048]{1,0:T(8,128)(2,1)S(1)} %copy-done.59), channel_id=1, source_target_pairs={{0,1},{1,0},{2,3},{3,2},{4,5},{5,4},{6,7},{7,6},{8,9},{9,8},{10,11... | collective-permute-start | bytes 786440 | tf_op jit(solution)/shard_map/ppermute | solution.py:408
  125.5 37.0 %collective-permute-start.21 = (bf16[64,2048]{1,0:T(8,128)(2,1)S(1)}, bf16[64,2048]{1,0:T(8,128)(2,1)}, u32[]{:S(2)}, u32[]{:S(2)}) collective-permute-start(bf16[64,2048]{1,0:T(8,128)(2,1)S(1)} %copy-done.59), channel_id=1, source_target_pairs={{0,4},{1,5},{2,6},{3,7},{4,0},{5,1},{6,2},{7,3},{8,12},{9,13},{10,... | collective-permute-start | bytes 786440 | tf_op jit(solution)/shard_map/ppermute | solution.py:408
  143.7 343.6 %all-gather.5.cloned.1.call-start = ((), (), s32[]{:S(2)}) async-start(), calls=%async_computation.3 | async-start | bytes 7077888 | tf_op jit(solution)/shard_map/all_gather | solution.py:1267
  227.4 47.2 %collective-permute-start.33 = (bf16[192,2048]{1,0:T(8,128)(2,1)S(1)}, bf16[192,2048]{1,0:T(8,128)(2,1)S(1)}, u32[]{:S(2)}, u32[]{:S(2)}) collective-permute-start(bf16[192,2048]{1,0:T(8,128)(2,1)S(1)} %get-tuple-element.105), channel_id=1, source_target_pairs={{0,2},{1,3},{2,4},{3,5},{4,6},{5,7},{6,0},{7,1},{8,10},{9,11},{10,... | collective-permute-start | bytes 2359304 | tf_op jit(solution)/shard_map/ppermute | solution.py:408
  227.4 44.2 %collective-permute-start.29 = (bf16[192,2048]{1,0:T(8,128)(2,1)S(1)}, bf16[192,2048]{1,0:T(8,128)(2,1)}, u32[]{:S(2)}, u32[]{:S(2)}) collective-permute-start(bf16[192,2048]{1,0:T(8,128)(2,1)S(1)} %get-tuple-element.105), channel_id=1, source_target_pairs={{0,6},{1,7},{2,0},{3,1},{4,2},{5,3},{6,4},{7,5},{8,14},{9,15},{10,... | collective-permute-start | bytes 2359304 | tf_op jit(solution)/shard_map/ppermute | solution.py:408
  231.6 77.4 %collective-permute-start.27 = (bf16[192,2048]{1,0:T(8,128)(2,1)S(1)}, bf16[192,2048]{1,0:T(8,128)(2,1)}, u32[]{:S(2)}, u32[]{:S(2)}) collective-permute-start(bf16[192,2048]{1,0:T(8,128)(2,1)S(1)} %get-tuple-element.105), channel_id=1, source_target_pairs={{0,1},{1,0},{2,3},{3,2},{4,5},{5,4},{6,7},{7,6},{8,9},{9,8},{10,11... | collective-permute-start | bytes 2359304 | tf_op jit(solution)/shard_map/ppermute | solution.py:408
  271.5 37.1 %collective-permute-start.32 = (bf16[192,2048]{1,0:T(8,128)(2,1)S(1)}, bf16[192,2048]{1,0:T(8,128)(2,1)S(1)}, u32[]{:S(2)}, u32[]{:S(2)}) collective-permute-start(bf16[192,2048]{1,0:T(8,128)(2,1)S(1)} %get-tuple-element.105), channel_id=1, source_target_pairs={{0,4},{1,5},{2,6},{3,7},{4,0},{5,1},{6,2},{7,3},{8,12},{9,13},{10,... | collective-permute-start | bytes 2359304 | tf_op jit(solution)/shard_map/ppermute | solution.py:408
  274.0 39.3 %collective-permute-start.30 = (bf16[192,2048]{1,0:T(8,128)(2,1)}, bf16[192,2048]{1,0:T(8,128)(2,1)}, u32[]{:S(2)}, u32[]{:S(2)}) collective-permute-start(bf16[192,2048]{1,0:T(8,128)(2,1)} %collective-permute-done.29), channel_id=1, source_target_pairs={{0,1},{1,0},{2,3},{3,2},{4,5},{5,4},{6,7},{7,6},{8,9},{9,8},{10,11... | collective-permute-start | bytes 2359304 | tf_op jit(solution)/shard_map/ppermute | solution.py:408
  274.6 54.7 %collective-permute-start.35 = (bf16[192,2048]{1,0:T(8,128)(2,1)S(1)}, bf16[192,2048]{1,0:T(8,128)(2,1)S(1)}, u32[]{:S(2)}, u32[]{:S(2)}) collective-permute-start(bf16[192,2048]{1,0:T(8,128)(2,1)S(1)} %collective-permute-done.33.refs_0_), channel_id=1, source_target_pairs={{0,1},{1,0},{2,3},{3,2},{4,5},{5,4},{6,7},{7,6},{8,9},{9,8},{10,11... | collective-permute-start | bytes 2359304 | tf_op jit(solution)/shard_map/ppermute | solution.py:408
  276.0 54.3 %collective-permute-start.36 = (bf16[1536,2048]{1,0:T(8,128)(2,1)}, bf16[1536,2048]{1,0:T(8,128)(2,1)}, u32[]{:S(2)}, u32[]{:S(2)}) collective-permute-start(bf16[1536,2048]{1,0:T(8,128)(2,1)} %all-gather.3.cloned.1.call-done.refs_2_), channel_id=1, source_target_pairs={{0,8},{1,9},{2,10},{3,11},{4,12},{5,13},{6,14},{7,15},{8,0},{9,1},... | collective-permute-start | bytes 18874376 | tf_op jit(solution)/shard_map/ppermute | solution.py:408
  349.4 45.8 %collective-permute-start.37 = (bf16[1536,2048]{1,0:T(8,128)(2,1)}, bf16[1536,2048]{1,0:T(8,128)(2,1)}, u32[]{:S(2)}, u32[]{:S(2)}) collective-permute-start(bf16[1536,2048]{1,0:T(8,128)(2,1)} %constant_dynamic-update-slice_fusion.18.refs_1_), channel_id=1, source_target_pairs={{0,8},{1,9},{2,10},{3,11},{4,12},{5,13},{6,14},{7,15},{8,0},{9,1},... | collective-permute-start | bytes 18874376 | tf_op jit(solution)/shard_map/ppermute | solution.py:408
  349.4 405.2 %reduce-scatter.3.cloned.1.call-start = ((), (), s32[]{:S(2)}) async-start(), calls=%async_computation.4 | async-start | bytes 7077888 | tf_op jit(solution)/shard_map/reduce_scatter | solution.py:1309
  352.2 70.8 %collective-permute-start.28 = (bf16[384,2048]{1,0:T(8,128)(2,1)}, bf16[384,2048]{1,0:T(8,128)(2,1)}, u32[]{:S(2)}, u32[]{:S(2)}) collective-permute-start(bf16[384,2048]{1,0:T(8,128)(2,1)} %pad_maximum_fusion.16), channel_id=1, source_target_pairs={{0,16},{1,17},{2,18},{3,19},{4,20},{5,21},{6,22},{7,23},{8,24},{9,... | collective-permute-start | bytes 4718600 | tf_op jit(solution)/shard_map/ppermute | solution.py:408
  356.3 66.7 %collective-permute-start.31 = (bf16[384,2048]{1,0:T(8,128)(2,1)}, bf16[384,2048]{1,0:T(8,128)(2,1)}, u32[]{:S(2)}, u32[]{:S(2)}) collective-permute-start(bf16[384,2048]{1,0:T(8,128)(2,1)} %pad_maximum_fusion.17), channel_id=1, source_target_pairs={{0,16},{1,17},{2,18},{3,19},{4,20},{5,21},{6,22},{7,23},{8,24},{9,... | collective-permute-start | bytes 4718600 | tf_op jit(solution)/shard_map/ppermute | solution.py:408
  447.7 29.7 %collective-permute-start.38 = (bf16[8,192,2176]{2,1,0:T(8,128)(2,1)}, bf16[8,192,2176]{2,1,0:T(8,128)(2,1)S(1)}, u32[]{:S(2)}, u32[]{:S(2)}) collective-permute-start(bf16[8,192,2176]{2,1,0:T(8,128)(2,1)} %bitcast.296), channel_id=1, source_target_pairs={{0,8},{1,9},{2,10},{3,11},{4,12},{5,13},{6,14},{7,15},{8,0},{9,1},... | collective-permute-start | bytes 20054024 | tf_op jit(solution)/shard_map/ppermute | solution.py:408
  450.3 37.0 %collective-permute-start.40 = (bf16[384,2048]{1,0:T(8,128)(2,1)}, bf16[384,2048]{1,0:T(8,128)(2,1)}, u32[]{:S(2)}, u32[]{:S(2)}) collective-permute-start(bf16[384,2048]{1,0:T(8,128)(2,1)} %pad_maximum_fusion.18), channel_id=1, source_target_pairs={{0,16},{1,17},{2,18},{3,19},{4,20},{5,21},{6,22},{7,23},{8,24},{9,... | collective-permute-start | bytes 4718600 | tf_op jit(solution)/shard_map/ppermute | solution.py:408
  504.4 25.2 %collective-permute-start.41 = (bf16[1536,2048]{1,0:T(8,128)(2,1)}, bf16[1536,2048]{1,0:T(8,128)(2,1)}, u32[]{:S(2)}, u32[]{:S(2)}) collective-permute-start(bf16[1536,2048]{1,0:T(8,128)(2,1)} %shard_map.248), channel_id=1, source_target_pairs={{0,8},{1,9},{2,10},{3,11},{4,12},{5,13},{6,14},{7,15},{8,0},{9,1},... | collective-permute-start | bytes 18874376 | tf_op jit(solution)/shard_map/ppermute | solution.py:408
  510.9 95.4 %collective-permute-start.53 = (bf16[384,2048]{1,0:T(8,128)(2,1)}, bf16[384,2048]{1,0:T(8,128)(2,1)}, u32[]{:S(2)}, u32[]{:S(2)}) collective-permute-start(bf16[384,2048]{1,0:T(8,128)(2,1)} %pad_maximum_fusion.20), channel_id=1, source_target_pairs={{0,16},{1,17},{2,18},{3,19},{4,20},{5,21},{6,22},{7,23},{8,24},{9,... | collective-permute-start | bytes 4718600 | tf_op jit(solution)/shard_map/ppermute | solution.py:408
  529.4 69.8 %collective-permute-start.46 = (bf16[192,2176]{1,0:T(8,128)(2,1)}, bf16[192,2176]{1,0:T(8,128)(2,1)}, u32[]{:S(2)}, u32[]{:S(2)}) collective-permute-start(bf16[192,2176]{1,0:T(8,128)(2,1)} %get-tuple-element.233.refs_0_), channel_id=1, source_target_pairs={{0,4},{1,5},{2,6},{3,7},{4,0},{5,1},{6,2},{7,3},{8,12},{9,13},{10,... | collective-permute-start | bytes 2506760 | tf_op jit(solution)/shard_map/ppermute | solution.py:408
  552.9 46.3 %collective-permute-start.47 = (bf16[192,2176]{1,0:T(8,128)(2,1)}, bf16[192,2176]{1,0:T(8,128)(2,1)}, u32[]{:S(2)}, u32[]{:S(2)}) collective-permute-start(bf16[192,2176]{1,0:T(8,128)(2,1)} %get-tuple-element.230.refs_0_), channel_id=1, source_target_pairs={{0,2},{1,3},{2,4},{3,5},{4,6},{5,7},{6,0},{7,1},{8,10},{9,11},{10,... | collective-permute-start | bytes 2506760 | tf_op jit(solution)/shard_map/ppermute | solution.py:408
  576.1 27.5 %collective-permute-start.48 = (bf16[192,2176]{1,0:T(8,128)(2,1)S(1)}, bf16[192,2176]{1,0:T(8,128)(2,1)S(1)}, u32[]{:S(2)}, u32[]{:S(2)}) collective-permute-start(bf16[192,2176]{1,0:T(8,128)(2,1)S(1)} %get-tuple-element.229.refs_0_), channel_id=1, source_target_pairs={{0,6},{1,7},{2,0},{3,1},{4,2},{5,3},{6,4},{7,5},{8,14},{9,15},{10,... | collective-permute-start | bytes 2506760 | tf_op jit(solution)/shard_map/ppermute | solution.py:408
  606.4 252.9 %reduce-scatter.5.cloned.1.call-start = ((), (), s32[]{:S(2)}) async-start(), calls=%async_computation.5 | async-start | bytes 2359296 | tf_op jit(solution)/shard_map/reduce_scatter | solution.py:1399
  637.0 83.9 %collective-permute-start.54 = (bf16[1536,2048]{1,0:T(8,128)(2,1)}, bf16[1536,2048]{1,0:T(8,128)(2,1)}, u32[]{:S(2)}, u32[]{:S(2)}) collective-permute-start(bf16[1536,2048]{1,0:T(8,128)(2,1)} %constant_dynamic-update-slice_fusion.26.refs_3_), channel_id=1, source_target_pairs={{0,8},{1,9},{2,10},{3,11},{4,12},{5,13},{6,14},{7,15},{8,0},{9,1},... | collective-permute-start | bytes 18874376 | tf_op jit(solution)/shard_map/ppermute | solution.py:408
  683.0 25.4 %collective-permute-start.56 = (bf16[2,192,2048]{2,1,0:T(8,128)(2,1)}, bf16[2,192,2048]{2,1,0:T(8,128)(2,1)}, u32[]{:S(2)}, u32[]{:S(2)}) collective-permute-start(bf16[2,192,2048]{2,1,0:T(8,128)(2,1)} %slice_bitcast_fusion), channel_id=1, source_target_pairs={{0,8},{1,9},{2,10},{3,11},{4,12},{5,13},{6,14},{7,15},{8,0},{9,1},... | collective-permute-start | bytes 4718600 | tf_op jit(solution)/shard_map/ppermute | solution.py:408
  703.9 45.0 %collective-permute-start.55 = (bf16[256,1664]{1,0:T(8,128)(2,1)}, bf16[256,1664]{1,0:T(8,128)(2,1)}, u32[]{:S(2)}, u32[]{:S(2)}) collective-permute-start(bf16[256,1664]{1,0:T(8,128)(2,1)} %pad_maximum_fusion.24.refs_0_), channel_id=1, source_target_pairs={{0,1},{1,0},{2,3},{3,2},{4,5},{5,4},{6,7},{7,6},{8,9},{9,8},{10,11... | collective-permute-start | bytes 2555912 | tf_op jit(solution)/shard_map/ppermute | solution.py:408
  711.7 96.5 %collective-permute-start.60 = (bf16[192,2048]{1,0:T(8,128)(2,1)}, bf16[192,2048]{1,0:T(8,128)(2,1)}, u32[]{:S(2)}, u32[]{:S(2)}) collective-permute-start(bf16[192,2048]{1,0:T(8,128)(2,1)} %slice_bitcast_fusion.11), channel_id=1, source_target_pairs={{0,16},{1,17},{2,18},{3,19},{4,20},{5,21},{6,22},{7,23},{8,24},{9,... | collective-permute-start | bytes 2359304 | tf_op jit(solution)/shard_map/ppermute | solution.py:408
  751.2 56.9 %collective-permute-start.58 = (bf16[256,1664]{1,0:T(8,128)(2,1)}, bf16[256,1664]{1,0:T(8,128)(2,1)}, u32[]{:S(2)}, u32[]{:S(2)}) collective-permute-start(bf16[256,1664]{1,0:T(8,128)(2,1)} %add_convert_fusion.4.refs_0_), channel_id=1, source_target_pairs={{0,4},{1,5},{2,6},{3,7},{4,0},{5,1},{6,2},{7,3},{8,12},{9,13},{10,... | collective-permute-start | bytes 2555912 | tf_op jit(solution)/shard_map/ppermute | solution.py:408
  752.0 53.7 %collective-permute-start.59 = (bf16[256,1664]{1,0:T(8,128)(2,1)}, bf16[256,1664]{1,0:T(8,128)(2,1)}, u32[]{:S(2)}, u32[]{:S(2)}) collective-permute-start(bf16[256,1664]{1,0:T(8,128)(2,1)} %pad_maximum_fusion.25), channel_id=1, source_target_pairs={{0,1},{1,0},{2,3},{3,2},{4,5},{5,4},{6,7},{7,6},{8,9},{9,8},{10,11... | collective-permute-start | bytes 2555912 | tf_op jit(solution)/shard_map/ppermute | solution.py:408
  752.6 55.5 %collective-permute-start.61 = (bf16[256,1664]{1,0:T(8,128)(2,1)}, bf16[256,1664]{1,0:T(8,128)(2,1)}, u32[]{:S(2)}, u32[]{:S(2)}) collective-permute-start(bf16[256,1664]{1,0:T(8,128)(2,1)} %pad_maximum_fusion.26), channel_id=1, source_target_pairs={{0,1},{1,0},{2,3},{3,2},{4,5},{5,4},{6,7},{7,6},{8,9},{9,8},{10,11... | collective-permute-start | bytes 2555912 | tf_op jit(solution)/shard_map/ppermute | solution.py:408
  754.0 65.5 %collective-permute-start.63 = (bf16[256,1664]{1,0:T(8,128)(2,1)}, bf16[256,1664]{1,0:T(8,128)(2,1)S(1)}, u32[]{:S(2)}, u32[]{:S(2)}) collective-permute-start(bf16[256,1664]{1,0:T(8,128)(2,1)} %pad_maximum_fusion.27), channel_id=1, source_target_pairs={{0,1},{1,0},{2,3},{3,2},{4,5},{5,4},{6,7},{7,6},{8,9},{9,8},{10,11... | collective-permute-start | bytes 2555912 | tf_op jit(solution)/shard_map/ppermute | solution.py:408
  810.4 35.7 %collective-permute-start.62 = (bf16[256,1664]{1,0:T(8,128)(2,1)}, bf16[256,1664]{1,0:T(8,128)(2,1)}, u32[]{:S(2)}, u32[]{:S(2)}) collective-permute-start(bf16[256,1664]{1,0:T(8,128)(2,1)} %add_convert_fusion.2), channel_id=1, source_target_pairs={{0,2},{1,3},{2,4},{3,5},{4,6},{5,7},{6,0},{7,1},{8,10},{9,11},{10,... | collective-permute-start | bytes 2555912 | tf_op jit(solution)/shard_map/ppermute | solution.py:408
  820.6 38.7 %collective-permute-start.64 = (bf16[256,1664]{1,0:T(8,128)(2,1)}, bf16[256,1664]{1,0:T(8,128)(2,1)}, u32[]{:S(2)}, u32[]{:S(2)}) collective-permute-start(bf16[256,1664]{1,0:T(8,128)(2,1)} %add_convert_fusion.1), channel_id=1, source_target_pairs={{0,6},{1,7},{2,0},{3,1},{4,2},{5,3},{6,4},{7,5},{8,14},{9,15},{10,... | collective-permute-start | bytes 2555912 | tf_op jit(solution)/shard_map/ppermute | solution.py:408
  822.7 64.4 %collective-permute-start.65 = (bf16[2,1024,2048]{2,1,0:T(8,128)(2,1)}, bf16[2,1024,2048]{2,1,0:T(8,128)(2,1)}, u32[]{:S(2)}, u32[]{:S(2)}) collective-permute-start(bf16[2,1024,2048]{2,1,0:T(8,128)(2,1)} %fusion.38), channel_id=1, source_target_pairs={{0,8},{1,9},{2,10},{3,11},{4,12},{5,13},{6,14},{7,15},{8,0},{9,1},... | collective-permute-start | bytes 25165832 | tf_op jit(solution)/shard_map/ppermute | solution.py:408
  859.3 74.5 %collective-permute-start.69 = (bf16[2,2048,1024]{2,1,0:T(8,128)(2,1)}, bf16[2,2048,1024]{2,1,0:T(8,128)(2,1)}, u32[]{:S(2)}, u32[]{:S(2)}) collective-permute-start(bf16[2,2048,1024]{2,1,0:T(8,128)(2,1)} %fusion.46), channel_id=1, source_target_pairs={{0,8},{1,9},{2,10},{3,11},{4,12},{5,13},{6,14},{7,15},{8,0},{9,1},... | collective-permute-start | bytes 25165832 | tf_op jit(solution)/shard_map/ppermute | solution.py:408
  882.0 76.2 %collective-permute-start.71 = (bf16[2,2048,1024]{2,1,0:T(8,128)(2,1)}, bf16[2,2048,1024]{2,1,0:T(8,128)(2,1)}, u32[]{:S(2)}, u32[]{:S(2)}) collective-permute-start(bf16[2,2048,1024]{2,1,0:T(8,128)(2,1)} %fusion.43.refs_0_), channel_id=1, source_target_pairs={{0,8},{1,9},{2,10},{3,11},{4,12},{5,13},{6,14},{7,15},{8,0},{9,1},... | collective-permute-start | bytes 25165832 | tf_op jit(solution)/shard_map/ppermute | solution.py:408
  885.0 25.9 %collective-permute-start.66 = (bf16[256,1664]{1,0:T(8,128)(2,1)S(1)}, bf16[256,1664]{1,0:T(8,128)(2,1)}, u32[]{:S(2)}, u32[]{:S(2)}) collective-permute-start(bf16[256,1664]{1,0:T(8,128)(2,1)S(1)} %add_convert_fusion), channel_id=1, source_target_pairs={{0,16},{1,17},{2,18},{3,19},{4,20},{5,21},{6,22},{7,23},{8,24},{9,... | collective-permute-start | bytes 2555912 | tf_op jit(solution)/shard_map/ppermute | solution.py:408
  (143 other events, 2053.3 us)
Sparse Core Ops, SparseCore 0:
  143.8 117.3 all-gather.2
  349.5 97.7 all-gather.4
  606.5 117.4 reduce-scatter.2
  754.8 91.4 reduce-scatter.4

commit v6 on v5

--- a/solution.py
+++ b/solution.py
@@ -415,11 +415,12 @@
 def gather_small(values, hold):
     low = jnp.stack([values, move(values, SHARD_SWAP[1])])
     high = jnp.stack([low, move(after(low, *hold), SHARD_SWAP[2])])
-    both = jnp.stack([high, move(high, SHARD_SWAP[0])], axis=2)
-    return both.reshape((SHARDS,) + values.shape)
-
-
-def gather_rows(values, early=(), late=(), fill=None, first=()):
+    last = move(high, SHARD_SWAP[0])
+    both = jnp.stack([high, last], axis=2)
+    return both.reshape((SHARDS,) + values.shape), last
+
+
+def gather_rows(values, early=(), late=None, fill=None, first=()):
     moved = {k: move(values, Z_FROM[k]) for k in (1, 3)}
     moved[2] = move(after(values, moved[1], *first), Z_FROM[2])
     mine, beside = {0: values}, {0: move(values, Y_SWAP)}
@@ -428,8 +429,8 @@
         if k == 2 and fill is not None:
             mine[k] = after(mine[k], *fill(mine[3]))
         beside[k] = move(mine[k], Y_SWAP)
-    if late:
-        beside = {k: after(beside[k], *late) for k in beside}
+    if late is not None:
+        beside = {k: after(beside[k], *late()) for k in beside}
     return [(mine[k], beside[k]) for k in range(LINE)]
 
 
@@ -1128,7 +1129,7 @@
     in_pieces = gather_rows(
         thin_columns(in_proj, rep_ref, width), first=(inputs_across, segment_rows)
     )
-    small_in = gather_small(small_in, (in_pieces[2][0], in_pieces[1][1], in_pieces[3][1]))
+    small_in, small_last = gather_small(small_in, (in_pieces[2][0], in_pieces[1][1], in_pieces[3][1]))
     ranks = small_in[:, 4 + expert_count :, :tokens]
     ranks = jnp.take(ranks, near_shards ^ shard, axis=0)
     ranks = ranks.reshape(SHARDS, REPS, expert_count + 1, tokens)[:, :, :expert_count]
@@ -1166,7 +1167,7 @@
 
     out_rows = rows_each // 4
     out_own = lax.dynamic_slice_in_dim(out_proj, rep * out_rows, out_rows, 0)
-    out_own = after(out_own, in_pieces[2][0])
+    out_own = after(out_own, small_last)
 
     projected = jnp.dot(normed_low, in_part, preferred_element_type=f32)
     squares = jnp.stack(
@@ -1188,7 +1189,7 @@
         segment_rows[:, None, :],
     )
     attended = attend(*attention_operands).reshape(2, 2, tokens, part_width)
-    out_pieces = gather_rows(out_own, early=(projected,), late=(attended,))
+    out_pieces = gather_rows(out_own, early=(projected,), late=lambda: (attended,))
     out_own = flat(out_pieces).reshape(SHARDS, out_rows, width)
     out_other = move(out_own, CORE_SWAP)
     out_part = jnp.where(
@@ -1258,10 +1259,10 @@
         return [own_part[1]]
 
     ffn_pieces = gather_rows(
-        ffn_low, fill=fill_cot
+        ffn_low, fill=fill_cot, late=lambda: (made["cot"][1][1],)
     )
     near_cot = made["cot"]
-    ffn_own = after(flat(ffn_pieces), near_cot[1][1])
+    ffn_own = flat(ffn_pieces)
     ffn_beside = move(ffn_own, CORE_SWAP)
     ffn_far = [move(jnp.concatenate(pair, axis=0), X_SWAP) for pair in ffn_pieces]
     cot_across = lax.all_gather(after(cot_across, ffn_pieces[2][0]), "shard", tiled=True)

time: 994 us -> 992 us (level)
  waiting for transfers between devices: 208 us -> 190 us
    ppermute x72, waiting for transfers between devices: 208 us -> 190 us  [move(): return lax.ppermute(values, AXES, moves)]
    unnamed x256 -> x228, local copies, waits for them, and re-layouts: 70.3 us -> 73.8 us
  transfers between devices with their start and end apart: 76 -> 76, of which waited for: 23 -> 24; matrix products, arithmetic and copies ran while one was open for 30% -> 29% of each run, Pallas kernels for 32% -> 34%
where the time goes in v6:
time: 992 us; the launch traced here: 982 us
  Pallas kernels  369 us (37%)
  waiting for transfers between devices  190 us (19%)
  local copies, waits for them, and re-layouts  126 us (13%)
  other arithmetic  108 us (11%)
  matrix products  101 us (10%)
  starting transfers between devices  72.3 us (7%)
  between operations  15.9 us (2%)
    ppermute x72, waiting for transfers between devices, move(): return lax.ppermute(values, AXES, moves)  190 us
    pallas_call x4, Pallas kernels, forward_part(): pl.pallas_call(ordered(forward_kernel, len(behind)), grid_spec=pltpu.Pref...  112 us
    pallas_call x4, Pallas kernels, cotangent_part(): pl.pallas_call(ordered(cotangent_kernel, len(behind)), grid_spec=pltpu.Pr...  76.3 us
    unnamed x228, local copies, waits for them, and re-layouts  73.8 us
    ppermute x72, starting transfers between devices, move(): return lax.ppermute(values, AXES, moves)  71.7 us
    dot_general x3, matrix products, weight_grad(): jnp.einsum('ecd,ecf->edf', left, right, preferred_element_type=f32)  69.5 us
    pallas_call x3, Pallas kernels, widen(): pl.pallas_call(ordered(widen_kernel, len(behind)), grid_spec=pltpu.Prefet...  51 us
    pallas_call x2, Pallas kernels, backward_part(): pl.pallas_call(ordered(backward_kernel, len(behind)), grid_spec=pltpu.Pre...  49.1 us
  transfers between devices with their start and end apart: 76, of which 24 were waited for; matrix products, arithmetic and copies ran while one was open for 29% of the time, Pallas kernels for 34%

profile of v6, /device:TPU:0, one launch (start us, length us, event | category | flops | bytes accessed | tf_op | source)
XLA Modules:
  0.0 982.4 jit_solution(2303748850416618243)
XLA Ops:
  28.0 14.7 %collective-permute-done.3 = bf16[2,33,256]{2,1,0:T(8,128)(2,1)S(1)} collective-permute-done((bf16[2,33,256]{2,1,0:T(8,128)(2,1)S(1)}, bf16[2,33,256]{2,1,0:T(8,128)(2,1)S(1)}, u32[]{:S(2)}, u32[]{:S(2)}) %collective-permute-start.3) | collective-permute-done | bytes 33824 | tf_op jit(solution)/shard_map/ppermute | solution.py:408
  45.4 5.4 collective-permute-done.5
  64.1 22.2 %collective-permute-done.9 = bf16[256,1536]{1,0:T(8,128)(2,1)} collective-permute-done((bf16[256,1536]{1,0:T(8,128)(2,1)}, bf16[256,1536]{1,0:T(8,128)(2,1)}, u32[]{:S(2)}, u32[]{:S(2)}) %collective-permute-start.9) | collective-permute-done | bytes 786464 | tf_op jit(solution)/shard_map/ppermute | solution.py:408
  91.2 5.1 collective-permute-done.10
  101.1 13.9 %collective-permute-done.11 = bf16[2,2,168,256]{3,2,1,0:T(8,128)(2,1)S(1)} collective-permute-done((bf16[2,2,168,256]{3,2,1,0:T(8,128)(2,1)S(1)}, bf16[2,2,168,256]{3,2,1,0:T(8,128)(2,1)S(1)}, u32[]{:S(2)}, u32[]{:S(2)}) %collective-permute-start.11) | collective-permute-done | bytes 344096 | tf_op jit(solution)/shard_map/ppermute | solution.py:408
  139.3 4.4 fusion.35
  143.7 8.4 fusion.124.raw_ref.refs_0_
  163.6 10.2 %shard_map.240 = bf16[768,512]{1,0:T(8,128)(2,1)} custom-call(f32[768,1536]{1,0:T(8,128)} %copy-done.12, f32[768,2]{1,0:T(8,128)} %fusion.82.rate_ref.refs_1_, f32[2,512]{1,0:T(2,128)} %bitcast.348, f32[768,128]{1,0:T(8,128)} %get-tuple-element.274.cos_ref.refs_3_, f32[768,128]{1,0:T(8,128)} %get-tuple-element.273.sin_ref.refs_4_, ...), custom_call_target="tpu_custom_call" | custom-call | tf_op jit(solution)/shard_map/pallas_call | solution.py:1009
  177.2 6.4 collective-permute-done.21
  186.5 6.9 collective-permute-done.22
  197.3 3.9 collective-permute-done.17
  202.5 5.7 maximum_select_fusion
  213.2 16.8 %collective-permute-done.26 = bf16[192,2048]{1,0:T(8,128)(2,1)} collective-permute-done((bf16[192,2048]{1,0:T(8,128)(2,1)S(1)}, bf16[192,2048]{1,0:T(8,128)(2,1)}, u32[]{:S(2)}, u32[]{:S(2)}) %collective-permute-start.26) | collective-permute-done | bytes 786464 | tf_op jit(solution)/shard_map/ppermute | solution.py:408
  240.0 4.4 convert_reduce_fusion.1
  247.7 13.7 %collective-permute-done.31 = bf16[192,2048]{1,0:T(8,128)(2,1)} collective-permute-done((bf16[192,2048]{1,0:T(8,128)(2,1)}, bf16[192,2048]{1,0:T(8,128)(2,1)}, u32[]{:S(2)}, u32[]{:S(2)}) %collective-permute-start.31) | collective-permute-done | bytes 786464 | tf_op jit(solution)/shard_map/ppermute | solution.py:408
  264.9 15.9 %collective-permute-done.28.refs_0_ = bf16[192,2048]{1,0:T(8,128)(2,1)} collective-permute-done((bf16[192,2048]{1,0:T(8,128)(2,1)}, bf16[192,2048]{1,0:T(8,128)(2,1)}, u32[]{:S(2)}, u32[]{:S(2)}) %collective-permute-start.28) | collective-permute-done | bytes 786464 | tf_op jit(solution)/shard_map/ppermute | solution.py:408
  281.3 19.0 %shard_map.242 = (bf16[2,480,2048]{2,1,0:T(8,128)(2,1)}, f32[2,480,1024]{2,1,0:T(8,128)}) custom-call(s32[1]{0:T(128)} %bitcast.32.scalar_ref, bf16[192,2048]{1,0:T(8,128)(2,1)} %collective-permute-done.28.refs_0_, s32[2,1,1536]{2,1,0:T(1,128)} %broadcast_in_dim_squeeze.24.refs_1_, bf16[1536,2048]{1,0:T(8,128)(2,1)} %all-gather.3.cloned.1.call-done.refs_2_, ...), custom_call_target="tpu_custom_call" | custom-call | flops 99999997952 | tf_op jit(solution)/shard_map/pallas_call | solution.py:651
  300.3 13.4 %collective-permute-done.34 = bf16[192,2048]{1,0:T(8,128)(2,1)S(1)} collective-permute-done((bf16[192,2048]{1,0:T(8,128)(2,1)}, bf16[192,2048]{1,0:T(8,128)(2,1)S(1)}, u32[]{:S(2)}, u32[]{:S(2)}) %collective-permute-start.34) | collective-permute-done | bytes 786464 | tf_op jit(solution)/shard_map/ppermute | solution.py:408
  317.0 19.0 %shard_map.243 = (bf16[2,480,2048]{2,1,0:T(8,128)(2,1)}, f32[2,480,1024]{2,1,0:T(8,128)}) custom-call(s32[1]{0:T(128)} %bitcast.32.scalar_ref, f32[2,480,1024]{2,1,0:T(8,128)} %get-tuple-element.109.refs_0_.refs_5_, s32[2,1,1536]{2,1,0:T(1,128)} %broadcast_in_dim_squeeze.25.refs_1_, bf16[1536,2048]{1,0:T(8,128)(2,1)} %copy-done.93, ...), custom_call_target="tpu_custom_call" | custom-call | flops 99999997952 | tf_op jit(solution)/shard_map/pallas_call | solution.py:651
  366.3 28.4 %shard_map.244 = (bf16[2,480,2048]{2,1,0:T(8,128)(2,1)}, bf16[2,480,1024]{2,1,0:T(8,128)(2,1)}, bf16[2,480,1024]{2,1,0:T(8,128)(2,1)}, bf16[2,480,1024]{2,1,0:T(8,128)(2,1)}, bf16[2,480,128]{2,1,0:T(8,128)(2,1)}) custom-call(s32[2]{0:T(128)} %pad_add_fusion.scalar_ref, s32[2,1,1536]{2,1,0:T(1,128)} %broadcast_in_dim_squeeze.26.refs_0_, ...), custom_call_target="tpu_custom_call" | custom-call | tf_op jit(solution)/shard_map/pallas_call | solution.py:736
  394.7 27.9 %shard_map.245 = (bf16[2,480,2048]{2,1,0:T(8,128)(2,1)}, bf16[2,480,1024]{2,1,0:T(8,128)(2,1)}, bf16[2,480,1024]{2,1,0:T(8,128)(2,1)}, bf16[2,480,1024]{2,1,0:T(8,128)(2,1)}, bf16[2,480,128]{2,1,0:T(8,128)(2,1)}) custom-call(s32[2]{0:T(128)} %pad_add_fusion.scalar_ref, bf16[2,480,1024]{2,1,0:T(8,128)(2,1)} %get-tuple-element.117.refs_0_.refs_2_, ...), custom_call_target="tpu_custom_call" | custom-call | tf_op jit(solution)/shard_map/pallas_call | solution.py:736
  422.6 24.7 %shard_map.246 = bf16[1536,2176]{1,0:T(8,128)(2,1)} custom-call(s32[1]{0:T(128)} %bitcast.32.scalar_ref, bf16[384,2048]{1,0:T(8,128)(2,1)} %collective-permute-done.30.refs_0_, bf16[384,2048]{1,0:T(8,128)(2,1)} %collective-permute-done.33.refs_1_, s32[1536,2]{1,0:T(8,128)} %get-tuple-element.255.refs_2_, bf16[2,480,1024]{2,1,0:T(8,128)(2,1)} %get-tuple-element.118.refs_3_, ...), custom_call_target="tpu_custom_call" | custom-call | tf_op jit(solution)/shard_map/pallas_call | solution.py:810
  452.9 24.4 %shard_map.247 = bf16[1536,2176]{1,0:T(8,128)(2,1)} custom-call(s32[1]{0:T(128)} %bitcast.32.scalar_ref, bf16[8,192,2176]{2,1,0:T(8,128)(2,1)} %bitcast.297, s32[1536,2]{1,0:T(8,128)} %get-tuple-element.254.refs_1_, bf16[2,480,1024]{2,1,0:T(8,128)(2,1)} %get-tuple-element.121.refs_2_, bf16[2,480,1024]{2,1,0:T(8,128)(2,1)} %get-tuple-element.122.refs_3_, ...), custom_call_target="tpu_custom_call" | custom-call | tf_op jit(solution)/shard_map/pallas_call | solution.py:810
  482.4 4.5 collective-permute-done.40.refs_1_
  487.0 16.8 %shard_map.248 = bf16[1536,2048]{1,0:T(8,128)(2,1)} custom-call(s32[1]{0:T(128)} %bitcast.32.scalar_ref, bf16[192,2176]{1,0:T(8,128)(2,1)} %fusion.60.refs_0_, bf16[384,2048]{1,0:T(8,128)(2,1)} %collective-permute-done.40.refs_1_, bf16[1536,2048]{1,0:T(8,128)(2,1)} %all-gather.5.cloned.1.call-done.refs_2_, s32[1536,2]{1,0:T(8,128)} %get-tuple-element.253.refs_3_, ...), custom_call_target="tpu_custom_call" | custom-call | flops 99999997952 | tf_op jit(solution)/shard_map/pallas_call | solution.py:872
  515.7 9.1 collective-permute-done.39
  529.8 17.2 %shard_map.249 = bf16[1536,2048]{1,0:T(8,128)(2,1)} custom-call(s32[1]{0:T(128)} %bitcast.32.scalar_ref, bf16[192,2176]{1,0:T(8,128)(2,1)} %get-tuple-element.239.refs_0_, s32[1536,2]{1,0:T(8,128)} %get-tuple-element.252.refs_1_, bf16[2,480,1024]{2,1,0:T(8,128)(2,1)} %get-tuple-element.117.refs_0_.refs_2_, bf16[4,1024,2048]{2,1,0:T(8,128)(2,1)} %refs_3_.11, ...), custom_call_target="tpu_custom_call" | custom-call | flops 99999997952 | tf_op jit(solution)/shard_map/pallas_call | solution.py:872
  553.4 19.0 %shard_map.250 = (bf16[2,480,2048]{2,1,0:T(8,128)(2,1)}, f32[2,480,1024]{2,1,0:T(8,128)}) custom-call(s32[1]{0:T(128)} %bitcast.32.scalar_ref, bf16[192,2176]{1,0:T(8,128)(2,1)} %get-tuple-element.236.refs_0_, s32[2,1,1536]{2,1,0:T(1,128)} %broadcast_in_dim_squeeze.28.refs_1_, bf16[1536,2048]{1,0:T(8,128)(2,1)} %all-gather.5.cloned.1.call-done.refs_2_, ...), custom_call_target="tpu_custom_call" | custom-call | flops 99999997952 | tf_op jit(solution)/shard_map/pallas_call | solution.py:651
  575.3 3.7 collective-permute-start.48
  579.0 19.2 %shard_map.251 = (bf16[2,480,2048]{2,1,0:T(8,128)(2,1)}, f32[2,480,1024]{2,1,0:T(8,128)}) custom-call(s32[1]{0:T(128)} %bitcast.32.scalar_ref, bf16[192,2176]{1,0:T(8,128)(2,1)} %copy-done.52, s32[2,1,1536]{2,1,0:T(1,128)} %broadcast_in_dim_squeeze.29.refs_1_, bf16[1536,2048]{1,0:T(8,128)(2,1)} %collective-permute-done.45.refs_2_, ...), custom_call_target="tpu_custom_call" | custom-call | flops 99999997952 | tf_op jit(solution)/shard_map/pallas_call | solution.py:651
  598.3 3.8 collective-permute-done.48
  618.7 9.6 collective-permute-done.49
  638.1 20.3 %shard_map.253 = (f32[768,1024]{1,0:T(8,128)}, bf16[768,512]{1,0:T(8,128)(2,1)}, f32[768,2]{1,0:T(8,128)}, f32[4,2,512]{2,1,0:T(2,128)}) custom-call(f32[768,1536]{1,0:T(8,128)} %copy-done.12, f32[768,2]{1,0:T(8,128)} %fusion.82.rate_ref.refs_1_, f32[2,512]{1,0:T(2,128)} %bitcast.349, f32[768,128]{1,0:T(8,128)} %get-tuple-element.274.cos_ref.refs_3_, ...), custom_call_target="tpu_custom_call" | custom-call | tf_op jit(solution)/shard_map/pallas_call | solution.py:1029
  666.6 6.4 shard_map.254
  672.9 8.1 fusion.117
  690.9 5.4 convolution_convert_fusion
  719.4 28.0 %shard_map.255 = (bf16[2,480,2048]{2,1,0:T(8,128)(2,1)}, bf16[2,480,1024]{2,1,0:T(8,128)(2,1)}, bf16[2,480,1024]{2,1,0:T(8,128)(2,1)}, bf16[2,480,1024]{2,1,0:T(8,128)(2,1)}, bf16[2,480,128]{2,1,0:T(8,128)(2,1)}) custom-call(s32[2]{0:T(128)} %pad_add_fusion.scalar_ref, bf16[256,1664]{1,0:T(8,128)(2,1)} %pad_maximum_fusion.24.refs_0_, ...), custom_call_target="tpu_custom_call" | custom-call | flops 99999997952 | tf_op jit(solution)/shard_map/pallas_call | solution.py:736
  753.9 27.8 %shard_map.256 = (bf16[2,480,2048]{2,1,0:T(8,128)(2,1)}, bf16[2,480,1024]{2,1,0:T(8,128)(2,1)}, bf16[2,480,1024]{2,1,0:T(8,128)(2,1)}, bf16[2,480,1024]{2,1,0:T(8,128)(2,1)}, bf16[2,480,128]{2,1,0:T(8,128)(2,1)}) custom-call(s32[2]{0:T(128)} %pad_add_fusion.scalar_ref, bf16[256,1664]{1,0:T(8,128)(2,1)} %add_convert_fusion.4.refs_0_, ...), custom_call_target="tpu_custom_call" | custom-call | flops 99999997952 | tf_op jit(solution)/shard_map/pallas_call | solution.py:736
  781.7 23.3 %fusion.38 = bf16[2,1024,2048]{2,1,0:T(8,128)(2,1)} fusion(bf16[2,480,2048]{2,1,0:T(8,128)(2,1)} %get-tuple-element.151, bf16[2,480,2048]{2,1,0:T(8,128)(2,1)} %get-tuple-element.150, bf16[2,480,2048]{2,1,0:T(8,128)(2,1)} %get-tuple-element.149, bf16[2,480,2048]{2,1,0:T(8,128)(2,1)} %get-tuple-element.148, bf16[2,480,1024]{2,1,0:T(8,128)(2,1)} %get-tuple-element.147, ...), kind=kOutput, calls=%fused_computation.57 | convolution fusion | flops 16204693504 | bytes 31981568 | tf_op jit(solution)/shard_map/ecd,ecf->edf/dot_general | solution.py:1391
  811.9 5.1 collective-permute-done.63
  821.4 23.4 %fusion.46 = bf16[2,2048,1024]{2,1,0:T(8,128)(2,1)} fusion(bf16[2,480,1024]{2,1,0:T(8,128)(2,1)} %get-tuple-element.160, bf16[2,480,1024]{2,1,0:T(8,128)(2,1)} %get-tuple-element.159, bf16[2,480,1024]{2,1,0:T(8,128)(2,1)} %get-tuple-element.118.refs_3_, bf16[2,480,1024]{2,1,0:T(8,128)(2,1)} %get-tuple-element.121.refs_2_, ...), kind=kOutput, calls=%fused_computation.59 | convolution fusion | flops 16204693504 | bytes 31981568 | tf_op jit(solution)/shard_map/ecd,ecf->edf/dot_general | solution.py:1391
  844.8 12.6 %collective-permute-done.64 = bf16[256,1664]{1,0:T(8,128)(2,1)} collective-permute-done((bf16[256,1664]{1,0:T(8,128)(2,1)}, bf16[256,1664]{1,0:T(8,128)(2,1)}, u32[]{:S(2)}, u32[]{:S(2)}) %collective-permute-start.64) | collective-permute-done | bytes 852000 | tf_op jit(solution)/shard_map/ppermute | solution.py:408
  857.4 22.8 %fusion.43.refs_0_ = bf16[2,2048,1024]{2,1,0:T(8,128)(2,1)} fusion(bf16[2,480,1024]{2,1,0:T(8,128)(2,1)} %get-tuple-element.153, bf16[2,480,1024]{2,1,0:T(8,128)(2,1)} %get-tuple-element.144.refs_1_, bf16[2,480,1024]{2,1,0:T(8,128)(2,1)} %get-tuple-element.119.refs_4_, bf16[2,480,1024]{2,1,0:T(8,128)(2,1)S(1)} %copy-done.44, ...), kind=kOutput, calls=%fused_computation.58 | convolution fusion | flops 16204693504 | bytes 31981568 | tf_op jit(solution)/shard_map/ecd,ecf->edf/dot_general | solution.py:1391
  892.5 16.9 %shard_map.257 = f32[4096,2048]{1,0:T(8,128)} custom-call(s32[1]{0:T(128)} %bitcast.32.scalar_ref, bf16[2,2048,1024]{2,1,0:T(8,128)(2,1)S(1)} %copy-done.2, bf16[2048,2048]{1,0:T(8,128)(2,1)S(1)} %bitcast.287, bf16[2048,2048]{1,0:T(8,128)(2,1)} %bitcast.89.refs_2_), custom_call_target="tpu_custom_call" | custom-call | tf_op jit(solution)/shard_map/pallas_call | solution.py:592
  932.3 3.4 copy-done.7
  935.7 17.0 %shard_map.259 = f32[8192,1024]{1,0:T(8,128)} custom-call(s32[1]{0:T(128)} %bitcast.32.scalar_ref, f32[4,1024,2048]{2,1,0:T(8,128)} %bitcast.293, bf16[64,2048]{1,0:T(8,128)(2,1)S(1)} %collective-permute-done.68.refs_1_, bf16[4096,1024]{1,0:T(8,128)(2,1)S(1)} %bitcast.286, bf16[4096,1024]{1,0:T(8,128)(2,1)} %bitcast.100.refs_3_), custom_call_target="tpu_custom_call" | custom-call | tf_op jit(solution)/shard_map/pallas_call | solution.py:592
  952.8 4.0 shard_map.260
  958.5 17.0 %shard_map.261 = f32[8192,1024]{1,0:T(8,128)} custom-call(s32[1]{0:T(128)} %bitcast.32.scalar_ref, f32[4,2048,1024]{2,1,0:T(8,128)} %bitcast.291, bf16[4096,1024]{1,0:T(8,128)(2,1)S(1)} %bitcast.281, bf16[4096,1024]{1,0:T(8,128)(2,1)} %bitcast.111.refs_2_), custom_call_target="tpu_custom_call" | custom-call | tf_op jit(solution)/shard_map/pallas_call | solution.py:592
  (594 shorter events, 307.6 us)
Async XLA Ops:
  7.2 274.1 %all-gather.3.cloned.1.call-start = ((), (), s32[]{:S(2)}) async-start(), calls=%async_computation.2 | async-start | bytes 7077888 | tf_op jit(solution)/shard_map/all_gather | solution.py:1162
  9.7 52.3 %collective-permute-start.13 = (bf16[256,1536]{1,0:T(8,128)(2,1)S(1)}, bf16[256,1536]{1,0:T(8,128)(2,1)}, u32[]{:S(2)}, u32[]{:S(2)}) collective-permute-start(bf16[256,1536]{1,0:T(8,128)(2,1)S(1)} %shard_map.239), channel_id=1, source_target_pairs={{0,1},{1,0},{2,3},{3,2},{4,5},{5,4},{6,7},{7,6},{8,9},{9,8},{10,11... | collective-permute-start | bytes 2359304 | tf_op jit(solution)/shard_map/ppermute | solution.py:408
  12.8 39.9 %collective-permute-start.8 = (bf16[256,1536]{1,0:T(8,128)(2,1)S(1)}, bf16[256,1536]{1,0:T(8,128)(2,1)}, u32[]{:S(2)}, u32[]{:S(2)}) collective-permute-start(bf16[256,1536]{1,0:T(8,128)(2,1)S(1)} %shard_map.239), channel_id=1, source_target_pairs={{0,2},{1,3},{2,4},{3,5},{4,6},{5,7},{6,0},{7,1},{8,10},{9,11},{10,... | collective-permute-start | bytes 2359304 | tf_op jit(solution)/shard_map/ppermute | solution.py:408
  14.3 36.4 %collective-permute-start.5 = (bf16[256,1536]{1,0:T(8,128)(2,1)S(1)}, bf16[256,1536]{1,0:T(8,128)(2,1)}, u32[]{:S(2)}, u32[]{:S(2)}) collective-permute-start(bf16[256,1536]{1,0:T(8,128)(2,1)S(1)} %shard_map.239), channel_id=1, source_target_pairs={{0,6},{1,7},{2,0},{3,1},{4,2},{5,3},{6,4},{7,5},{8,14},{9,15},{10,... | collective-permute-start | bytes 2359304 | tf_op jit(solution)/shard_map/ppermute | solution.py:408
  21.9 28.9 %collective-permute-start = (bf16[192,2048]{1,0:T(8,128)(2,1)S(1)}, bf16[192,2048]{1,0:T(8,128)(2,1)}, u32[]{:S(2)}, u32[]{:S(2)}) collective-permute-start(bf16[192,2048]{1,0:T(8,128)(2,1)S(1)} %copy-done.16), channel_id=1, source_target_pairs={{0,16},{1,17},{2,18},{3,19},{4,20},{5,21},{6,22},{7,23},{8,24},{9,... | collective-permute-start | bytes 2359304 | tf_op jit(solution)/shard_map/ppermute | solution.py:408
  50.8 35.9 %collective-permute-start.6 = (bf16[256,1536]{1,0:T(8,128)(2,1)S(1)}, bf16[256,1536]{1,0:T(8,128)(2,1)}, u32[]{:S(2)}, u32[]{:S(2)}) collective-permute-start(bf16[256,1536]{1,0:T(8,128)(2,1)S(1)} %shard_map.239), channel_id=1, source_target_pairs={{0,4},{1,5},{2,6},{3,7},{4,0},{5,1},{6,2},{7,3},{8,12},{9,13},{10,... | collective-permute-start | bytes 2359304 | tf_op jit(solution)/shard_map/ppermute | solution.py:408
  52.1 34.3 %collective-permute-start.7 = (bf16[256,1536]{1,0:T(8,128)(2,1)}, bf16[256,1536]{1,0:T(8,128)(2,1)}, u32[]{:S(2)}, u32[]{:S(2)}) collective-permute-start(bf16[256,1536]{1,0:T(8,128)(2,1)} %collective-permute-done.5), channel_id=1, source_target_pairs={{0,1},{1,0},{2,3},{3,2},{4,5},{5,4},{6,7},{7,6},{8,9},{9,8},{10,11... | collective-permute-start | bytes 2359304 | tf_op jit(solution)/shard_map/ppermute | solution.py:408
  52.6 33.8 %collective-permute-start.9 = (bf16[256,1536]{1,0:T(8,128)(2,1)}, bf16[256,1536]{1,0:T(8,128)(2,1)}, u32[]{:S(2)}, u32[]{:S(2)}) collective-permute-start(bf16[256,1536]{1,0:T(8,128)(2,1)} %collective-permute-done.8), channel_id=1, source_target_pairs={{0,1},{1,0},{2,3},{3,2},{4,5},{5,4},{6,7},{7,6},{8,9},{9,8},{10,11... | collective-permute-start | bytes 2359304 | tf_op jit(solution)/shard_map/ppermute | solution.py:408
  57.5 86.2 %collective-permute-start.12 = (bf16[192,2048]{1,0:T(8,128)(2,1)S(1)}, bf16[192,2048]{1,0:T(8,128)(2,1)}, u32[]{:S(2)}, u32[]{:S(2)}) collective-permute-start(bf16[192,2048]{1,0:T(8,128)(2,1)S(1)} %copy-done.28), channel_id=1, source_target_pairs={{0,16},{1,17},{2,18},{3,19},{4,20},{5,21},{6,22},{7,23},{8,24},{9,... | collective-permute-start | bytes 2359304 | tf_op jit(solution)/shard_map/ppermute | solution.py:408
  62.0 62.9 %collective-permute-start.1 = (bf16[2,192,2048]{2,1,0:T(8,128)(2,1)}, bf16[2,192,2048]{2,1,0:T(8,128)(2,1)}, u32[]{:S(2)}, u32[]{:S(2)}) collective-permute-start(bf16[2,192,2048]{2,1,0:T(8,128)(2,1)} %get-tuple-element.257), channel_id=1, source_target_pairs={{0,8},{1,9},{2,10},{3,11},{4,12},{5,13},{6,14},{7,15},{8,0},{9,1},... | collective-permute-start | bytes 4718600 | tf_op jit(solution)/shard_map/ppermute | solution.py:408
  90.7 40.7 %collective-permute-start.14 = (bf16[256,1536]{1,0:T(8,128)(2,1)}, bf16[256,1536]{1,0:T(8,128)(2,1)S(1)}, u32[]{:S(2)}, u32[]{:S(2)}) collective-permute-start(bf16[256,1536]{1,0:T(8,128)(2,1)} %collective-permute-done.6), channel_id=1, source_target_pairs={{0,1},{1,0},{2,3},{3,2},{4,5},{5,4},{6,7},{7,6},{8,9},{9,8},{10,11... | collective-permute-start | bytes 2359304 | tf_op jit(solution)/shard_map/ppermute | solution.py:408
  114.9 41.4 %collective-permute-start.23 = (bf16[64,2048]{1,0:T(8,128)(2,1)S(1)}, bf16[64,2048]{1,0:T(8,128)(2,1)}, u32[]{:S(2)}, u32[]{:S(2)}) collective-permute-start(bf16[64,2048]{1,0:T(8,128)(2,1)S(1)} %copy-done.48), channel_id=1, source_target_pairs={{0,2},{1,3},{2,4},{3,5},{4,6},{5,7},{6,0},{7,1},{8,10},{9,11},{10,... | collective-permute-start | bytes 786440 | tf_op jit(solution)/shard_map/ppermute | solution.py:408
  118.1 37.2 %collective-permute-start.19 = (bf16[64,2048]{1,0:T(8,128)(2,1)S(1)}, bf16[64,2048]{1,0:T(8,128)(2,1)}, u32[]{:S(2)}, u32[]{:S(2)}) collective-permute-start(bf16[64,2048]{1,0:T(8,128)(2,1)S(1)} %copy-done.48), channel_id=1, source_target_pairs={{0,6},{1,7},{2,0},{3,1},{4,2},{5,3},{6,4},{7,5},{8,14},{9,15},{10,... | collective-permute-start | bytes 786440 | tf_op jit(solution)/shard_map/ppermute | solution.py:408
  124.9 48.9 %collective-permute-start.18 = (bf16[64,2048]{1,0:T(8,128)(2,1)S(1)}, bf16[64,2048]{1,0:T(8,128)(2,1)}, u32[]{:S(2)}, u32[]{:S(2)}) collective-permute-start(bf16[64,2048]{1,0:T(8,128)(2,1)S(1)} %copy-done.48), channel_id=1, source_target_pairs={{0,1},{1,0},{2,3},{3,2},{4,5},{5,4},{6,7},{7,6},{8,9},{9,8},{10,11... | collective-permute-start | bytes 786440 | tf_op jit(solution)/shard_map/ppermute | solution.py:408
  136.5 350.4 %all-gather.5.cloned.1.call-start = ((), (), s32[]{:S(2)}) async-start(), calls=%async_computation.3 | async-start | bytes 7077888 | tf_op jit(solution)/shard_map/all_gather | solution.py:1268
  155.3 28.3 %collective-permute-start.21 = (bf16[64,2048]{1,0:T(8,128)(2,1)S(1)}, bf16[64,2048]{1,0:T(8,128)(2,1)S(1)}, u32[]{:S(2)}, u32[]{:S(2)}) collective-permute-start(bf16[64,2048]{1,0:T(8,128)(2,1)S(1)} %copy-done.48), channel_id=1, source_target_pairs={{0,4},{1,5},{2,6},{3,7},{4,0},{5,1},{6,2},{7,3},{8,12},{9,13},{10,... | collective-permute-start | bytes 786440 | tf_op jit(solution)/shard_map/ppermute | solution.py:408
  156.4 28.7 %collective-permute-start.20 = (bf16[64,2048]{1,0:T(8,128)(2,1)}, bf16[64,2048]{1,0:T(8,128)(2,1)S(1)}, u32[]{:S(2)}, u32[]{:S(2)}) collective-permute-start(bf16[64,2048]{1,0:T(8,128)(2,1)} %collective-permute-done.19), channel_id=1, source_target_pairs={{0,1},{1,0},{2,3},{3,2},{4,5},{5,4},{6,7},{7,6},{8,9},{9,8},{10,11... | collective-permute-start | bytes 786440 | tf_op jit(solution)/shard_map/ppermute | solution.py:408
  158.0 27.8 %collective-permute-start.24 = (bf16[64,2048]{1,0:T(8,128)(2,1)}, bf16[64,2048]{1,0:T(8,128)(2,1)S(1)}, u32[]{:S(2)}, u32[]{:S(2)}) collective-permute-start(bf16[64,2048]{1,0:T(8,128)(2,1)} %collective-permute-done.23), channel_id=1, source_target_pairs={{0,1},{1,0},{2,3},{3,2},{4,5},{5,4},{6,7},{7,6},{8,9},{9,8},{10,11... | collective-permute-start | bytes 786440 | tf_op jit(solution)/shard_map/ppermute | solution.py:408
  234.8 26.5 %collective-permute-start.31 = (bf16[192,2048]{1,0:T(8,128)(2,1)}, bf16[192,2048]{1,0:T(8,128)(2,1)}, u32[]{:S(2)}, u32[]{:S(2)}) collective-permute-start(bf16[192,2048]{1,0:T(8,128)(2,1)} %get-tuple-element.113), channel_id=1, source_target_pairs={{0,6},{1,7},{2,0},{3,1},{4,2},{5,3},{6,4},{7,5},{8,14},{9,15},{10,... | collective-permute-start | bytes 2359304 | tf_op jit(solution)/shard_map/ppermute | solution.py:408
  234.8 45.9 %collective-permute-start.28 = (bf16[192,2048]{1,0:T(8,128)(2,1)}, bf16[192,2048]{1,0:T(8,128)(2,1)}, u32[]{:S(2)}, u32[]{:S(2)}) collective-permute-start(bf16[192,2048]{1,0:T(8,128)(2,1)} %get-tuple-element.113), channel_id=1, source_target_pairs={{0,2},{1,3},{2,4},{3,5},{4,6},{5,7},{6,0},{7,1},{8,10},{9,11},{10,... | collective-permute-start | bytes 2359304 | tf_op jit(solution)/shard_map/ppermute | solution.py:408
  237.2 98.8 %collective-permute-start.27 = (bf16[192,2048]{1,0:T(8,128)(2,1)}, bf16[192,2048]{1,0:T(8,128)(2,1)}, u32[]{:S(2)}, u32[]{:S(2)}) collective-permute-start(bf16[192,2048]{1,0:T(8,128)(2,1)} %get-tuple-element.113), channel_id=1, source_target_pairs={{0,1},{1,0},{2,3},{3,2},{4,5},{5,4},{6,7},{7,6},{8,9},{9,8},{10,11... | collective-permute-start | bytes 2359304 | tf_op jit(solution)/shard_map/ppermute | solution.py:408
  261.4 52.3 %collective-permute-start.34 = (bf16[192,2048]{1,0:T(8,128)(2,1)}, bf16[192,2048]{1,0:T(8,128)(2,1)S(1)}, u32[]{:S(2)}, u32[]{:S(2)}) collective-permute-start(bf16[192,2048]{1,0:T(8,128)(2,1)} %get-tuple-element.113), channel_id=1, source_target_pairs={{0,4},{1,5},{2,6},{3,7},{4,0},{5,1},{6,2},{7,3},{8,12},{9,13},{10,... | collective-permute-start | bytes 2359304 | tf_op jit(solution)/shard_map/ppermute | solution.py:408
  264.4 71.6 %collective-permute-start.32 = (bf16[192,2048]{1,0:T(8,128)(2,1)}, bf16[192,2048]{1,0:T(8,128)(2,1)}, u32[]{:S(2)}, u32[]{:S(2)}) collective-permute-start(bf16[192,2048]{1,0:T(8,128)(2,1)} %collective-permute-done.31), channel_id=1, source_target_pairs={{0,1},{1,0},{2,3},{3,2},{4,5},{5,4},{6,7},{7,6},{8,9},{9,8},{10,11... | collective-permute-start | bytes 2359304 | tf_op jit(solution)/shard_map/ppermute | solution.py:408
  280.8 55.2 %collective-permute-start.36 = (bf16[192,2048]{1,0:T(8,128)(2,1)}, bf16[192,2048]{1,0:T(8,128)(2,1)}, u32[]{:S(2)}, u32[]{:S(2)}) collective-permute-start(bf16[192,2048]{1,0:T(8,128)(2,1)} %collective-permute-done.28.refs_0_), channel_id=1, source_target_pairs={{0,1},{1,0},{2,3},{3,2},{4,5},{5,4},{6,7},{7,6},{8,9},{9,8},{10,11... | collective-permute-start | bytes 2359304 | tf_op jit(solution)/shard_map/ppermute | solution.py:408
  281.3 33.0 %collective-permute-start.29 = (bf16[1536,2048]{1,0:T(8,128)(2,1)}, bf16[1536,2048]{1,0:T(8,128)(2,1)S(1)}, u32[]{:S(2)}, u32[]{:S(2)}) collective-permute-start(bf16[1536,2048]{1,0:T(8,128)(2,1)} %all-gather.3.cloned.1.call-done.refs_2_), channel_id=1, source_target_pairs={{0,8},{1,9},{2,10},{3,11},{4,12},{5,13},{6,14},{7,15},{8,0},{9,1},... | collective-permute-start | bytes 18874376 | tf_op jit(solution)/shard_map/ppermute | solution.py:408
  348.7 46.0 %collective-permute-start.37 = (bf16[1536,2048]{1,0:T(8,128)(2,1)}, bf16[1536,2048]{1,0:T(8,128)(2,1)}, u32[]{:S(2)}, u32[]{:S(2)}) collective-permute-start(bf16[1536,2048]{1,0:T(8,128)(2,1)} %constant_dynamic-update-slice_fusion.18.refs_1_), channel_id=1, source_target_pairs={{0,8},{1,9},{2,10},{3,11},{4,12},{5,13},{6,14},{7,15},{8,0},{9,1},... | collective-permute-start | bytes 18874376 | tf_op jit(solution)/shard_map/ppermute | solution.py:408
  348.7 405.1 %reduce-scatter.3.cloned.1.call-start = ((), (), s32[]{:S(2)}) async-start(), calls=%async_computation.4 | async-start | bytes 7077888 | tf_op jit(solution)/shard_map/reduce_scatter | solution.py:1310
  351.7 70.9 %collective-permute-start.30 = (bf16[384,2048]{1,0:T(8,128)(2,1)}, bf16[384,2048]{1,0:T(8,128)(2,1)}, u32[]{:S(2)}, u32[]{:S(2)}) collective-permute-start(bf16[384,2048]{1,0:T(8,128)(2,1)} %pad_maximum_fusion.16), channel_id=1, source_target_pairs={{0,16},{1,17},{2,18},{3,19},{4,20},{5,21},{6,22},{7,23},{8,24},{9,... | collective-permute-start | bytes 4718600 | tf_op jit(solution)/shard_map/ppermute | solution.py:408
  356.0 66.7 %collective-permute-start.33 = (bf16[384,2048]{1,0:T(8,128)(2,1)}, bf16[384,2048]{1,0:T(8,128)(2,1)}, u32[]{:S(2)}, u32[]{:S(2)}) collective-permute-start(bf16[384,2048]{1,0:T(8,128)(2,1)} %pad_maximum_fusion.17), channel_id=1, source_target_pairs={{0,16},{1,17},{2,18},{3,19},{4,20},{5,21},{6,22},{7,23},{8,24},{9,... | collective-permute-start | bytes 4718600 | tf_op jit(solution)/shard_map/ppermute | solution.py:408
  447.3 30.0 %collective-permute-start.38 = (bf16[8,192,2176]{2,1,0:T(8,128)(2,1)}, bf16[8,192,2176]{2,1,0:T(8,128)(2,1)S(1)}, u32[]{:S(2)}, u32[]{:S(2)}) collective-permute-start(bf16[8,192,2176]{2,1,0:T(8,128)(2,1)} %bitcast.296), channel_id=1, source_target_pairs={{0,8},{1,9},{2,10},{3,11},{4,12},{5,13},{6,14},{7,15},{8,0},{9,1},... | collective-permute-start | bytes 20054024 | tf_op jit(solution)/shard_map/ppermute | solution.py:408
  449.9 37.0 %collective-permute-start.40 = (bf16[384,2048]{1,0:T(8,128)(2,1)}, bf16[384,2048]{1,0:T(8,128)(2,1)}, u32[]{:S(2)}, u32[]{:S(2)}) collective-permute-start(bf16[384,2048]{1,0:T(8,128)(2,1)} %pad_maximum_fusion.18), channel_id=1, source_target_pairs={{0,16},{1,17},{2,18},{3,19},{4,20},{5,21},{6,22},{7,23},{8,24},{9,... | collective-permute-start | bytes 4718600 | tf_op jit(solution)/shard_map/ppermute | solution.py:408
  514.2 90.6 %collective-permute-start.53 = (bf16[384,2048]{1,0:T(8,128)(2,1)}, bf16[384,2048]{1,0:T(8,128)(2,1)}, u32[]{:S(2)}, u32[]{:S(2)}) collective-permute-start(bf16[384,2048]{1,0:T(8,128)(2,1)} %pad_maximum_fusion.20), channel_id=1, source_target_pairs={{0,16},{1,17},{2,18},{3,19},{4,20},{5,21},{6,22},{7,23},{8,24},{9,... | collective-permute-start | bytes 4718600 | tf_op jit(solution)/shard_map/ppermute | solution.py:408
  529.8 68.5 %collective-permute-start.46 = (bf16[192,2176]{1,0:T(8,128)(2,1)}, bf16[192,2176]{1,0:T(8,128)(2,1)}, u32[]{:S(2)}, u32[]{:S(2)}) collective-permute-start(bf16[192,2176]{1,0:T(8,128)(2,1)} %get-tuple-element.239.refs_0_), channel_id=1, source_target_pairs={{0,4},{1,5},{2,6},{3,7},{4,0},{5,1},{6,2},{7,3},{8,12},{9,13},{10,... | collective-permute-start | bytes 2506760 | tf_op jit(solution)/shard_map/ppermute | solution.py:408
  553.3 44.9 %collective-permute-start.47 = (bf16[192,2176]{1,0:T(8,128)(2,1)}, bf16[192,2176]{1,0:T(8,128)(2,1)}, u32[]{:S(2)}, u32[]{:S(2)}) collective-permute-start(bf16[192,2176]{1,0:T(8,128)(2,1)} %get-tuple-element.236.refs_0_), channel_id=1, source_target_pairs={{0,2},{1,3},{2,4},{3,5},{4,6},{5,7},{6,0},{7,1},{8,10},{9,11},{10,... | collective-permute-start | bytes 2506760 | tf_op jit(solution)/shard_map/ppermute | solution.py:408
  575.3 26.7 %collective-permute-start.48 = (bf16[192,2176]{1,0:T(8,128)(2,1)S(1)}, bf16[192,2176]{1,0:T(8,128)(2,1)S(1)}, u32[]{:S(2)}, u32[]{:S(2)}) collective-permute-start(bf16[192,2176]{1,0:T(8,128)(2,1)S(1)} %get-tuple-element.235.refs_0_), channel_id=1, source_target_pairs={{0,6},{1,7},{2,0},{3,1},{4,2},{5,3},{6,4},{7,5},{8,14},{9,15},{10,... | collective-permute-start | bytes 2506760 | tf_op jit(solution)/shard_map/ppermute | solution.py:408
  604.8 252.5 %reduce-scatter.5.cloned.1.call-start = ((), (), s32[]{:S(2)}) async-start(), calls=%async_computation.5 | async-start | bytes 2359296 | tf_op jit(solution)/shard_map/reduce_scatter | solution.py:1400
  636.7 82.7 %collective-permute-start.54 = (bf16[1536,2048]{1,0:T(8,128)(2,1)}, bf16[1536,2048]{1,0:T(8,128)(2,1)}, u32[]{:S(2)}, u32[]{:S(2)}) collective-permute-start(bf16[1536,2048]{1,0:T(8,128)(2,1)} %constant_dynamic-update-slice_fusion.26.refs_3_), channel_id=1, source_target_pairs={{0,8},{1,9},{2,10},{3,11},{4,12},{5,13},{6,14},{7,15},{8,0},{9,1},... | collective-permute-start | bytes 18874376 | tf_op jit(solution)/shard_map/ppermute | solution.py:408
  703.4 44.0 %collective-permute-start.55 = (bf16[256,1664]{1,0:T(8,128)(2,1)}, bf16[256,1664]{1,0:T(8,128)(2,1)}, u32[]{:S(2)}, u32[]{:S(2)}) collective-permute-start(bf16[256,1664]{1,0:T(8,128)(2,1)} %pad_maximum_fusion.24.refs_0_), channel_id=1, source_target_pairs={{0,1},{1,0},{2,3},{3,2},{4,5},{5,4},{6,7},{7,6},{8,9},{9,8},{10,11... | collective-permute-start | bytes 2555912 | tf_op jit(solution)/shard_map/ppermute | solution.py:408
  710.2 97.2 %collective-permute-start.60 = (bf16[192,2048]{1,0:T(8,128)(2,1)}, bf16[192,2048]{1,0:T(8,128)(2,1)}, u32[]{:S(2)}, u32[]{:S(2)}) collective-permute-start(bf16[192,2048]{1,0:T(8,128)(2,1)} %slice_bitcast_fusion.11), channel_id=1, source_target_pairs={{0,16},{1,17},{2,18},{3,19},{4,20},{5,21},{6,22},{7,23},{8,24},{9,... | collective-permute-start | bytes 2359304 | tf_op jit(solution)/shard_map/ppermute | solution.py:408
  749.6 57.8 %collective-permute-start.58 = (bf16[256,1664]{1,0:T(8,128)(2,1)}, bf16[256,1664]{1,0:T(8,128)(2,1)}, u32[]{:S(2)}, u32[]{:S(2)}) collective-permute-start(bf16[256,1664]{1,0:T(8,128)(2,1)} %add_convert_fusion.4.refs_0_), channel_id=1, source_target_pairs={{0,4},{1,5},{2,6},{3,7},{4,0},{5,1},{6,2},{7,3},{8,12},{9,13},{10,... | collective-permute-start | bytes 2555912 | tf_op jit(solution)/shard_map/ppermute | solution.py:408
  750.4 54.7 %collective-permute-start.59 = (bf16[256,1664]{1,0:T(8,128)(2,1)}, bf16[256,1664]{1,0:T(8,128)(2,1)}, u32[]{:S(2)}, u32[]{:S(2)}) collective-permute-start(bf16[256,1664]{1,0:T(8,128)(2,1)} %pad_maximum_fusion.25), channel_id=1, source_target_pairs={{0,1},{1,0},{2,3},{3,2},{4,5},{5,4},{6,7},{7,6},{8,9},{9,8},{10,11... | collective-permute-start | bytes 2555912 | tf_op jit(solution)/shard_map/ppermute | solution.py:408
  751.8 55.6 %collective-permute-start.61 = (bf16[256,1664]{1,0:T(8,128)(2,1)}, bf16[256,1664]{1,0:T(8,128)(2,1)}, u32[]{:S(2)}, u32[]{:S(2)}) collective-permute-start(bf16[256,1664]{1,0:T(8,128)(2,1)} %pad_maximum_fusion.26), channel_id=1, source_target_pairs={{0,1},{1,0},{2,3},{3,2},{4,5},{5,4},{6,7},{7,6},{8,9},{9,8},{10,11... | collective-permute-start | bytes 2555912 | tf_op jit(solution)/shard_map/ppermute | solution.py:408
  752.4 64.6 %collective-permute-start.63 = (bf16[256,1664]{1,0:T(8,128)(2,1)}, bf16[256,1664]{1,0:T(8,128)(2,1)S(1)}, u32[]{:S(2)}, u32[]{:S(2)}) collective-permute-start(bf16[256,1664]{1,0:T(8,128)(2,1)} %pad_maximum_fusion.27), channel_id=1, source_target_pairs={{0,1},{1,0},{2,3},{3,2},{4,5},{5,4},{6,7},{7,6},{8,9},{9,8},{10,11... | collective-permute-start | bytes 2555912 | tf_op jit(solution)/shard_map/ppermute | solution.py:408
  809.7 35.1 %collective-permute-start.62 = (bf16[256,1664]{1,0:T(8,128)(2,1)}, bf16[256,1664]{1,0:T(8,128)(2,1)}, u32[]{:S(2)}, u32[]{:S(2)}) collective-permute-start(bf16[256,1664]{1,0:T(8,128)(2,1)} %add_convert_fusion.2), channel_id=1, source_target_pairs={{0,2},{1,3},{2,4},{3,5},{4,6},{5,7},{6,0},{7,1},{8,10},{9,11},{10,... | collective-permute-start | bytes 2555912 | tf_op jit(solution)/shard_map/ppermute | solution.py:408
  818.1 39.2 %collective-permute-start.64 = (bf16[256,1664]{1,0:T(8,128)(2,1)}, bf16[256,1664]{1,0:T(8,128)(2,1)}, u32[]{:S(2)}, u32[]{:S(2)}) collective-permute-start(bf16[256,1664]{1,0:T(8,128)(2,1)} %add_convert_fusion.1), channel_id=1, source_target_pairs={{0,6},{1,7},{2,0},{3,1},{4,2},{5,3},{6,4},{7,5},{8,14},{9,15},{10,... | collective-permute-start | bytes 2555912 | tf_op jit(solution)/shard_map/ppermute | solution.py:408
  821.4 64.3 %collective-permute-start.65 = (bf16[2,1024,2048]{2,1,0:T(8,128)(2,1)}, bf16[2,1024,2048]{2,1,0:T(8,128)(2,1)}, u32[]{:S(2)}, u32[]{:S(2)}) collective-permute-start(bf16[2,1024,2048]{2,1,0:T(8,128)(2,1)} %fusion.38), channel_id=1, source_target_pairs={{0,8},{1,9},{2,10},{3,11},{4,12},{5,13},{6,14},{7,15},{8,0},{9,1},... | collective-permute-start | bytes 25165832 | tf_op jit(solution)/shard_map/ppermute | solution.py:408
  857.4 75.0 %collective-permute-start.69 = (bf16[2,2048,1024]{2,1,0:T(8,128)(2,1)}, bf16[2,2048,1024]{2,1,0:T(8,128)(2,1)}, u32[]{:S(2)}, u32[]{:S(2)}) collective-permute-start(bf16[2,2048,1024]{2,1,0:T(8,128)(2,1)} %fusion.46), channel_id=1, source_target_pairs={{0,8},{1,9},{2,10},{3,11},{4,12},{5,13},{6,14},{7,15},{8,0},{9,1},... | collective-permute-start | bytes 25165832 | tf_op jit(solution)/shard_map/ppermute | solution.py:408
  880.2 76.5 %collective-permute-start.71 = (bf16[2,2048,1024]{2,1,0:T(8,128)(2,1)}, bf16[2,2048,1024]{2,1,0:T(8,128)(2,1)}, u32[]{:S(2)}, u32[]{:S(2)}) collective-permute-start(bf16[2,2048,1024]{2,1,0:T(8,128)(2,1)} %fusion.43.refs_0_), channel_id=1, source_target_pairs={{0,8},{1,9},{2,10},{3,11},{4,12},{5,13},{6,14},{7,15},{8,0},{9,1},... | collective-permute-start | bytes 25165832 | tf_op jit(solution)/shard_map/ppermute | solution.py:408
  (129 other events, 1854.5 us)
Sparse Core Ops, SparseCore 0:
  136.6 115.2 all-gather.2
  348.8 97.4 all-gather.4
  604.9 117.3 reduce-scatter.2
  754.0 90.3 reduce-scatter.4

commit v7 on v6

--- a/solution.py
+++ b/solution.py
@@ -465,7 +465,7 @@
 
 
 LIMIT = 56 * 2**20
-HIDDEN_BLOCK = 256
+HIDDEN_BLOCK = 1024
 WIDTH_BLOCK = 512
 QUIET = pl.CostEstimate(flops=0, bytes_accessed=0, transcendentals=0)
 LOUD = pl.CostEstimate(flops=10**11, bytes_accessed=0, transcendentals=0)

time: 992 us -> 987 us (level)
  Pallas kernels: 369 us -> 351 us
  waiting for transfers between devices: 190 us -> 208 us
    ppermute x72, waiting for transfers between devices: 190 us -> 208 us  [move(): return lax.ppermute(values, AXES, moves)]
    pallas_call x4, Pallas kernels: 76.3 us -> 63.7 us  [cotangent_part(): pl.pallas_call(ordered(cotangent_kernel, len(behind)), grid_spec=pltpu.Pr...]
  transfers between devices with their start and end apart: 76 -> 76, of which waited for: 24 -> 28; matrix products, arithmetic and copies ran while one was open for 29% -> 30% of each run, Pallas kernels for 34% -> 32%
where the time goes in v7:
time: 987 us; the launch traced here: 978 us
  Pallas kernels  351 us (36%)
  waiting for transfers between devices  208 us (21%)
  local copies, waits for them, and re-layouts  126 us (13%)
  other arithmetic  108 us (11%)
  matrix products  101 us (10%)
  starting transfers between devices  67.7 us (7%)
  between operations  15.7 us (2%)
    ppermute x72, waiting for transfers between devices, move(): return lax.ppermute(values, AXES, moves)  208 us
    pallas_call x4, Pallas kernels, forward_part(): pl.pallas_call(ordered(forward_kernel, len(behind)), grid_spec=pltpu.Pref...  107 us
    unnamed x228, local copies, waits for them, and re-layouts  73.7 us
    dot_general x3, matrix products, weight_grad(): jnp.einsum('ecd,ecf->edf', left, right, preferred_element_type=f32)  69.5 us
    ppermute x72, starting transfers between devices, move(): return lax.ppermute(values, AXES, moves)  67.4 us
    pallas_call x4, Pallas kernels, cotangent_part(): pl.pallas_call(ordered(cotangent_kernel, len(behind)), grid_spec=pltpu.Pr...  63.7 us
    pallas_call x3, Pallas kernels, widen(): pl.pallas_call(ordered(widen_kernel, len(behind)), grid_spec=pltpu.Prefet...  51 us
    pallas_call x2, Pallas kernels, backward_part(): pl.pallas_call(ordered(backward_kernel, len(behind)), grid_spec=pltpu.Pre...  49 us
  transfers between devices with their start and end apart: 76, of which 28 were waited for; matrix products, arithmetic and copies ran while one was open for 30% of the time, Pallas kernels for 32%

profile of v7, /device:TPU:0, one launch (start us, length us, event | category | flops | bytes accessed | tf_op | source)
XLA Modules:
  0.0 978.0 jit_solution(15272036779090860808)
XLA Ops:
  28.0 14.7 %collective-permute-done.3 = bf16[2,33,256]{2,1,0:T(8,128)(2,1)S(1)} collective-permute-done((bf16[2,33,256]{2,1,0:T(8,128)(2,1)S(1)}, bf16[2,33,256]{2,1,0:T(8,128)(2,1)S(1)}, u32[]{:S(2)}, u32[]{:S(2)}) %collective-permute-start.3) | collective-permute-done | bytes 33824 | tf_op jit(solution)/shard_map/ppermute | solution.py:408
  45.4 5.4 collective-permute-done.5
  64.1 22.2 %collective-permute-done.9 = bf16[256,1536]{1,0:T(8,128)(2,1)} collective-permute-done((bf16[256,1536]{1,0:T(8,128)(2,1)}, bf16[256,1536]{1,0:T(8,128)(2,1)}, u32[]{:S(2)}, u32[]{:S(2)}) %collective-permute-start.9) | collective-permute-done | bytes 786464 | tf_op jit(solution)/shard_map/ppermute | solution.py:408
  91.2 5.1 collective-permute-done.10
  101.1 13.9 %collective-permute-done.11 = bf16[2,2,168,256]{3,2,1,0:T(8,128)(2,1)S(1)} collective-permute-done((bf16[2,2,168,256]{3,2,1,0:T(8,128)(2,1)S(1)}, bf16[2,2,168,256]{3,2,1,0:T(8,128)(2,1)S(1)}, u32[]{:S(2)}, u32[]{:S(2)}) %collective-permute-start.11) | collective-permute-done | bytes 344096 | tf_op jit(solution)/shard_map/ppermute | solution.py:408
  139.3 4.4 fusion.35
  143.7 8.4 fusion.124.raw_ref.refs_0_
  163.6 10.2 %shard_map.240 = bf16[768,512]{1,0:T(8,128)(2,1)} custom-call(f32[768,1536]{1,0:T(8,128)} %copy-done.12, f32[768,2]{1,0:T(8,128)} %fusion.82.rate_ref.refs_1_, f32[2,512]{1,0:T(2,128)} %bitcast.348, f32[768,128]{1,0:T(8,128)} %get-tuple-element.274.cos_ref.refs_3_, f32[768,128]{1,0:T(8,128)} %get-tuple-element.273.sin_ref.refs_4_, ...), custom_call_target="tpu_custom_call" | custom-call | tf_op jit(solution)/shard_map/pallas_call | solution.py:1009
  177.2 6.4 collective-permute-done.21
  186.5 6.8 collective-permute-done.22
  197.2 3.9 collective-permute-done.17
  202.5 5.7 maximum_select_fusion
  213.2 16.8 %collective-permute-done.26 = bf16[192,2048]{1,0:T(8,128)(2,1)} collective-permute-done((bf16[192,2048]{1,0:T(8,128)(2,1)S(1)}, bf16[192,2048]{1,0:T(8,128)(2,1)}, u32[]{:S(2)}, u32[]{:S(2)}) %collective-permute-start.26) | collective-permute-done | bytes 786464 | tf_op jit(solution)/shard_map/ppermute | solution.py:408
  239.8 4.4 convert_reduce_fusion.1
  247.5 13.9 %collective-permute-done.31 = bf16[192,2048]{1,0:T(8,128)(2,1)} collective-permute-done((bf16[192,2048]{1,0:T(8,128)(2,1)}, bf16[192,2048]{1,0:T(8,128)(2,1)}, u32[]{:S(2)}, u32[]{:S(2)}) %collective-permute-start.31) | collective-permute-done | bytes 786464 | tf_op jit(solution)/shard_map/ppermute | solution.py:408
  264.9 15.9 %collective-permute-done.28.refs_0_ = bf16[192,2048]{1,0:T(8,128)(2,1)} collective-permute-done((bf16[192,2048]{1,0:T(8,128)(2,1)}, bf16[192,2048]{1,0:T(8,128)(2,1)}, u32[]{:S(2)}, u32[]{:S(2)}) %collective-permute-start.28) | collective-permute-done | bytes 786464 | tf_op jit(solution)/shard_map/ppermute | solution.py:408
  281.3 15.9 %shard_map.242 = (bf16[2,480,2048]{2,1,0:T(8,128)(2,1)}, f32[2,480,1024]{2,1,0:T(8,128)}) custom-call(s32[1]{0:T(128)} %bitcast.32.scalar_ref, bf16[192,2048]{1,0:T(8,128)(2,1)} %collective-permute-done.28.refs_0_, s32[2,1,1536]{2,1,0:T(1,128)} %broadcast_in_dim_squeeze.24.refs_1_, bf16[1536,2048]{1,0:T(8,128)(2,1)} %all-gather.3.cloned.1.call-done.refs_2_, ...), custom_call_target="tpu_custom_call" | custom-call | flops 99999997952 | tf_op jit(solution)/shard_map/pallas_call | solution.py:651
  297.2 16.5 %collective-permute-done.34 = bf16[192,2048]{1,0:T(8,128)(2,1)S(1)} collective-permute-done((bf16[192,2048]{1,0:T(8,128)(2,1)}, bf16[192,2048]{1,0:T(8,128)(2,1)S(1)}, u32[]{:S(2)}, u32[]{:S(2)}) %collective-permute-start.34) | collective-permute-done | bytes 786464 | tf_op jit(solution)/shard_map/ppermute | solution.py:408
  317.0 15.9 %shard_map.243 = (bf16[2,480,2048]{2,1,0:T(8,128)(2,1)}, f32[2,480,1024]{2,1,0:T(8,128)}) custom-call(s32[1]{0:T(128)} %bitcast.32.scalar_ref, f32[2,480,1024]{2,1,0:T(8,128)} %get-tuple-element.109.refs_0_.refs_5_, s32[2,1,1536]{2,1,0:T(1,128)} %broadcast_in_dim_squeeze.25.refs_1_, bf16[1536,2048]{1,0:T(8,128)(2,1)} %copy-done.93, ...), custom_call_target="tpu_custom_call" | custom-call | flops 99999997952 | tf_op jit(solution)/shard_map/pallas_call | solution.py:651
  363.3 26.9 %shard_map.244 = (bf16[2,480,2048]{2,1,0:T(8,128)(2,1)}, bf16[2,480,1024]{2,1,0:T(8,128)(2,1)}, bf16[2,480,1024]{2,1,0:T(8,128)(2,1)}, bf16[2,480,1024]{2,1,0:T(8,128)(2,1)}, bf16[2,480,128]{2,1,0:T(8,128)(2,1)}) custom-call(s32[2]{0:T(128)} %pad_add_fusion.scalar_ref, s32[2,1,1536]{2,1,0:T(1,128)} %broadcast_in_dim_squeeze.26.refs_0_, ...), custom_call_target="tpu_custom_call" | custom-call | tf_op jit(solution)/shard_map/pallas_call | solution.py:736
  390.2 26.7 %shard_map.245 = (bf16[2,480,2048]{2,1,0:T(8,128)(2,1)}, bf16[2,480,1024]{2,1,0:T(8,128)(2,1)}, bf16[2,480,1024]{2,1,0:T(8,128)(2,1)}, bf16[2,480,1024]{2,1,0:T(8,128)(2,1)}, bf16[2,480,128]{2,1,0:T(8,128)(2,1)}) custom-call(s32[2]{0:T(128)} %pad_add_fusion.scalar_ref, bf16[2,480,1024]{2,1,0:T(8,128)(2,1)} %get-tuple-element.117.refs_0_.refs_2_, ...), custom_call_target="tpu_custom_call" | custom-call | tf_op jit(solution)/shard_map/pallas_call | solution.py:736
  419.5 24.6 %shard_map.246 = bf16[1536,2176]{1,0:T(8,128)(2,1)} custom-call(s32[1]{0:T(128)} %bitcast.32.scalar_ref, bf16[384,2048]{1,0:T(8,128)(2,1)} %collective-permute-done.30.refs_0_, bf16[384,2048]{1,0:T(8,128)(2,1)} %collective-permute-done.33.refs_1_, s32[1536,2]{1,0:T(8,128)} %get-tuple-element.255.refs_2_, bf16[2,480,1024]{2,1,0:T(8,128)(2,1)} %get-tuple-element.118.refs_3_, ...), custom_call_target="tpu_custom_call" | custom-call | tf_op jit(solution)/shard_map/pallas_call | solution.py:810
  449.5 24.4 %shard_map.247 = bf16[1536,2176]{1,0:T(8,128)(2,1)} custom-call(s32[1]{0:T(128)} %bitcast.32.scalar_ref, bf16[8,192,2176]{2,1,0:T(8,128)(2,1)} %bitcast.297, s32[1536,2]{1,0:T(8,128)} %get-tuple-element.254.refs_1_, bf16[2,480,1024]{2,1,0:T(8,128)(2,1)} %get-tuple-element.121.refs_2_, bf16[2,480,1024]{2,1,0:T(8,128)(2,1)} %get-tuple-element.122.refs_3_, ...), custom_call_target="tpu_custom_call" | custom-call | tf_op jit(solution)/shard_map/pallas_call | solution.py:810
  479.0 4.7 collective-permute-done.40.refs_1_
  483.8 16.8 %shard_map.248 = bf16[1536,2048]{1,0:T(8,128)(2,1)} custom-call(s32[1]{0:T(128)} %bitcast.32.scalar_ref, bf16[192,2176]{1,0:T(8,128)(2,1)} %fusion.60.refs_0_, bf16[384,2048]{1,0:T(8,128)(2,1)} %collective-permute-done.40.refs_1_, bf16[1536,2048]{1,0:T(8,128)(2,1)} %all-gather.5.cloned.1.call-done.refs_2_, s32[1536,2]{1,0:T(8,128)} %get-tuple-element.253.refs_3_, ...), custom_call_target="tpu_custom_call" | custom-call | flops 99999997952 | tf_op jit(solution)/shard_map/pallas_call | solution.py:872
  512.0 9.5 collective-permute-done.39
  526.2 17.2 %shard_map.249 = bf16[1536,2048]{1,0:T(8,128)(2,1)} custom-call(s32[1]{0:T(128)} %bitcast.32.scalar_ref, bf16[192,2176]{1,0:T(8,128)(2,1)} %get-tuple-element.239.refs_0_, s32[1536,2]{1,0:T(8,128)} %get-tuple-element.252.refs_1_, bf16[2,480,1024]{2,1,0:T(8,128)(2,1)} %get-tuple-element.117.refs_0_.refs_2_, bf16[4,1024,2048]{2,1,0:T(8,128)(2,1)} %refs_3_.11, ...), custom_call_target="tpu_custom_call" | custom-call | flops 99999997952 | tf_op jit(solution)/shard_map/pallas_call | solution.py:872
  549.8 16.0 %shard_map.250 = (bf16[2,480,2048]{2,1,0:T(8,128)(2,1)}, f32[2,480,1024]{2,1,0:T(8,128)}) custom-call(s32[1]{0:T(128)} %bitcast.32.scalar_ref, bf16[192,2176]{1,0:T(8,128)(2,1)} %get-tuple-element.236.refs_0_, s32[2,1,1536]{2,1,0:T(1,128)} %broadcast_in_dim_squeeze.28.refs_1_, bf16[1536,2048]{1,0:T(8,128)(2,1)} %all-gather.5.cloned.1.call-done.refs_2_, ...), custom_call_target="tpu_custom_call" | custom-call | flops 99999997952 | tf_op jit(solution)/shard_map/pallas_call | solution.py:651
  572.8 15.9 %shard_map.251 = (bf16[2,480,2048]{2,1,0:T(8,128)(2,1)}, f32[2,480,1024]{2,1,0:T(8,128)}) custom-call(s32[1]{0:T(128)} %bitcast.32.scalar_ref, bf16[192,2176]{1,0:T(8,128)(2,1)} %copy-done.52, s32[2,1,1536]{2,1,0:T(1,128)} %broadcast_in_dim_squeeze.29.refs_1_, bf16[1536,2048]{1,0:T(8,128)(2,1)} %collective-permute-done.45.refs_2_, ...), custom_call_target="tpu_custom_call" | custom-call | flops 99999997952 | tf_op jit(solution)/shard_map/pallas_call | solution.py:651
  589.3 9.4 collective-permute-done.48
  615.3 9.7 collective-permute-done.49
  634.9 20.2 %shard_map.253 = (f32[768,1024]{1,0:T(8,128)}, bf16[768,512]{1,0:T(8,128)(2,1)}, f32[768,2]{1,0:T(8,128)}, f32[4,2,512]{2,1,0:T(2,128)}) custom-call(f32[768,1536]{1,0:T(8,128)} %copy-done.12, f32[768,2]{1,0:T(8,128)} %fusion.82.rate_ref.refs_1_, f32[2,512]{1,0:T(2,128)} %bitcast.349, f32[768,128]{1,0:T(8,128)} %get-tuple-element.274.cos_ref.refs_3_, ...), custom_call_target="tpu_custom_call" | custom-call | tf_op jit(solution)/shard_map/pallas_call | solution.py:1029
  663.4 6.2 shard_map.254
  669.6 8.1 fusion.117
  687.5 5.4 convolution_convert_fusion
  716.3 26.9 %shard_map.255 = (bf16[2,480,2048]{2,1,0:T(8,128)(2,1)}, bf16[2,480,1024]{2,1,0:T(8,128)(2,1)}, bf16[2,480,1024]{2,1,0:T(8,128)(2,1)}, bf16[2,480,1024]{2,1,0:T(8,128)(2,1)}, bf16[2,480,128]{2,1,0:T(8,128)(2,1)}) custom-call(s32[2]{0:T(128)} %pad_add_fusion.scalar_ref, bf16[256,1664]{1,0:T(8,128)(2,1)} %pad_maximum_fusion.24.refs_0_, ...), custom_call_target="tpu_custom_call" | custom-call | flops 99999997952 | tf_op jit(solution)/shard_map/pallas_call | solution.py:736
  749.8 26.8 %shard_map.256 = (bf16[2,480,2048]{2,1,0:T(8,128)(2,1)}, bf16[2,480,1024]{2,1,0:T(8,128)(2,1)}, bf16[2,480,1024]{2,1,0:T(8,128)(2,1)}, bf16[2,480,1024]{2,1,0:T(8,128)(2,1)}, bf16[2,480,128]{2,1,0:T(8,128)(2,1)}) custom-call(s32[2]{0:T(128)} %pad_add_fusion.scalar_ref, bf16[256,1664]{1,0:T(8,128)(2,1)} %add_convert_fusion.4.refs_0_, ...), custom_call_target="tpu_custom_call" | custom-call | flops 99999997952 | tf_op jit(solution)/shard_map/pallas_call | solution.py:736
  776.7 23.5 %fusion.38 = bf16[2,1024,2048]{2,1,0:T(8,128)(2,1)} fusion(bf16[2,480,2048]{2,1,0:T(8,128)(2,1)} %get-tuple-element.151, bf16[2,480,2048]{2,1,0:T(8,128)(2,1)} %get-tuple-element.150, bf16[2,480,2048]{2,1,0:T(8,128)(2,1)} %get-tuple-element.149, bf16[2,480,2048]{2,1,0:T(8,128)(2,1)} %get-tuple-element.148, bf16[2,480,1024]{2,1,0:T(8,128)(2,1)} %get-tuple-element.147, ...), kind=kOutput, calls=%fused_computation.57 | convolution fusion | flops 16204693504 | bytes 31981568 | tf_op jit(solution)/shard_map/ecd,ecf->edf/dot_general | solution.py:1391
  806.8 7.5 collective-permute-done.63
  817.4 23.2 %fusion.46 = bf16[2,2048,1024]{2,1,0:T(8,128)(2,1)} fusion(bf16[2,480,1024]{2,1,0:T(8,128)(2,1)} %get-tuple-element.160, bf16[2,480,1024]{2,1,0:T(8,128)(2,1)} %get-tuple-element.159, bf16[2,480,1024]{2,1,0:T(8,128)(2,1)} %get-tuple-element.118.refs_3_, bf16[2,480,1024]{2,1,0:T(8,128)(2,1)} %get-tuple-element.121.refs_2_, ...), kind=kOutput, calls=%fused_computation.59 | convolution fusion | flops 16204693504 | bytes 31981568 | tf_op jit(solution)/shard_map/ecd,ecf->edf/dot_general | solution.py:1391
  840.6 12.5 %collective-permute-done.64 = bf16[256,1664]{1,0:T(8,128)(2,1)} collective-permute-done((bf16[256,1664]{1,0:T(8,128)(2,1)}, bf16[256,1664]{1,0:T(8,128)(2,1)}, u32[]{:S(2)}, u32[]{:S(2)}) %collective-permute-start.64) | collective-permute-done | bytes 852000 | tf_op jit(solution)/shard_map/ppermute | solution.py:408
  853.1 22.8 %fusion.43.refs_0_ = bf16[2,2048,1024]{2,1,0:T(8,128)(2,1)} fusion(bf16[2,480,1024]{2,1,0:T(8,128)(2,1)} %get-tuple-element.153, bf16[2,480,1024]{2,1,0:T(8,128)(2,1)} %get-tuple-element.144.refs_1_, bf16[2,480,1024]{2,1,0:T(8,128)(2,1)} %get-tuple-element.119.refs_4_, bf16[2,480,1024]{2,1,0:T(8,128)(2,1)S(1)} %copy-done.44, ...), kind=kOutput, calls=%fused_computation.58 | convolution fusion | flops 16204693504 | bytes 31981568 | tf_op jit(solution)/shard_map/ecd,ecf->edf/dot_general | solution.py:1391
  884.8 3.4 copy-done.8
  888.2 16.9 %shard_map.257 = f32[4096,2048]{1,0:T(8,128)} custom-call(s32[1]{0:T(128)} %bitcast.32.scalar_ref, bf16[2,2048,1024]{2,1,0:T(8,128)(2,1)S(1)} %copy-done.2, bf16[2048,2048]{1,0:T(8,128)(2,1)S(1)} %bitcast.287, bf16[2048,2048]{1,0:T(8,128)(2,1)} %bitcast.89.refs_2_), custom_call_target="tpu_custom_call" | custom-call | tf_op jit(solution)/shard_map/pallas_call | solution.py:592
  928.1 3.4 copy-done.7
  931.5 17.0 %shard_map.259 = f32[8192,1024]{1,0:T(8,128)} custom-call(s32[1]{0:T(128)} %bitcast.32.scalar_ref, f32[4,1024,2048]{2,1,0:T(8,128)} %bitcast.293, bf16[64,2048]{1,0:T(8,128)(2,1)S(1)} %collective-permute-done.68.refs_1_, bf16[4096,1024]{1,0:T(8,128)(2,1)S(1)} %bitcast.286, bf16[4096,1024]{1,0:T(8,128)(2,1)} %bitcast.100.refs_3_), custom_call_target="tpu_custom_call" | custom-call | tf_op jit(solution)/shard_map/pallas_call | solution.py:592
  948.5 4.0 shard_map.260
  954.2 17.0 %shard_map.261 = f32[8192,1024]{1,0:T(8,128)} custom-call(s32[1]{0:T(128)} %bitcast.32.scalar_ref, f32[4,2048,1024]{2,1,0:T(8,128)} %bitcast.291, bf16[4096,1024]{1,0:T(8,128)(2,1)S(1)} %bitcast.281, bf16[4096,1024]{1,0:T(8,128)(2,1)} %bitcast.111.refs_2_), custom_call_target="tpu_custom_call" | custom-call | tf_op jit(solution)/shard_map/pallas_call | solution.py:592
  (594 shorter events, 309.3 us)
Async XLA Ops:
  7.2 274.1 %all-gather.3.cloned.1.call-start = ((), (), s32[]{:S(2)}) async-start(), calls=%async_computation.2 | async-start | bytes 7077888 | tf_op jit(solution)/shard_map/all_gather | solution.py:1162
  9.7 52.3 %collective-permute-start.13 = (bf16[256,1536]{1,0:T(8,128)(2,1)S(1)}, bf16[256,1536]{1,0:T(8,128)(2,1)}, u32[]{:S(2)}, u32[]{:S(2)}) collective-permute-start(bf16[256,1536]{1,0:T(8,128)(2,1)S(1)} %shard_map.239), channel_id=1, source_target_pairs={{0,1},{1,0},{2,3},{3,2},{4,5},{5,4},{6,7},{7,6},{8,9},{9,8},{10,11... | collective-permute-start | bytes 2359304 | tf_op jit(solution)/shard_map/ppermute | solution.py:408
  12.8 39.9 %collective-permute-start.8 = (bf16[256,1536]{1,0:T(8,128)(2,1)S(1)}, bf16[256,1536]{1,0:T(8,128)(2,1)}, u32[]{:S(2)}, u32[]{:S(2)}) collective-permute-start(bf16[256,1536]{1,0:T(8,128)(2,1)S(1)} %shard_map.239), channel_id=1, source_target_pairs={{0,2},{1,3},{2,4},{3,5},{4,6},{5,7},{6,0},{7,1},{8,10},{9,11},{10,... | collective-permute-start | bytes 2359304 | tf_op jit(solution)/shard_map/ppermute | solution.py:408
  14.3 36.4 %collective-permute-start.5 = (bf16[256,1536]{1,0:T(8,128)(2,1)S(1)}, bf16[256,1536]{1,0:T(8,128)(2,1)}, u32[]{:S(2)}, u32[]{:S(2)}) collective-permute-start(bf16[256,1536]{1,0:T(8,128)(2,1)S(1)} %shard_map.239), channel_id=1, source_target_pairs={{0,6},{1,7},{2,0},{3,1},{4,2},{5,3},{6,4},{7,5},{8,14},{9,15},{10,... | collective-permute-start | bytes 2359304 | tf_op jit(solution)/shard_map/ppermute | solution.py:408
  21.9 28.9 %collective-permute-start = (bf16[192,2048]{1,0:T(8,128)(2,1)S(1)}, bf16[192,2048]{1,0:T(8,128)(2,1)}, u32[]{:S(2)}, u32[]{:S(2)}) collective-permute-start(bf16[192,2048]{1,0:T(8,128)(2,1)S(1)} %copy-done.16), channel_id=1, source_target_pairs={{0,16},{1,17},{2,18},{3,19},{4,20},{5,21},{6,22},{7,23},{8,24},{9,... | collective-permute-start | bytes 2359304 | tf_op jit(solution)/shard_map/ppermute | solution.py:408
  50.8 35.9 %collective-permute-start.6 = (bf16[256,1536]{1,0:T(8,128)(2,1)S(1)}, bf16[256,1536]{1,0:T(8,128)(2,1)}, u32[]{:S(2)}, u32[]{:S(2)}) collective-permute-start(bf16[256,1536]{1,0:T(8,128)(2,1)S(1)} %shard_map.239), channel_id=1, source_target_pairs={{0,4},{1,5},{2,6},{3,7},{4,0},{5,1},{6,2},{7,3},{8,12},{9,13},{10,... | collective-permute-start | bytes 2359304 | tf_op jit(solution)/shard_map/ppermute | solution.py:408
  52.1 34.3 %collective-permute-start.7 = (bf16[256,1536]{1,0:T(8,128)(2,1)}, bf16[256,1536]{1,0:T(8,128)(2,1)}, u32[]{:S(2)}, u32[]{:S(2)}) collective-permute-start(bf16[256,1536]{1,0:T(8,128)(2,1)} %collective-permute-done.5), channel_id=1, source_target_pairs={{0,1},{1,0},{2,3},{3,2},{4,5},{5,4},{6,7},{7,6},{8,9},{9,8},{10,11... | collective-permute-start | bytes 2359304 | tf_op jit(solution)/shard_map/ppermute | solution.py:408
  52.6 33.8 %collective-permute-start.9 = (bf16[256,1536]{1,0:T(8,128)(2,1)}, bf16[256,1536]{1,0:T(8,128)(2,1)}, u32[]{:S(2)}, u32[]{:S(2)}) collective-permute-start(bf16[256,1536]{1,0:T(8,128)(2,1)} %collective-permute-done.8), channel_id=1, source_target_pairs={{0,1},{1,0},{2,3},{3,2},{4,5},{5,4},{6,7},{7,6},{8,9},{9,8},{10,11... | collective-permute-start | bytes 2359304 | tf_op jit(solution)/shard_map/ppermute | solution.py:408
  57.5 86.2 %collective-permute-start.12 = (bf16[192,2048]{1,0:T(8,128)(2,1)S(1)}, bf16[192,2048]{1,0:T(8,128)(2,1)}, u32[]{:S(2)}, u32[]{:S(2)}) collective-permute-start(bf16[192,2048]{1,0:T(8,128)(2,1)S(1)} %copy-done.28), channel_id=1, source_target_pairs={{0,16},{1,17},{2,18},{3,19},{4,20},{5,21},{6,22},{7,23},{8,24},{9,... | collective-permute-start | bytes 2359304 | tf_op jit(solution)/shard_map/ppermute | solution.py:408
  62.0 62.9 %collective-permute-start.1 = (bf16[2,192,2048]{2,1,0:T(8,128)(2,1)}, bf16[2,192,2048]{2,1,0:T(8,128)(2,1)}, u32[]{:S(2)}, u32[]{:S(2)}) collective-permute-start(bf16[2,192,2048]{2,1,0:T(8,128)(2,1)} %get-tuple-element.257), channel_id=1, source_target_pairs={{0,8},{1,9},{2,10},{3,11},{4,12},{5,13},{6,14},{7,15},{8,0},{9,1},... | collective-permute-start | bytes 4718600 | tf_op jit(solution)/shard_map/ppermute | solution.py:408
  90.7 40.7 %collective-permute-start.14 = (bf16[256,1536]{1,0:T(8,128)(2,1)}, bf16[256,1536]{1,0:T(8,128)(2,1)S(1)}, u32[]{:S(2)}, u32[]{:S(2)}) collective-permute-start(bf16[256,1536]{1,0:T(8,128)(2,1)} %collective-permute-done.6), channel_id=1, source_target_pairs={{0,1},{1,0},{2,3},{3,2},{4,5},{5,4},{6,7},{7,6},{8,9},{9,8},{10,11... | collective-permute-start | bytes 2359304 | tf_op jit(solution)/shard_map/ppermute | solution.py:408
  114.9 41.4 %collective-permute-start.23 = (bf16[64,2048]{1,0:T(8,128)(2,1)S(1)}, bf16[64,2048]{1,0:T(8,128)(2,1)}, u32[]{:S(2)}, u32[]{:S(2)}) collective-permute-start(bf16[64,2048]{1,0:T(8,128)(2,1)S(1)} %copy-done.48), channel_id=1, source_target_pairs={{0,2},{1,3},{2,4},{3,5},{4,6},{5,7},{6,0},{7,1},{8,10},{9,11},{10,... | collective-permute-start | bytes 786440 | tf_op jit(solution)/shard_map/ppermute | solution.py:408
  118.1 37.2 %collective-permute-start.19 = (bf16[64,2048]{1,0:T(8,128)(2,1)S(1)}, bf16[64,2048]{1,0:T(8,128)(2,1)}, u32[]{:S(2)}, u32[]{:S(2)}) collective-permute-start(bf16[64,2048]{1,0:T(8,128)(2,1)S(1)} %copy-done.48), channel_id=1, source_target_pairs={{0,6},{1,7},{2,0},{3,1},{4,2},{5,3},{6,4},{7,5},{8,14},{9,15},{10,... | collective-permute-start | bytes 786440 | tf_op jit(solution)/shard_map/ppermute | solution.py:408
  124.9 48.8 %collective-permute-start.18 = (bf16[64,2048]{1,0:T(8,128)(2,1)S(1)}, bf16[64,2048]{1,0:T(8,128)(2,1)}, u32[]{:S(2)}, u32[]{:S(2)}) collective-permute-start(bf16[64,2048]{1,0:T(8,128)(2,1)S(1)} %copy-done.48), channel_id=1, source_target_pairs={{0,1},{1,0},{2,3},{3,2},{4,5},{5,4},{6,7},{7,6},{8,9},{9,8},{10,11... | collective-permute-start | bytes 786440 | tf_op jit(solution)/shard_map/ppermute | solution.py:408
  136.5 347.2 %all-gather.5.cloned.1.call-start = ((), (), s32[]{:S(2)}) async-start(), calls=%async_computation.3 | async-start | bytes 7077888 | tf_op jit(solution)/shard_map/all_gather | solution.py:1268
  155.3 28.3 %collective-permute-start.21 = (bf16[64,2048]{1,0:T(8,128)(2,1)S(1)}, bf16[64,2048]{1,0:T(8,128)(2,1)S(1)}, u32[]{:S(2)}, u32[]{:S(2)}) collective-permute-start(bf16[64,2048]{1,0:T(8,128)(2,1)S(1)} %copy-done.48), channel_id=1, source_target_pairs={{0,4},{1,5},{2,6},{3,7},{4,0},{5,1},{6,2},{7,3},{8,12},{9,13},{10,... | collective-permute-start | bytes 786440 | tf_op jit(solution)/shard_map/ppermute | solution.py:408
  156.3 28.7 %collective-permute-start.20 = (bf16[64,2048]{1,0:T(8,128)(2,1)}, bf16[64,2048]{1,0:T(8,128)(2,1)S(1)}, u32[]{:S(2)}, u32[]{:S(2)}) collective-permute-start(bf16[64,2048]{1,0:T(8,128)(2,1)} %collective-permute-done.19), channel_id=1, source_target_pairs={{0,1},{1,0},{2,3},{3,2},{4,5},{5,4},{6,7},{7,6},{8,9},{9,8},{10,11... | collective-permute-start | bytes 786440 | tf_op jit(solution)/shard_map/ppermute | solution.py:408
  157.9 27.9 %collective-permute-start.24 = (bf16[64,2048]{1,0:T(8,128)(2,1)}, bf16[64,2048]{1,0:T(8,128)(2,1)S(1)}, u32[]{:S(2)}, u32[]{:S(2)}) collective-permute-start(bf16[64,2048]{1,0:T(8,128)(2,1)} %collective-permute-done.23), channel_id=1, source_target_pairs={{0,1},{1,0},{2,3},{3,2},{4,5},{5,4},{6,7},{7,6},{8,9},{9,8},{10,11... | collective-permute-start | bytes 786440 | tf_op jit(solution)/shard_map/ppermute | solution.py:408
  234.8 26.6 %collective-permute-start.31 = (bf16[192,2048]{1,0:T(8,128)(2,1)}, bf16[192,2048]{1,0:T(8,128)(2,1)}, u32[]{:S(2)}, u32[]{:S(2)}) collective-permute-start(bf16[192,2048]{1,0:T(8,128)(2,1)} %get-tuple-element.113), channel_id=1, source_target_pairs={{0,6},{1,7},{2,0},{3,1},{4,2},{5,3},{6,4},{7,5},{8,14},{9,15},{10,... | collective-permute-start | bytes 2359304 | tf_op jit(solution)/shard_map/ppermute | solution.py:408
  234.8 46.0 %collective-permute-start.28 = (bf16[192,2048]{1,0:T(8,128)(2,1)}, bf16[192,2048]{1,0:T(8,128)(2,1)}, u32[]{:S(2)}, u32[]{:S(2)}) collective-permute-start(bf16[192,2048]{1,0:T(8,128)(2,1)} %get-tuple-element.113), channel_id=1, source_target_pairs={{0,2},{1,3},{2,4},{3,5},{4,6},{5,7},{6,0},{7,1},{8,10},{9,11},{10,... | collective-permute-start | bytes 2359304 | tf_op jit(solution)/shard_map/ppermute | solution.py:408
  237.0 96.1 %collective-permute-start.27 = (bf16[192,2048]{1,0:T(8,128)(2,1)}, bf16[192,2048]{1,0:T(8,128)(2,1)}, u32[]{:S(2)}, u32[]{:S(2)}) collective-permute-start(bf16[192,2048]{1,0:T(8,128)(2,1)} %get-tuple-element.113), channel_id=1, source_target_pairs={{0,1},{1,0},{2,3},{3,2},{4,5},{5,4},{6,7},{7,6},{8,9},{9,8},{10,11... | collective-permute-start | bytes 2359304 | tf_op jit(solution)/shard_map/ppermute | solution.py:408
  261.4 52.3 %collective-permute-start.34 = (bf16[192,2048]{1,0:T(8,128)(2,1)}, bf16[192,2048]{1,0:T(8,128)(2,1)S(1)}, u32[]{:S(2)}, u32[]{:S(2)}) collective-permute-start(bf16[192,2048]{1,0:T(8,128)(2,1)} %get-tuple-element.113), channel_id=1, source_target_pairs={{0,4},{1,5},{2,6},{3,7},{4,0},{5,1},{6,2},{7,3},{8,12},{9,13},{10,... | collective-permute-start | bytes 2359304 | tf_op jit(solution)/shard_map/ppermute | solution.py:408
  264.4 68.8 %collective-permute-start.32 = (bf16[192,2048]{1,0:T(8,128)(2,1)}, bf16[192,2048]{1,0:T(8,128)(2,1)}, u32[]{:S(2)}, u32[]{:S(2)}) collective-permute-start(bf16[192,2048]{1,0:T(8,128)(2,1)} %collective-permute-done.31), channel_id=1, source_target_pairs={{0,1},{1,0},{2,3},{3,2},{4,5},{5,4},{6,7},{7,6},{8,9},{9,8},{10,11... | collective-permute-start | bytes 2359304 | tf_op jit(solution)/shard_map/ppermute | solution.py:408
  280.8 52.1 %collective-permute-start.36 = (bf16[192,2048]{1,0:T(8,128)(2,1)}, bf16[192,2048]{1,0:T(8,128)(2,1)}, u32[]{:S(2)}, u32[]{:S(2)}) collective-permute-start(bf16[192,2048]{1,0:T(8,128)(2,1)} %collective-permute-done.28.refs_0_), channel_id=1, source_target_pairs={{0,1},{1,0},{2,3},{3,2},{4,5},{5,4},{6,7},{7,6},{8,9},{9,8},{10,11... | collective-permute-start | bytes 2359304 | tf_op jit(solution)/shard_map/ppermute | solution.py:408
  281.3 33.0 %collective-permute-start.29 = (bf16[1536,2048]{1,0:T(8,128)(2,1)}, bf16[1536,2048]{1,0:T(8,128)(2,1)S(1)}, u32[]{:S(2)}, u32[]{:S(2)}) collective-permute-start(bf16[1536,2048]{1,0:T(8,128)(2,1)} %all-gather.3.cloned.1.call-done.refs_2_), channel_id=1, source_target_pairs={{0,8},{1,9},{2,10},{3,11},{4,12},{5,13},{6,14},{7,15},{8,0},{9,1},... | collective-permute-start | bytes 18874376 | tf_op jit(solution)/shard_map/ppermute | solution.py:408
  345.8 44.4 %collective-permute-start.37 = (bf16[1536,2048]{1,0:T(8,128)(2,1)}, bf16[1536,2048]{1,0:T(8,128)(2,1)}, u32[]{:S(2)}, u32[]{:S(2)}) collective-permute-start(bf16[1536,2048]{1,0:T(8,128)(2,1)} %constant_dynamic-update-slice_fusion.18.refs_1_), channel_id=1, source_target_pairs={{0,8},{1,9},{2,10},{3,11},{4,12},{5,13},{6,14},{7,15},{8,0},{9,1},... | collective-permute-start | bytes 18874376 | tf_op jit(solution)/shard_map/ppermute | solution.py:408
  345.9 403.9 %reduce-scatter.3.cloned.1.call-start = ((), (), s32[]{:S(2)}) async-start(), calls=%async_computation.4 | async-start | bytes 7077888 | tf_op jit(solution)/shard_map/reduce_scatter | solution.py:1310
  348.7 68.2 %collective-permute-start.30 = (bf16[384,2048]{1,0:T(8,128)(2,1)}, bf16[384,2048]{1,0:T(8,128)(2,1)}, u32[]{:S(2)}, u32[]{:S(2)}) collective-permute-start(bf16[384,2048]{1,0:T(8,128)(2,1)} %pad_maximum_fusion.16), channel_id=1, source_target_pairs={{0,16},{1,17},{2,18},{3,19},{4,20},{5,21},{6,22},{7,23},{8,24},{9,... | collective-permute-start | bytes 4718600 | tf_op jit(solution)/shard_map/ppermute | solution.py:408
  353.0 66.5 %collective-permute-start.33 = (bf16[384,2048]{1,0:T(8,128)(2,1)}, bf16[384,2048]{1,0:T(8,128)(2,1)}, u32[]{:S(2)}, u32[]{:S(2)}) collective-permute-start(bf16[384,2048]{1,0:T(8,128)(2,1)} %pad_maximum_fusion.17), channel_id=1, source_target_pairs={{0,16},{1,17},{2,18},{3,19},{4,20},{5,21},{6,22},{7,23},{8,24},{9,... | collective-permute-start | bytes 4718600 | tf_op jit(solution)/shard_map/ppermute | solution.py:408
  444.1 29.7 %collective-permute-start.38 = (bf16[8,192,2176]{2,1,0:T(8,128)(2,1)}, bf16[8,192,2176]{2,1,0:T(8,128)(2,1)S(1)}, u32[]{:S(2)}, u32[]{:S(2)}) collective-permute-start(bf16[8,192,2176]{2,1,0:T(8,128)(2,1)} %bitcast.296), channel_id=1, source_target_pairs={{0,8},{1,9},{2,10},{3,11},{4,12},{5,13},{6,14},{7,15},{8,0},{9,1},... | collective-permute-start | bytes 20054024 | tf_op jit(solution)/shard_map/ppermute | solution.py:408
  446.7 37.0 %collective-permute-start.40 = (bf16[384,2048]{1,0:T(8,128)(2,1)}, bf16[384,2048]{1,0:T(8,128)(2,1)}, u32[]{:S(2)}, u32[]{:S(2)}) collective-permute-start(bf16[384,2048]{1,0:T(8,128)(2,1)} %pad_maximum_fusion.18), channel_id=1, source_target_pairs={{0,16},{1,17},{2,18},{3,19},{4,20},{5,21},{6,22},{7,23},{8,24},{9,... | collective-permute-start | bytes 4718600 | tf_op jit(solution)/shard_map/ppermute | solution.py:408
  510.6 90.8 %collective-permute-start.53 = (bf16[384,2048]{1,0:T(8,128)(2,1)}, bf16[384,2048]{1,0:T(8,128)(2,1)}, u32[]{:S(2)}, u32[]{:S(2)}) collective-permute-start(bf16[384,2048]{1,0:T(8,128)(2,1)} %pad_maximum_fusion.20), channel_id=1, source_target_pairs={{0,16},{1,17},{2,18},{3,19},{4,20},{5,21},{6,22},{7,23},{8,24},{9,... | collective-permute-start | bytes 4718600 | tf_op jit(solution)/shard_map/ppermute | solution.py:408
  526.2 63.1 %collective-permute-start.46 = (bf16[192,2176]{1,0:T(8,128)(2,1)}, bf16[192,2176]{1,0:T(8,128)(2,1)}, u32[]{:S(2)}, u32[]{:S(2)}) collective-permute-start(bf16[192,2176]{1,0:T(8,128)(2,1)} %get-tuple-element.239.refs_0_), channel_id=1, source_target_pairs={{0,4},{1,5},{2,6},{3,7},{4,0},{5,1},{6,2},{7,3},{8,12},{9,13},{10,... | collective-permute-start | bytes 2506760 | tf_op jit(solution)/shard_map/ppermute | solution.py:408
  549.8 39.5 %collective-permute-start.47 = (bf16[192,2176]{1,0:T(8,128)(2,1)}, bf16[192,2176]{1,0:T(8,128)(2,1)}, u32[]{:S(2)}, u32[]{:S(2)}) collective-permute-start(bf16[192,2176]{1,0:T(8,128)(2,1)} %get-tuple-element.236.refs_0_), channel_id=1, source_target_pairs={{0,2},{1,3},{2,4},{3,5},{4,6},{5,7},{6,0},{7,1},{8,10},{9,11},{10,... | collective-permute-start | bytes 2506760 | tf_op jit(solution)/shard_map/ppermute | solution.py:408
  571.8 27.0 %collective-permute-start.48 = (bf16[192,2176]{1,0:T(8,128)(2,1)S(1)}, bf16[192,2176]{1,0:T(8,128)(2,1)S(1)}, u32[]{:S(2)}, u32[]{:S(2)}) collective-permute-start(bf16[192,2176]{1,0:T(8,128)(2,1)S(1)} %get-tuple-element.235.refs_0_), channel_id=1, source_target_pairs={{0,6},{1,7},{2,0},{3,1},{4,2},{5,3},{6,4},{7,5},{8,14},{9,15},{10,... | collective-permute-start | bytes 2506760 | tf_op jit(solution)/shard_map/ppermute | solution.py:408
  601.5 251.6 %reduce-scatter.5.cloned.1.call-start = ((), (), s32[]{:S(2)}) async-start(), calls=%async_computation.5 | async-start | bytes 2359296 | tf_op jit(solution)/shard_map/reduce_scatter | solution.py:1400
  633.5 82.8 %collective-permute-start.54 = (bf16[1536,2048]{1,0:T(8,128)(2,1)}, bf16[1536,2048]{1,0:T(8,128)(2,1)}, u32[]{:S(2)}, u32[]{:S(2)}) collective-permute-start(bf16[1536,2048]{1,0:T(8,128)(2,1)} %constant_dynamic-update-slice_fusion.26.refs_3_), channel_id=1, source_target_pairs={{0,8},{1,9},{2,10},{3,11},{4,12},{5,13},{6,14},{7,15},{8,0},{9,1},... | collective-permute-start | bytes 18874376 | tf_op jit(solution)/shard_map/ppermute | solution.py:408
  700.0 43.2 %collective-permute-start.55 = (bf16[256,1664]{1,0:T(8,128)(2,1)}, bf16[256,1664]{1,0:T(8,128)(2,1)}, u32[]{:S(2)}, u32[]{:S(2)}) collective-permute-start(bf16[256,1664]{1,0:T(8,128)(2,1)} %pad_maximum_fusion.24.refs_0_), channel_id=1, source_target_pairs={{0,1},{1,0},{2,3},{3,2},{4,5},{5,4},{6,7},{7,6},{8,9},{9,8},{10,11... | collective-permute-start | bytes 2555912 | tf_op jit(solution)/shard_map/ppermute | solution.py:408
  707.2 95.4 %collective-permute-start.60 = (bf16[192,2048]{1,0:T(8,128)(2,1)}, bf16[192,2048]{1,0:T(8,128)(2,1)}, u32[]{:S(2)}, u32[]{:S(2)}) collective-permute-start(bf16[192,2048]{1,0:T(8,128)(2,1)} %slice_bitcast_fusion.11), channel_id=1, source_target_pairs={{0,16},{1,17},{2,18},{3,19},{4,20},{5,21},{6,22},{7,23},{8,24},{9,... | collective-permute-start | bytes 2359304 | tf_op jit(solution)/shard_map/ppermute | solution.py:408
  745.5 57.0 %collective-permute-start.58 = (bf16[256,1664]{1,0:T(8,128)(2,1)}, bf16[256,1664]{1,0:T(8,128)(2,1)}, u32[]{:S(2)}, u32[]{:S(2)}) collective-permute-start(bf16[256,1664]{1,0:T(8,128)(2,1)} %add_convert_fusion.4.refs_0_), channel_id=1, source_target_pairs={{0,4},{1,5},{2,6},{3,7},{4,0},{5,1},{6,2},{7,3},{8,12},{9,13},{10,... | collective-permute-start | bytes 2555912 | tf_op jit(solution)/shard_map/ppermute | solution.py:408
  746.7 53.5 %collective-permute-start.59 = (bf16[256,1664]{1,0:T(8,128)(2,1)}, bf16[256,1664]{1,0:T(8,128)(2,1)}, u32[]{:S(2)}, u32[]{:S(2)}) collective-permute-start(bf16[256,1664]{1,0:T(8,128)(2,1)} %pad_maximum_fusion.25), channel_id=1, source_target_pairs={{0,1},{1,0},{2,3},{3,2},{4,5},{5,4},{6,7},{7,6},{8,9},{9,8},{10,11... | collective-permute-start | bytes 2555912 | tf_op jit(solution)/shard_map/ppermute | solution.py:408
  747.8 54.8 %collective-permute-start.61 = (bf16[256,1664]{1,0:T(8,128)(2,1)}, bf16[256,1664]{1,0:T(8,128)(2,1)}, u32[]{:S(2)}, u32[]{:S(2)}) collective-permute-start(bf16[256,1664]{1,0:T(8,128)(2,1)} %pad_maximum_fusion.26), channel_id=1, source_target_pairs={{0,1},{1,0},{2,3},{3,2},{4,5},{5,4},{6,7},{7,6},{8,9},{9,8},{10,11... | collective-permute-start | bytes 2555912 | tf_op jit(solution)/shard_map/ppermute | solution.py:408
  748.7 65.7 %collective-permute-start.63 = (bf16[256,1664]{1,0:T(8,128)(2,1)}, bf16[256,1664]{1,0:T(8,128)(2,1)S(1)}, u32[]{:S(2)}, u32[]{:S(2)}) collective-permute-start(bf16[256,1664]{1,0:T(8,128)(2,1)} %pad_maximum_fusion.27), channel_id=1, source_target_pairs={{0,1},{1,0},{2,3},{3,2},{4,5},{5,4},{6,7},{7,6},{8,9},{9,8},{10,11... | collective-permute-start | bytes 2555912 | tf_op jit(solution)/shard_map/ppermute | solution.py:408
  804.8 35.8 %collective-permute-start.62 = (bf16[256,1664]{1,0:T(8,128)(2,1)}, bf16[256,1664]{1,0:T(8,128)(2,1)}, u32[]{:S(2)}, u32[]{:S(2)}) collective-permute-start(bf16[256,1664]{1,0:T(8,128)(2,1)} %add_convert_fusion.2), channel_id=1, source_target_pairs={{0,2},{1,3},{2,4},{3,5},{4,6},{5,7},{6,0},{7,1},{8,10},{9,11},{10,... | collective-permute-start | bytes 2555912 | tf_op jit(solution)/shard_map/ppermute | solution.py:408
  815.5 37.7 %collective-permute-start.64 = (bf16[256,1664]{1,0:T(8,128)(2,1)}, bf16[256,1664]{1,0:T(8,128)(2,1)}, u32[]{:S(2)}, u32[]{:S(2)}) collective-permute-start(bf16[256,1664]{1,0:T(8,128)(2,1)} %add_convert_fusion.1), channel_id=1, source_target_pairs={{0,6},{1,7},{2,0},{3,1},{4,2},{5,3},{6,4},{7,5},{8,14},{9,15},{10,... | collective-permute-start | bytes 2555912 | tf_op jit(solution)/shard_map/ppermute | solution.py:408
  817.4 64.0 %collective-permute-start.65 = (bf16[2,1024,2048]{2,1,0:T(8,128)(2,1)}, bf16[2,1024,2048]{2,1,0:T(8,128)(2,1)}, u32[]{:S(2)}, u32[]{:S(2)}) collective-permute-start(bf16[2,1024,2048]{2,1,0:T(8,128)(2,1)} %fusion.38), channel_id=1, source_target_pairs={{0,8},{1,9},{2,10},{3,11},{4,12},{5,13},{6,14},{7,15},{8,0},{9,1},... | collective-permute-start | bytes 25165832 | tf_op jit(solution)/shard_map/ppermute | solution.py:408
  853.1 74.9 %collective-permute-start.69 = (bf16[2,2048,1024]{2,1,0:T(8,128)(2,1)}, bf16[2,2048,1024]{2,1,0:T(8,128)(2,1)}, u32[]{:S(2)}, u32[]{:S(2)}) collective-permute-start(bf16[2,2048,1024]{2,1,0:T(8,128)(2,1)} %fusion.46), channel_id=1, source_target_pairs={{0,8},{1,9},{2,10},{3,11},{4,12},{5,13},{6,14},{7,15},{8,0},{9,1},... | collective-permute-start | bytes 25165832 | tf_op jit(solution)/shard_map/ppermute | solution.py:408
  876.0 76.5 %collective-permute-start.71 = (bf16[2,2048,1024]{2,1,0:T(8,128)(2,1)}, bf16[2,2048,1024]{2,1,0:T(8,128)(2,1)}, u32[]{:S(2)}, u32[]{:S(2)}) collective-permute-start(bf16[2,2048,1024]{2,1,0:T(8,128)(2,1)} %fusion.43.refs_0_), channel_id=1, source_target_pairs={{0,8},{1,9},{2,10},{3,11},{4,12},{5,13},{6,14},{7,15},{8,0},{9,1},... | collective-permute-start | bytes 25165832 | tf_op jit(solution)/shard_map/ppermute | solution.py:408
  (129 other events, 1841.3 us)
Sparse Core Ops, SparseCore 0:
  136.6 115.2 all-gather.2
  346.0 97.0 all-gather.4
  601.6 117.6 reduce-scatter.2
  749.9 90.1 reduce-scatter.4
